TPU v7x, 32 devices: a whole 2x2x4 slice. The times are simulated.
32 devices in a mesh: seq: 8 (over z, y), tp: 4 (over x, core).
Axes of the slice: x: 2, y: 2, z: 4, core: 2. Of those that a mesh axis runs over, the one named last changes fastest.
Arguments:
- tokens: bfloat16 [2, 4096, 512], P(None, ('seq', 'tp')), may hold values from -6 to 6
- cotangent: bfloat16 [2, 4096, 512], P(None, ('seq', 'tp')), may hold values from -6 to 6
- valid_lengths: int32 [2], replicated, may hold values from 1024 to 4096, as said below
- norm1_gain: float32 [512], replicated, may hold values from 0.25 to 1.75
- ema_rate: float32 [512, 16], replicated, may hold values from 0.00012207031 to 0.035
- ema_beta: float32 [512, 16], replicated, may hold values from -4 to 4
- ema_eta: float32 [512, 16], replicated, may hold values from -1.5 to 1.5
- ema_skip: float32 [512], replicated, may hold values from -4 to 4
- w_shared: bfloat16 [512, 128], replicated, may hold values from -0.25 to 0.25
- query_gain: float32 [128], replicated, may hold values from -2.5 to 2.5
- key_gain: float32 [128], replicated, may hold values from -2.5 to 2.5
- rel_bias: float32 [128], replicated, may hold values from -4 to 4
- w_value: bfloat16 [512, 1024], P(None, 'tp'), may hold values from -0.25 to 0.25
- w_reset: bfloat16 [512, 1024], P(None, 'tp'), may hold values from -0.25 to 0.25
- w_update: bfloat16 [512, 512], P('tp'), may hold values from -0.25 to 0.25
- w_hidden: bfloat16 [512, 512], P('tp'), may hold values from -0.25 to 0.25
- u_hidden: bfloat16 [1024, 512], P('tp'), may hold values from -0.5 to 0.5
- norm2_gain: float32 [512], replicated, may hold values from 0.25 to 1.75
- w_in: bfloat16 [512, 1024], P(None, 'tp'), may hold values from -0.25 to 0.25
- w_out: bfloat16 [1024, 512], P('tp'), may hold values from -0.1875 to 0.1875
Outputs:
- output: bfloat16 [2, 4096, 512], P(None, ('seq', 'tp'))
- grad_tokens: bfloat16 [2, 4096, 512], P(None, ('seq', 'tp'))
- grad_norm1_gain: float32 [512], replicated
- grad_ema_rate: float32 [512, 16], replicated
- grad_ema_beta: float32 [512, 16], replicated
- grad_ema_eta: float32 [512, 16], replicated
- grad_ema_skip: float32 [512], replicated
- grad_w_shared: float32 [512, 128], replicated
- grad_query_gain: float32 [128], replicated
- grad_key_gain: float32 [128], replicated
- grad_rel_bias: float32 [128], replicated
- grad_w_value: float32 [512, 1024], P(None, 'tp')
- grad_w_reset: float32 [512, 1024], P(None, 'tp')
- grad_w_update: float32 [512, 512], P('tp')
- grad_w_hidden: float32 [512, 512], P('tp')
- grad_u_hidden: float32 [1024, 512], P('tp')
- grad_norm2_gain: float32 [512], replicated
- grad_w_in: float32 [512, 1024], P(None, 'tp')
- grad_w_out: float32 [1024, 512], P('tp')
Inputs may be any that keep to these rules, and one draw needn't show every extreme that they name: `valid_lengths`: one length per sequence; at least one sequence, drawn from the seed, has all 4096 positions valid.
All inputs are finite; a program needn't handle non-finite values.
Results may differ from a plain program's by a relative error of at most 0.018.
The roundings to bfloat16 on the way count: a program that leaves them out, or rounds other values in their place, can miss the bound.
Values may be sent and summed in bfloat16 or wider, within the bound.
No kernel may reach another device: no remote copies, remote signals or barrier semaphores. Data moves between devices by JAX's collectives and lax.ppermute only.
A program may use at most 320 MiB of HBM per device.

v0:
```python
import jax
import jax.numpy as jnp
from jax import lax
from jax.sharding import PartitionSpec as P

Z = 128
NDIM = 16
CH = 128


highest = lax.Precision.HIGHEST
epsilon = 1e-05


def entering(value, axis, join, neutral):
    count, mine = (lax.axis_size(axis), lax.axis_index(axis))
    pieces = jax.tree.map(lambda part: lax.all_gather(part, axis), value)
    so_far = jax.tree.map(
        lambda part, zero: jnp.full_like(part, 0) + jnp.asarray(zero, part.dtype), value, neutral
    )

    def hop(position, so_far):
        longer = join(so_far, jax.tree.map(lambda part: part[position], pieces))
        return jax.tree.map(lambda new, old: jnp.where(position < mine, new, old), longer, so_far)

    return lax.fori_loop(0, count - 1, hop, so_far)


def carried_in(value, axis, join, neutral):
    count = lax.axis_size(axis)
    place = lax.axis_index(axis)
    ahead = count - 1 - place
    gathered = jax.tree.map(
        lambda a, kind: lax.all_gather(a.astype(kind), axis),
        value,
        jax.tree.map(lambda a: jnp.bfloat16 if a.dtype == jnp.float32 else a.dtype, value),
    )
    state = jax.tree.map(lambda a, e: jnp.zeros_like(a) + jnp.asarray(e, a.dtype), value, neutral)

    def one(hop, state):
        source = count - 1 - hop
        return join(
            state,
            jax.tree.map(
                lambda a, own: lax.dynamic_index_in_dim(a, source, 0, False).astype(own.dtype),
                gathered,
                value,
            ),
        )

    return lax.fori_loop(0, ahead, one, state)


def product(left, right, form):
    return jnp.einsum(form, left, right, preferred_element_type=jnp.float32)


def silu_slope(value):
    sigma = jax.nn.sigmoid(value)
    return sigma * (1.0 + value * (1.0 - sigma))


def layer_norm(rows, gain):
    center = rows - jnp.mean(rows, axis=-1, keepdims=True)
    spread = jnp.mean(center * center, axis=-1, keepdims=True)
    return center * lax.rsqrt(spread + epsilon) * gain


def ema_inflow(rate, beta):
    return jnp.sqrt(rate * (2.0 - rate)) * beta


def ema_within(values, rate, beta, eta, state):
    log_decay = jnp.log(1.0 - rate)
    inflow = ema_inflow(rate, beta)
    span = min(32, CH)
    seqs, length, width = values.shape
    count = length // span
    lags = jnp.arange(span, dtype=jnp.float32)
    powers = jnp.exp(lags[:, None, None] * log_decay[None])
    offset = lags[:, None] - lags[None, :]
    causal = offset >= 0.0
    lagged = jnp.exp(jnp.maximum(offset, 0.0)[:, :, None, None] * log_decay[None, None])
    toeplitz = jnp.where(
        causal[:, :, None], jnp.sum(lagged * (eta * inflow)[None, None], axis=3), 0.0
    )
    spans = values.reshape(seqs, count, span, width)
    inside = jnp.einsum("tsc,nksc->nktc", toeplitz, spans, precision=highest)
    end_weights = jnp.flip(powers, 0) * inflow[None]
    ends = jnp.einsum("scj,nksc->nkcj", end_weights, spans, precision=highest)
    step_power = jnp.exp(span * log_decay)
    starts = []
    for index in range(count):
        starts.append(state)
        state = step_power[None] * state + ends[:, index]
    starts = jnp.stack(starts, axis=1)
    carry_weights = powers * ((1.0 - rate) * eta)[None]
    carried = jnp.einsum("tcj,nkcj->nktc", carry_weights, starts, precision=highest)
    return (inside + carried).reshape(seqs, length, width)


def ema_end(values, rate, beta, state):
    log_decay = jnp.log(1.0 - rate)
    length = values.shape[1]
    lags = jnp.arange(length, dtype=jnp.float32)
    weights = (
        jnp.exp((length - 1.0 - lags)[:, None, None] * log_decay[None])
        * ema_inflow(rate, beta)[None]
    )
    ends = jnp.einsum("scj,nsc->ncj", weights, values, precision=highest)
    return jnp.exp(length * log_decay)[None] * state + ends


def link_states(earlier, later):
    return (earlier[0] * later[0], later[0][None] * earlier[1] + later[1])


def per_device(
    tokens,
    cotangent,
    valid_lengths,
    norm1_gain,
    ema_rate,
    ema_beta,
    ema_eta,
    ema_skip,
    w_shared,
    query_gain,
    key_gain,
    rel_bias,
    w_value,
    w_reset,
    w_update,
    w_hidden,
    u_hidden,
    norm2_gain,
    w_in,
    w_out,
):
    part = lax.axis_index("tp")
    place = lax.axis_index("seq")
    seqs, local_rows, width = tokens.shape
    block = local_rows * lax.axis_size("tp")
    narrow = w_update.shape[0]
    rows = tokens.astype(jnp.float32)
    normed, norm1_pull = jax.vjp(layer_norm, rows, norm1_gain)
    normed_low = normed.astype(jnp.bfloat16)
    normed_all = lax.all_gather(normed_low, "tp", axis=1, tiled=True)
    normed_f = normed_all.astype(jnp.float32)
    positions = place * block + jnp.arange(block)
    live = positions[None, :] < valid_lengths[:, None]
    local_positions = place * block + part * local_rows + jnp.arange(local_rows)
    live_local = local_positions[None, :] < valid_lengths[:, None]
    zero_state = jnp.zeros((seqs, width, NDIM), jnp.float32)
    block_power = jnp.exp(block * jnp.log(1.0 - ema_rate))
    local_end = ema_end(normed_f, ema_rate, ema_beta, zero_state)
    identity = (jnp.ones_like(block_power), jnp.zeros_like(local_end))
    state_in = entering((block_power, local_end), "seq", link_states, identity)[1]
    smooth, ema_pull = jax.vjp(ema_within, normed_f, ema_rate, ema_beta, ema_eta, state_in)
    skip_pre = smooth + ema_skip * normed_f
    mixed_low = jax.nn.silu(skip_pre).astype(jnp.bfloat16)
    shared_pre = product(mixed_low, w_shared, "nbd,dz->nbz")
    shared = jax.nn.silu(shared_pre)
    query = (shared * query_gain).astype(jnp.bfloat16)
    keys = (shared * key_gain).astype(jnp.bfloat16)
    value_pre = product(normed_all, w_value, "nbd,dv->nbv")
    values = jax.nn.silu(value_pre).astype(jnp.bfloat16)
    count = seqs * block // CH
    query_c = query.reshape(count, CH, -1)
    keys_c = keys.reshape(count, CH, -1)
    values_c = values.reshape(count, CH, -1)
    offset = jnp.arange(CH)[:, None] - jnp.arange(CH)[None, :]
    raw = product(query_c, keys_c, "ntz,nsz->nts") * Z ** (-0.5)
    scores = raw + rel_bias[jnp.clip(offset, 0, CH - 1)][None]
    live_c = live.reshape(count, CH)
    allowed = (offset >= 0)[None] & (live_c[:, None, :] | (offset == 0)[None])
    masked = jnp.where(allowed, scores, -1e30)
    top = jnp.max(masked, axis=-1, keepdims=True)
    weights = jnp.where(allowed, jnp.exp(masked - top), 0.0)
    prob = weights / jnp.sum(weights, axis=-1, keepdims=True)
    prob_low = prob.astype(jnp.bfloat16)
    attended_c = product(prob_low, values_c, "nts,nsv->ntv")
    attended = attended_c.reshape(seqs, block, -1)
    reset_pre = product(mixed_low, w_reset, "nbd,dv->nbv")
    reset = jax.nn.silu(reset_pre)
    gated = (reset * attended).astype(jnp.bfloat16)
    mixed_cols = lax.dynamic_slice_in_dim(mixed_low, part * narrow, narrow, 2)
    hidden_part = product(mixed_cols, w_hidden, "nbk,kd->nbd") + product(
        gated, u_hidden, "nbv,vd->nbd"
    )
    update_part = product(mixed_cols, w_update, "nbk,kd->nbd")
    hidden_pre, update_pre = (
        lax.psum_scatter(hidden_part, "tp", scatter_dimension=1, tiled=True),
        lax.psum_scatter(update_part, "tp", scatter_dimension=1, tiled=True),
    )
    candidate = jax.nn.silu(hidden_pre)
    update = jax.nn.sigmoid(update_pre)
    middle = rows + update * (candidate - rows)
    normed2, norm2_pull = jax.vjp(layer_norm, middle, norm2_gain)
    normed2_low = normed2.astype(jnp.bfloat16)
    live_grad_local = jnp.where(live_local[:, :, None], cotangent.astype(jnp.float32), 0.0)
    normed2_all, cot_all = (
        lax.all_gather(normed2_low, "tp", axis=1, tiled=True),
        lax.all_gather(cotangent, "tp", axis=1, tiled=True),
    )
    inner_pre = product(normed2_all, w_in, "nbd,df->nbf")
    inner_low = jax.nn.silu(inner_pre).astype(jnp.bfloat16)
    ffn_part = product(inner_low, w_out, "nbf,fd->nbd")
    output = middle + lax.psum_scatter(
        ffn_part.astype(jnp.bfloat16), "tp", scatter_dimension=1, tiled=True
    ).astype(jnp.float32)
    live_grad_all = jnp.where(live[:, :, None], cot_all, jnp.zeros_like(cot_all))
    grad_w_out = product(inner_low, live_grad_all, "nbf,nbd->fd")
    grad_inner = product(live_grad_all, w_out, "nbd,fd->nbf")
    grad_inner_pre = (grad_inner * silu_slope(inner_pre)).astype(jnp.bfloat16)
    grad_w_in = product(normed2_all, grad_inner_pre, "nbd,nbf->df")
    grad_normed2_part = product(grad_inner_pre, w_in, "nbf,df->nbd")
    grad_normed2 = lax.psum_scatter(grad_normed2_part, "tp", scatter_dimension=1, tiled=True)
    grad_middle_norm, grad_norm2_gain = norm2_pull(grad_normed2)
    grad_middle = live_grad_local + grad_middle_norm
    grad_hidden_pre = (grad_middle * update * silu_slope(hidden_pre)).astype(jnp.bfloat16)
    grad_update_pre = (grad_middle * (candidate - rows) * update * (1.0 - update)).astype(
        jnp.bfloat16
    )
    grad_rows_residual = grad_middle * (1.0 - update)
    grad_hidden_all, grad_update_all = (
        lax.all_gather(grad_hidden_pre, "tp", axis=1, tiled=True),
        lax.all_gather(grad_update_pre, "tp", axis=1, tiled=True),
    )
    grad_w_hidden = product(mixed_cols, grad_hidden_all, "nbk,nbd->kd")
    grad_w_update = product(mixed_cols, grad_update_all, "nbk,nbd->kd")
    grad_u_hidden = product(gated, grad_hidden_all, "nbv,nbd->vd")
    grad_gated = product(grad_hidden_all, u_hidden, "nbd,vd->nbv")
    grad_mixed_cols = product(grad_hidden_all, w_hidden, "nbd,kd->nbk") + product(
        grad_update_all, w_update, "nbd,kd->nbk"
    )
    grad_attended = (grad_gated * reset).astype(jnp.bfloat16)
    grad_reset_pre = (grad_gated * attended * silu_slope(reset_pre)).astype(jnp.bfloat16)
    grad_w_reset = product(mixed_low, grad_reset_pre, "nbd,nbv->dv")
    mixed_part = product(grad_reset_pre, w_reset, "nbv,dv->nbd")
    mixed_part = mixed_part + lax.dynamic_update_slice_in_dim(
        jnp.zeros_like(mixed_part), grad_mixed_cols, part * narrow, 2
    )
    grad_attended_c = grad_attended.reshape(count, CH, -1)
    grad_values = product(prob_low, grad_attended_c, "nts,ntv->nsv").reshape(seqs, block, -1)
    grad_value_pre = (grad_values * silu_slope(value_pre)).astype(jnp.bfloat16)
    grad_w_value = product(normed_all, grad_value_pre, "nbd,nbv->dv")
    normed_part = product(grad_value_pre, w_value, "nbv,dv->nbd")
    grad_prob = product(grad_attended_c, values_c, "ntv,nsv->nts")
    score_part = prob * (grad_prob - jnp.sum(prob * grad_prob, axis=-1, keepdims=True))
    score_sum, mixed_sum = lax.psum((score_part, mixed_part), "tp")
    score_low = score_sum.astype(jnp.bfloat16)
    totals = jnp.sum(score_low.astype(jnp.float32), axis=0)
    grad_rel_bias = jnp.sum(
        jnp.where(offset[:, :, None] == jnp.arange(CH)[None, None, :], totals[:, :, None], 0.0),
        axis=(0, 1),
    )
    grad_query = (product(score_low, keys_c, "nts,nsz->ntz") * Z ** (-0.5)).reshape(seqs, block, -1)
    grad_keys = (product(score_low, query_c, "nts,ntz->nsz") * Z ** (-0.5)).reshape(seqs, block, -1)
    grad_query_gain = jnp.sum(grad_query * shared, axis=(0, 1))
    grad_key_gain = jnp.sum(grad_keys * shared, axis=(0, 1))
    grad_shared_pre = (
        (grad_query * query_gain + grad_keys * key_gain) * silu_slope(shared_pre)
    ).astype(jnp.bfloat16)
    grad_w_shared = product(mixed_low, grad_shared_pre, "nbd,nbz->dz")
    grad_mixed = mixed_sum + product(grad_shared_pre, w_shared, "nbz,dz->nbd")
    grad_skip_pre = grad_mixed * silu_slope(skip_pre)
    grad_ema_skip = jnp.sum(grad_skip_pre * normed_f, axis=(0, 1))
    grad_values_a, grad_rate_a, grad_beta_a, grad_ema_eta, state_back = ema_pull(grad_skip_pre)
    identity_back = (jnp.ones_like(block_power), jnp.zeros_like(state_back))
    adjoint_out = carried_in((block_power, state_back), "seq", link_states, identity_back)[1]
    _, end_pull = jax.vjp(
        lambda source, rate, beta: ema_end(source, rate, beta, state_in),
        normed_f,
        ema_rate,
        ema_beta,
    )
    grad_values_b, grad_rate_b, grad_beta_b = end_pull(adjoint_out)
    grad_ema_rate = grad_rate_a + grad_rate_b
    grad_ema_beta = grad_beta_a + grad_beta_b
    grad_normed_full = grad_values_a + grad_values_b + grad_skip_pre * ema_skip
    grad_normed = lax.psum_scatter(
        normed_part.astype(jnp.bfloat16), "tp", scatter_dimension=1, tiled=True
    ).astype(jnp.float32)
    grad_normed = grad_normed + lax.dynamic_slice_in_dim(
        grad_normed_full, part * local_rows, local_rows, 1
    )
    grad_rows_norm, grad_norm1_gain = norm1_pull(grad_normed)
    grad_tokens = (grad_rows_residual + grad_rows_norm).astype(jnp.bfloat16)
    (
        grad_w_value,
        grad_w_reset,
        grad_w_update,
        grad_w_hidden,
        grad_u_hidden,
        grad_w_in,
        grad_w_out,
    ) = (
        lax.psum(grad_w_value.astype(jnp.bfloat16), "seq").astype(jnp.float32),
        lax.psum(grad_w_reset.astype(jnp.bfloat16), "seq").astype(jnp.float32),
        lax.psum(grad_w_update.astype(jnp.bfloat16), "seq").astype(jnp.float32),
        lax.psum(grad_w_hidden.astype(jnp.bfloat16), "seq").astype(jnp.float32),
        lax.psum(grad_u_hidden.astype(jnp.bfloat16), "seq").astype(jnp.float32),
        lax.psum(grad_w_in.astype(jnp.bfloat16), "seq").astype(jnp.float32),
        lax.psum(grad_w_out.astype(jnp.bfloat16), "seq").astype(jnp.float32),
    )
    first = (part == 0).astype(jnp.float32)
    (
        grad_norm1_gain,
        grad_ema_rate,
        grad_ema_beta,
        grad_ema_eta,
        grad_ema_skip,
        grad_w_shared,
        grad_query_gain,
        grad_key_gain,
        grad_rel_bias,
        grad_norm2_gain,
    ) = lax.psum(
        (
            grad_norm1_gain,
            grad_ema_rate * first,
            grad_ema_beta * first,
            grad_ema_eta * first,
            grad_ema_skip * first,
            grad_w_shared * first,
            grad_query_gain * first,
            grad_key_gain * first,
            grad_rel_bias * first,
            grad_norm2_gain,
        ),
        ("seq", "tp"),
    )
    return (
        output.astype(jnp.bfloat16),
        grad_tokens,
        grad_norm1_gain,
        grad_ema_rate,
        grad_ema_beta,
        grad_ema_eta,
        grad_ema_skip,
        grad_w_shared,
        grad_query_gain,
        grad_key_gain,
        grad_rel_bias,
        grad_w_value,
        grad_w_reset,
        grad_w_update,
        grad_w_hidden,
        grad_u_hidden,
        grad_norm2_gain,
        grad_w_in,
        grad_w_out,
    )


def solution(mesh):
    in_specs = (
        P(None, ("seq", "tp"), None),
        P(None, ("seq", "tp"), None),
        P(),
        P(),
        P(),
        P(),
        P(),
        P(),
        P(),
        P(),
        P(),
        P(),
        P(None, "tp"),
        P(None, "tp"),
        P("tp", None),
        P("tp", None),
        P("tp", None),
        P(),
        P(None, "tp"),
        P("tp", None),
    )
    out_specs = (
        P(None, ("seq", "tp"), None),
        P(None, ("seq", "tp"), None),
        P(),
        P(),
        P(),
        P(),
        P(),
        P(),
        P(),
        P(),
        P(),
        P(None, "tp"),
        P(None, "tp"),
        P("tp", None),
        P("tp", None),
        P("tp", None),
        P(),
        P(None, "tp"),
        P("tp", None),
    )
    return jax.shard_map(
        per_device, mesh=mesh, in_specs=in_specs, out_specs=out_specs, check_vma=False
    )
```

profile of v0, /device:TPU:0, one launch (start us, length us, event | category | flops | bytes accessed | tf_op | source)
XLA Modules:
  0.0 2000.0 jit_solution(62793426416362984)
XLA Ops:
  15.6 32.5 %all-gather = f32[4096,16]{0,1:T(8,128)S(1)} all-gather(f32[512,16]{0,1:T(8,128)S(1)} %get-tuple-element.522), channel_id=2, replica_groups=mesh['seq'=8,'tp'=4] {'seq'}, dimensions={0}, use_global_device_ids=true | all-gather | bytes 294912 | tf_op jit(solution)/shard_map/all_gather | solution.py:17
  52.5 7.2 rev.8
  60.3 9.5 multiply_reduce_fusion.2
  70.1 7.6 copy.669
  77.7 3.7 copy.568
  81.4 12.3 fusion.71
  93.8 31.3 %all-gather.1 = f32[16,512,16]{1,2,0:T(8,128)S(1)} all-gather(f32[2,512,16]{1,2,0:T(8,128)S(1)} %copy.569), channel_id=3, replica_groups=mesh['seq'=8,'tp'=4] {'seq'}, dimensions={0}, use_global_device_ids=true | all-gather | bytes 589824 | tf_op jit(solution)/shard_map/all_gather | solution.py:17
  125.2 7.3 while.29
  133.8 6.5 copy.563
  140.3 14.8 fusion.198
  155.1 6.0 fusion.40
  161.2 27.2 %fusion.194 = (f32[2,1,512,16]{3,1,0,2:T(1,128)S(1)}, f32[2,1,512,16]{3,1,0,2:T(1,128)S(1)}, f32[2,1,512,16]{3,1,0,2:T(1,128)S(1)}, f32[2,1,512,16]{3,1,0,2:T(1,...) fusion(f32[2,16,512,16]{3,1,0,2:T(8,128)} %fusion.40), kind=kLoop, calls=%fused_computation.379 | loop fusion | bytes 1966080 | tf_op jit(solution)/shard_map/jvp()/slice | solution.py:95
  213.2 12.2 copy.627
  225.4 20.0 %add_bitcast_fusion.2 = f32[2,16,32,512]{2,1,0,3:T(8,128)} fusion(f32[512,2,16,32]{3,2,1,0:T(8,128)} %fusion.198, f32[2,16,512,16]{1,3,0,2:T(8,128)} %copy.627, f32[512,16]{1,0:T(8,128)S(1)} %copy.592, f32[512,16]{1,0:T(8,128)S(1)} %copy.566), kind=kOutput, calls=%fused_computation.30 | convolution fusion | flops 101711872 | bytes 5308416 | tf_op jit(solution)/shard_map/jvp(tcj,nkcj->nktc)/dot_general | solution.py:98
  245.5 6.3 copy.594
  257.2 61.0 %copy.692 = f32[2,512,512]{0,2,1:T(8,128)} copy(f32[2,512,512]{2,1,0:T(8,128)} %fusion.149) | data formatting | bytes 4194304
  318.2 92.9 %reshape.639 = f32[512,1024]{1,0:T(8,128)} reshape(f32[512,512,2]{2,1,0:T(8,128)} %bitcast.129) | data formatting | bytes 4194304
  411.8 97.4 %gather_fusion = f32[16384]{0:T(1024)S(1)} fusion(f32[128]{0:T(128)S(1)} %copy-done.1, s32[16384]{0:T(1024)S(1)} %fusion.165), kind=kCustom, calls=%fused_computation | custom fusion | bytes 196608 | tf_op jit(solution)/shard_map/gather | solution.py:174
  520.2 60.4 %copy.694 = f32[2,512,512]{0,2,1:T(8,128)} copy(f32[2,512,512]{2,1,0:T(8,128)S(1)} %convolution_add_fusion) | data formatting | bytes 4194304
  580.6 92.9 %reshape.641 = f32[512,1024]{1,0:T(8,128)} reshape(f32[512,512,2]{2,1,0:T(8,128)} %bitcast.132) | data formatting | bytes 4194304
  673.6 35.6 %reshape.640 = f32[128,512,2]{2,1,0:T(8,128)} reshape(f32[128,1024]{1,0:T(8,128)} %reduce-scatter.16.cloned.1.call-done) | data formatting | bytes 1048576
  709.2 19.4 copy.596
  728.7 35.6 %reshape.642 = f32[128,512,2]{2,1,0:T(8,128)} reshape(f32[128,1024]{1,0:T(8,128)} %reduce-scatter.18.cloned.1.call-done) | data formatting | bytes 1048576
  764.4 19.5 copy.601
  786.1 17.2 all-gather.11.cloned.1.call-done
  805.0 16.5 all-gather.13.cloned.1.call-done
  824.7 60.6 %copy.698 = f32[2,512,512]{0,2,1:T(8,128)} copy(f32[2,512,512]{2,1,0:T(8,128)S(1)} %fusion.130) | data formatting | bytes 4194304
  885.3 92.9 %reshape.645 = f32[512,1024]{1,0:T(8,128)} reshape(f32[512,512,2]{2,1,0:T(8,128)} %bitcast.138) | data formatting | bytes 4194304
  978.4 31.4 %reduce-scatter.22.cloned.1.call-done = f32[128,1024]{1,0:T(8,128)} async-done(((f32[512,1024]{1,0:T(8,128)}), f32[128,1024]{1,0:T(8,128)}) %reduce-scatter.22.cloned.1.call-update) | async-done | bytes 524304
  1009.8 35.6 %reshape.646 = f32[128,512,2]{2,1,0:T(8,128)} reshape(f32[128,1024]{1,0:T(8,128)} %reduce-scatter.22.cloned.1.call-done) | data formatting | bytes 1048576
  1045.4 19.6 copy.605
  1070.0 42.9 %copy.696 = bf16[2,512,512]{0,2,1:T(8,128)(2,1)} copy(bf16[2,512,512]{2,1,0:T(8,128)(2,1)S(1)} %convolution_convert_fusion.1) | data formatting | bytes 2097152
  1113.0 97.8 %reshape.643 = bf16[512,1024]{1,0:T(8,128)(2,1)} reshape(bf16[512,512,2]{2,1,0:T(8,128)(2,1)} %bitcast.135) | data formatting | bytes 2097152
  1245.0 30.7 %all-gather.2 = bf16[4096,16]{0,1:T(8,128)(2,1)S(1)} all-gather(bf16[512,16]{0,1:T(8,128)(2,1)S(1)} %copy-done.109), channel_id=4, replica_groups=mesh['seq'=8,'tp'=4] {'seq'}, dimensions={0}, use_global_device_ids=true | all-gather | bytes 147456 | tf_op jit(solution)/shard_map/all_gather | solution.py:34
  1275.7 37.8 %reshape.644 = bf16[128,512,2]{2,1,0:T(8,128)(2,1)} reshape(bf16[128,1024]{1,0:T(8,128)(2,1)} %reduce-scatter.20.cloned.1.call-done) | data formatting | bytes 524288
  1313.5 14.8 copy.603
  1330.5 42.9 %copy.700 = bf16[2,512,512]{0,2,1:T(8,128)(2,1)} copy(bf16[2,512,512]{2,1,0:T(8,128)(2,1)S(1)} %convolution_convert_fusion) | data formatting | bytes 2097152
  1373.4 97.6 %reshape.647 = bf16[512,1024]{1,0:T(8,128)(2,1)} reshape(bf16[512,512,2]{2,1,0:T(8,128)(2,1)} %bitcast.141) | data formatting | bytes 2097152
  1471.0 16.4 all-reduce.30
  1492.2 6.4 select_reduce_fusion
  1503.4 4.7 fusion.46
  1508.1 8.4 copy.614
  1516.5 14.4 fusion.199
  1530.9 9.2 fusion.12
  1540.2 9.8 fusion.29
  1550.0 16.5 copy.734
  1578.7 8.1 multiply_reduce_fusion.16
  1586.8 4.7 multiply_reduce_fusion.4
  1591.5 5.3 multiply_add_fusion
  1597.0 30.8 %all_gather.48 = bf16[8,2,512,16]{2,3,1,0:T(8,128)(2,1)S(1)} all-gather(bf16[1,2,512,16]{2,3,1,0:T(8,128)(2,1)S(1)} %copy.622), channel_id=1, replica_groups=mesh['seq'=8,'tp'=4] {'seq'}, dimensions={0}, use_global_device_ids=true | all-gather | bytes 294912 | tf_op jit(solution)/shard_map/all_gather | solution.py:34
  1628.5 17.4 fusion.3
  1645.9 12.6 fusion.8
  1659.1 5.1 copy.633
  1664.3 11.3 multiply_reduce_fusion.1
  1701.1 8.8 add_bitcast_fusion.1
  1709.9 12.3 copy.629
  1722.2 12.6 fusion.19
  1734.8 18.7 add_bitcast_fusion
  1753.6 6.4 copy.620
  1762.9 7.2 rev.9
  1770.3 16.9 fusion.20
  1801.1 37.8 %reshape.648 = bf16[128,512,2]{2,1,0:T(8,128)(2,1)} reshape(bf16[128,1024]{1,0:T(8,128)(2,1)} %reduce-scatter.24.cloned.1.call-done) | data formatting | bytes 524288
  1839.1 13.9 copy.608
  1856.9 123.3 %all-reduce.27.cloned.1.call-done = (f32[512]{0:T(512)}, f32[512,16]{0,1:T(8,128)}, f32[512,16]{0,1:T(8,128)}, f32[512,16]{0,1:T(8,128)}, f32[512]{0:T(512)}, /*...) async-done(((f32[512]{0:T(512)}, f32[512,16]{0,1:T(8,128)}, f32[512,16]{0,1:T(8,128)}, f32[512,16]{0,1:T(8,128)}, f32[512]{0:T(512)}, /*index=5*/f32[128]{0:T(128)}, ...) | async-done | bytes 106000 | tf_op jit(solution)/shard_map/psum | solution.py:319
  (545 shorter events, 194.3 us)
Async XLA Ops:
  7.2 506.1 %copy-start = (bf16[512,256]{1,0:T(8,128)(2,1)S(1)}, bf16[512,256]{1,0:T(8,128)(2,1)}, u32[]{:S(2)}) copy-start(bf16[512,256]{1,0:T(8,128)(2,1)} %param.36) | copy-start | bytes 786436
  7.2 70.5 %all-gather.9.cloned.1.call-start = ((), (), s32[]{:S(2)}) async-start(), calls=%async_computation.5 | async-start | bytes 1310720 | tf_op jit(solution)/shard_map/all_gather | solution.py:148
  12.6 661.1 %reduce-scatter.16.cloned.1.call-start = ((), (), s32[]{:S(2)}) async-start(), calls=%async_computation.12 | async-start | bytes 2621440
  14.1 45.7 %copy-start.107 = (f32[512,16]{0,1:T(8,128)}, f32[512,16]{0,1:T(8,128)S(1)}, u32[]{:S(2)}) copy-start(f32[512,16]{0,1:T(8,128)S(1)} %get-tuple-element.524) | copy-start | bytes 98308
  14.1 45.7 %copy-start.119 = (f32[512,16]{0,1:T(8,128)}, f32[512,16]{0,1:T(8,128)S(1)}, u32[]{:S(2)}) copy-start(f32[512,16]{0,1:T(8,128)S(1)} %get-tuple-element.526) | copy-start | bytes 98308
  14.2 197.8 %copy-start.3 = (f32[512,16]{1,0:T(8,128)}, f32[512,16]{1,0:T(8,128)S(1)}, u32[]{:S(2)}) copy-start(f32[512,16]{1,0:T(8,128)S(1)} %copy.572) | copy-start | bytes 98308
  14.3 211.1 %copy-start.26 = (f32[512,16]{1,0:T(8,128)}, f32[512,16]{1,0:T(8,128)S(1)}, u32[]{:S(2)}) copy-start(f32[512,16]{1,0:T(8,128)S(1)} %copy.566) | copy-start | bytes 98308
  14.7 140.5 %copy-start.62 = (f32[512,16]{1,0:T(8,128)}, f32[512,16]{1,0:T(8,128)S(1)}, u32[]{:S(2)}) copy-start(f32[512,16]{1,0:T(8,128)S(1)} %copy.567) | copy-start | bytes 98308
  14.8 210.6 %copy-start.60 = (f32[512,16]{1,0:T(8,128)}, f32[512,16]{1,0:T(8,128)S(1)}, u32[]{:S(2)}) copy-start(f32[512,16]{1,0:T(8,128)S(1)} %copy.592) | copy-start | bytes 98308
  81.4 52.4 %copy-start.18 = (bf16[2,512,512]{2,1,0:T(8,128)(2,1)S(1)}, bf16[2,512,512]{2,1,0:T(8,128)(2,1)}, u32[]{:S(2)}) copy-start(bf16[2,512,512]{2,1,0:T(8,128)(2,1)} %all-gather.9.cloned.1.call-done) | copy-start | bytes 3145732
  132.5 22.6 %copy-start.64 = (f32[2,512,16]{1,2,0:T(8,128)}, f32[2,512,16]{1,2,0:T(8,128)S(1)}, u32[]{:S(2)}) copy-start(f32[2,512,16]{1,2,0:T(8,128)S(1)} %get-tuple-element.197) | copy-start | bytes 196612
  132.8 55.6 %copy-start.30 = (f32[2,512,16]{2,0,1:T(2,128)}, f32[2,512,16]{2,0,1:T(2,128)S(1)}, u32[]{:S(2)}) copy-start(f32[2,512,16]{2,0,1:T(2,128)S(1)} %copy.571) | copy-start | bytes 196612
  255.3 261.9 %copy-start.13 = (bf16[2,512,512]{2,1,0:T(8,128)(2,1)}, bf16[2,512,512]{2,1,0:T(8,128)(2,1)S(1)}, u32[]{:S(2)}) copy-start(bf16[2,512,512]{2,1,0:T(8,128)(2,1)S(1)} %get-tuple-element.507) | copy-start | bytes 3145732
  318.2 93.0 %copy-start.148 = (s32[2]{0:T(128)S(1)}, s32[2]{0:T(128)}, u32[]{:S(2)}) copy-start(s32[2]{0:T(128)} %param.26) | copy-start | bytes 28
  411.2 317.5 %reduce-scatter.18.cloned.1.call-start = ((), (), s32[]{:S(2)}) async-start(), calls=%async_computation.13 | async-start | bytes 2621440
  411.8 97.6 %copy-start.144 = (f32[128]{0:T(128)S(1)}, f32[128]{0:T(128)}, u32[]{:S(2)}) copy-start(f32[128]{0:T(128)} %param.34) | copy-start | bytes 1540
  411.8 97.6 %copy-start.146 = (f32[128]{0:T(128)S(1)}, f32[128]{0:T(128)}, u32[]{:S(2)}) copy-start(f32[128]{0:T(128)} %param.33) | copy-start | bytes 1540
  411.8 97.6 %copy-start.150 = (bf16[512,128]{1,0:T(8,128)(2,1)S(1)}, bf16[512,128]{1,0:T(8,128)(2,1)}, u32[]{:S(2)}) copy-start(bf16[512,128]{1,0:T(8,128)(2,1)} %param.32) | copy-start | bytes 393220
  673.5 129.8 %all-gather.11.cloned.1.call-start = ((), (), s32[]{:S(2)}) async-start(), calls=%async_computation.6 | async-start | bytes 1310720 | tf_op jit(solution)/shard_map/all_gather | solution.py:203
  728.7 55.2 %copy-start.23 = (f32[2,128,512]{2,1,0:T(8,128)}, f32[2,128,512]{2,1,0:T(8,128)S(1)}, u32[]{:S(2)}) copy-start(f32[2,128,512]{2,1,0:T(8,128)S(1)} %copy.596) | copy-start | bytes 1572868
  764.4 19.5 copy-start.11
  764.4 20.2 %copy-start.110 = (f32[512]{0:T(512)S(1)}, f32[512]{0:T(512)}, u32[]{:S(2)}) copy-start(f32[512]{0:T(512)} %param.41) | copy-start | bytes 6148
  764.4 39.0 %copy-start.79 = (bf16[512,256]{1,0:T(8,128)(2,1)S(1)}, bf16[512,256]{1,0:T(8,128)(2,1)}, u32[]{:S(2)}) copy-start(bf16[512,256]{1,0:T(8,128)(2,1)} %param.42) | copy-start | bytes 786436
  783.9 37.7 %copy-start.28 = (f32[2,128,512]{2,1,0:T(8,128)}, f32[2,128,512]{2,1,0:T(8,128)S(1)}, u32[]{:S(2)}) copy-start(f32[2,128,512]{2,1,0:T(8,128)S(1)} %copy.601) | copy-start | bytes 1572868
  784.3 281.8 %copy-start.9 = (f32[2,128,512]{2,1,0:T(8,128)}, f32[2,128,512]{2,1,0:T(8,128)S(1)}, u32[]{:S(2)}) copy-start(f32[2,128,512]{2,1,0:T(8,128)S(1)} %get-tuple-element.457) | copy-start | bytes 1572868
  784.3 281.8 %copy-start.112 = (f32[2,128]{1,0:T(2,128)}, f32[2,128]{1,0:T(2,128)S(1)}, u32[]{:S(2)}) copy-start(f32[2,128]{1,0:T(2,128)S(1)} %broadcast_multiply_fusion.3) | copy-start | bytes 3076
  784.5 281.5 %copy-start.122 = (f32[2,128]{1,0:T(2,128)}, f32[2,128]{1,0:T(2,128)S(1)}, u32[]{:S(2)}) copy-start(f32[2,128]{1,0:T(2,128)S(1)} %fusion.184) | copy-start | bytes 3076
  785.4 36.1 %all-gather.13.cloned.1.call-start = ((), (), s32[]{:S(2)}) async-start(), calls=%async_computation.7 | async-start | bytes 1310720 | tf_op jit(solution)/shard_map/all_gather | solution.py:204
  786.0 223.8 %reduce-scatter.22.cloned.1.call-start = ((), (), s32[]{:S(2)}) async-start(), calls=%async_computation.15 | async-start | bytes 2621440
  978.2 237.5 %all-gather.15.cloned.1.call-start = ((), (), s32[]{:S(2)}) async-start(), calls=%async_computation.8 | async-start | bytes 1310720 | tf_op jit(solution)/shard_map/all_gather | solution.py:227
  978.4 87.7 %copy-start.139 = (pred[2,128]{1,0:T(4,128)(4,1)}, pred[2,128]{1,0:T(4,128)(4,1)S(1)}, u32[]{:S(2)}) copy-start(pred[2,128]{1,0:T(4,128)(4,1)S(1)} %broadcast_compare_fusion.2) | copy-start | bytes 772
  1045.4 20.7 %copy-start.24 = (f32[2,128,512]{2,1,0:T(8,128)S(1)}, f32[2,128,512]{2,1,0:T(8,128)}, u32[]{:S(2)}) copy-start(f32[2,128,512]{2,1,0:T(8,128)} %copy-done.23) | copy-start | bytes 1572868
  1045.4 20.7 %copy-start.29 = (f32[2,128,512]{2,1,0:T(8,128)S(1)}, f32[2,128,512]{2,1,0:T(8,128)}, u32[]{:S(2)}) copy-start(f32[2,128,512]{2,1,0:T(8,128)} %copy-done.28) | copy-start | bytes 1572868
  1045.4 20.7 %copy-start.67 = (bf16[2,128,512]{2,1,0:T(8,128)(2,1)S(1)}, bf16[2,128,512]{2,1,0:T(8,128)(2,1)}, u32[]{:S(2)}) copy-start(bf16[2,128,512]{2,1,0:T(8,128)(2,1)} %param.25) | copy-start | bytes 786436
  1045.4 22.9 %copy-start.149 = (bf16[256,512]{1,0:T(8,128)(2,1)S(1)}, bf16[256,512]{1,0:T(8,128)(2,1)}, u32[]{:S(2)}) copy-start(bf16[256,512]{1,0:T(8,128)(2,1)} %param.43) | copy-start | bytes 786436
  1065.0 48.0 %copy-start.15 = (f32[2,128,512]{2,1,0:T(8,128)}, f32[2,128,512]{2,1,0:T(8,128)S(1)}, u32[]{:S(2)}) copy-start(f32[2,128,512]{2,1,0:T(8,128)S(1)} %copy.605) | copy-start | bytes 1572868
  1065.2 47.7 %copy-start.131 = (f32[2,128]{1,0:T(2,128)}, f32[2,128]{1,0:T(2,128)S(1)}, u32[]{:S(2)}) copy-start(f32[2,128]{1,0:T(2,128)S(1)} %multiply_multiply_fusion.3) | copy-start | bytes 3076
  1066.1 46.8 %copy-start.133 = (f32[2,128]{1,0:T(2,128)}, f32[2,128]{1,0:T(2,128)S(1)}, u32[]{:S(2)}) copy-start(f32[2,128]{1,0:T(2,128)S(1)} %negate_multiply_fusion.1) | copy-start | bytes 3076
  1067.5 161.6 %all-gather.17.cloned.1.call-start = ((), (), s32[]{:S(2)}) async-start(), calls=%async_computation.9 | async-start | bytes 1310720 | tf_op jit(solution)/shard_map/all_gather | solution.py:228
  1068.3 207.5 %reduce-scatter.20.cloned.1.call-start = ((), (), s32[]{:S(2)}) async-start(), calls=%async_computation.14 | async-start | bytes 1310720
  1112.9 97.9 %copy-start.78 = (f32[2,512,256]{2,1,0:T(8,128)S(1)}, f32[2,512,256]{2,1,0:T(8,128)}, u32[]{:S(2)}) copy-start(f32[2,512,256]{2,1,0:T(8,128)} %copy-done.77) | copy-start | bytes 3145732
  1113.0 100.5 %copy-start.76 = (bf16[2,512,512]{2,1,0:T(8,128)(2,1)S(1)}, bf16[2,512,512]{2,1,0:T(8,128)(2,1)}, u32[]{:S(2)}) copy-start(bf16[2,512,512]{2,1,0:T(8,128)(2,1)} %all-gather.11.cloned.1.call-done) | copy-start | bytes 3145732
  1210.8 292.6 %all-reduce.23.cloned.1.call-start = ((), (), s32[]{:S(2)}) async-start(), calls=%async_computation.10 | async-start | bytes 4194304 | tf_op jit(solution)/shard_map/psum | solution.py:251
  1232.4 556.5 %all-reduce.29.cloned.1.call-start = ((), (), s32[]{:S(2)}) async-start(), calls=%async_computation.18 | async-start | bytes 3145728 | tf_op jit(solution)/shard_map/psum | solution.py:299
  1244.2 556.9 %reduce-scatter.24.cloned.1.call-start = ((), (), s32[]{:S(2)}) async-start(), calls=%async_computation.16 | async-start | bytes 1310720
  1373.4 125.7 %copy-start.145 = (f32[128]{0:T(128)S(1)}, f32[128]{0:T(128)}, u32[]{:S(2)}) copy-start(f32[128]{0:T(128)} %param.34) | copy-start | bytes 1540
  1373.4 125.7 %copy-start.147 = (f32[128]{0:T(128)S(1)}, f32[128]{0:T(128)}, u32[]{:S(2)}) copy-start(f32[128]{0:T(128)} %param.33) | copy-start | bytes 1540
  1471.0 32.3 %copy-start.19 = (bf16[2,512,512]{2,1,0:T(8,128)(2,1)S(1)}, bf16[2,512,512]{2,1,0:T(8,128)(2,1)}, u32[]{:S(2)}) copy-start(bf16[2,512,512]{2,1,0:T(8,128)(2,1)} %all-gather.9.cloned.1.call-done) | copy-start | bytes 3145732
  1487.5 369.4 %all-reduce.25.cloned.1.call-start = ((), (), s32[]{:S(2)}) async-start(), calls=%async_computation.11 | async-start | bytes 524288 | tf_op jit(solution)/shard_map/psum | solution.py:319
  1503.1 477.1 %all-reduce.27.cloned.1.call-start = ((), (), s32[]{:S(2)}) async-start(), calls=%async_computation.17 | async-start | bytes 211968 | tf_op jit(solution)/shard_map/psum | solution.py:319
  1591.5 36.7 %copy-start.65 = (f32[2,512,16]{1,2,0:T(8,128)S(1)}, f32[2,512,16]{1,2,0:T(8,128)}, u32[]{:S(2)}) copy-start(f32[2,512,16]{1,2,0:T(8,128)} %copy-done.64) | copy-start | bytes 196612
  1591.5 37.0 %copy-start.63 = (f32[512,16]{1,0:T(8,128)S(1)}, f32[512,16]{1,0:T(8,128)}, u32[]{:S(2)}) copy-start(f32[512,16]{1,0:T(8,128)} %copy-done.62) | copy-start | bytes 98308
  1591.5 37.0 %copy-start.75 = (bf16[2,512,512]{1,0,2:T(2,128)(2,1)S(1)}, bf16[2,512,512]{1,0,2:T(2,128)(2,1)}, u32[]{:S(2)}) copy-start(bf16[2,512,512]{1,0,2:T(2,128)(2,1)} %copy.568) | copy-start | bytes 3145732
  1591.5 37.0 %copy-start.142 = (f32[512]{0:T(512)S(1)}, f32[512]{0:T(512)}, u32[]{:S(2)}) copy-start(f32[512]{0:T(512)} %copy-done.141) | copy-start | bytes 6148
  1770.1 17.9 copy-start.92
  1770.1 17.9 copy-start.93
  1770.1 17.9 copy-start.94
  1770.2 17.9 copy-start.95
  1770.2 17.9 copy-start.96
  1770.2 17.9 copy-start.97
  1770.2 17.9 copy-start.98
  1770.2 17.9 copy-start.99
  1770.2 17.9 copy-start.100
  1770.2 17.9 copy-start.101
  (105 other events, 1049.2 us)
Sparse Core Ops, SparseCore 0:
  12.7 19.4 all-gather.8
  411.3 32.5 reduce-scatter.15
  673.7 32.5 reduce-scatter.17
  785.5 17.8 all-gather.10
  804.8 16.7 all-gather.12
  978.3 31.4 reduce-scatter.21
  1067.6 16.7 all-gather.14
  1086.6 16.7 all-gather.16
  1210.9 24.8 reduce-scatter.19
  1238.0 51.3 all-reduce.22
  1294.3 91.8 all-reduce.28
  1487.6 24.9 reduce-scatter.23
  1518.1 124.9 all-reduce.24
  1855.6 124.5 all-reduce.26
where the time goes:
time: 2020 us; the launch traced here: 2000 us
  local copies, waits for them, and re-layouts  1300 us (64%)
  matrix products  216 us (11%)
  waiting for transfers between devices  190 us (9%)
  blocking collectives  142 us (7%)
  other arithmetic  134 us (7%)
    unnamed x337, local copies, waits for them, and re-layouts  947 us
    psum x2, waiting for transfers between devices, per_device(): lax.psum((grad_norm1_gain, grad_ema_rate * first, grad_ema_beta * first,...  123 us
    gather x2, local copies, waits for them, and re-layouts, per_device(): scores = raw + rel_bias[jnp.clip(offset, 0, CH - 1)][None]  97.4 us
    all_gather x2, blocking collectives, entering(): pieces = jax.tree.map(lambda part: lax.all_gather(part, axis), value)  63.9 us
    all_gather x2, blocking collectives, carried_in(): lax.all_gather(a.astype(kind), axis)  61.5 us
    dot_general x29, matrix products, product(): return jnp.einsum(form, left, right, preferred_element_type=jnp.float32)  49.4 us
    dot_general x3, matrix products, ema_within(): jnp.einsum('tcj,nkcj->nktc', carry_weights, starts, precision=highest)  46.8 us
    dot_general x3, matrix products, ema_end(): ends = jnp.einsum('scj,nsc->ncj', weights, values, precision=highest)  42.3 us
  transfers between devices with their start and end apart: 14, of which 4 were waited for; matrix products, arithmetic and copies ran while one was open for 53% of the time, Pallas kernels for 0%

commit v1 on v0

v1 whole, which is shorter than its diff:
```python
import functools

import jax
import jax.numpy as jnp
from jax import lax
from jax.experimental import pallas as pl
from jax.experimental.pallas import tpu as pltpu
from jax.sharding import PartitionSpec as P

D = 512
Z = 128
NDIM = 16
CH = 128
PIECE = 16
PIECES = CH // PIECE
LANES = 128
BLOCKS = D // LANES
EPS = 1e-05
F32 = jnp.float32
BF16 = jnp.bfloat16
SMALL_ROWS = 64

VMEM = pl.BlockSpec(memory_space=pltpu.VMEM)
SMEM = pl.BlockSpec(memory_space=pltpu.SMEM)
ANY = pl.BlockSpec(memory_space=pl.ANY)


def sigmoid(v):
    return 0.5 * jnp.tanh(0.5 * v) + 0.5


def silu(v):
    return v * sigmoid(v)


def silu_slope(v):
    s = sigmoid(v)
    return s * (1.0 + v * (1.0 - s))


def mm(a, b):
    return jnp.dot(a, b, preferred_element_type=F32)


def mm_nt(a, b):
    return lax.dot_general(a, b, (((1,), (1,)), ((), ())), preferred_element_type=F32)


def mm_tn(a, b):
    return lax.dot_general(a, b, (((0,), (0,)), ((), ())), preferred_element_type=F32)


def normalized(v):
    center = v - jnp.mean(v, axis=-1, keepdims=True)
    scale = lax.rsqrt(jnp.mean(center * center, axis=-1, keepdims=True) + EPS)
    return center * scale, scale


def norm_back(grad, xhat, scale, gain):
    full = grad * gain
    return scale * (
        full
        - jnp.mean(full, axis=-1, keepdims=True)
        - xhat * jnp.mean(full * xhat, axis=-1, keepdims=True)
    )


def rows_of(s):
    return pl.ds(s * CH, CH)


def lanes_of(i):
    return pl.ds(pl.multiple_of((i % BLOCKS) * LANES, LANES), LANES)


def spread(row):
    return jnp.broadcast_to(row, (PIECES, LANES))


def piece_rows(s, t):
    return pl.ds(s * CH + t, PIECES, stride=PIECE)


def put_rows(ref, rows, value):
    for b in range(BLOCKS):
        ref[b, rows, :] = value[:, b * LANES : (b + 1) * LANES]


def get_rows(ref, rows):
    return jnp.concatenate([ref[b, rows, :] for b in range(BLOCKS)], axis=1)


def call(body, out, scratch, operands, specs, name, flops=0, moved=0):
    return pl.pallas_call(
        body,
        out_shape=out,
        in_specs=specs,
        out_specs=jax.tree.map(lambda _: VMEM, out),
        scratch_shapes=scratch,
        name=name,
        cost_estimate=pl.CostEstimate(flops=flops, bytes_accessed=moved, transcendentals=0),
        compiler_params=pltpu.CompilerParams(vmem_limit_bytes=48 * 1024 * 1024),
    )(*operands)


def shape(dims, dtype=F32):
    return jax.ShapeDtypeStruct(dims, dtype)


def enter_kernel(seqs, tok, gain, rate, beta, eta, normed, par, before, ends, nf, tab):
    r = rate[...].T
    d = 1.0 - r
    par[0] = d
    par[1] = jnp.log(d)
    par[2] = jnp.sqrt(r * (2.0 - r)) * beta[...].T
    par[3] = eta[...].T
    d2 = d * d
    d4 = d2 * d2
    d8 = d4 * d4
    d15 = d8 * d4 * d2 * d
    q = d8 * d8
    tab[0] = q
    tab[1] = 16.0 * d15
    tab[2] = q * q
    tab[3] = 32.0 * q * d15
    tab[4] = q * q * q * q
    tab[5] = 64.0 * q * q * q * d15
    for s in range(seqs):
        xhat, _ = normalized(tok[s].astype(F32))
        low = (xhat * gain[...]).astype(BF16)
        normed[rows_of(s), :] = low
        put_rows(nf, rows_of(s), low.astype(F32))
    place = lax.broadcasted_iota(jnp.int32, (PIECES, LANES), 0)

    def body(i, carry):
        s = i // BLOCKS
        lane = lanes_of(i)
        xs = [nf[i % BLOCKS, piece_rows(s, t), :] for t in range(PIECE)]
        for j0 in range(0, NDIM, 8):
            ds = [spread(par[0, j0 + j : j0 + j + 1, lane]) for j in range(8)]
            st = [xs[0]] * 8
            ta = [jnp.zeros((PIECES, LANES), F32)] * 8
            for t in range(1, PIECE):
                for j in range(8):
                    ta[j] = ds[j] * ta[j] + st[j]
                    st[j] = ds[j] * st[j] + xs[t]
            for j in range(8):
                a, b = st[j], ta[j]
                for k, step in enumerate((1, 2, 4)):
                    qm = spread(tab[2 * k, j0 + j : j0 + j + 1, lane])
                    rm = spread(tab[2 * k + 1, j0 + j : j0 + j + 1, lane])
                    sa = jnp.where(place >= step, pltpu.roll(a, step, 0), 0.0)
                    sb = jnp.where(place >= step, pltpu.roll(b, step, 0), 0.0)
                    b = b + qm * sb + rm * sa
                    a = a + qm * sa
                before[0, s, j0 + j, :, lane] = jnp.where(place >= 1, pltpu.roll(a, 1, 0), 0.0)
                before[1, s, j0 + j, :, lane] = jnp.where(place >= 1, pltpu.roll(b, 1, 0), 0.0)
                ends[0, s, j0 + j : j0 + j + 1, lane] = a[PIECES - 1 :]
                ends[1, s, j0 + j : j0 + j + 1, lane] = b[PIECES - 1 :]
        return carry

    lax.fori_loop(0, seqs * BLOCKS, body, 0)


def piece_powers(par, pw):
    k = lax.broadcasted_iota(jnp.int32, (PIECES, D), 0).astype(F32) * PIECE
    for j in range(NDIM):
        pw[j] = jnp.exp(k * par[1, j : j + 1, :])


def mix_kernel(
    seqs, tp, levels, first_bit,
    ids, tok, normed, par, before, skip, wsh, qg, kg, rb, *refs,
):
    recvs, refs = refs[:levels], refs[levels:]
    w1s, refs = refs[:tp], refs[tp:]
    w2s, refs = refs[:tp], refs[tp:]
    (
        st_in, skip_pre, mixed, shared_pre, prob, values, value_pre, reset_pre, attended, gated,
        hidden_pre, update_pre, middle,
        w1, whu, uh, nf, sm, pw, sems,
    ) = refs
    vb = values.shape[2]
    nb = D // tp
    me = ids[0]
    place = ids[1]
    copies = []
    for r in range(tp):
        b = jnp.bitwise_xor(me, r)
        row = pl.ds(pl.multiple_of(b * nb, nb), nb)
        copies.append(pltpu.make_async_copy(w1s[r], w1.at[r], sems.at[4 * r]))
        copies.append(
            pltpu.make_async_copy(
                w2s[r].at[pl.ds(0, nb), :], whu.at[row, pl.ds(0, D)], sems.at[4 * r + 1]
            )
        )
        copies.append(
            pltpu.make_async_copy(
                w2s[r].at[pl.ds(nb, nb), :], whu.at[row, pl.ds(D, D)], sems.at[4 * r + 2]
            )
        )
        copies.append(
            pltpu.make_async_copy(w2s[r].at[pl.ds(2 * nb, vb), :], uh.at[r], sems.at[4 * r + 3])
        )
    for c in copies:
        c.start()
    put_rows(nf, slice(None), normed[...].astype(F32))
    piece_powers(par, pw)
    logd = par[1]
    dinv = 1.0 / par[0]
    for s in range(seqs):
        a = jnp.zeros((NDIM, D), F32)
        b = jnp.zeros((NDIM, D), F32)
        for k in range(levels):
            mine = jnp.bitwise_and(place, 1 << k) > 0
            off = jnp.bitwise_and(place, (1 << k) - 1).astype(F32) * float(CH)
            power = jnp.where(mine, jnp.exp(off * logd), 0.0)
            oa = recvs[k][0, s].astype(F32) * power
            b = b + recvs[k][1, s].astype(F32) * power + off * oa * dinv
            a = a + oa
        st_in[0, s] = a
        st_in[1, s] = b

    def ema(i, carry):
        s = i // BLOCKS
        lane = lanes_of(i)
        row = [pl.ds(j, 1) for j in range(NDIM)]
        ds = [spread(par[0, row[j], lane]) for j in range(NDIM)]
        ws = [spread(par[2, row[j], lane] * par[3, row[j], lane]) for j in range(NDIM)]
        st = [
            before[0, s, j, :, lane] + pw[j, :, lane] * st_in[0, s, row[j], lane]
            for j in range(NDIM)
        ]
        for t in range(PIECE):
            x = nf[i % BLOCKS, piece_rows(s, t), :]
            parts = [None, None]
            for j in range(NDIM):
                st[j] = ds[j] * st[j] + x
                term = ws[j] * st[j]
                parts[j % 2] = term if parts[j % 2] is None else parts[j % 2] + term
            sm[i % BLOCKS, piece_rows(s, t), :] = parts[0] + parts[1]
        return carry

    lax.fori_loop(0, seqs * BLOCKS, ema, 0)
    for s in range(seqs):
        pre = get_rows(sm, rows_of(s)) + skip[...] * get_rows(nf, rows_of(s))
        skip_pre[rows_of(s), :] = pre
        mixed[rows_of(s), :] = silu(pre).astype(BF16)
    sp = mm(mixed[...], wsh[...])
    shared_pre[...] = sp
    shared = silu(sp)
    query = (shared * qg[...]).astype(BF16)
    keys = (shared * kg[...]).astype(BF16)
    t_at = lax.broadcasted_iota(jnp.int32, (CH, CH), 0)
    s_at = lax.broadcasted_iota(jnp.int32, (CH, CH), 1)
    bias_t = jnp.broadcast_to(rb[...], (CH, CH))
    for bit in range(7):
        bias_t = jnp.where(
            jnp.bitwise_and(t_at, 1 << bit) > 0, pltpu.roll(bias_t, 1 << bit, 1), bias_t
        )
    bias = bias_t.T
    for s in range(seqs):
        raw = mm_nt(query[s * CH : (s + 1) * CH], keys[s * CH : (s + 1) * CH]) * Z ** (-0.5)
        live = (place * CH + s_at) < ids[2 + s]
        allowed = (s_at <= t_at) & (live | (s_at == t_at))
        masked = jnp.where(allowed, raw + bias, -1e30)
        top = jnp.max(masked, axis=-1, keepdims=True)
        weights = jnp.where(allowed, jnp.exp(masked - top), 0.0)
        prob[s] = weights / jnp.sum(weights, axis=-1, keepdims=True)
    for c in copies:
        c.wait()
    hu = mm(mixed[...], whu[...])
    hidden_pre[...] = hu[:, :D]
    update_pre[...] = hu[:, D:]

    def block(r, carry):
        vp = mm(normed[...], w1[r, :, :vb])
        value_pre[r] = vp
        v = silu(vp).astype(BF16)
        values[r] = v
        rp = mm(mixed[...], w1[r, :, vb:])
        reset_pre[r] = rp
        gate = silu(rp)
        for s in range(seqs):
            att = mm(prob[s].astype(BF16), v[s * CH : (s + 1) * CH])
            attended[r, rows_of(s), :] = att
            gated[r, rows_of(s), :] = (gate[s * CH : (s + 1) * CH] * att).astype(BF16)
        hidden_pre[...] += mm(gated[r], uh[r])
        return carry

    lax.fori_loop(0, tp, block, 0)
    for s in range(seqs):
        x = tok[s].astype(F32)
        middle[rows_of(s), :] = x + sigmoid(update_pre[rows_of(s), :]) * (
            silu(hidden_pre[rows_of(s), :]) - x
        )


def ffn_kernel(seqs, tp, ids, tok, cot, middle, hidden_pre, update_pre, gain2, *refs):
    w3s, refs = refs[:tp], refs[tp:]
    (
        out, keep, send, grad_hu, resid, grad_gain2,
        wi, wo, n2, lg, acc, gn2, sems,
    ) = refs
    vb = wi.shape[2]
    cuts = D // vb
    copies = []
    for r in range(tp):
        copies.append(
            pltpu.make_async_copy(
                w3s[r].at[:, pl.ds(0, vb)], wi.at[r], sems.at[r * (cuts + 1)]
            )
        )
        for k in range(cuts):
            copies.append(
                pltpu.make_async_copy(
                    w3s[r].at[pl.ds(k * vb, vb), pl.ds(vb, vb)],
                    wo.at[r, :, pl.ds(k * vb, vb)],
                    sems.at[r * (cuts + 1) + 1 + k],
                )
            )
    for c in copies:
        c.start()
    place = ids[1]
    xhat, scale = normalized(middle[...])
    n2[...] = (xhat * gain2[...]).astype(BF16)
    at = lax.broadcasted_iota(jnp.int32, (CH, D), 0) + place * CH
    for s in range(seqs):
        lg[rows_of(s), :] = jnp.where(at < ids[2 + s], cot[s].astype(F32), 0.0).astype(BF16)
    acc[...] = jnp.zeros_like(acc)
    gn2[...] = jnp.zeros_like(gn2)
    for c in copies:
        c.wait()

    def block(h, carry):
        for odd in range(2):
            r = 2 * h + odd
            grads = (keep, send)[odd]
            pre = mm(n2[...], wi[r])
            inner = silu(pre).astype(BF16)
            acc[...] += mm(inner, wo[r])
            gip = (mm_nt(lg[...], wo[r]) * silu_slope(pre)).astype(BF16)
            gn2[...] += mm_nt(gip, wi[r])
            grads[h, :, :vb] = mm_tn(n2[...], gip).astype(BF16)
            gwo = mm_tn(inner, lg[...]).astype(BF16)
            for k in range(cuts):
                grads[h, k * vb : (k + 1) * vb, vb:] = gwo[:, k * vb : (k + 1) * vb]
        return carry

    lax.fori_loop(0, tp // 2, block, 0)
    mid = middle[...]
    out[...] = (mid + acc[...]).astype(BF16)
    grad = gn2[...]
    grad_gain2[...] = jnp.sum(grad * xhat, axis=0, keepdims=True)
    gm = lg[...].astype(F32) + norm_back(grad, xhat, scale, gain2[...])
    for s in range(seqs):
        x = tok[s].astype(F32)
        g = gm[s * CH : (s + 1) * CH]
        hp = hidden_pre[rows_of(s), :]
        update = sigmoid(update_pre[rows_of(s), :])
        grad_hu[rows_of(s), :D] = (g * update * silu_slope(hp)).astype(BF16)
        grad_hu[rows_of(s), D:] = (g * (silu(hp) - x) * update * (1.0 - update)).astype(BF16)
        resid[rows_of(s), :] = g * (1.0 - update)


def back_kernel(
    seqs, tp,
    ids, normed, mixed, skip_pre, shared_pre, prob, values, value_pre, reset_pre, attended, gated,
    grad_hu, par, wsh, qg, kg, *refs,
):
    w1s, refs = refs[:tp], refs[tp:]
    w2s, refs = refs[:tp], refs[tp:]
    (
        keep2, send2, keep1, send1, grad_skip, grad_normed, after, ends, grad_wsh, misc,
        w1, whu, uh, ghu, gm, gp, tab, sems,
    ) = refs
    vb = values.shape[2]
    nb = D // tp
    me = ids[0]
    copies = []
    for r in range(tp):
        b = jnp.bitwise_xor(me, r)
        row = pl.ds(pl.multiple_of(b * nb, nb), nb)
        copies.append(pltpu.make_async_copy(w1s[r], w1.at[r], sems.at[4 * r]))
        copies.append(
            pltpu.make_async_copy(
                w2s[r].at[pl.ds(0, nb), :], whu.at[row, pl.ds(0, D)], sems.at[4 * r + 1]
            )
        )
        copies.append(
            pltpu.make_async_copy(
                w2s[r].at[pl.ds(nb, nb), :], whu.at[row, pl.ds(D, D)], sems.at[4 * r + 2]
            )
        )
        copies.append(
            pltpu.make_async_copy(w2s[r].at[pl.ds(2 * nb, vb), :], uh.at[r], sems.at[4 * r + 3])
        )
    for c in copies:
        c.start()
    ghu[...] = mm_tn(mixed[...], grad_hu[...])
    gp[...] = jnp.zeros_like(gp)
    grad_normed[...] = jnp.zeros_like(grad_normed)
    for c in copies:
        c.wait()
    gm[...] = mm_nt(grad_hu[...], whu[...])

    def block(h, carry):
        for odd in range(2):
            r = 2 * h + odd
            g1 = (keep1, send1)[odd]
            g2 = (keep2, send2)[odd]
            row = pl.ds(pl.multiple_of(jnp.bitwise_xor(me, r) * nb, nb), nb)
            g2[h, pl.ds(0, nb), :] = ghu[row, pl.ds(0, D)].astype(BF16)
            g2[h, pl.ds(nb, nb), :] = ghu[row, pl.ds(D, D)].astype(BF16)
            ghp = grad_hu[:, :D]
            g2[h, pl.ds(2 * nb, vb), :] = mm_tn(gated[r], ghp).astype(BF16)
            gg = mm_nt(ghp, uh[r])
            rp = reset_pre[r]
            sig = sigmoid(rp)
            ga = (gg * (rp * sig)).astype(BF16)
            grp = (gg * attended[r] * (sig * (1.0 + rp * (1.0 - sig)))).astype(BF16)
            g1[h, :, vb:] = mm_tn(mixed[...], grp).astype(BF16)
            gm[...] += mm_nt(grp, w1[r, :, vb:])
            gvs = []
            for s in range(seqs):
                part = ga[s * CH : (s + 1) * CH]
                gvs.append(mm_tn(prob[s].astype(BF16), part))
                gp[s] += mm_nt(part, values[r, rows_of(s), :])
            gv = jnp.concatenate(gvs, axis=0) if seqs > 1 else gvs[0]
            gvp = (gv * silu_slope(value_pre[r])).astype(BF16)
            g1[h, :, :vb] = mm_tn(normed[...], gvp).astype(BF16)
            grad_normed[...] += mm_nt(gvp, w1[r, :, :vb])
        return carry

    lax.fori_loop(0, tp // 2, block, 0)
    sp = shared_pre[...]
    shared = silu(sp)
    query = (shared * qg[...]).astype(BF16)
    keys = (shared * kg[...]).astype(BF16)
    total = jnp.zeros((CH, CH), F32)
    gqs = []
    gks = []
    for s in range(seqs):
        pr = prob[s]
        low = (pr * (gp[s] - jnp.sum(pr * gp[s], axis=-1, keepdims=True))).astype(BF16)
        total = total + low.astype(F32)
        gqs.append(mm(low, keys[s * CH : (s + 1) * CH]) * Z ** (-0.5))
        gks.append(mm_tn(low, query[s * CH : (s + 1) * CH]) * Z ** (-0.5))
    gq = jnp.concatenate(gqs, axis=0) if seqs > 1 else gqs[0]
    gk = jnp.concatenate(gks, axis=0) if seqs > 1 else gks[0]
    turned = total.T
    s_at = lax.broadcasted_iota(jnp.int32, (CH, CH), 0)
    for bit in range(7):
        turned = jnp.where(
            jnp.bitwise_and(s_at, 1 << bit) > 0, pltpu.roll(turned, CH - (1 << bit), 1), turned
        )
    misc[...] = jnp.concatenate(
        [
            jnp.sum(gq * shared, axis=0, keepdims=True),
            jnp.sum(gk * shared, axis=0, keepdims=True),
            jnp.sum(turned, axis=0, keepdims=True),
            jnp.zeros((1, D - 3 * Z), F32),
        ],
        axis=1,
    )
    gsp = ((gq * qg[...] + gk * kg[...]) * silu_slope(sp)).astype(BF16)
    grad_wsh[...] = mm_tn(mixed[...], gsp)
    put_rows(
        grad_skip,
        slice(None),
        (gm[...] + mm_nt(gsp, wsh[...])) * silu_slope(skip_pre[...]),
    )
    d = par[0]
    d2 = d * d
    d4 = d2 * d2
    d8 = d4 * d4
    q = d8 * d8
    tab[0] = q
    tab[1] = q * q
    tab[2] = q * q * q * q
    place = lax.broadcasted_iota(jnp.int32, (PIECES, LANES), 0)

    def body(i, carry):
        s = i // BLOCKS
        lane = lanes_of(i)
        ds = [spread(par[0, j : j + 1, lane]) for j in range(NDIM)]
        ad = [grad_skip[i % BLOCKS, piece_rows(s, PIECE - 1), :]] * NDIM
        for t in range(PIECE - 2, -1, -1):
            g = grad_skip[i % BLOCKS, piece_rows(s, t), :]
            for j in range(NDIM):
                ad[j] = ds[j] * ad[j] + g
        for j in range(NDIM):
            a = ad[j]
            for k, step in enumerate((1, 2, 4)):
                qm = spread(tab[k, j : j + 1, lane])
                a = a + qm * jnp.where(place < PIECES - step, pltpu.roll(a, PIECES - step, 0), 0.0)
            after[s, j, :, lane] = jnp.where(
                place < PIECES - 1, pltpu.roll(a, PIECES - 1, 0), 0.0
            )
            ends[s, j : j + 1, lane] = a[:1]
        return carry

    lax.fori_loop(0, seqs * BLOCKS, body, 0)


def sums_kernel(
    seqs,
    tok, normed, grad_skip, grad_normed, par, before, st_in, after, skip, gain2_row, misc,
    local, small, nf, pw,
):
    put_rows(nf, slice(None), normed[...].astype(F32))
    piece_powers(par, pw)
    small[...] = jnp.zeros_like(small)

    def body(i, carry):
        s = i // BLOCKS
        lane = lanes_of(i)
        k16 = lax.broadcasted_iota(jnp.int32, (PIECES, LANES), 0).astype(F32) * PIECE
        for j0 in range(0, NDIM, 8):
            row = [pl.ds(j0 + j, 1) for j in range(8)]
            ds = [spread(par[0, row[j], lane]) for j in range(8)]
            st, ta, q, r = [], [], [], []
            for j in range(8):
                e = pw[j0 + j, :, lane] * st_in[0, s, row[j], lane]
                st.append(before[0, s, j0 + j, :, lane] + e)
                ta.append(
                    before[1, s, j0 + j, :, lane]
                    + pw[j0 + j, :, lane] * st_in[1, s, row[j], lane]
                    + k16 * e / ds[j]
                )
                q.append(jnp.zeros((PIECES, LANES), F32))
                r.append(jnp.zeros((PIECES, LANES), F32))
            for t in range(PIECE):
                x = nf[i % BLOCKS, piece_rows(s, t), :]
                g = grad_skip[i % BLOCKS, piece_rows(s, t), :]
                for j in range(8):
                    ta[j] = ds[j] * ta[j] + st[j]
                    st[j] = ds[j] * st[j] + x
                    q[j] = q[j] + g * st[j]
                    r[j] = r[j] + g * ta[j]
            for j in range(8):
                small[pl.ds(j0 + j, 1), lane] += jnp.sum(q[j], axis=0, keepdims=True)
                small[pl.ds(NDIM + j0 + j, 1), lane] += jnp.sum(r[j], axis=0, keepdims=True)
        ds = [spread(par[0, pl.ds(j, 1), lane]) for j in range(NDIM)]
        ws = [
            spread(par[2, pl.ds(j, 1), lane] * par[3, pl.ds(j, 1), lane]) for j in range(NDIM)
        ]
        ad = [after[s, j, :, lane] for j in range(NDIM)]
        for t in range(PIECE - 1, -1, -1):
            g = grad_skip[i % BLOCKS, piece_rows(s, t), :]
            parts = [None, None]
            for j in range(NDIM):
                ad[j] = ds[j] * ad[j] + g
                term = ws[j] * ad[j]
                parts[j % 2] = term if parts[j % 2] is None else parts[j % 2] + term
            local[i % BLOCKS, piece_rows(s, t), :] = parts[0] + parts[1]
        return carry

    lax.fori_loop(0, seqs * BLOCKS, body, 0)
    gsk = jnp.zeros((1, D), F32)
    gn1 = jnp.zeros((1, D), F32)
    for s in range(seqs):
        xhat, _ = normalized(tok[s].astype(F32))
        g = get_rows(grad_skip, rows_of(s))
        direct = g * skip[...] + grad_normed[rows_of(s), :]
        gsk = gsk + jnp.sum(g * get_rows(nf, rows_of(s)), axis=0, keepdims=True)
        gn1 = gn1 + jnp.sum(direct * xhat, axis=0, keepdims=True)
        put_rows(local, rows_of(s), get_rows(local, rows_of(s)) + direct)
    small[2 * NDIM : 2 * NDIM + 1, :] = gsk
    small[2 * NDIM + 1 : 2 * NDIM + 2, :] = gn1
    small[2 * NDIM + 2 : 2 * NDIM + 3, :] = gain2_row[...]
    small[2 * NDIM + 3 : 2 * NDIM + 4, :] = misc[...]


def leave_kernel(seqs, levels, ids, tok, par, local, resid, gain, *refs):
    recvs, refs = refs[:levels], refs[levels:]
    grad_tokens, ad_in, pw, sm = refs
    place = ids[1]
    logd = par[1]
    w = par[2] * par[3]
    for s in range(seqs):
        a = jnp.zeros((NDIM, D), F32)
        for k in range(levels):
            low = jnp.bitwise_and(place, 1 << k) == 0
            off = jnp.bitwise_and(place, (1 << k) - 1)
            away = ((1 << k) - 1 - off).astype(F32) * float(CH)
            a = a + recvs[k][s].astype(F32) * jnp.where(low, jnp.exp(away * logd), 0.0)
        ad_in[s] = a * w
    k = (PIECES - 1 - lax.broadcasted_iota(jnp.int32, (PIECES, D), 0)).astype(F32) * PIECE
    for j in range(NDIM):
        pw[j] = jnp.exp(k * par[1, j : j + 1, :])

    def body(i, carry):
        s = i // BLOCKS
        lane = lanes_of(i)
        ds = [spread(par[0, pl.ds(j, 1), lane]) for j in range(NDIM)]
        ad = [pw[j, :, lane] * ad_in[s, pl.ds(j, 1), lane] for j in range(NDIM)]
        for t in range(PIECE - 1, -1, -1):
            parts = [None, None]
            for j in range(NDIM):
                ad[j] = ds[j] * ad[j]
                parts[j % 2] = ad[j] if parts[j % 2] is None else parts[j % 2] + ad[j]
            sm[i % BLOCKS, piece_rows(s, t), :] = parts[0] + parts[1]
        return carry

    lax.fori_loop(0, seqs * BLOCKS, body, 0)
    for s in range(seqs):
        xhat, scale = normalized(tok[s].astype(F32))
        grad = get_rows(local, rows_of(s)) + get_rows(sm, rows_of(s))
        grad_tokens[s] = (
            resid[rows_of(s), :] + norm_back(grad, xhat, scale, gain[...])
        ).astype(BF16)


def swap(value, axis, bit):
    count = lax.axis_size(axis)
    return lax.ppermute(value, axis, [(i, i ^ bit) for i in range(count)])


def bits_of(count):
    return [1 << k for k in range(count.bit_length() - 1)]


def has(index, bit):
    return jnp.bitwise_and(index, bit) > 0


def gathered(own, tp):
    pieces = {0: own}
    for bit in reversed(bits_of(tp)):
        for r in list(pieces):
            pieces[r ^ bit] = swap(pieces[r], "tp", bit)
    return [pieces[r] for r in range(tp)]


def add_low(a, b):
    return (a.astype(F32) + b.astype(F32)).astype(BF16)


def half_of(value, upper):
    half = value.shape[0] // 2
    return lax.dynamic_slice_in_dim(value, jnp.where(upper, half, 0), half, 0)


def joined(mine, other, upper):
    return jnp.where(
        upper,
        jnp.concatenate([other, mine], axis=0),
        jnp.concatenate([mine, other], axis=0),
    )


def summed(keep, send, tp, seq, place):
    total = add_low(keep, swap(send, "tp", 1))
    for bit in reversed(bits_of(tp)[1:]):
        half = total.shape[0] // 2
        total = add_low(total[:half], swap(total[half:], "tp", bit))
    total = total[0]
    for bit in bits_of(seq):
        upper = has(place, bit)
        other = swap(half_of(total, ~upper), "seq", bit)
        total = add_low(half_of(total, upper), other)
    for bit in reversed(bits_of(seq)):
        total = joined(total, swap(total, "seq", bit), has(place, bit))
    return total


def per_device(
    tokens,
    cotangent,
    valid_lengths,
    norm1_gain,
    ema_rate,
    ema_beta,
    ema_eta,
    ema_skip,
    w_shared,
    query_gain,
    key_gain,
    rel_bias,
    w_value,
    w_reset,
    w_update,
    w_hidden,
    u_hidden,
    norm2_gain,
    w_in,
    w_out,
):
    part = lax.axis_index("tp")
    place = lax.axis_index("seq")
    tp = lax.axis_size("tp")
    seq = lax.axis_size("seq")
    all_seqs, local_rows, _ = tokens.shape
    vb = w_value.shape[1]
    nb = D // tp
    index = place * tp + part
    traded = local_rows < CH
    lower = part % 2 == 0

    def trade(value):
        if not traded:
            return value
        other = swap(jnp.where(lower, value[1], value[0]), "tp", 1)
        mine = jnp.where(lower, value[0], value[1])
        return joined(mine, other, ~lower)[None]

    def trade_back(value):
        if not traded:
            return value
        first, second = value[0, :local_rows], value[0, local_rows:]
        other = swap(jnp.where(lower, second, first), "tp", 1)
        mine = jnp.where(lower, first, second)
        return jnp.where(lower, jnp.stack([mine, other]), jnp.stack([other, mine]))

    if traded:
        assert all_seqs == 2 and 2 * local_rows == CH
        seqs = 1
        stretch = index // 2
        lengths = jnp.where(lower, valid_lengths[0], valid_lengths[1])[None]
    else:
        assert local_rows == CH
        seqs = all_seqs
        stretch = index
        lengths = valid_lengths
    rows = seqs * CH
    ids = jnp.concatenate([jnp.stack([part, stretch]), lengths]).astype(jnp.int32)
    scan_bits = [("tp", b) for b in bits_of(tp)[int(traded) :]] + [
        ("seq", b) for b in bits_of(seq)
    ]
    levels = len(scan_bits)

    pack1 = jnp.concatenate([w_value, w_reset], axis=1)
    pack2 = jnp.concatenate([w_hidden, w_update, u_hidden], axis=0)
    pack3 = jnp.concatenate(
        [w_in, jnp.concatenate([w_out[:, k * vb : (k + 1) * vb] for k in range(D // vb)], axis=0)],
        axis=1,
    )
    w1 = gathered(pack1, tp)
    w2 = gathered(pack2, tp)
    w3 = gathered(pack3, tp)

    tok = trade(tokens)
    cot = trade(cotangent)
    gain1 = norm1_gain[None]
    gain2 = norm2_gain[None]
    skip = ema_skip[None]
    qg, kg, rb = query_gain[None], key_gain[None], rel_bias[None]

    normed, par, before, ends = call(
        functools.partial(enter_kernel, seqs),
        (
            shape((rows, D), BF16),
            shape((4, NDIM, D)),
            shape((2, seqs, NDIM, PIECES, D)),
            shape((2, seqs, NDIM, D)),
        ),
        [pltpu.VMEM((BLOCKS, rows, LANES), F32), pltpu.VMEM((6, NDIM, D), F32)],
        (tok, gain1, ema_rate, ema_beta, ema_eta),
        [VMEM] * 5,
        "enter",
        flops=20_000_000,
        moved=2_000_000,
    )

    logd = par[1]
    state = ends
    recvs = []
    for k, (axis, bit) in enumerate(scan_bits):
        other = swap(state.astype(BF16), axis, bit)
        recvs.append(other)
        if k + 1 < levels:
            upper = has(stretch, 1 << k)
            other = other.astype(F32)
            early = jnp.where(upper, other, state)
            late = jnp.where(upper, state, other)
            span = float(CH << k)
            power = jnp.exp(span * logd)
            slope = span * jnp.exp((span - 1.0) * logd)
            state = jnp.stack(
                [
                    power * early[0] + late[0],
                    power * early[1] + slope * early[0] + late[1],
                ]
            )

    (
        st_in, skip_pre, mixed, shared_pre, prob, values, value_pre, reset_pre, attended, gated,
        hidden_pre, update_pre, middle,
    ) = call(
        functools.partial(mix_kernel, seqs, tp, levels, 0),
        (
            shape((2, seqs, NDIM, D)),
            shape((rows, D)),
            shape((rows, D), BF16),
            shape((rows, Z)),
            shape((seqs, CH, CH)),
            shape((tp, rows, vb), BF16),
            shape((tp, rows, vb)),
            shape((tp, rows, vb)),
            shape((tp, rows, vb)),
            shape((tp, rows, vb), BF16),
            shape((rows, D)),
            shape((rows, D)),
            shape((rows, D)),
        ),
        [
            pltpu.VMEM((tp, D, 2 * vb), BF16),
            pltpu.VMEM((D, 2 * D), BF16),
            pltpu.VMEM((tp, vb, D), BF16),
            pltpu.VMEM((BLOCKS, rows, LANES), F32),
            pltpu.VMEM((BLOCKS, rows, LANES), F32),
            pltpu.VMEM((NDIM, PIECES, D), F32),
            pltpu.SemaphoreType.DMA((4 * tp,)),
        ],
        (ids, tok, normed, par, before, skip, w_shared, qg, kg, rb, *recvs, *w1, *w2),
        [SMEM] + [VMEM] * (9 + levels) + [ANY] * (2 * tp),
        "mix",
        flops=2 * rows * D * 4 * D * 2,
        moved=12_000_000,
    )

    out, keep3, send3, grad_hu, resid, grad_gain2 = call(
        functools.partial(ffn_kernel, seqs, tp),
        (
            shape((rows, D), BF16),
            shape((tp // 2, D, 2 * vb), BF16),
            shape((tp // 2, D, 2 * vb), BF16),
            shape((rows, 2 * D), BF16),
            shape((rows, D)),
            shape((1, D)),
        ),
        [
            pltpu.VMEM((tp, D, vb), BF16),
            pltpu.VMEM((tp, vb, D), BF16),
            pltpu.VMEM((rows, D), BF16),
            pltpu.VMEM((rows, D), BF16),
            pltpu.VMEM((rows, D), F32),
            pltpu.VMEM((rows, D), F32),
            pltpu.SemaphoreType.DMA((tp * (D // vb + 1),)),
        ],
        (ids, tok, cot, middle, hidden_pre, update_pre, gain2, *w3),
        [SMEM] + [VMEM] * 6 + [ANY] * tp,
        "ffn",
        flops=6 * rows * D * 4 * D,
        moved=8_000_000,
    )

    (
        keep2, send2, keep1, send1, grad_skip, grad_normed, after, back_ends, grad_wsh, misc,
    ) = call(
        functools.partial(back_kernel, seqs, tp),
        (
            shape((tp // 2, 2 * nb + vb, D), BF16),
            shape((tp // 2, 2 * nb + vb, D), BF16),
            shape((tp // 2, D, 2 * vb), BF16),
            shape((tp // 2, D, 2 * vb), BF16),
            shape((BLOCKS, rows, LANES)),
            shape((rows, D)),
            shape((seqs, NDIM, PIECES, D)),
            shape((seqs, NDIM, D)),
            shape((D, Z)),
            shape((1, D)),
        ),
        [
            pltpu.VMEM((tp, D, 2 * vb), BF16),
            pltpu.VMEM((D, 2 * D), BF16),
            pltpu.VMEM((tp, vb, D), BF16),
            pltpu.VMEM((D, 2 * D), F32),
            pltpu.VMEM((rows, D), F32),
            pltpu.VMEM((seqs, CH, CH), F32),
            pltpu.VMEM((3, NDIM, D), F32),
            pltpu.SemaphoreType.DMA((4 * tp,)),
        ],
        (
            ids, normed, mixed, skip_pre, shared_pre, prob, values, value_pre, reset_pre, attended,
            gated, grad_hu, par, w_shared, qg, kg, *w1, *w2,
        ),
        [SMEM] + [VMEM] * 15 + [ANY] * (2 * tp),
        "back",
        flops=4 * rows * D * 8 * D,
        moved=16_000_000,
    )

    local, small = call(
        functools.partial(sums_kernel, seqs),
        (shape((BLOCKS, rows, LANES)), shape((SMALL_ROWS, D))),
        [pltpu.VMEM((BLOCKS, rows, LANES), F32), pltpu.VMEM((NDIM, PIECES, D), F32)],
        (tok, normed, grad_skip, grad_normed, par, before, st_in, after, skip, grad_gain2, misc),
        [VMEM] * 11,
        "sums",
        flops=40_000_000,
        moved=5_000_000,
    )

    wide = grad_wsh.reshape(D // Z, D // (D // Z), Z).transpose(1, 0, 2).reshape(-1, D)
    sums = jnp.concatenate([wide, small], axis=0)
    adjoint = back_ends
    back_recvs = []

    def adjoint_after(k, other):
        upper = has(stretch, 1 << k)
        early = jnp.where(upper, other, adjoint)
        late = jnp.where(upper, adjoint, other)
        return early + jnp.exp(float(CH << k) * logd) * late

    level = 0
    for bit in bits_of(tp):
        upper = has(part, bit)
        send = half_of(sums, ~upper)
        if bit == 1:
            other = swap(send, "tp", bit)
            if not traded:
                got = swap(adjoint, "tp", bit)
                back_recvs.append(got)
                adjoint = adjoint_after(level, got)
                level += 1
        else:
            both = swap(
                jnp.concatenate([adjoint.reshape(-1, D), send], axis=0), "tp", bit
            )
            got = both[: seqs * NDIM].reshape(seqs, NDIM, D)
            other = both[seqs * NDIM :]
            back_recvs.append(got)
            adjoint = adjoint_after(level, got)
            level += 1
        sums = half_of(sums, upper) + other
    for bit in bits_of(seq):
        both = swap(jnp.concatenate([adjoint.reshape(-1, D), sums], axis=0), "seq", bit)
        got = both[: seqs * NDIM].reshape(seqs, NDIM, D)
        back_recvs.append(got)
        adjoint = adjoint_after(level, got)
        level += 1
        sums = sums + both[seqs * NDIM :]

    (grad_tokens,) = call(
        functools.partial(leave_kernel, seqs, levels),
        (shape((seqs, CH, D), BF16),),
        [
            pltpu.VMEM((seqs, NDIM, D), F32),
            pltpu.VMEM((NDIM, PIECES, D), F32),
            pltpu.VMEM((BLOCKS, rows, LANES), F32),
        ],
        (ids, tok, par, local, resid, gain1, *back_recvs),
        [SMEM] + [VMEM] * (5 + levels),
        "leave",
        flops=10_000_000,
        moved=3_000_000,
    )

    for bit in reversed(bits_of(tp)):
        sums = joined(sums, swap(sums, "tp", bit), has(part, bit))
    wide, small = sums[: D * Z // D], sums[D * Z // D :]
    grad_wsh = wide.reshape(-1, D // Z, Z).transpose(1, 0, 2).reshape(D, Z)
    inflow, eta = par[2], par[3]
    q_sum, r_sum = small[:NDIM], small[NDIM : 2 * NDIM]
    tail = small[2 * NDIM : 2 * NDIM + 4]
    root = jnp.sqrt(ema_rate * (2.0 - ema_rate))
    grad_ema_eta = (inflow * q_sum).T
    grad_inflow = (eta * q_sum).T
    grad_decay = (eta * inflow * r_sum).T
    grad_ema_rate = grad_inflow * ema_beta * (1.0 - ema_rate) / root - grad_decay
    grad_ema_beta = grad_inflow * root
    grad_norm1_gain = tail[1] + jnp.sum(inflow * eta * q_sum, axis=0) / norm1_gain

    g3 = summed(keep3, send3, tp, seq, place).astype(F32)
    g2 = summed(keep2, send2, tp, seq, place).astype(F32)
    g1 = summed(keep1, send1, tp, seq, place).astype(F32)
    return (
        trade_back(out.reshape(seqs, CH, D)),
        trade_back(grad_tokens),
        grad_norm1_gain,
        grad_ema_rate,
        grad_ema_beta,
        grad_ema_eta,
        tail[0],
        grad_wsh,
        tail[3, :Z],
        tail[3, Z : 2 * Z],
        tail[3, 2 * Z : 3 * Z],
        g1[:, :vb],
        g1[:, vb:],
        g2[nb : 2 * nb],
        g2[:nb],
        g2[2 * nb :],
        tail[2],
        g3[:, :vb],
        jnp.concatenate([g3[k * vb : (k + 1) * vb, vb:] for k in range(D // vb)], axis=1),
    )


def solution(mesh):
    rows = P(None, ("seq", "tp"), None)
    cols = P(None, "tp")
    tall = P("tp", None)
    whole = P()
    return jax.shard_map(
        per_device,
        mesh=mesh,
        in_specs=(rows, rows) + (whole,) * 10 + (cols, cols, tall, tall, tall, whole, cols, tall),
        out_specs=(rows, rows) + (whole,) * 9 + (cols, cols, tall, tall, tall, whole, cols, tall),
        check_vma=False,
    )
```

time: 2020 us -> 200 us (0.10)
  local copies, waits for them, and re-layouts: 1300 us -> 12.3 us
  matrix products: 216 us -> 0 us
  blocking collectives: 142 us -> 0 us
  other arithmetic: 134 us -> 9.55 us
  waiting for transfers between devices: 190 us -> 86.6 us
  starting transfers between devices: 1.15 us -> 53.9 us
  Pallas kernels: 0 us -> 35.8 us
    unnamed x337 -> x61, local copies, waits for them, and re-layouts: 947 us -> 4.68 us
    dot_general x41 -> x0, matrix products: 214 us -> none  [the longest x29 49.4 us: product(): return jnp.einsum(form, left, right, preferred_element_type=jnp.float32)]
    all_gather x4 -> x0, blocking collectives: 125 us -> none  [the longest x2 63.9 us: entering(): pieces = jax.tree.map(lambda part: lax.all_gather(part, axis), value)]
    psum x4 -> x0, waiting for transfers between devices: 123 us -> none  [the longest x2 123 us: per_device(): lax.psum((grad_norm1_gain, grad_ema_rate * first, grad_ema_beta * first,...]
    gather x2 -> x0, local copies, waits for them, and re-layouts: 97.4 us -> none  [per_device(): scores = raw + rel_bias[jnp.clip(offset, 0, CH - 1)][None]]
    reduce_scatter x5 -> x0, local copies, waits for them, and re-layouts: 87.1 us -> none  [the longest x1 19.6 us: per_device(): lax.psum_scatter(grad_normed2_part, 'tp', scatter_dimension=1, tiled=True)]
    ppermute x0 -> x46, waiting for transfers between devices: none -> 86.6 us  [swap(): return lax.ppermute(value, axis, [(i, i ^ bit) for i in range(count)])]
    reduce_sum x21 -> x0, other arithmetic: 57.4 us -> none  [the longest x7 22.1 us: ema_within(): state = step_power[None] * state + ends[:, index]]
  transfers between devices with their start and end apart: 14 -> 46, of which waited for: 4 -> 27; matrix products, arithmetic and copies ran while one was open for 53% -> 7% of each run, Pallas kernels for 0% -> 9%
where the time goes in v1:
time: 200 us
  waiting for transfers between devices  86.6 us (43%)
  starting transfers between devices  53.9 us (27%)
  Pallas kernels  35.8 us (18%)
  local copies, waits for them, and re-layouts  12.3 us (6%)
  other arithmetic  9.55 us (5%)
    ppermute x46, waiting for transfers between devices, swap(): return lax.ppermute(value, axis, [(i, i ^ bit) for i in range(count)])  86.6 us
    ppermute x46, starting transfers between devices, swap(): return lax.ppermute(value, axis, [(i, i ^ bit) for i in range(count)])  53.9 us
    pallas_call x6, Pallas kernels, call(): pl.pallas_call(body, out_shape=out, in_specs=specs, out_specs=jax.tree.ma...  35.8 us
    convert_element_type x15, other arithmetic, add_low(): return (a.astype(F32) + b.astype(F32)).astype(BF16)  5.32 us
    unnamed x61, local copies, waits for them, and re-layouts  4.68 us
  transfers between devices with their start and end apart: 46, of which 27 were waited for; matrix products, arithmetic and copies ran while one was open for 7% of the time, Pallas kernels for 9%

profile of v1, /device:TPU:0, one launch (start us, length us, event | category | flops | bytes accessed | tf_op | source)
XLA Modules:
  0.0 199.7 jit_solution(9282982326218063704)
XLA Ops:
  0.7 1.6 constant_dynamic-update-slice_fusion.4
  2.3 1.6 constant_dynamic-update-slice_fusion.3
  3.9 1.7 constant_dynamic-update-slice_fusion.2.refs_9_.refs_4_
  5.6 2.9 %collective-permute-start.9 = (bf16[512,512]{1,0:T(8,128)(2,1)}, bf16[512,512]{1,0:T(8,128)(2,1)}, u32[]{:S(2)}, u32[]{:S(2)}) collective-permute-start(bf16[512,512]{1,0:T(8,128)(2,1)} %constant_dynamic-update-slice_fusion.2.refs_9_.refs_4_), channel_id=1, source_target_pairs={{0,2},{1,3},{2,0},{3,1},{4,6},{5,7},{6,4},{7,5},{8,10},{9,11},{10,... | collective-permute-start | bytes 1572872 | tf_op jit(solution)/shard_map/ppermute | solution.py:617
  8.9 2.4 %enter.1 = (bf16[256,512]{1,0:T(8,128)(2,1)S(1)}, f32[4,16,512]{2,1,0:T(8,128)S(1)}, f32[2,2,16,8,512]{4,3,2,1,0:T(8,128)S(1)}, f32[2,2,16,512]{3,2,1,0:T(8,128)S(1)}) custom-call(bf16[2,128,512]{2,1,0:T(8,128)(2,1)S(1)} %copy-done.2, f32[1,512]{1,0:T(1,128)S(1)} %bitcast.108, f32[512,16]{1,0:T(8,128)S(1)} %copy.39.rate, f32[512,16]{1,0:T(8,128)S(1)} %copy.40.beta, ...), custom_call_target="tpu_custom_call" | custom-call | flops 20000000 | bytes 2000000 | tf_op jit(solution)/shard_map/enter/pallas_call | solution.py:94
  11.4 0.9 copy-done
  14.0 2.1 %collective-permute-start.6 = (bf16[512,512]{1,0:T(8,128)(2,1)S(1)}, bf16[512,512]{1,0:T(8,128)(2,1)}, u32[]{:S(2)}, u32[]{:S(2)}) collective-permute-start(bf16[512,512]{1,0:T(8,128)(2,1)S(1)} %constant_dynamic-update-slice_fusion.refs_5_.refs_0_), channel_id=1, source_target_pairs={{0,2},{1,3},{2,0},{3,1},{4,6},{5,7},{6,4},{7,5},{8,10},{9,11},{10,... | collective-permute-start | bytes 1572872 | tf_op jit(solution)/shard_map/ppermute | solution.py:617
  16.1 6.8 %collective-permute-done.1.refs_1_ = bf16[2,2,16,512]{3,2,1,0:T(8,128)(2,1)S(1)} collective-permute-done((bf16[2,2,16,512]{3,2,1,0:T(8,128)(2,1)S(1)}, bf16[2,2,16,512]{3,2,1,0:T(8,128)(2,1)S(1)}, u32[]{:S(2)}, u32[]{:S(2)}) %collective-permute-start.1) | collective-permute-done | bytes 65568 | tf_op jit(solution)/shard_map/ppermute | solution.py:617
  23.0 2.2 %collective-permute-start.2 = (bf16[2,2,16,512]{3,2,1,0:T(8,128)(2,1)S(1)}, bf16[2,2,16,512]{3,2,1,0:T(8,128)(2,1)S(1)}, u32[]{:S(2)}, u32[]{:S(2)}) collective-permute-start(bf16[2,2,16,512]{3,2,1,0:T(8,128)(2,1)S(1)} %fusion.7), channel_id=1, source_target_pairs={{0,4},{4,0},{8,12},{12,8},{16,20},{20,16},{24,28},{28,24},{1,5},{5... | collective-permute-start | bytes 196616 | tf_op jit(solution)/shard_map/ppermute | solution.py:617
  25.1 2.2 %collective-permute-done.2.refs_2_ = bf16[2,2,16,512]{3,2,1,0:T(8,128)(2,1)S(1)} collective-permute-done((bf16[2,2,16,512]{3,2,1,0:T(8,128)(2,1)S(1)}, bf16[2,2,16,512]{3,2,1,0:T(8,128)(2,1)S(1)}, u32[]{:S(2)}, u32[]{:S(2)}) %collective-permute-start.2) | collective-permute-done | bytes 65568 | tf_op jit(solution)/shard_map/ppermute | solution.py:617
  27.5 2.1 %collective-permute-start.3 = (bf16[2,2,16,512]{3,2,1,0:T(8,128)(2,1)S(1)}, bf16[2,2,16,512]{3,2,1,0:T(8,128)(2,1)S(1)}, u32[]{:S(2)}, u32[]{:S(2)}) collective-permute-start(bf16[2,2,16,512]{3,2,1,0:T(8,128)(2,1)S(1)} %fusion.6), channel_id=1, source_target_pairs={{0,8},{4,12},{8,0},{12,4},{16,24},{20,28},{24,16},{28,20},{1,9},{5... | collective-permute-start | bytes 196616 | tf_op jit(solution)/shard_map/ppermute | solution.py:617
  29.7 1.6 collective-permute-start.12
  32.0 3.6 %collective-permute-start.4 = (bf16[2,2,16,512]{3,2,1,0:T(8,128)(2,1)S(1)}, bf16[2,2,16,512]{3,2,1,0:T(8,128)(2,1)S(1)}, u32[]{:S(2)}, u32[]{:S(2)}) collective-permute-start(bf16[2,2,16,512]{3,2,1,0:T(8,128)(2,1)S(1)} %pad_maximum_fusion.8), channel_id=1, source_target_pairs={{0,16},{4,20},{8,24},{12,28},{16,0},{20,4},{24,8},{28,12},{1,17},{... | collective-permute-start | bytes 196616 | tf_op jit(solution)/shard_map/ppermute | solution.py:617
  35.5 2.2 %collective-permute-done.4.refs_4_ = bf16[2,2,16,512]{3,2,1,0:T(8,128)(2,1)S(1)} collective-permute-done((bf16[2,2,16,512]{3,2,1,0:T(8,128)(2,1)S(1)}, bf16[2,2,16,512]{3,2,1,0:T(8,128)(2,1)S(1)}, u32[]{:S(2)}, u32[]{:S(2)}) %collective-permute-start.4) | collective-permute-done | bytes 65568 | tf_op jit(solution)/shard_map/ppermute | solution.py:617
  38.8 5.7 %collective-permute-done.12.refs_2_ = bf16[512,512]{1,0:T(8,128)(2,1)S(1)} collective-permute-done((bf16[512,512]{1,0:T(8,128)(2,1)S(1)}, bf16[512,512]{1,0:T(8,128)(2,1)S(1)}, u32[]{:S(2)}, u32[]{:S(2)}) %collective-permute-start.12) | collective-permute-done | bytes 524320 | tf_op jit(solution)/shard_map/ppermute | solution.py:617
  44.7 8.3 %mix.1 = (f32[2,2,16,512]{3,2,1,0:T(8,128)S(1)}, f32[256,512]{1,0:T(8,128)S(1)}, bf16[256,512]{1,0:T(8,128)(2,1)S(1)}, f32[256,128]{1,0:T(8,128)S(1)}, f32[2,128...) custom-call(s32[4]{0:T(128)S(1)} %pad_add_fusion.ids, ...), custom_call_target="tpu_custom_call" | custom-call | flops 1073741824 | bytes 12000000 | tf_op jit(solution)/shard_map/mix/pallas_call | solution.py:94
  53.0 6.0 %ffn.1 = (bf16[256,512]{1,0:T(8,128)(2,1)}, bf16[2,512,512]{2,1,0:T(8,128)(2,1)}, bf16[2,512,512]{2,1,0:T(8,128)(2,1)}, bf16[256,1024]{1,0:T(8,128)(2,1)S(1)}, f...) custom-call(s32[4]{0:T(128)S(1)} %pad_add_fusion.ids, bf16[2,128,512]{2,1,0:T(8,128)(2,1)S(1)} %copy-done.2, ...), custom_call_target="tpu_custom_call" | custom-call | flops 1610612736 | bytes 8000000 | tf_op jit(solution)/shard_map/ffn/pallas_call | solution.py:94
  59.1 11.8 %back.1 = (bf16[2,512,512]{2,1,0:T(8,128)(2,1)}, bf16[2,512,512]{2,1,0:T(8,128)(2,1)}, bf16[2,512,512]{2,1,0:T(8,128)(2,1)}, bf16[2,512,512]{2,1,0:T(8,128)(2,1)...) custom-call(s32[4]{0:T(128)S(1)} %pad_add_fusion.ids, ...), custom_call_target="tpu_custom_call" | custom-call | flops 2147483648 | bytes 16000000 | tf_op jit(solution)/shard_map/back/pallas_call | solution.py:94
  71.4 4.7 %sums.1 = (f32[4,256,128]{2,1,0:T(8,128)S(1)}, f32[64,512]{1,0:T(8,128)S(1)}) custom-call(bf16[2,128,512]{2,1,0:T(8,128)(2,1)S(1)} %copy-done.2, bf16[256,512]{1,0:T(8,128)(2,1)S(1)} %get-tuple-element.54.normed, f32[4,256,128]{2,1,0:T(8,128)S(1)} %get-tuple-element.72.grad_skip, f32[256,512]{1,0:T(8,128)S(1)} %get-tuple-element.73.grad_normed, ...), custom_call_target="tpu_custom_call" | custom-call | flops 40000000 | bytes 5000000 | tf_op jit(solution)/shard_map/sums/pallas_call | solution.py:94
  76.3 1.4 collective-permute-done.15
  77.8 1.8 collective-permute-start.16
  79.6 4.5 %collective-permute-done.16 = f32[80,512]{1,0:T(8,128)S(1)} collective-permute-done((f32[80,512]{1,0:T(8,128)S(1)}, f32[80,512]{1,0:T(8,128)S(1)}, u32[]{:S(2)}, u32[]{:S(2)}) %collective-permute-start.16) | collective-permute-done | bytes 163872 | tf_op jit(solution)/shard_map/ppermute | solution.py:617
  84.2 1.8 collective-permute-start.17
  86.0 3.7 %collective-permute-done.17 = f32[80,512]{1,0:T(8,128)S(1)} collective-permute-done((f32[80,512]{1,0:T(8,128)S(1)}, f32[80,512]{1,0:T(8,128)S(1)}, u32[]{:S(2)}, u32[]{:S(2)}) %collective-permute-start.17) | collective-permute-done | bytes 163872 | tf_op jit(solution)/shard_map/ppermute | solution.py:617
  89.8 1.9 collective-permute-start.18
  92.1 3.0 %collective-permute-done.18 = f32[80,512]{1,0:T(8,128)S(1)} collective-permute-done((f32[80,512]{1,0:T(8,128)S(1)}, f32[80,512]{1,0:T(8,128)S(1)}, u32[]{:S(2)}, u32[]{:S(2)}) %collective-permute-start.18) | collective-permute-done | bytes 163872 | tf_op jit(solution)/shard_map/ppermute | solution.py:617
  95.2 2.9 %collective-permute-start.19 = (f32[80,512]{1,0:T(8,128)S(1)}, f32[80,512]{1,0:T(8,128)S(1)}, u32[]{:S(2)}, u32[]{:S(2)}) collective-permute-start(f32[80,512]{1,0:T(8,128)S(1)} %pad_maximum_fusion.4), channel_id=1, source_target_pairs={{0,16},{4,20},{8,24},{12,28},{16,0},{20,4},{24,8},{28,12},{1,17},{... | collective-permute-start | bytes 491528 | tf_op jit(solution)/shard_map/ppermute | solution.py:617
  98.2 5.1 %collective-permute-done.19 = f32[80,512]{1,0:T(8,128)S(1)} collective-permute-done((f32[80,512]{1,0:T(8,128)S(1)}, f32[80,512]{1,0:T(8,128)S(1)}, u32[]{:S(2)}, u32[]{:S(2)}) %collective-permute-start.19) | collective-permute-done | bytes 163872 | tf_op jit(solution)/shard_map/ppermute | solution.py:617
  103.3 1.8 collective-permute-start.20
  105.1 2.6 %leave.1 = bf16[2,128,512]{2,1,0:T(8,128)(2,1)} custom-call(s32[4]{0:T(128)S(1)} %pad_add_fusion.ids, bf16[2,128,512]{2,1,0:T(8,128)(2,1)S(1)} %copy-done.2, f32[4,16,512]{2,1,0:T(8,128)S(1)} %get-tuple-element.55.par, f32[4,256,128]{2,1,0:T(8,128)S(1)} %get-tuple-element.78.local, f32[256,512]{1,0:T(8,128)S(1)} %get-tuple-element.79.resid, ...), custom_call_target="tpu_custom_call" | custom-call | flops 10000000 | bytes 3000000 | tf_op jit(solution)/shard_map/leave/pallas_call | solution.py:94
  108.1 1.6 add_convert_fusion
  109.7 1.8 collective-permute-start.39
  111.5 1.5 add_convert_fusion.1
  113.0 1.2 collective-permute-start.31
  114.2 1.5 add_convert_fusion.2
  115.7 1.2 collective-permute-start.23
  119.4 5.1 %collective-permute-done.39 = bf16[1,512,512]{2,1,0:T(8,128)(2,1)S(1)} collective-permute-done((bf16[1,512,512]{2,1,0:T(8,128)(2,1)S(1)}, bf16[1,512,512]{2,1,0:T(8,128)(2,1)S(1)}, u32[]{:S(2)}, u32[]{:S(2)}) %collective-permute-start.39) | collective-permute-done | bytes 524320 | tf_op jit(solution)/shard_map/ppermute | solution.py:617
  124.7 1.8 collective-permute-start.40
  126.5 9.3 %collective-permute-done.31 = bf16[1,512,512]{2,1,0:T(8,128)(2,1)S(1)} collective-permute-done((bf16[1,512,512]{2,1,0:T(8,128)(2,1)S(1)}, bf16[1,512,512]{2,1,0:T(8,128)(2,1)S(1)}, u32[]{:S(2)}, u32[]{:S(2)}) %collective-permute-start.31) | collective-permute-done | bytes 524320 | tf_op jit(solution)/shard_map/ppermute | solution.py:617
  135.9 1.8 collective-permute-start.32
  137.7 8.8 %collective-permute-done.23 = bf16[1,512,512]{2,1,0:T(8,128)(2,1)S(1)} collective-permute-done((bf16[1,512,512]{2,1,0:T(8,128)(2,1)S(1)}, bf16[1,512,512]{2,1,0:T(8,128)(2,1)S(1)}, u32[]{:S(2)}, u32[]{:S(2)}) %collective-permute-start.23) | collective-permute-done | bytes 524320 | tf_op jit(solution)/shard_map/ppermute | solution.py:617
  146.7 1.8 collective-permute-start.24
  149.6 1.3 collective-permute-start.33
  150.9 3.8 %collective-permute-done.24 = bf16[256,512]{1,0:T(8,128)(2,1)S(1)} collective-permute-done((bf16[256,512]{1,0:T(8,128)(2,1)S(1)}, bf16[256,512]{1,0:T(8,128)(2,1)S(1)}, u32[]{:S(2)}, u32[]{:S(2)}) %collective-permute-start.24) | collective-permute-done | bytes 262176 | tf_op jit(solution)/shard_map/ppermute | solution.py:617
  154.8 1.0 collective-permute-start.25
  155.9 3.4 %collective-permute-start.42 = (bf16[64,512]{1,0:T(8,128)(2,1)S(1)}, bf16[64,512]{1,0:T(8,128)(2,1)S(1)}, u32[]{:S(2)}, u32[]{:S(2)}) collective-permute-start(bf16[64,512]{1,0:T(8,128)(2,1)S(1)} %constant_dynamic-slice_fusion), channel_id=1, source_target_pairs={{0,16},{4,20},{8,24},{12,28},{16,0},{20,4},{24,8},{28,12},{1,17},{... | collective-permute-start | bytes 196616 | tf_op jit(solution)/shard_map/ppermute | solution.py:617
  159.5 1.0 collective-permute-done.25
  160.6 2.6 %collective-permute-start.26 = (bf16[64,512]{1,0:T(8,128)(2,1)S(1)}, bf16[64,512]{1,0:T(8,128)(2,1)S(1)}, u32[]{:S(2)}, u32[]{:S(2)}) collective-permute-start(bf16[64,512]{1,0:T(8,128)(2,1)S(1)} %constant_dynamic-slice_fusion.4), channel_id=1, source_target_pairs={{0,16},{4,20},{8,24},{12,28},{16,0},{20,4},{24,8},{28,12},{1,17},{... | collective-permute-start | bytes 196616 | tf_op jit(solution)/shard_map/ppermute | solution.py:617
  163.2 1.7 collective-permute-done.42
  165.2 3.2 %collective-permute-done.34 = bf16[64,512]{1,0:T(8,128)(2,1)S(1)} collective-permute-done((bf16[64,512]{1,0:T(8,128)(2,1)S(1)}, bf16[64,512]{1,0:T(8,128)(2,1)S(1)}, u32[]{:S(2)}, u32[]{:S(2)}) %collective-permute-start.34) | collective-permute-done | bytes 65568 | tf_op jit(solution)/shard_map/ppermute | solution.py:617
  168.5 2.0 %collective-permute-done.26 = bf16[64,512]{1,0:T(8,128)(2,1)S(1)} collective-permute-done((bf16[64,512]{1,0:T(8,128)(2,1)S(1)}, bf16[64,512]{1,0:T(8,128)(2,1)S(1)}, u32[]{:S(2)}, u32[]{:S(2)}) %collective-permute-start.26) | collective-permute-done | bytes 65568 | tf_op jit(solution)/shard_map/ppermute | solution.py:617
  170.6 1.0 collective-permute-start.27
  171.5 1.8 collective-permute-done.43
  173.5 1.8 collective-permute-done.35
  176.4 1.1 collective-permute-start.28
  177.5 2.4 %collective-permute-done.44 = bf16[128,512]{1,0:T(8,128)(2,1)S(1)} collective-permute-done((bf16[128,512]{1,0:T(8,128)(2,1)S(1)}, bf16[128,512]{1,0:T(8,128)(2,1)S(1)}, u32[]{:S(2)}, u32[]{:S(2)}) %collective-permute-start.44) | collective-permute-done | bytes 131104 | tf_op jit(solution)/shard_map/ppermute | solution.py:617
  179.9 1.6 collective-permute-start.45
  183.0 1.4 collective-permute-start.37
  184.4 1.8 collective-permute-start.29
  186.2 3.0 %collective-permute-done.45 = bf16[256,512]{1,0:T(8,128)(2,1)S(1)} collective-permute-done((bf16[256,512]{1,0:T(8,128)(2,1)S(1)}, bf16[256,512]{1,0:T(8,128)(2,1)S(1)}, u32[]{:S(2)}, u32[]{:S(2)}) %collective-permute-start.45) | collective-permute-done | bytes 262176 | tf_op jit(solution)/shard_map/ppermute | solution.py:617
  189.4 5.3 %collective-permute-done.37 = bf16[256,512]{1,0:T(8,128)(2,1)S(1)} collective-permute-done((bf16[256,512]{1,0:T(8,128)(2,1)S(1)}, bf16[256,512]{1,0:T(8,128)(2,1)S(1)}, u32[]{:S(2)}, u32[]{:S(2)}) %collective-permute-start.37) | collective-permute-done | bytes 262176 | tf_op jit(solution)/shard_map/ppermute | solution.py:617
  195.0 0.8 slice.267
  197.8 1.0 fusion.23
  198.8 0.9 pad_maximum_fusion
  (186 shorter events, 15.9 us)
Async XLA Ops:
  0.7 7.8 %copy-start.20 = (f32[512,16]{0,1:T(8,128)S(1)}, f32[512,16]{0,1:T(8,128)}, u32[]{:S(2)}) copy-start(f32[512,16]{0,1:T(8,128)} %param.24) | copy-start | bytes 98308
  0.7 8.0 %copy-start.22 = (f32[512,16]{0,1:T(8,128)S(1)}, f32[512,16]{0,1:T(8,128)}, u32[]{:S(2)}) copy-start(f32[512,16]{0,1:T(8,128)} %param.25) | copy-start | bytes 98308
  0.7 8.1 %copy-start.24 = (f32[512,16]{0,1:T(8,128)S(1)}, f32[512,16]{0,1:T(8,128)}, u32[]{:S(2)}) copy-start(f32[512,16]{0,1:T(8,128)} %param.26) | copy-start | bytes 98308
  0.7 8.2 %copy-start.4 = (f32[512]{0:T(512)S(1)}, f32[512]{0:T(512)}, u32[]{:S(2)}) copy-start(f32[512]{0:T(512)} %param.23) | copy-start | bytes 6148
  0.7 8.2 %copy-start.2 = (bf16[2,128,512]{2,1,0:T(8,128)(2,1)S(1)}, bf16[2,128,512]{2,1,0:T(8,128)(2,1)}, u32[]{:S(2)}) copy-start(bf16[2,128,512]{2,1,0:T(8,128)(2,1)} %tok.9) | copy-start | bytes 786436
  5.6 32.2 %collective-permute-start.9 = (bf16[512,512]{1,0:T(8,128)(2,1)}, bf16[512,512]{1,0:T(8,128)(2,1)}, u32[]{:S(2)}, u32[]{:S(2)}) collective-permute-start(bf16[512,512]{1,0:T(8,128)(2,1)} %constant_dynamic-update-slice_fusion.2.refs_9_.refs_4_), channel_id=1, source_target_pairs={{0,2},{1,3},{2,0},{3,1},{4,6},{5,7},{6,4},{7,5},{8,10},{9,11},{10,... | collective-permute-start | bytes 1572872 | tf_op jit(solution)/shard_map/ppermute | solution.py:617
  8.5 29.9 %collective-permute-start.8 = (bf16[512,512]{1,0:T(8,128)(2,1)}, bf16[512,512]{1,0:T(8,128)(2,1)}, u32[]{:S(2)}, u32[]{:S(2)}) collective-permute-start(bf16[512,512]{1,0:T(8,128)(2,1)} %constant_dynamic-update-slice_fusion.2.refs_9_.refs_4_), channel_id=1, source_target_pairs={{0,1},{1,0},{2,3},{3,2},{4,5},{5,4},{6,7},{7,6},{8,9},{9,8},{10,11... | collective-permute-start | bytes 1572872 | tf_op jit(solution)/shard_map/ppermute | solution.py:617
  12.3 1.5 collective-permute-start
  13.0 19.0 %copy-start.14 = (f32[16,512]{1,0:T(8,128)}, f32[16,512]{1,0:T(8,128)S(1)}, u32[]{:S(2)}) copy-start(f32[16,512]{1,0:T(8,128)S(1)} %get-tuple-element.123) | copy-start | bytes 98308
  13.8 11.3 %copy-start.18 = (bf16[256,512]{1,0:T(8,128)(2,1)S(1)}, bf16[256,512]{1,0:T(8,128)(2,1)}, u32[]{:S(2)}) copy-start(bf16[256,512]{1,0:T(8,128)(2,1)} %param.39) | copy-start | bytes 786436
  13.9 9.0 %collective-permute-start.1 = (bf16[2,2,16,512]{3,2,1,0:T(8,128)(2,1)S(1)}, bf16[2,2,16,512]{3,2,1,0:T(8,128)(2,1)S(1)}, u32[]{:S(2)}, u32[]{:S(2)}) collective-permute-start(bf16[2,2,16,512]{3,2,1,0:T(8,128)(2,1)S(1)} %fusion.8), channel_id=1, source_target_pairs={{0,2},{1,3},{2,0},{3,1},{4,6},{5,7},{6,4},{7,5},{8,10},{9,11},{10,... | collective-permute-start | bytes 196616 | tf_op jit(solution)/shard_map/ppermute | solution.py:617
  14.0 24.3 %collective-permute-start.6 = (bf16[512,512]{1,0:T(8,128)(2,1)S(1)}, bf16[512,512]{1,0:T(8,128)(2,1)}, u32[]{:S(2)}, u32[]{:S(2)}) collective-permute-start(bf16[512,512]{1,0:T(8,128)(2,1)S(1)} %constant_dynamic-update-slice_fusion.refs_5_.refs_0_), channel_id=1, source_target_pairs={{0,2},{1,3},{2,0},{3,1},{4,6},{5,7},{6,4},{7,5},{8,10},{9,11},{10,... | collective-permute-start | bytes 1572872 | tf_op jit(solution)/shard_map/ppermute | solution.py:617
  23.0 4.4 %collective-permute-start.2 = (bf16[2,2,16,512]{3,2,1,0:T(8,128)(2,1)S(1)}, bf16[2,2,16,512]{3,2,1,0:T(8,128)(2,1)S(1)}, u32[]{:S(2)}, u32[]{:S(2)}) collective-permute-start(bf16[2,2,16,512]{3,2,1,0:T(8,128)(2,1)S(1)} %fusion.7), channel_id=1, source_target_pairs={{0,4},{4,0},{8,12},{12,8},{16,20},{20,16},{24,28},{28,24},{1,5},{5... | collective-permute-start | bytes 196616 | tf_op jit(solution)/shard_map/ppermute | solution.py:617
  27.4 17.1 %copy-start.25 = (s32[2]{0:T(128)S(1)}, s32[2]{0:T(128)}, u32[]{:S(2)}) copy-start(s32[2]{0:T(128)} %param.22) | copy-start | bytes 28
  27.4 17.2 %copy-start.3 = (bf16[512,128]{1,0:T(8,128)(2,1)S(1)}, bf16[512,128]{1,0:T(8,128)(2,1)}, u32[]{:S(2)}) copy-start(bf16[512,128]{1,0:T(8,128)(2,1)} %wsh.3) | copy-start | bytes 393220
  27.5 17.2 %copy-start.5 = (f32[512]{0:T(512)S(1)}, f32[512]{0:T(512)}, u32[]{:S(2)}) copy-start(f32[512]{0:T(512)} %param.27) | copy-start | bytes 6148
  27.5 17.2 %copy-start.6 = (f32[128]{0:T(128)S(1)}, f32[128]{0:T(128)}, u32[]{:S(2)}) copy-start(f32[128]{0:T(128)} %param.29) | copy-start | bytes 1540
  27.5 17.2 %copy-start.7 = (f32[128]{0:T(128)S(1)}, f32[128]{0:T(128)}, u32[]{:S(2)}) copy-start(f32[128]{0:T(128)} %param.30) | copy-start | bytes 1540
  27.5 17.1 %copy-start.8 = (f32[128]{0:T(128)S(1)}, f32[128]{0:T(128)}, u32[]{:S(2)}) copy-start(f32[128]{0:T(128)} %param.31) | copy-start | bytes 1540
  27.5 4.4 %collective-permute-start.3 = (bf16[2,2,16,512]{3,2,1,0:T(8,128)(2,1)S(1)}, bf16[2,2,16,512]{3,2,1,0:T(8,128)(2,1)S(1)}, u32[]{:S(2)}, u32[]{:S(2)}) collective-permute-start(bf16[2,2,16,512]{3,2,1,0:T(8,128)(2,1)S(1)} %fusion.6), channel_id=1, source_target_pairs={{0,8},{4,12},{8,0},{12,4},{16,24},{20,28},{24,16},{28,20},{1,9},{5... | collective-permute-start | bytes 196616 | tf_op jit(solution)/shard_map/ppermute | solution.py:617
  29.7 14.8 %collective-permute-start.12 = (bf16[512,512]{1,0:T(8,128)(2,1)S(1)}, bf16[512,512]{1,0:T(8,128)(2,1)S(1)}, u32[]{:S(2)}, u32[]{:S(2)}) collective-permute-start(bf16[512,512]{1,0:T(8,128)(2,1)S(1)} %maximum_maximum_fusion.refs_0_), channel_id=1, source_target_pairs={{0,2},{1,3},{2,0},{3,1},{4,6},{5,7},{6,4},{7,5},{8,10},{9,11},{10,... | collective-permute-start | bytes 1572872 | tf_op jit(solution)/shard_map/ppermute | solution.py:617
  32.0 5.8 %collective-permute-start.4 = (bf16[2,2,16,512]{3,2,1,0:T(8,128)(2,1)S(1)}, bf16[2,2,16,512]{3,2,1,0:T(8,128)(2,1)S(1)}, u32[]{:S(2)}, u32[]{:S(2)}) collective-permute-start(bf16[2,2,16,512]{3,2,1,0:T(8,128)(2,1)S(1)} %pad_maximum_fusion.8), channel_id=1, source_target_pairs={{0,16},{4,20},{8,24},{12,28},{16,0},{20,4},{24,8},{28,12},{1,17},{... | collective-permute-start | bytes 196616 | tf_op jit(solution)/shard_map/ppermute | solution.py:617
  37.8 6.8 %collective-permute-start.5 = (bf16[512,512]{1,0:T(8,128)(2,1)S(1)}, bf16[512,512]{1,0:T(8,128)(2,1)S(1)}, u32[]{:S(2)}, u32[]{:S(2)}) collective-permute-start(bf16[512,512]{1,0:T(8,128)(2,1)S(1)} %constant_dynamic-update-slice_fusion.refs_5_.refs_0_), channel_id=1, source_target_pairs={{0,1},{1,0},{2,3},{3,2},{4,5},{5,4},{6,7},{7,6},{8,9},{9,8},{10,11... | collective-permute-start | bytes 1572872 | tf_op jit(solution)/shard_map/ppermute | solution.py:617
  37.8 6.8 %collective-permute-start.10 = (bf16[512,512]{1,0:T(8,128)(2,1)}, bf16[512,512]{1,0:T(8,128)(2,1)}, u32[]{:S(2)}, u32[]{:S(2)}) collective-permute-start(bf16[512,512]{1,0:T(8,128)(2,1)} %collective-permute-done.9.refs_11_.refs_6_), channel_id=1, source_target_pairs={{0,1},{1,0},{2,3},{3,2},{4,5},{5,4},{6,7},{7,6},{8,9},{9,8},{10,11... | collective-permute-start | bytes 1572872 | tf_op jit(solution)/shard_map/ppermute | solution.py:617
  38.3 6.3 %collective-permute-start.7 = (bf16[512,512]{1,0:T(8,128)(2,1)}, bf16[512,512]{1,0:T(8,128)(2,1)}, u32[]{:S(2)}, u32[]{:S(2)}) collective-permute-start(bf16[512,512]{1,0:T(8,128)(2,1)} %collective-permute-done.6.refs_7_.refs_2_), channel_id=1, source_target_pairs={{0,1},{1,0},{2,3},{3,2},{4,5},{5,4},{6,7},{7,6},{8,9},{9,8},{10,11... | collective-permute-start | bytes 1572872 | tf_op jit(solution)/shard_map/ppermute | solution.py:617
  38.4 14.6 %collective-permute-start.11 = (bf16[512,512]{1,0:T(8,128)(2,1)S(1)}, bf16[512,512]{1,0:T(8,128)(2,1)}, u32[]{:S(2)}, u32[]{:S(2)}) collective-permute-start(bf16[512,512]{1,0:T(8,128)(2,1)S(1)} %maximum_maximum_fusion.refs_0_), channel_id=1, source_target_pairs={{0,1},{1,0},{2,3},{3,2},{4,5},{5,4},{6,7},{7,6},{8,9},{9,8},{10,11... | collective-permute-start | bytes 1572872 | tf_op jit(solution)/shard_map/ppermute | solution.py:617
  44.5 8.5 %collective-permute-start.13 = (bf16[512,512]{1,0:T(8,128)(2,1)S(1)}, bf16[512,512]{1,0:T(8,128)(2,1)}, u32[]{:S(2)}, u32[]{:S(2)}) collective-permute-start(bf16[512,512]{1,0:T(8,128)(2,1)S(1)} %collective-permute-done.12.refs_2_), channel_id=1, source_target_pairs={{0,1},{1,0},{2,3},{3,2},{4,5},{5,4},{6,7},{7,6},{8,9},{9,8},{10,11... | collective-permute-start | bytes 1572872 | tf_op jit(solution)/shard_map/ppermute | solution.py:617
  44.7 8.4 %copy-start.9 = (bf16[2,128,512]{2,1,0:T(8,128)(2,1)S(1)}, bf16[2,128,512]{2,1,0:T(8,128)(2,1)}, u32[]{:S(2)}) copy-start(bf16[2,128,512]{2,1,0:T(8,128)(2,1)} %cot.1) | copy-start | bytes 786436
  44.7 8.4 %copy-start.10 = (f32[512]{0:T(512)S(1)}, f32[512]{0:T(512)}, u32[]{:S(2)}) copy-start(f32[512]{0:T(512)} %param.37) | copy-start | bytes 6148
  59.1 12.4 %copy-start.1 = (f32[2,2,16,8,512]{4,3,2,1,0:T(8,128)S(1)}, f32[2,2,16,8,512]{4,3,2,1,0:T(8,128)}, u32[]{:S(2)}) copy-start(f32[2,2,16,8,512]{4,3,2,1,0:T(8,128)} %copy-done) | copy-start | bytes 3145732
  70.9 5.4 %collective-permute-start.14 = (f32[2,16,512]{2,1,0:T(8,128)S(1)}, f32[2,16,512]{2,1,0:T(8,128)S(1)}, u32[]{:S(2)}, u32[]{:S(2)}) collective-permute-start(f32[2,16,512]{2,1,0:T(8,128)S(1)} %get-tuple-element.80), channel_id=1, source_target_pairs={{0,1},{1,0},{2,3},{3,2},{4,5},{5,4},{6,7},{7,6},{8,9},{9,8},{10,11... | collective-permute-start | bytes 196616 | tf_op jit(solution)/shard_map/ppermute | solution.py:617
  76.2 1.5 collective-permute-start.15
  77.8 6.3 %collective-permute-start.16 = (f32[80,512]{1,0:T(8,128)S(1)}, f32[80,512]{1,0:T(8,128)S(1)}, u32[]{:S(2)}, u32[]{:S(2)}) collective-permute-start(f32[80,512]{1,0:T(8,128)S(1)} %pad_maximum_fusion.1), channel_id=1, source_target_pairs={{0,2},{1,3},{2,0},{3,1},{4,6},{5,7},{6,4},{7,5},{8,10},{9,11},{10,... | collective-permute-start | bytes 491528 | tf_op jit(solution)/shard_map/ppermute | solution.py:617
  84.1 11.1 %copy-start.15 = (f32[16,512]{1,0:T(8,128)S(1)}, f32[16,512]{1,0:T(8,128)}, u32[]{:S(2)}) copy-start(f32[16,512]{1,0:T(8,128)} %copy-done.14) | copy-start | bytes 98308
  84.2 14.0 %copy-start.26 = (bf16[2,512,512]{2,1,0:T(8,128)(2,1)S(1)}, bf16[2,512,512]{2,1,0:T(8,128)(2,1)}, u32[]{:S(2)}) copy-start(bf16[2,512,512]{2,1,0:T(8,128)(2,1)} %get-tuple-element.84) | copy-start | bytes 3145732
  84.2 5.5 %collective-permute-start.17 = (f32[80,512]{1,0:T(8,128)S(1)}, f32[80,512]{1,0:T(8,128)S(1)}, u32[]{:S(2)}, u32[]{:S(2)}) collective-permute-start(f32[80,512]{1,0:T(8,128)S(1)} %pad_maximum_fusion.2), channel_id=1, source_target_pairs={{0,4},{4,0},{8,12},{12,8},{16,20},{20,16},{24,28},{28,24},{1,5},{5... | collective-permute-start | bytes 491528 | tf_op jit(solution)/shard_map/ppermute | solution.py:617
  89.8 5.4 %collective-permute-start.18 = (f32[80,512]{1,0:T(8,128)S(1)}, f32[80,512]{1,0:T(8,128)S(1)}, u32[]{:S(2)}, u32[]{:S(2)}) collective-permute-start(f32[80,512]{1,0:T(8,128)S(1)} %pad_maximum_fusion.3), channel_id=1, source_target_pairs={{0,8},{4,12},{8,0},{12,4},{16,24},{20,28},{24,16},{28,20},{1,9},{5... | collective-permute-start | bytes 491528 | tf_op jit(solution)/shard_map/ppermute | solution.py:617
  91.6 16.4 %collective-permute-start.38 = (bf16[2,512,512]{2,1,0:T(8,128)(2,1)}, bf16[2,512,512]{2,1,0:T(8,128)(2,1)}, u32[]{:S(2)}, u32[]{:S(2)}) collective-permute-start(bf16[2,512,512]{2,1,0:T(8,128)(2,1)} %get-tuple-element.88), channel_id=1, source_target_pairs={{0,1},{1,0},{2,3},{3,2},{4,5},{5,4},{6,7},{7,6},{8,9},{9,8},{10,11... | collective-permute-start | bytes 3145736 | tf_op jit(solution)/shard_map/ppermute | solution.py:617
  91.6 19.9 %collective-permute-start.30 = (bf16[2,512,512]{2,1,0:T(8,128)(2,1)}, bf16[2,512,512]{2,1,0:T(8,128)(2,1)}, u32[]{:S(2)}, u32[]{:S(2)}) collective-permute-start(bf16[2,512,512]{2,1,0:T(8,128)(2,1)} %get-tuple-element.86), channel_id=1, source_target_pairs={{0,1},{1,0},{2,3},{3,2},{4,5},{5,4},{6,7},{7,6},{8,9},{9,8},{10,11... | collective-permute-start | bytes 3145736 | tf_op jit(solution)/shard_map/ppermute | solution.py:617
  95.2 8.0 %collective-permute-start.19 = (f32[80,512]{1,0:T(8,128)S(1)}, f32[80,512]{1,0:T(8,128)S(1)}, u32[]{:S(2)}, u32[]{:S(2)}) collective-permute-start(f32[80,512]{1,0:T(8,128)S(1)} %pad_maximum_fusion.4), channel_id=1, source_target_pairs={{0,16},{4,20},{8,24},{12,28},{16,0},{20,4},{24,8},{28,12},{1,17},{... | collective-permute-start | bytes 491528 | tf_op jit(solution)/shard_map/ppermute | solution.py:617
  98.2 16.0 %collective-permute-start.22 = (bf16[2,512,512]{2,1,0:T(8,128)(2,1)S(1)}, bf16[2,512,512]{2,1,0:T(8,128)(2,1)}, u32[]{:S(2)}, u32[]{:S(2)}) collective-permute-start(bf16[2,512,512]{2,1,0:T(8,128)(2,1)S(1)} %copy-done.26), channel_id=1, source_target_pairs={{0,1},{1,0},{2,3},{3,2},{4,5},{5,4},{6,7},{7,6},{8,9},{9,8},{10,11... | collective-permute-start | bytes 3145736 | tf_op jit(solution)/shard_map/ppermute | solution.py:617
  103.3 4.7 %collective-permute-start.20 = (f32[48,512]{1,0:T(8,128)S(1)}, f32[48,512]{1,0:T(8,128)S(1)}, u32[]{:S(2)}, u32[]{:S(2)}) collective-permute-start(f32[48,512]{1,0:T(8,128)S(1)} %slice_add_fusion), channel_id=1, source_target_pairs={{0,2},{1,3},{2,0},{3,1},{4,6},{5,7},{6,4},{7,5},{8,10},{9,11},{10,... | collective-permute-start | bytes 294920 | tf_op jit(solution)/shard_map/ppermute | solution.py:617
  108.0 8.9 %collective-permute-start.21 = (f32[96,512]{1,0:T(8,128)S(1)}, f32[96,512]{1,0:T(8,128)S(1)}, u32[]{:S(2)}, u32[]{:S(2)}) collective-permute-start(f32[96,512]{1,0:T(8,128)S(1)} %maximum_select_fusion.7), channel_id=1, source_target_pairs={{0,1},{1,0},{2,3},{3,2},{4,5},{5,4},{6,7},{7,6},{8,9},{9,8},{10,11... | collective-permute-start | bytes 589832 | tf_op jit(solution)/shard_map/ppermute | solution.py:617
  109.7 14.8 %collective-permute-start.39 = (bf16[1,512,512]{2,1,0:T(8,128)(2,1)S(1)}, bf16[1,512,512]{2,1,0:T(8,128)(2,1)S(1)}, u32[]{:S(2)}, u32[]{:S(2)}) collective-permute-start(bf16[1,512,512]{2,1,0:T(8,128)(2,1)S(1)} %slice.266), channel_id=1, source_target_pairs={{0,2},{1,3},{2,0},{3,1},{4,6},{5,7},{6,4},{7,5},{8,10},{9,11},{10,... | collective-permute-start | bytes 1572872 | tf_op jit(solution)/shard_map/ppermute | solution.py:617
  113.0 22.7 %collective-permute-start.31 = (bf16[1,512,512]{2,1,0:T(8,128)(2,1)S(1)}, bf16[1,512,512]{2,1,0:T(8,128)(2,1)S(1)}, u32[]{:S(2)}, u32[]{:S(2)}) collective-permute-start(bf16[1,512,512]{2,1,0:T(8,128)(2,1)S(1)} %slice.260), channel_id=1, source_target_pairs={{0,2},{1,3},{2,0},{3,1},{4,6},{5,7},{6,4},{7,5},{8,10},{9,11},{10,... | collective-permute-start | bytes 1572872 | tf_op jit(solution)/shard_map/ppermute | solution.py:617
  115.7 30.8 %collective-permute-start.23 = (bf16[1,512,512]{2,1,0:T(8,128)(2,1)S(1)}, bf16[1,512,512]{2,1,0:T(8,128)(2,1)S(1)}, u32[]{:S(2)}, u32[]{:S(2)}) collective-permute-start(bf16[1,512,512]{2,1,0:T(8,128)(2,1)S(1)} %slice.256), channel_id=1, source_target_pairs={{0,2},{1,3},{2,0},{3,1},{4,6},{5,7},{6,4},{7,5},{8,10},{9,11},{10,... | collective-permute-start | bytes 1572872 | tf_op jit(solution)/shard_map/ppermute | solution.py:617
  124.7 23.9 %collective-permute-start.40 = (bf16[256,512]{1,0:T(8,128)(2,1)S(1)}, bf16[256,512]{1,0:T(8,128)(2,1)S(1)}, u32[]{:S(2)}, u32[]{:S(2)}) collective-permute-start(bf16[256,512]{1,0:T(8,128)(2,1)S(1)} %dynamic-slice_bitcast_fusion), channel_id=1, source_target_pairs={{0,4},{4,0},{8,12},{12,8},{16,20},{20,16},{24,28},{28,24},{1,5},{5... | collective-permute-start | bytes 786440 | tf_op jit(solution)/shard_map/ppermute | solution.py:617
  135.9 13.5 %collective-permute-start.32 = (bf16[256,512]{1,0:T(8,128)(2,1)S(1)}, bf16[256,512]{1,0:T(8,128)(2,1)S(1)}, u32[]{:S(2)}, u32[]{:S(2)}) collective-permute-start(bf16[256,512]{1,0:T(8,128)(2,1)S(1)} %dynamic-slice_bitcast_fusion.1), channel_id=1, source_target_pairs={{0,4},{4,0},{8,12},{12,8},{16,20},{20,16},{24,28},{28,24},{1,5},{5... | collective-permute-start | bytes 786440 | tf_op jit(solution)/shard_map/ppermute | solution.py:617
  146.7 8.0 %collective-permute-start.24 = (bf16[256,512]{1,0:T(8,128)(2,1)S(1)}, bf16[256,512]{1,0:T(8,128)(2,1)S(1)}, u32[]{:S(2)}, u32[]{:S(2)}) collective-permute-start(bf16[256,512]{1,0:T(8,128)(2,1)S(1)} %dynamic-slice_bitcast_fusion.2), channel_id=1, source_target_pairs={{0,4},{4,0},{8,12},{12,8},{16,20},{20,16},{24,28},{28,24},{1,5},{5... | collective-permute-start | bytes 786440 | tf_op jit(solution)/shard_map/ppermute | solution.py:617
  148.6 7.2 %collective-permute-start.41 = (bf16[128,512]{1,0:T(8,128)(2,1)S(1)}, bf16[128,512]{1,0:T(8,128)(2,1)S(1)}, u32[]{:S(2)}, u32[]{:S(2)}) collective-permute-start(bf16[128,512]{1,0:T(8,128)(2,1)S(1)} %constant_dynamic-slice_fusion.1), channel_id=1, source_target_pairs={{0,8},{4,12},{8,0},{12,4},{16,24},{20,28},{24,16},{28,20},{1,9},{5... | collective-permute-start | bytes 393224 | tf_op jit(solution)/shard_map/ppermute | solution.py:617
  149.6 9.8 %collective-permute-start.33 = (bf16[128,512]{1,0:T(8,128)(2,1)S(1)}, bf16[128,512]{1,0:T(8,128)(2,1)S(1)}, u32[]{:S(2)}, u32[]{:S(2)}) collective-permute-start(bf16[128,512]{1,0:T(8,128)(2,1)S(1)} %constant_dynamic-slice_fusion.3), channel_id=1, source_target_pairs={{0,8},{4,12},{8,0},{12,4},{16,24},{20,28},{24,16},{28,20},{1,9},{5... | collective-permute-start | bytes 393224 | tf_op jit(solution)/shard_map/ppermute | solution.py:617
  154.8 5.7 %collective-permute-start.25 = (bf16[128,512]{1,0:T(8,128)(2,1)S(1)}, bf16[128,512]{1,0:T(8,128)(2,1)S(1)}, u32[]{:S(2)}, u32[]{:S(2)}) collective-permute-start(bf16[128,512]{1,0:T(8,128)(2,1)S(1)} %constant_dynamic-slice_fusion.5), channel_id=1, source_target_pairs={{0,8},{4,12},{8,0},{12,4},{16,24},{20,28},{24,16},{28,20},{1,9},{5... | collective-permute-start | bytes 393224 | tf_op jit(solution)/shard_map/ppermute | solution.py:617
  155.9 9.0 %collective-permute-start.42 = (bf16[64,512]{1,0:T(8,128)(2,1)S(1)}, bf16[64,512]{1,0:T(8,128)(2,1)S(1)}, u32[]{:S(2)}, u32[]{:S(2)}) collective-permute-start(bf16[64,512]{1,0:T(8,128)(2,1)S(1)} %constant_dynamic-slice_fusion), channel_id=1, source_target_pairs={{0,16},{4,20},{8,24},{12,28},{16,0},{20,4},{24,8},{28,12},{1,17},{... | collective-permute-start | bytes 196616 | tf_op jit(solution)/shard_map/ppermute | solution.py:617
  159.4 9.0 %collective-permute-start.34 = (bf16[64,512]{1,0:T(8,128)(2,1)S(1)}, bf16[64,512]{1,0:T(8,128)(2,1)S(1)}, u32[]{:S(2)}, u32[]{:S(2)}) collective-permute-start(bf16[64,512]{1,0:T(8,128)(2,1)S(1)} %constant_dynamic-slice_fusion.2), channel_id=1, source_target_pairs={{0,16},{4,20},{8,24},{12,28},{16,0},{20,4},{24,8},{28,12},{1,17},{... | collective-permute-start | bytes 196616 | tf_op jit(solution)/shard_map/ppermute | solution.py:617
  160.6 9.9 %collective-permute-start.26 = (bf16[64,512]{1,0:T(8,128)(2,1)S(1)}, bf16[64,512]{1,0:T(8,128)(2,1)S(1)}, u32[]{:S(2)}, u32[]{:S(2)}) collective-permute-start(bf16[64,512]{1,0:T(8,128)(2,1)S(1)} %constant_dynamic-slice_fusion.4), channel_id=1, source_target_pairs={{0,16},{4,20},{8,24},{12,28},{16,0},{20,4},{24,8},{28,12},{1,17},{... | collective-permute-start | bytes 196616 | tf_op jit(solution)/shard_map/ppermute | solution.py:617
  164.9 8.4 %collective-permute-start.43 = (bf16[64,512]{1,0:T(8,128)(2,1)S(1)}, bf16[64,512]{1,0:T(8,128)(2,1)S(1)}, u32[]{:S(2)}, u32[]{:S(2)}) collective-permute-start(bf16[64,512]{1,0:T(8,128)(2,1)S(1)} %add_convert_fusion.9), channel_id=1, source_target_pairs={{0,16},{4,20},{8,24},{12,28},{16,0},{20,4},{24,8},{28,12},{1,17},{... | collective-permute-start | bytes 196616 | tf_op jit(solution)/shard_map/ppermute | solution.py:617
  168.5 6.8 %collective-permute-start.35 = (bf16[64,512]{1,0:T(8,128)(2,1)S(1)}, bf16[64,512]{1,0:T(8,128)(2,1)S(1)}, u32[]{:S(2)}, u32[]{:S(2)}) collective-permute-start(bf16[64,512]{1,0:T(8,128)(2,1)S(1)} %add_convert_fusion.10), channel_id=1, source_target_pairs={{0,16},{4,20},{8,24},{12,28},{16,0},{20,4},{24,8},{28,12},{1,17},{... | collective-permute-start | bytes 196616 | tf_op jit(solution)/shard_map/ppermute | solution.py:617
  170.6 5.8 %collective-permute-start.27 = (bf16[64,512]{1,0:T(8,128)(2,1)S(1)}, bf16[64,512]{1,0:T(8,128)(2,1)S(1)}, u32[]{:S(2)}, u32[]{:S(2)}) collective-permute-start(bf16[64,512]{1,0:T(8,128)(2,1)S(1)} %add_convert_fusion.11), channel_id=1, source_target_pairs={{0,16},{4,20},{8,24},{12,28},{16,0},{20,4},{24,8},{28,12},{1,17},{... | collective-permute-start | bytes 196616 | tf_op jit(solution)/shard_map/ppermute | solution.py:617
  173.4 6.5 %collective-permute-start.44 = (bf16[128,512]{1,0:T(8,128)(2,1)S(1)}, bf16[128,512]{1,0:T(8,128)(2,1)S(1)}, u32[]{:S(2)}, u32[]{:S(2)}) collective-permute-start(bf16[128,512]{1,0:T(8,128)(2,1)S(1)} %maximum_select_fusion.10), channel_id=1, source_target_pairs={{0,8},{4,12},{8,0},{12,4},{16,24},{20,28},{24,16},{28,20},{1,9},{5... | collective-permute-start | bytes 393224 | tf_op jit(solution)/shard_map/ppermute | solution.py:617
  175.3 7.6 %collective-permute-start.36 = (bf16[128,512]{1,0:T(8,128)(2,1)S(1)}, bf16[128,512]{1,0:T(8,128)(2,1)S(1)}, u32[]{:S(2)}, u32[]{:S(2)}) collective-permute-start(bf16[128,512]{1,0:T(8,128)(2,1)S(1)} %maximum_select_fusion.9), channel_id=1, source_target_pairs={{0,8},{4,12},{8,0},{12,4},{16,24},{20,28},{24,16},{28,20},{1,9},{5... | collective-permute-start | bytes 393224 | tf_op jit(solution)/shard_map/ppermute | solution.py:617
  176.4 7.9 %collective-permute-start.28 = (bf16[128,512]{1,0:T(8,128)(2,1)S(1)}, bf16[128,512]{1,0:T(8,128)(2,1)S(1)}, u32[]{:S(2)}, u32[]{:S(2)}) collective-permute-start(bf16[128,512]{1,0:T(8,128)(2,1)S(1)} %maximum_select_fusion.8), channel_id=1, source_target_pairs={{0,8},{4,12},{8,0},{12,4},{16,24},{20,28},{24,16},{28,20},{1,9},{5... | collective-permute-start | bytes 393224 | tf_op jit(solution)/shard_map/ppermute | solution.py:617
  179.9 9.2 %collective-permute-start.45 = (bf16[256,512]{1,0:T(8,128)(2,1)S(1)}, bf16[256,512]{1,0:T(8,128)(2,1)S(1)}, u32[]{:S(2)}, u32[]{:S(2)}) collective-permute-start(bf16[256,512]{1,0:T(8,128)(2,1)S(1)} %maximum_select_fusion.6), channel_id=1, source_target_pairs={{0,4},{4,0},{8,12},{12,8},{16,20},{20,16},{24,28},{28,24},{1,5},{5... | collective-permute-start | bytes 786440 | tf_op jit(solution)/shard_map/ppermute | solution.py:617
  183.0 11.8 %collective-permute-start.37 = (bf16[256,512]{1,0:T(8,128)(2,1)S(1)}, bf16[256,512]{1,0:T(8,128)(2,1)S(1)}, u32[]{:S(2)}, u32[]{:S(2)}) collective-permute-start(bf16[256,512]{1,0:T(8,128)(2,1)S(1)} %maximum_select_fusion.5), channel_id=1, source_target_pairs={{0,4},{4,0},{8,12},{12,8},{16,20},{20,16},{24,28},{28,24},{1,5},{5... | collective-permute-start | bytes 786440 | tf_op jit(solution)/shard_map/ppermute | solution.py:617
  184.4 13.2 %collective-permute-start.29 = (bf16[256,512]{1,0:T(8,128)(2,1)S(1)}, bf16[256,512]{1,0:T(8,128)(2,1)S(1)}, u32[]{:S(2)}, u32[]{:S(2)}) collective-permute-start(bf16[256,512]{1,0:T(8,128)(2,1)S(1)} %maximum_select_fusion.4), channel_id=1, source_target_pairs={{0,4},{4,0},{8,12},{12,8},{16,20},{20,16},{24,28},{28,24},{1,5},{5... | collective-permute-start | bytes 786440 | tf_op jit(solution)/shard_map/ppermute | solution.py:617
  (9 other events, 24.8 us)

commit v2 on v1

v2 whole, which is shorter than its diff:
```python
import functools

import jax
import jax.numpy as jnp
from jax import lax
from jax.experimental import pallas as pl
from jax.experimental.pallas import tpu as pltpu
from jax.sharding import PartitionSpec as P

D = 512
Z = 128
NDIM = 16
CH = 128
PIECE = 16
PIECES = CH // PIECE
LANES = 128
BLOCKS = D // LANES
EPS = 1e-05
F32 = jnp.float32
BF16 = jnp.bfloat16
SMALL_ROWS = 64

VMEM = pl.BlockSpec(memory_space=pltpu.VMEM)
SMEM = pl.BlockSpec(memory_space=pltpu.SMEM)
ANY = pl.BlockSpec(memory_space=pl.ANY)


def sigmoid(v):
    return 0.5 * jnp.tanh(0.5 * v) + 0.5


def silu(v):
    return v * sigmoid(v)


def silu_slope(v):
    s = sigmoid(v)
    return s * (1.0 + v * (1.0 - s))


def mm(a, b):
    return jnp.dot(a, b, preferred_element_type=F32)


def mm_nt(a, b):
    return lax.dot_general(a, b, (((1,), (1,)), ((), ())), preferred_element_type=F32)


def mm_tn(a, b):
    return lax.dot_general(a, b, (((0,), (0,)), ((), ())), preferred_element_type=F32)


def normalized(v):
    center = v - jnp.mean(v, axis=-1, keepdims=True)
    scale = lax.rsqrt(jnp.mean(center * center, axis=-1, keepdims=True) + EPS)
    return center * scale, scale


def norm_back(grad, xhat, scale, gain):
    full = grad * gain
    return scale * (
        full
        - jnp.mean(full, axis=-1, keepdims=True)
        - xhat * jnp.mean(full * xhat, axis=-1, keepdims=True)
    )


def rows_of(s):
    return pl.ds(s * CH, CH)


def lanes_of(i):
    return pl.ds(pl.multiple_of((i % BLOCKS) * LANES, LANES), LANES)


def spread(row):
    return jnp.broadcast_to(row, (PIECES, LANES))


def piece_rows(s, t):
    return pl.ds(s * CH + t, PIECES, stride=PIECE)


def put_rows(ref, rows, value):
    for b in range(BLOCKS):
        ref[b, rows, :] = value[:, b * LANES : (b + 1) * LANES]


def get_rows(ref, rows):
    return jnp.concatenate([ref[b, rows, :] for b in range(BLOCKS)], axis=1)


def call(body, out, scratch, operands, specs, name, limit=2, outs=None):
    return pl.pallas_call(
        body,
        out_shape=out,
        in_specs=specs,
        out_specs=outs or jax.tree.map(lambda _: VMEM, out),
        scratch_shapes=scratch,
        name=name,
        compiler_params=pltpu.CompilerParams(vmem_limit_bytes=limit * 1024 * 1024),
    )(*operands)


def shape(dims, dtype=F32):
    return jax.ShapeDtypeStruct(dims, dtype)


def enter_kernel(seqs, *refs):
    far, refs = refs[:5], refs[5:]
    w_value, w_reset, w_hidden, w_update, u_hidden, w_in, w_out = refs[:7]
    normed, par, before, ends, low, p1, p2, p3, h1, h2, h3 = refs[7:18]
    tok, gain, rate, beta, eta, nf, tab, sems = refs[18:]
    copies = []

    def add(source, target):
        copies.append(pltpu.make_async_copy(source, target, sems.at[len(copies)]))

    for pair in zip(far, (tok, gain, rate, beta, eta)):
        add(*pair)
    vb, nb, cut = w_value.shape[1], w_hidden.shape[0], D // 2
    at = pl.ds(pl.multiple_of(jnp.bitwise_and(lax.axis_index("seq"), 1) * cut, cut), cut)
    for i, w in enumerate((w_value, w_reset)):
        lane = pl.ds(i * vb, vb)
        add(w.at[at, :], h1.at[:, lane])
        add(w, p1.at[:, lane])
    top = 0
    for w in (w_hidden, w_update, u_hidden):
        row = pl.ds(top, w.shape[0])
        add(w.at[:, at], h2.at[row, :])
        add(w, p2.at[row, :])
        top += w.shape[0]
    add(w_in.at[at, :], h3.at[:, pl.ds(0, vb)])
    add(w_in, p3.at[:, pl.ds(0, vb)])
    for k in range(D // vb):
        row = pl.ds(k * vb, vb)
        add(w_out.at[:, row], p3.at[row, pl.ds(vb, vb)])
        if k < cut // vb:
            first = pl.multiple_of(jnp.bitwise_and(lax.axis_index("seq"), 1) * cut + k * vb, vb)
            add(w_out.at[:, pl.ds(first, vb)], h3.at[row, pl.ds(vb, vb)])
    for c in copies:
        c.start()
    for c in copies[:5]:
        c.wait()
    r = rate[...]
    d = 1.0 - r
    par[0] = d
    par[1] = jnp.log(d)
    par[2] = jnp.sqrt(r * (2.0 - r)) * beta[...]
    par[3] = eta[...]
    d2 = d * d
    d4 = d2 * d2
    d8 = d4 * d4
    d15 = d8 * d4 * d2 * d
    q = d8 * d8
    tab[0] = q
    tab[1] = 16.0 * d15
    tab[2] = q * q
    tab[3] = 32.0 * q * d15
    tab[4] = q * q * q * q
    tab[5] = 64.0 * q * q * q * d15
    for s in range(seqs):
        xhat, _ = normalized(tok[s].astype(F32))
        scaled = (xhat * gain[...]).astype(BF16)
        normed[rows_of(s), :] = scaled
        put_rows(nf, rows_of(s), scaled.astype(F32))
    place = lax.broadcasted_iota(jnp.int32, (PIECES, LANES), 0)

    def body(i, carry):
        s = i // BLOCKS
        lane = lanes_of(i)
        xs = [nf[i % BLOCKS, piece_rows(s, t), :] for t in range(PIECE)]
        for j0 in range(0, NDIM, 8):
            ds = [spread(par[0, j0 + j : j0 + j + 1, lane]) for j in range(8)]
            st = [xs[0]] * 8
            ta = [jnp.zeros((PIECES, LANES), F32)] * 8
            for t in range(1, PIECE):
                for j in range(8):
                    ta[j] = ds[j] * ta[j] + st[j]
                    st[j] = ds[j] * st[j] + xs[t]
            for j in range(8):
                a, b = st[j], ta[j]
                for k, step in enumerate((1, 2, 4)):
                    qm = spread(tab[2 * k, j0 + j : j0 + j + 1, lane])
                    rm = spread(tab[2 * k + 1, j0 + j : j0 + j + 1, lane])
                    sa = jnp.where(place >= step, pltpu.roll(a, step, 0), 0.0)
                    sb = jnp.where(place >= step, pltpu.roll(b, step, 0), 0.0)
                    b = b + qm * sb + rm * sa
                    a = a + qm * sa
                before[0, s, j0 + j, :, lane] = jnp.where(place >= 1, pltpu.roll(a, 1, 0), 0.0)
                before[1, s, j0 + j, :, lane] = jnp.where(place >= 1, pltpu.roll(b, 1, 0), 0.0)
                ends[0, s, j0 + j : j0 + j + 1, lane] = a[PIECES - 1 :]
                ends[1, s, j0 + j : j0 + j + 1, lane] = b[PIECES - 1 :]
        return carry

    lax.fori_loop(0, seqs * BLOCKS, body, 0)
    low[...] = ends[...].astype(BF16)
    for c in copies[5:]:
        c.wait()


def piece_powers(par, pw):
    k = lax.broadcasted_iota(jnp.int32, (PIECES, D), 0).astype(F32) * PIECE
    for j in range(NDIM):
        pw[j] = jnp.exp(k * par[1, j : j + 1, :])


def take_weights(refs, tp, first, second):
    top = tp // 2
    near = [refs[r * first : (r + 1) * first] for r in range(top)]
    refs = refs[top * first :]
    far = [refs[r * second : (r + 1) * second] for r in range(top)]
    return near, far, refs[top * second :]


def gate_copies(tp, ids, near, far, w1, w2, sems):
    top, cut = tp // 2, D // 2
    upper = jnp.bitwise_and(ids[1], 1)
    copies = []

    def add(source, target):
        copies.append(pltpu.make_async_copy(source, target, sems.at[len(copies)]))

    for r in range(top):
        add(near[r][0], w1.at[r])
        add(near[r][1], w2.at[r])
        mine1, other1, mine2, other2 = far[r]
        for part1, part2, at in ((mine1, mine2, upper), (other1, other2, 1 - upper)):
            at = pl.ds(pl.multiple_of(at * cut, cut), cut)
            add(part1, w1.at[top + r, at, :])
            add(part2, w2.at[top + r, :, at])
    for c in copies:
        c.start()
    return copies


def gate_rows(tp, me, w2, whu):
    nb = D // tp
    for r in range(tp):
        row = pl.ds(pl.multiple_of(jnp.bitwise_xor(me, r) * nb, nb), nb)
        whu[row, pl.ds(0, D)] = w2[r, pl.ds(0, nb), :]
        whu[row, pl.ds(D, D)] = w2[r, pl.ds(nb, nb), :]


def look_kernel(
    seqs, hops, ids, normed, par, before, skip, wsh, qg, kg, rb, *refs
):
    recvs, refs = refs[: len(hops)], refs[len(hops) :]
    st_in, skip_pre, mixed, shared_pre, prob, nf, sm, pw = refs
    place = ids[2]
    put_rows(nf, slice(None), normed[...].astype(F32))
    piece_powers(par, pw)
    logd = par[1]
    dinv = 1.0 / par[0]
    for s in range(seqs):
        a = jnp.zeros((NDIM, D), F32)
        b = jnp.zeros((NDIM, D), F32)
        for (shift, k), got in zip(hops, recvs):
            end = jnp.left_shift(jnp.bitwise_xor(jnp.right_shift(place, shift), k) + 1, shift)
            off = (place - end).astype(F32) * float(CH)
            power = jnp.where(place >= end, jnp.exp(jnp.maximum(off, 0.0) * logd), 0.0)
            oa = got[0, s].astype(F32) * power
            b = b + got[1, s].astype(F32) * power + off * oa * dinv
            a = a + oa
        st_in[0, s] = a
        st_in[1, s] = b

    def ema(i, carry):
        s = i // BLOCKS
        lane = lanes_of(i)
        row = [pl.ds(j, 1) for j in range(NDIM)]
        ds = [spread(par[0, row[j], lane]) for j in range(NDIM)]
        ws = [spread(par[2, row[j], lane] * par[3, row[j], lane]) for j in range(NDIM)]
        st = [
            before[0, s, j, :, lane] + pw[j, :, lane] * st_in[0, s, row[j], lane]
            for j in range(NDIM)
        ]
        for t in range(PIECE):
            x = nf[i % BLOCKS, piece_rows(s, t), :]
            parts = [None, None]
            for j in range(NDIM):
                st[j] = ds[j] * st[j] + x
                term = ws[j] * st[j]
                parts[j % 2] = term if parts[j % 2] is None else parts[j % 2] + term
            sm[i % BLOCKS, piece_rows(s, t), :] = parts[0] + parts[1]
        return carry

    lax.fori_loop(0, seqs * BLOCKS, ema, 0)
    for s in range(seqs):
        pre = get_rows(sm, rows_of(s)) + skip[...] * get_rows(nf, rows_of(s))
        skip_pre[rows_of(s), :] = pre
        mixed[rows_of(s), :] = silu(pre).astype(BF16)
    sp = mm(mixed[...], wsh[...])
    shared_pre[...] = sp
    shared = silu(sp)
    query = (shared * qg[...]).astype(BF16)
    keys = (shared * kg[...]).astype(BF16)
    t_at = lax.broadcasted_iota(jnp.int32, (CH, CH), 0)
    s_at = lax.broadcasted_iota(jnp.int32, (CH, CH), 1)
    bias_t = jnp.broadcast_to(rb[...], (CH, CH))
    for bit in range(7):
        bias_t = jnp.where(
            jnp.bitwise_and(t_at, 1 << bit) > 0, pltpu.roll(bias_t, 1 << bit, 1), bias_t
        )
    bias = bias_t.T
    for s in range(seqs):
        raw = mm_nt(query[s * CH : (s + 1) * CH], keys[s * CH : (s + 1) * CH]) * Z ** (-0.5)
        live = (place * CH + s_at) < ids[3 + s]
        allowed = (s_at <= t_at) & (live | (s_at == t_at))
        masked = jnp.where(allowed, raw + bias, -1e30)
        top = jnp.max(masked, axis=-1, keepdims=True)
        weights = jnp.where(allowed, jnp.exp(masked - top), 0.0)
        prob[s] = weights / jnp.sum(weights, axis=-1, keepdims=True)


def mix_kernel(seqs, tp, ids, tok, normed, mixed, prob, *refs):
    near, far, refs = take_weights(refs, tp, 2, 4)
    (
        values, value_pre, reset_pre, attended, gated, hidden_pre, update_pre, middle,
        w1, w2, whu, sems,
    ) = refs
    vb = values.shape[2]
    nb = D // tp
    copies = gate_copies(tp, ids, near, far, w1, w2, sems)
    for c in copies:
        c.wait()
    gate_rows(tp, ids[0], w2, whu)
    hu = mm(mixed[...], whu[...])
    hidden_pre[...] = hu[:, :D]
    update_pre[...] = hu[:, D:]

    def block(r, carry):
        vp = mm(normed[...], w1[r, :, :vb])
        value_pre[r] = vp
        v = silu(vp).astype(BF16)
        values[r] = v
        rp = mm(mixed[...], w1[r, :, vb:])
        reset_pre[r] = rp
        gate = silu(rp)
        for s in range(seqs):
            att = mm(prob[s].astype(BF16), v[s * CH : (s + 1) * CH])
            attended[r, rows_of(s), :] = att
            gated[r, rows_of(s), :] = (gate[s * CH : (s + 1) * CH] * att).astype(BF16)
        hidden_pre[...] += mm(gated[r], w2[r, pl.ds(2 * nb, vb), :])
        return carry

    lax.fori_loop(0, tp, block, 0)
    for s in range(seqs):
        x = tok[s].astype(F32)
        middle[rows_of(s), :] = x + sigmoid(update_pre[rows_of(s), :]) * (
            silu(hidden_pre[rows_of(s), :]) - x
        )


def ffn_kernel(seqs, tp, ids, tok, cot, middle, hidden_pre, update_pre, gain2, *refs):
    near, far, refs = take_weights(refs, tp, 1, 2)
    (
        out, keep, send, grad_hu, resid, grad_gain2,
        w3, n2, lg, acc, gn2, sems,
    ) = refs
    vb = w3.shape[2] // 2
    top, half = tp // 2, D // 2
    cuts = D // vb
    upper = jnp.bitwise_and(ids[1], 1)
    copies = []

    def add(source, target):
        copies.append(pltpu.make_async_copy(source, target, sems.at[len(copies)]))

    for r in range(top):
        add(near[r][0], w3.at[r])
        for part, at in zip(far[r], (upper, 1 - upper)):
            add(part, w3.at[top + r, pl.ds(pl.multiple_of(at * half, half), half), :])
    for c in copies:
        c.start()
    place = ids[2]
    xhat, scale = normalized(middle[...])
    n2[...] = (xhat * gain2[...]).astype(BF16)
    at = lax.broadcasted_iota(jnp.int32, (CH, D), 0) + place * CH
    for s in range(seqs):
        lg[rows_of(s), :] = jnp.where(at < ids[3 + s], cot[s].astype(F32), 0.0).astype(BF16)
    acc[...] = jnp.zeros_like(acc)
    gn2[...] = jnp.zeros_like(gn2)
    for c in copies:
        c.wait()

    def block(h, carry):
        for odd in range(2):
            r = 2 * h + odd
            grads = (keep, send)[odd]
            pre = mm(n2[...], w3[r, :, :vb])
            inner = silu(pre).astype(BF16)
            back = None
            for k in range(cuts):
                cols = slice(k * vb, (k + 1) * vb)
                w_out = w3[r, cols, vb:]
                acc[:, cols] += mm(inner, w_out)
                term = mm_nt(lg[:, cols], w_out)
                back = term if back is None else back + term
            gip = (back * silu_slope(pre)).astype(BF16)
            gn2[...] += mm_nt(gip, w3[r, :, :vb])
            grads[h, :, :vb] = mm_tn(n2[...], gip).astype(BF16)
            gwo = mm_tn(inner, lg[...]).astype(BF16)
            for k in range(cuts):
                grads[h, k * vb : (k + 1) * vb, vb:] = gwo[:, k * vb : (k + 1) * vb]
        return carry

    lax.fori_loop(0, tp // 2, block, 0)
    mid = middle[...]
    out[...] = (mid + acc[...]).astype(BF16)
    grad = gn2[...]
    grad_gain2[...] = jnp.sum(grad * xhat, axis=0, keepdims=True)
    gm = lg[...].astype(F32) + norm_back(grad, xhat, scale, gain2[...])
    for s in range(seqs):
        x = tok[s].astype(F32)
        g = gm[s * CH : (s + 1) * CH]
        hp = hidden_pre[rows_of(s), :]
        update = sigmoid(update_pre[rows_of(s), :])
        grad_hu[rows_of(s), :D] = (g * update * silu_slope(hp)).astype(BF16)
        grad_hu[rows_of(s), D:] = (g * (silu(hp) - x) * update * (1.0 - update)).astype(BF16)
        resid[rows_of(s), :] = g * (1.0 - update)


def gates_kernel(tp, ids, mixed, gated, grad_hu, keep2, send2, ghu):
    nb = D // tp
    vb = gated.shape[2]
    wide = 2 * vb
    me = ids[0]
    ghu[...] = mm_tn(mixed[...], grad_hu[...])

    def block(h, carry):
        for odd in range(2):
            r = 2 * h + odd
            g2 = (keep2, send2)[odd]
            row = pl.ds(pl.multiple_of(jnp.bitwise_xor(me, r) * nb, nb), nb)
            gu = mm_tn(gated[r], grad_hu[:, :D]).astype(BF16)
            for k in range(D // wide):
                top = k * (2 * nb + vb)
                g2[h, pl.ds(top, nb), :] = ghu[row, pl.ds(k * wide, wide)].astype(BF16)
                g2[h, pl.ds(top + nb, nb), :] = ghu[row, pl.ds(D + k * wide, wide)].astype(BF16)
                g2[h, pl.ds(top + 2 * nb, vb), :] = gu[:, k * wide : (k + 1) * wide]
        return carry

    lax.fori_loop(0, tp // 2, block, 0)


def back_kernel(
    seqs, tp,
    ids, normed, mixed, skip_pre, shared_pre, prob, values, value_pre, reset_pre, attended,
    grad_hu, par, wsh, qg, kg, *refs,
):
    near, far, refs = take_weights(refs, tp, 2, 4)
    (
        keep1, send1, grad_skip, grad_normed, after, ends, grad_wsh, misc,
        w1, w2, whu, gm, gp, tab, sems,
    ) = refs
    vb = values.shape[2]
    nb = D // tp
    me = ids[0]
    copies = gate_copies(tp, ids, near, far, w1, w2, sems)
    gp[...] = jnp.zeros_like(gp)
    grad_normed[...] = jnp.zeros_like(grad_normed)
    for c in copies:
        c.wait()
    gate_rows(tp, me, w2, whu)
    gm[...] = mm_nt(grad_hu[...], whu[...])

    def block(h, carry):
        for odd in range(2):
            r = 2 * h + odd
            g1 = (keep1, send1)[odd]
            gg = mm_nt(grad_hu[:, :D], w2[r, pl.ds(2 * nb, vb), :])
            rp = reset_pre[r]
            sig = sigmoid(rp)
            ga = (gg * (rp * sig)).astype(BF16)
            grp = (gg * attended[r] * (sig * (1.0 + rp * (1.0 - sig)))).astype(BF16)
            g1[h, :, vb:] = mm_tn(mixed[...], grp).astype(BF16)
            gm[...] += mm_nt(grp, w1[r, :, vb:])
            gvs = []
            for s in range(seqs):
                part = ga[s * CH : (s + 1) * CH]
                gvs.append(mm_tn(prob[s].astype(BF16), part))
                gp[s] += mm_nt(part, values[r, rows_of(s), :])
            gv = jnp.concatenate(gvs, axis=0) if seqs > 1 else gvs[0]
            gvp = (gv * silu_slope(value_pre[r])).astype(BF16)
            g1[h, :, :vb] = mm_tn(normed[...], gvp).astype(BF16)
            grad_normed[...] += mm_nt(gvp, w1[r, :, :vb])
        return carry

    lax.fori_loop(0, tp // 2, block, 0)
    sp = shared_pre[...]
    shared = silu(sp)
    query = (shared * qg[...]).astype(BF16)
    keys = (shared * kg[...]).astype(BF16)
    total = jnp.zeros((CH, CH), F32)
    gqs = []
    gks = []
    for s in range(seqs):
        pr = prob[s]
        low = (pr * (gp[s] - jnp.sum(pr * gp[s], axis=-1, keepdims=True))).astype(BF16)
        total = total + low.astype(F32)
        gqs.append(mm(low, keys[s * CH : (s + 1) * CH]) * Z ** (-0.5))
        gks.append(mm_tn(low, query[s * CH : (s + 1) * CH]) * Z ** (-0.5))
    gq = jnp.concatenate(gqs, axis=0) if seqs > 1 else gqs[0]
    gk = jnp.concatenate(gks, axis=0) if seqs > 1 else gks[0]
    turned = total.T
    s_at = lax.broadcasted_iota(jnp.int32, (CH, CH), 0)
    for bit in range(7):
        turned = jnp.where(
            jnp.bitwise_and(s_at, 1 << bit) > 0, pltpu.roll(turned, CH - (1 << bit), 1), turned
        )
    misc[...] = jnp.concatenate(
        [
            jnp.sum(gq * shared, axis=0, keepdims=True),
            jnp.sum(gk * shared, axis=0, keepdims=True),
            jnp.sum(turned, axis=0, keepdims=True),
            jnp.zeros((1, D - 3 * Z), F32),
        ],
        axis=1,
    )
    gsp = ((gq * qg[...] + gk * kg[...]) * silu_slope(sp)).astype(BF16)
    grad_wsh[...] = mm_tn(mixed[...], gsp)
    put_rows(
        grad_skip,
        slice(None),
        (gm[...] + mm_nt(gsp, wsh[...])) * silu_slope(skip_pre[...]),
    )
    d = par[0]
    d2 = d * d
    d4 = d2 * d2
    d8 = d4 * d4
    q = d8 * d8
    tab[0] = q
    tab[1] = q * q
    tab[2] = q * q * q * q
    place = lax.broadcasted_iota(jnp.int32, (PIECES, LANES), 0)

    def body(i, carry):
        s = i // BLOCKS
        lane = lanes_of(i)
        ds = [spread(par[0, j : j + 1, lane]) for j in range(NDIM)]
        ad = [grad_skip[i % BLOCKS, piece_rows(s, PIECE - 1), :]] * NDIM
        for t in range(PIECE - 2, -1, -1):
            g = grad_skip[i % BLOCKS, piece_rows(s, t), :]
            for j in range(NDIM):
                ad[j] = ds[j] * ad[j] + g
        for j in range(NDIM):
            a = ad[j]
            for k, step in enumerate((1, 2, 4)):
                qm = spread(tab[k, j : j + 1, lane])
                a = a + qm * jnp.where(place < PIECES - step, pltpu.roll(a, PIECES - step, 0), 0.0)
            after[s, j, :, lane] = jnp.where(
                place < PIECES - 1, pltpu.roll(a, PIECES - 1, 0), 0.0
            )
            ends[s, j : j + 1, lane] = a[:1]
        return carry

    lax.fori_loop(0, seqs * BLOCKS, body, 0)


def sums_kernel(
    seqs,
    ids, tok, normed, grad_skip, grad_normed, par, before, st_in, skip, gain2_row, misc, grad_wsh,
    keep, send, table, nf, pw,
):
    put_rows(nf, slice(None), normed[...].astype(F32))
    piece_powers(par, pw)
    count = D // (D // Z)
    small = table.at[count:, :]
    small[...] = jnp.zeros_like(small)
    for k in range(D // Z):
        table[:count, k * Z : (k + 1) * Z] = grad_wsh[k * count : (k + 1) * count, :]

    def body(i, carry):
        s = i // BLOCKS
        lane = lanes_of(i)
        k16 = lax.broadcasted_iota(jnp.int32, (PIECES, LANES), 0).astype(F32) * PIECE
        for j0 in range(0, NDIM, 8):
            row = [pl.ds(j0 + j, 1) for j in range(8)]
            ds = [spread(par[0, row[j], lane]) for j in range(8)]
            st, ta, q, r = [], [], [], []
            for j in range(8):
                e = pw[j0 + j, :, lane] * st_in[0, s, row[j], lane]
                st.append(before[0, s, j0 + j, :, lane] + e)
                ta.append(
                    before[1, s, j0 + j, :, lane]
                    + pw[j0 + j, :, lane] * st_in[1, s, row[j], lane]
                    + k16 * e / ds[j]
                )
                q.append(jnp.zeros((PIECES, LANES), F32))
                r.append(jnp.zeros((PIECES, LANES), F32))
            for t in range(PIECE):
                x = nf[i % BLOCKS, piece_rows(s, t), :]
                g = grad_skip[i % BLOCKS, piece_rows(s, t), :]
                for j in range(8):
                    ta[j] = ds[j] * ta[j] + st[j]
                    st[j] = ds[j] * st[j] + x
                    q[j] = q[j] + g * st[j]
                    r[j] = r[j] + g * ta[j]
            for j in range(8):
                small[pl.ds(j0 + j, 1), lane] += jnp.sum(q[j], axis=0, keepdims=True)
                small[pl.ds(NDIM + j0 + j, 1), lane] += jnp.sum(r[j], axis=0, keepdims=True)
        return carry

    lax.fori_loop(0, seqs * BLOCKS, body, 0)
    gsk = jnp.zeros((1, D), F32)
    gn1 = jnp.zeros((1, D), F32)
    for s in range(seqs):
        xhat, _ = normalized(tok[s].astype(F32))
        g = get_rows(grad_skip, rows_of(s))
        direct = g * skip[...] + grad_normed[rows_of(s), :]
        gsk = gsk + jnp.sum(g * get_rows(nf, rows_of(s)), axis=0, keepdims=True)
        gn1 = gn1 + jnp.sum(direct * xhat, axis=0, keepdims=True)
    small[2 * NDIM : 2 * NDIM + 1, :] = gsk
    small[2 * NDIM + 1 : 2 * NDIM + 2, :] = gn1
    small[2 * NDIM + 2 : 2 * NDIM + 3, :] = gain2_row[...]
    small[2 * NDIM + 3 : 2 * NDIM + 4, :] = misc[...]
    half = keep.shape[0]
    mine = jnp.bitwise_and(ids[0], 1) * half
    keep[...] = table[pl.ds(pl.multiple_of(mine, 8), half), :]
    send[...] = table[pl.ds(pl.multiple_of(half - mine, 8), half), :]


def pair_kernel(bit, ids, mine, other, out):
    half = mine.shape[0]
    upper = jnp.where(jnp.bitwise_and(ids[0], bit) > 0, half, 0)
    out[pl.ds(pl.multiple_of(upper, 8), half), :] = mine[...]
    out[pl.ds(pl.multiple_of(half - upper, 8), half), :] = other[...]


def finish_kernel(
    ids, par, rate, beta, gain, mine, other,
    grad_gain, grad_rate, grad_beta, grad_eta, grad_skip, grad_wsh, grad_qg, grad_kg, grad_rb,
    grad_gain2, table,
):
    pair_kernel(1, ids, mine, other, table)
    count = D // (D // Z)
    for k in range(D // Z):
        grad_wsh[k * count : (k + 1) * count, :] = table[:count, k * Z : (k + 1) * Z]
    small = table.at[count:, :]
    inflow, eta, r = par[2], par[3], rate[...]
    root = jnp.sqrt(r * (2.0 - r))
    q_sum = small[:NDIM, :]
    grad_inflow = eta * q_sum
    grad_decay = eta * inflow * small[NDIM : 2 * NDIM, :]
    grad_rate[...] = grad_inflow * beta[...] * (1.0 - r) / root - grad_decay
    grad_beta[...] = grad_inflow * root
    grad_eta[...] = inflow * q_sum
    row = [small[2 * NDIM + i : 2 * NDIM + i + 1, :] for i in range(4)]
    grad_skip[...] = row[0]
    grad_gain[...] = row[1] + jnp.sum(inflow * grad_inflow, axis=0, keepdims=True) / gain[...]
    grad_gain2[...] = row[2]
    grad_qg[...] = row[3][:, :Z]
    grad_kg[...] = row[3][:, Z : 2 * Z]
    grad_rb[...] = row[3][:, 2 * Z : 3 * Z]


def leave_kernel(
    seqs, tops, ids, tok, par, grad_skip, grad_normed, behind, resid, gain, skip, *refs
):
    levels = len(tops)
    recvs, refs = refs[:levels], refs[levels:]
    grad_tokens, ad_in, pw, sm = refs
    place = ids[2]
    logd = par[1]
    gots = [get_wide(recvs[k], tops[k], seqs * NDIM) for k in range(levels)]
    for s in range(seqs):
        a = jnp.zeros((NDIM, D), F32)
        for k in range(levels):
            low = jnp.bitwise_and(place, 1 << k) == 0
            off = jnp.bitwise_and(place, (1 << k) - 1)
            away = ((1 << k) - 1 - off).astype(F32) * float(CH)
            got = gots[k][s * NDIM : (s + 1) * NDIM]
            a = a + got * jnp.where(low, jnp.exp(away * logd), 0.0)
        ad_in[s] = a
    k = (PIECES - 1 - lax.broadcasted_iota(jnp.int32, (PIECES, D), 0)).astype(F32) * PIECE
    for j in range(NDIM):
        pw[j] = jnp.exp(k * par[1, j : j + 1, :])

    def body(i, carry):
        s = i // BLOCKS
        lane = lanes_of(i)
        row = [pl.ds(j, 1) for j in range(NDIM)]
        ds = [spread(par[0, row[j], lane]) for j in range(NDIM)]
        ws = [spread(par[2, row[j], lane] * par[3, row[j], lane]) for j in range(NDIM)]
        ad = [
            behind[s, j, :, lane] + pw[j, :, lane] * ad_in[s, row[j], lane] for j in range(NDIM)
        ]
        for t in range(PIECE - 1, -1, -1):
            g = grad_skip[i % BLOCKS, piece_rows(s, t), :]
            parts = [None, None]
            for j in range(NDIM):
                ad[j] = ds[j] * ad[j] + g
                term = ws[j] * ad[j]
                parts[j % 2] = term if parts[j % 2] is None else parts[j % 2] + term
            sm[i % BLOCKS, piece_rows(s, t), :] = parts[0] + parts[1]
        return carry

    lax.fori_loop(0, seqs * BLOCKS, body, 0)
    for s in range(seqs):
        xhat, scale = normalized(tok[s].astype(F32))
        grad = (
            get_rows(sm, rows_of(s))
            + get_rows(grad_skip, rows_of(s)) * skip[...]
            + grad_normed[rows_of(s), :]
        )
        grad_tokens[s] = (
            resid[rows_of(s), :] + norm_back(grad, xhat, scale, gain[...])
        ).astype(BF16)


def hop_kernel(seqs, shift, count, ids, par, state, *refs):
    others, (total, low) = refs[: count - 1], refs[count - 1 :]
    mine = jnp.bitwise_and(jnp.right_shift(ids[2], shift), count - 1)
    logd = par[1]
    sums = [[None, None] for _ in range(seqs)]
    for k in range(count):
        after = (count - 1 - jnp.bitwise_xor(mine, k)).astype(F32) * float(CH << shift)
        power = jnp.exp(after * logd)
        slope = after * jnp.exp((after - 1.0) * logd)
        for s in range(seqs):
            a, b = (state[0, s], state[1, s]) if k == 0 else (
                others[k - 1][0, s].astype(F32), others[k - 1][1, s].astype(F32)
            )
            a, b = power * a, power * b + slope * a
            sums[s] = [a, b] if k == 0 else [sums[s][0] + a, sums[s][1] + b]
    for s in range(seqs):
        for i in range(2):
            total[i, s] = sums[s][i]
            low[i, s] = sums[s][i].astype(BF16)


def put_wide(ref, top, value):
    wide = ref.shape[1]
    count = value.shape[0]
    for k in range(D // wide):
        ref[pl.ds(top + k * count, count), :] = value[:, k * wide : (k + 1) * wide].astype(ref.dtype)


def get_wide(ref, top, count):
    wide = ref.shape[1]
    runs = [ref[pl.ds(top + k * count, count), :].astype(F32) for k in range(D // wide)]
    return jnp.concatenate(runs, axis=1) if len(runs) > 1 else runs[0]


def first_back_hop(seqs, joins, ids, par, own, other, sums, got, out, keep, payload):
    rows = seqs * NDIM
    fold_lanes = D // payload.shape[1]
    if joins:
        join_adjoint(seqs, 0, ids, par, own, other[...], out)
    else:
        out[...] = own[...]
    put_wide(payload, 0, out[...])
    half = keep.shape[0]
    upper = jnp.where(jnp.bitwise_and(ids[0], 2) > 0, half, 0)
    mine = pl.ds(pl.multiple_of(upper, 8), half)
    theirs = pl.ds(pl.multiple_of(half - upper, 8), half)
    keep[...] = sums[mine, :] + got[mine, :]
    put_wide(payload, rows * fold_lanes, sums[theirs, :] + got[theirs, :])


def join_adjoint(seqs, level, ids, par, own, got, out):
    upper = jnp.bitwise_and(ids[2], 1 << level) > 0
    power = jnp.exp(float(CH << level) * par[1])
    for s in range(seqs):
        row = slice(s * NDIM, (s + 1) * NDIM)
        early = jnp.where(upper, got[row], own[row, :])
        late = jnp.where(upper, own[row, :], got[row])
        out[row, :] = early + power * late


def chain_hop(seqs, level, split, halved, top, ids, par, own, kept, sent, other, out, keep, payload, base):
    rows = seqs * NDIM
    lanes = D // other.shape[1]
    if out is not None:
        join_adjoint(seqs, level, ids, par, own, get_wide(other, top, rows), out)
        put_wide(payload, base, out[...])
    half = keep.shape[0]
    if split:
        upper = jnp.bitwise_and(ids[0], split) > 0
        got = get_wide(other, top + rows * lanes, 2 * half)
        first, second = kept[:half, :] + got[:half], kept[half:, :] + got[half:]
        keep[...] = jnp.where(upper, second, first)
        put_wide(payload, base + rows * lanes, jnp.where(upper, first, second))
    else:
        mine = kept[...] if halved else get_wide(sent, top + rows * lanes, half)
        total = mine + get_wide(other, top + rows * lanes, half)
        keep[...] = total
        if payload is not None:
            put_wide(payload, base + rows * lanes, total)


def back_hop(seqs, level, split, halved, ids, par, own, kept, sent, other, out, keep, payload):
    chain_hop(
        seqs, level, split, halved, 0, ids, par, own, kept, sent, other, out, keep, payload, 0
    )


def split_rows(count, cut, place, k):
    shift, bits = cut
    rows = count >> bits
    sub = jnp.bitwise_and(jnp.right_shift(place, shift), (1 << bits) - 1)
    return pl.multiple_of(jnp.bitwise_xor(sub, k) * rows, rows), rows


def add_rows(parts, start, high, out, top, lane, width, at):
    step = min(64, high)

    def body(i, carry):
        row = pl.ds(pl.multiple_of(start + i * step, step), step)
        total = parts[0][row, lane : lane + width].astype(F32)
        for other in parts[1:]:
            total = total + other[row, lane : lane + width].astype(F32)
        out[pl.ds(pl.multiple_of(top + i * step, 16), step), at : at + width] = total.astype(BF16)
        return carry

    lax.fori_loop(0, high // step, body, 0)


def fold_kernel(jobs, inputs, ids, *refs):
    parts, outs = refs[:inputs], refs[inputs:]
    at = 0
    for count, lane, width, cut, targets in jobs:
        own = parts[at : at + count]
        at += count
        blocks, rows, _ = own[0].shape
        for k, (target, block, offset) in enumerate(targets):
            if cut == "tp":
                ranges, start, high = (k,), 0, rows
            elif cut is None:
                ranges, start, high = range(blocks), 0, rows
            else:
                start, high = split_rows(rows, cut, ids[1], k)
                ranges = range(blocks)
            for to, b in enumerate(ranges):
                add_rows(
                    [p.at[b] for p in own], start, high, outs[target].at[block + to], 0, lane,
                    width, offset,
                )


def fold(ids, shapes, jobs):
    arrays = [a for job in jobs for a in job[0]]
    plan = [(len(job[0]),) + tuple(job[1:]) for job in jobs]
    return call(
        functools.partial(fold_kernel, plan, len(arrays)),
        tuple(shape(dims, BF16) for dims in shapes),
        [],
        (ids, *arrays),
        [SMEM] + [VMEM] * len(arrays),
        "fold",
    )


def join_kernel(cut, ids, mine, other, out):
    blocks, rows, _ = mine.shape
    for k, part in enumerate((mine, other)):
        start, _ = split_rows(2 * rows, cut, ids[1], k)
        for b in range(blocks):
            out[b, pl.ds(pl.multiple_of(start, 16), rows), :] = part[b]


def join(ids, mine, other, cut):
    blocks, rows, lanes = mine.shape
    return call(
        functools.partial(join_kernel, cut),
        (shape((blocks, 2 * rows, lanes), BF16),),
        [],
        (ids, mine, other),
        [SMEM, VMEM, VMEM],
        "join",
    )[0]


def ride_kernel(
    seqs, level, split, halved, top, jobs, cut, last, ids, par, own, kept, sent, other, *refs
):
    count = 1 + max(p for job in jobs for p in job[0])
    parts, refs = refs[:count], refs[count:]
    if last:
        keep, kept_out = refs
        out = payload = None
        halves = ((0, keep, None),)
    else:
        keep, kept_out, out, payload = refs
        halves = ((0, keep, cut), (1, payload, cut))
    high = keep.shape[0]
    for picks, width, at in jobs:
        own_parts = [other if p < 0 else parts[p] for p in picks]
        for k, target, where in halves:
            start = 0 if where is None else split_rows(2 * high, where, ids[1], k)[0]
            add_rows(own_parts, start, high, target, 0, 0, width, at)
    chain_hop(
        seqs, level, split, halved, top, ids, par, own, kept, sent, other, out, kept_out, payload,
        high,
    )


def unpack_first(cut, ids, *refs):
    count = 1 << cut[1]
    pieces, refs = refs[:count], refs[count:]
    w_in, w_out = refs[:2]
    outs = refs[2:]
    vb = w_in.shape[1]
    wide = 2 * vb
    each = sum(out.shape[0] for out in outs)
    for k in range(count):
        row, rows = split_rows(D, cut, ids[1], k)
        w_in[pl.ds(row, rows), :] = pieces[k][0, :, :vb].astype(F32)
        for first in range(0, rows, vb):
            w_out[:, pl.ds(pl.multiple_of(row + first, vb), vb)] = pieces[k][
                0, first : first + vb, vb:
            ].astype(F32)
        for b in range(count):

            @pl.when(row == b * rows)
            def _(k=k, b=b, rows=rows):
                for run in range(D // wide):
                    start = run * each
                    for out in outs:
                        end = start + out.shape[0]
                        lo, hi = max(start, b * rows), min(end, (b + 1) * rows)
                        if lo < hi:
                            out[lo - start : hi - start, run * wide : (run + 1) * wide] = pieces[k][
                                1, lo - b * rows : hi - b * rows, :
                            ].astype(F32)
                        start = end


def unpack_sides(cut, ids, *refs):
    count = 1 << cut[1]
    pieces, (left, right) = refs[:count], refs[count:]
    vb = left.shape[1]
    for k in range(count):
        row, rows = split_rows(D, cut, ids[1], k)
        left[pl.ds(row, rows), :] = pieces[k][0, :, :vb].astype(F32)
        right[pl.ds(row, rows), :] = pieces[k][0, :, vb:].astype(F32)


def unpack(body, cut, ids, pieces, dims):
    return call(
        functools.partial(body, cut),
        tuple(shape(d) for d in dims),
        [],
        (ids, *pieces),
        [SMEM] + [VMEM] * len(pieces),
        "unpack",
    )


BOTH = ("seq", "tp")


def swap(value, mask):
    count = lax.axis_size("seq") * lax.axis_size("tp")
    return lax.ppermute(value, BOTH, [(i, i ^ mask) for i in range(count)])


def after(value, *others):
    return lax.optimization_barrier((value, *others))[0]


def bits_of(count):
    return [1 << k for k in range(count.bit_length() - 1)]


def has(index, bit):
    return jnp.bitwise_and(index, bit) > 0


def half_of(value, upper):
    half = value.shape[0] // 2
    return lax.dynamic_slice_in_dim(value, jnp.where(upper, half, 0), half, 0)


def joined(mine, other, upper):
    return jnp.where(
        upper,
        jnp.concatenate([other, mine], axis=0),
        jnp.concatenate([mine, other], axis=0),
    )


def spread_out(own, tp):
    pieces = {0: own}
    for bit in reversed(bits_of(tp // 2)):
        for r in list(pieces):
            pieces[r ^ bit] = [swap(a, bit) for a in pieces[r]]
    return [pieces[r] for r in range(tp // 2)]


def per_device(
    tokens,
    cotangent,
    valid_lengths,
    norm1_gain,
    ema_rate,
    ema_beta,
    ema_eta,
    ema_skip,
    w_shared,
    query_gain,
    key_gain,
    rel_bias,
    w_value,
    w_reset,
    w_update,
    w_hidden,
    u_hidden,
    norm2_gain,
    w_in,
    w_out,
):
    part = lax.axis_index("tp")
    place = lax.axis_index("seq")
    tp = lax.axis_size("tp")
    seq = lax.axis_size("seq")
    all_seqs, local_rows, _ = tokens.shape
    vb = w_value.shape[1]
    nb = D // tp
    index = place * tp + part
    ybits = (seq.bit_length() - 1) // 2
    traded = local_rows < CH
    lower = part % 2 == 0

    def trade(value):
        if not traded:
            return value
        other = swap(jnp.where(lower, value[1], value[0]), 1)
        mine = jnp.where(lower, value[0], value[1])
        return joined(mine, other, ~lower)[None]

    def trade_back(value):
        if not traded:
            return value
        first, second = value[0, :local_rows], value[0, local_rows:]
        other = swap(jnp.where(lower, second, first), 1)
        mine = jnp.where(lower, first, second)
        return jnp.where(lower, jnp.stack([mine, other]), jnp.stack([other, mine]))

    if traded:
        assert all_seqs == 2 and 2 * local_rows == CH
        seqs = 1
        stretch = index // 2
        lengths = jnp.where(lower, valid_lengths[0], valid_lengths[1])[None]
    else:
        assert local_rows == CH
        seqs = all_seqs
        stretch = index
        lengths = valid_lengths
    rows = seqs * CH
    ids = jnp.concatenate([jnp.stack([part, place, stretch]), lengths]).astype(jnp.int32)
    masks = bits_of(tp * seq)[int(traded) :]
    levels = len(masks)
    upper_y = has(place, 1)

    tok = trade(tokens)
    cot = trade(cotangent)
    gain1 = norm1_gain[None]
    gain2 = norm2_gain[None]
    skip = ema_skip[None]
    rate, beta = ema_rate.T, ema_beta.T
    qg, kg, rb = query_gain[None], key_gain[None], rel_bias[None]

    top = tp // 2
    weights = (w_value, w_reset, w_hidden, w_update, u_hidden, w_in, w_out)
    rows2 = 2 * nb + vb
    normed, par, before, ends, low, pack1, pack2, pack3, half1, half2, half3 = call(
        functools.partial(enter_kernel, seqs),
        (
            shape((rows, D), BF16),
            shape((4, NDIM, D)),
            shape((2, seqs, NDIM, PIECES, D)),
            shape((2, seqs, NDIM, D)),
            shape((2, seqs, NDIM, D), BF16),
            shape((D, 2 * vb), BF16),
            shape((rows2, D), BF16),
            shape((D, 2 * vb), BF16),
            shape((D // 2, 2 * vb), BF16),
            shape((rows2, D // 2), BF16),
            shape((D // 2, 2 * vb), BF16),
        ),
        [
            pltpu.VMEM((seqs, CH, D), BF16),
            pltpu.VMEM((1, D), F32),
            pltpu.VMEM((NDIM, D), F32),
            pltpu.VMEM((NDIM, D), F32),
            pltpu.VMEM((NDIM, D), F32),
            pltpu.VMEM((BLOCKS, rows, LANES), F32),
            pltpu.VMEM((6, NDIM, D), F32),
            pltpu.SemaphoreType.DMA((17 + 2 * (D // vb),)),
        ],
        (tok, gain1, rate, beta, ema_eta.T, *weights),
        [ANY] * 12,
        "enter",
        limit=60,
        outs=(pl.BlockSpec(),) * 11,
    )

    start = 1 - int(traded)
    groups = [(0, 1)] * start + [(start, 2)] + [(i, 1) for i in range(start + 2, levels)]
    hops = []
    state = ends
    for i, (shift, bits) in enumerate(groups):
        if i == start:
            mine1 = swap(half1, top)
            near_gates = spread_out([pack1, pack2], tp)
        if i == start + 1:
            low = after(low, mine1)
            mine2 = swap(after(half2, low), top)
            other1 = swap(after(mine1, low), tp)
        if i == start + 2:
            low = after(low, mine2, *near_gates[-1])
            mine3 = swap(after(half3, low), top)
            near_feeds = spread_out([after(pack3, low)], tp)
        got = []
        for k in range(1, 1 << bits):
            got.append(swap(low, k << (shift + int(traded))))
            hops.append((shift, k, got[-1]))
        if i + 1 < len(groups):
            state, low = call(
                functools.partial(hop_kernel, seqs, shift, 1 << bits),
                (shape((2, seqs, NDIM, D)), shape((2, seqs, NDIM, D), BF16)),
                [],
                (ids, par, state, *got),
                [SMEM] + [VMEM] * (2 + len(got)),
                "hop",
            )
    st_in, skip_pre, mixed, shared_pre, prob = call(
        functools.partial(look_kernel, seqs, [h[:2] for h in hops]),
        (
            shape((2, seqs, NDIM, D)),
            shape((rows, D)),
            shape((rows, D), BF16),
            shape((rows, Z)),
            shape((seqs, CH, CH)),
        ),
        [
            pltpu.VMEM((BLOCKS, rows, LANES), F32),
            pltpu.VMEM((BLOCKS, rows, LANES), F32),
            pltpu.VMEM((NDIM, PIECES, D), F32),
        ],
        (
            ids, after(normed, mine3), par, before, skip, w_shared, qg, kg, rb,
            *[h[2] for h in hops],
        ),
        [SMEM] + [VMEM] * (8 + len(hops)),
        "look",
        limit=10,
    )
    other2 = swap(after(mine2, low), tp)
    far_gates = spread_out([mine1, other1, mine2, other2], tp)
    other3 = swap(after(mine3, *got), tp)
    gates = [w for group in near_gates + far_gates for w in group]

    values, value_pre, reset_pre, attended, gated, hidden_pre, update_pre, middle = call(
        functools.partial(mix_kernel, seqs, tp),
        (
            shape((tp, rows, vb), BF16),
            shape((tp, rows, vb)),
            shape((tp, rows, vb)),
            shape((tp, rows, vb)),
            shape((tp, rows, vb), BF16),
            shape((rows, D)),
            shape((rows, D)),
            shape((rows, D)),
        ),
        [
            pltpu.VMEM((tp, D, 2 * vb), BF16),
            pltpu.VMEM((tp, rows2, D), BF16),
            pltpu.VMEM((D, 2 * D), BF16),
            pltpu.SemaphoreType.DMA((3 * tp,)),
        ],
        (ids, tok, normed, mixed, prob, *gates),
        [SMEM] + [VMEM] * 4 + [ANY] * len(gates),
        "mix",
        limit=10,
    )

    far_feeds = spread_out([mine3, after(other3, middle)], tp)
    feeds = [w for group in near_feeds + far_feeds for w in group]
    out, keep3, send3, grad_hu, resid, grad_gain2 = call(
        functools.partial(ffn_kernel, seqs, tp),
        (
            shape((rows, D), BF16),
            shape((tp // 2, D, 2 * vb), BF16),
            shape((tp // 2, D, 2 * vb), BF16),
            shape((rows, 2 * D), BF16),
            shape((rows, D)),
            shape((1, D)),
        ),
        [
            pltpu.VMEM((tp, D, 2 * vb), BF16),
            pltpu.VMEM((rows, D), BF16),
            pltpu.VMEM((rows, D), BF16),
            pltpu.VMEM((rows, D), F32),
            pltpu.VMEM((rows, D), F32),
            pltpu.SemaphoreType.DMA((3 * tp // 2,)),
        ],
        (ids, tok, cot, middle, hidden_pre, update_pre, gain2, *feeds),
        [SMEM] + [VMEM] * 6 + [ANY] * len(feeds),
        "ffn",
        limit=10,
    )

    half = tp // 2
    yn = 1 << ybits
    wide = 2 * vb
    runs = D // wide
    cut_of_y = (0, ybits)
    zcuts = [(shift, 1) for shift in range(ybits, seq.bit_length() - 1)]

    def over_tp(pieces):
        return [pieces[0]] + [swap(p, 2 * k) for k, p in enumerate(pieces) if k]

    def over_y(pieces):
        return [pieces[0]] + [swap(p, tp * k) for k, p in enumerate(pieces) if k]

    def over_z(value, cut):
        return swap(value, tp << cut[0])

    def cut_tp(parts, dims):
        n = dims[0]
        return fold(
            ids,
            [(1,) + dims[1:]] * n,
            [(parts, 0, dims[2], "tp", [(k, 0, 0) for k in range(n)])],
        )

    def cut_y(parts, dims):
        return fold(
            ids,
            [(dims[0], dims[1] // yn, dims[2])] * yn,
            [(parts, 0, dims[2], cut_of_y, [(k, 0, 0) for k in range(yn)])],
        )

    last = [None]

    def now(value):
        return value if last[0] is None else after(value, last[0])

    chunk = (half, D, wide)
    got3 = swap(send3, 1)
    keep2, send2 = call(
        functools.partial(gates_kernel, tp),
        (shape(chunk, BF16), shape(chunk, BF16)),
        [pltpu.VMEM((D, 2 * D), F32)],
        (ids, mixed, gated, grad_hu),
        [SMEM] + [VMEM] * 3,
        "gates",
        limit=10,
    )
    got2 = swap(send2, 1)
    g3 = cut_tp([keep3, got3], chunk)
    g3 = over_tp(g3)
    g2 = cut_y([keep2, after(got2, g3[0])], chunk)
    g2 = over_y(g2)

    (
        keep1, send1, grad_skip, grad_normed, behind, back_ends, grad_wsh, misc,
    ) = call(
        functools.partial(back_kernel, seqs, tp),
        (
            shape((half, D, 2 * vb), BF16),
            shape((half, D, 2 * vb), BF16),
            shape((BLOCKS, rows, LANES)),
            shape((rows, D)),
            shape((seqs, NDIM, PIECES, D)),
            shape((seqs, NDIM, D)),
            shape((D, Z)),
            shape((1, D)),
        ),
        [
            pltpu.VMEM((tp, D, 2 * vb), BF16),
            pltpu.VMEM((tp, rows2, D), BF16),
            pltpu.VMEM((D, 2 * D), BF16),
            pltpu.VMEM((rows, D), F32),
            pltpu.VMEM((seqs, CH, CH), F32),
            pltpu.VMEM((3, NDIM, D), F32),
            pltpu.SemaphoreType.DMA((3 * tp,)),
        ],
        (
            ids, normed, mixed, skip_pre, shared_pre, prob, values, value_pre, reset_pre, attended,
            after(grad_hu, g2[0]), par, w_shared, qg, kg, *gates,
        ),
        [SMEM] + [VMEM] * 14 + [ANY] * len(gates),
        "back",
        limit=10,
    )

    g3 = cut_y([after(g3[0], send1)] + g3[1:], (1, D, wide))
    g2 = cut_tp([after(g2[0], g3[0])] + g2[1:], (half, D // yn, wide))
    keep1, send1, grad_skip, grad_normed, behind, back_ends, grad_wsh, misc, _ = (
        lax.optimization_barrier(
            (keep1, send1, grad_skip, grad_normed, behind, back_ends, grad_wsh, misc, g2[0])
        )
    )
    adjoint = back_ends.reshape(seqs * NDIM, D)
    last[0] = g2[0]
    g3 = over_y(g3)
    g2 = over_tp(g2)
    got1 = swap(send1, 1)
    got_adjoint = adjoint if traded else swap(adjoint, 1)
    done = {}

    def first_chunks():
        high = D // yn >> 1
        keep, send = fold(
            ids,
            [(2, high, wide)] * 2,
            [
                ([now(g3[0])] + g3[1:], 0, wide, zcuts[0], [(0, 0, 0), (1, 0, 0)]),
                (g2, 0, wide, zcuts[0], [(0, 1, 0), (1, 1, 0)]),
            ],
        )
        for cut in zcuts[1:]:
            other = over_z(send, zcuts[zcuts.index(cut) - 1])
            yield keep
            high //= 2
            keep, send = fold(
                ids,
                [(2, high, wide)] * 2,
                [([now(keep), other], 0, wide, cut, [(0, 0, 0), (1, 0, 0)])],
            )
        other = over_z(send, zcuts[-1])
        yield keep
        (total,) = fold(ids, [keep.shape], [([now(keep), other], 0, wide, None, [(0, 0, 0)])])
        for cut in reversed(zcuts):
            other = over_z(total, cut)
            yield total
            total = join(ids, now(total), other, cut)
        pieces = over_y([total] * yn)
        yield total
        done["first"] = unpack(
            unpack_first,
            cut_of_y,
            ids,
            [now(pieces[0])] + pieces[1:],
            [(D, vb), (vb, D), (nb, D), (nb, D), (vb, D)],
        )
        yield done["first"][0]

    def second_chunk():
        parts = fold(
            ids,
            [(1, D, vb)] * half + [(half, D // yn, vb)] * yn,
            [
                ([now(keep1), got1], 0, vb, "tp", [(k, 0, 0) for k in range(half)]),
                ([keep1, got1], vb, vb, cut_of_y, [(half + k, 0, 0) for k in range(yn)]),
            ],
        )
        left, right = over_tp(parts[:half]), over_y(parts[half:])
        yield parts[0]
        count = Z + SMALL_ROWS
        count += -count % (16 * tp)
        sums, send = call(
            functools.partial(sums_kernel, seqs),
            (shape((count // 2, D)), shape((count // 2, D))),
            [
                pltpu.VMEM((count, D), F32),
                pltpu.VMEM((BLOCKS, rows, LANES), F32),
                pltpu.VMEM((NDIM, PIECES, D), F32),
            ],
            (
                ids, tok, normed, now(grad_skip), grad_normed, par, before, st_in, skip, grad_gain2,
                misc, grad_wsh,
            ),
            [SMEM] + [VMEM] * 11,
            "sums",
            limit=10,
        )
        got_sums = swap(send, 1)
        yield sums
        small_high = count // 4
        ad_rows = seqs * NDIM

        def payload_rows():
            return (ad_rows + small_high) * runs

        own, kept, payload = call(
            functools.partial(first_back_hop, seqs, not traded),
            (
                shape((ad_rows, D)),
                shape((small_high, D)),
                shape((payload_rows(), wide), BF16),
            ),
            [],
            (ids, par, now(adjoint), got_adjoint, sums, got_sums),
            [SMEM] + [VMEM] * 5,
            "hop",
        )
        got = [] if traded else [(got_adjoint, 0)]
        level = int(not traded)
        halved = True
        other = swap(payload, masks[level])
        yield payload
        parts = fold(
            ids,
            [(1, D // yn, vb)] * (yn + half),
            [
                ([now(left[0])] + left[1:], 0, vb, cut_of_y, [(k, 0, 0) for k in range(yn)]),
                (right, 0, vb, "tp", [(yn + k, 0, 0) for k in range(half)]),
            ],
        )
        left, right = over_y(parts[:yn]), over_tp(parts[yn:])
        yield parts[0]
        while level + 1 < levels - len(zcuts):
            got.append((other, 0))
            split = 2 * masks[level] if 2 * masks[level] < tp else 0
            small_high = small_high // 2 if split else small_high
            own, kept, payload = call(
                functools.partial(back_hop, seqs, level, split, halved),
                (
                    shape((ad_rows, D)),
                    shape((small_high, D)),
                    shape((payload_rows(), wide), BF16),
                ),
                [],
                (ids, par, now(own), kept, payload, other),
                [SMEM] + [VMEM] * 5,
                "hop",
            )
            halved = bool(split)
            level += 1
            other = swap(payload, masks[level])
            yield payload
        high = D // yn
        top = 0
        flat = [p.reshape(p.shape[1:]) for p in left + right]
        jobs = [
            (tuple(range(len(left))), vb, 0),
            (tuple(range(len(left), len(flat))), vb, vb),
        ]
        for cut in zcuts:
            got.append((other, top))
            high //= 2
            keep, kept, own, payload = call(
                functools.partial(
                    ride_kernel, seqs, level, 0, halved, top, jobs, cut, False
                ),
                (
                    shape((high, wide), BF16),
                    shape((small_high, D)),
                    shape((ad_rows, D)),
                    shape((high + payload_rows(), wide), BF16),
                ),
                [],
                (ids, par, now(own), kept, payload, other, *flat),
                [SMEM] + [VMEM] * (5 + len(flat)),
                "ride",
            )
            halved = False
            level += 1
            top = high
            flat = [keep]
            jobs = [((0, -1), wide, 0)]
            other = swap(payload, masks[level])
            yield keep
        got.append((other, top))
        total, kept = call(
            functools.partial(ride_kernel, seqs, level, 0, False, top, jobs, None, True),
            (shape((high, wide), BF16), shape((small_high, D))),
            [],
            (ids, par, now(own), kept, payload, other, *flat),
            [SMEM] + [VMEM] * (5 + len(flat)),
            "ride",
        )
        bits = list(reversed(bits_of(tp)))
        total = total[None]
        far = swap(kept, bits[0])
        for i, cut in enumerate(reversed(zcuts)):
            other = over_z(total, cut)
            yield total
            total = join(ids, now(total), other, cut)
            if i + 1 < len(bits):
                (kept,) = call(
                    functools.partial(pair_kernel, bits[i]),
                    (shape((2 * kept.shape[0], D)),),
                    [],
                    (ids, after(kept, total), far),
                    [SMEM, VMEM, VMEM],
                    "pair",
                )
                far = swap(kept, bits[i + 1])
        pieces = over_y([total] * yn)
        yield total
        done["small"] = call(
            finish_kernel,
            (
                shape((1, D)),
                shape((NDIM, D)),
                shape((NDIM, D)),
                shape((NDIM, D)),
                shape((1, D)),
                shape((D, Z)),
                shape((1, Z)),
                shape((1, Z)),
                shape((1, Z)),
                shape((1, D)),
            ),
            [pltpu.VMEM((count, D), F32)],
            (ids, par, rate, beta, gain1, now(kept), far),
            [SMEM] + [VMEM] * 6,
            "finish",
        )
        (done["tokens"],) = call(
            functools.partial(leave_kernel, seqs, [at for _, at in got]),
            (shape((seqs, CH, D), BF16),),
            [
                pltpu.VMEM((seqs, NDIM, D), F32),
                pltpu.VMEM((NDIM, PIECES, D), F32),
                pltpu.VMEM((BLOCKS, rows, LANES), F32),
            ],
            (
                ids, tok, par, after(grad_skip, done["small"][0]), grad_normed, behind, resid,
                gain1, skip, *[g for g, _ in got],
            ),
            [SMEM] + [VMEM] * (8 + levels),
            "leave",
            limit=10,
        )
        yield done["tokens"]
        done["second"] = unpack(
            unpack_sides, cut_of_y, ids, [now(pieces[0])] + pieces[1:], [(D, vb), (D, vb)]
        )
        yield done["second"][0]

    walks = {"f": first_chunks(), "s": second_chunk()}
    order = "s s f s s f s f s f s f s s s s f s".replace(" ", "")

    def advance(name):
        try:
            last[0] = next(walks[name])
        except StopIteration:
            del walks[name]

    for name in order:
        if name in walks:
            advance(name)
    while walks:
        for name in list(walks):
            advance(name)

    grad_w_in, grad_w_out, grad_w_hidden, grad_w_update, grad_u_hidden = done["first"]
    grad_w_value, grad_w_reset = done["second"]
    firsts = [
        small.T if small.shape[0] == NDIM else small[0] if small.shape[0] == 1 else small
        for small in done["small"]
    ]
    grad_norm2_gain = firsts.pop()
    return (
        trade_back(out.reshape(seqs, CH, D)),
        trade_back(done["tokens"]),
        *firsts,
        grad_w_value,
        grad_w_reset,
        grad_w_update,
        grad_w_hidden,
        grad_u_hidden,
        grad_norm2_gain,
        grad_w_in,
        grad_w_out,
    )


def solution(mesh):
    rows = P(None, ("seq", "tp"), None)
    cols = P(None, "tp")
    tall = P("tp", None)
    whole = P()
    return jax.shard_map(
        per_device,
        mesh=mesh,
        in_specs=(rows, rows) + (whole,) * 10 + (cols, cols, tall, tall, tall, whole, cols, tall),
        out_specs=(rows, rows) + (whole,) * 9 + (cols, cols, tall, tall, tall, whole, cols, tall),
        check_vma=False,
    )
```

time: 200 us -> 157 us (0.79)
  waiting for transfers between devices: 86.6 us -> 59 us
  Pallas kernels: 35.8 us -> 53.5 us
  starting transfers between devices: 53.9 us -> 38.4 us
  other arithmetic: 9.55 us -> 0.08 us
  local copies, waits for them, and re-layouts: 12.3 us -> 5.06 us
    ppermute x46 -> x48, waiting for transfers between devices: 86.6 us -> 59 us  [swap(): return lax.ppermute(value, BOTH, [(i, i ^ mask) for i in range(count)])]
    pallas_call x6 -> x33, Pallas kernels: 35.8 us -> 53.5 us  [call(): pl.pallas_call(body, out_shape=out, in_specs=specs, out_specs=outs or jax...]
    ppermute x46 -> x48, starting transfers between devices: 53.9 us -> 38.4 us  [swap(): return lax.ppermute(value, BOTH, [(i, i ^ mask) for i in range(count)])]
    convert_element_type x22 -> x0, other arithmetic: 5.96 us -> none  [the longest x15 5.32 us: add_low(): return (a.astype(F32) + b.astype(F32)).astype(BF16)]
    slice x15 -> x0, local copies, waits for them, and re-layouts: 4.32 us -> none  [the longest x1 1.05 us: per_device(): g1[:, vb:]]
    unnamed x61 -> x42, local copies, waits for them, and re-layouts: 4.68 us -> 5.06 us
  transfers between devices with their start and end apart: 46 -> 48, of which waited for: 27 -> 24; matrix products, arithmetic and copies ran while one was open for 7% -> 0% of each run, Pallas kernels for 9% -> 26%
where the time goes in v2:
time: 157 us
  waiting for transfers between devices  59 us (38%)
  Pallas kernels  53.5 us (34%)
  starting transfers between devices  38.4 us (24%)
  local copies, waits for them, and re-layouts  5.06 us (3%)
    ppermute x48, waiting for transfers between devices, swap(): return lax.ppermute(value, BOTH, [(i, i ^ mask) for i in range(count)])  59 us
    pallas_call x33, Pallas kernels, call(): pl.pallas_call(body, out_shape=out, in_specs=specs, out_specs=outs or jax...  53.5 us
    ppermute x48, starting transfers between devices, swap(): return lax.ppermute(value, BOTH, [(i, i ^ mask) for i in range(count)])  38.4 us
    unnamed x42, local copies, waits for them, and re-layouts  5.06 us
  transfers between devices with their start and end apart: 48, of which 24 were waited for; matrix products, arithmetic and copies ran while one was open for 0% of the time, Pallas kernels for 26%

profile of v2, /device:TPU:0, one launch (start us, length us, event | category | flops | bytes accessed | tf_op | source)
XLA Modules:
  0.0 157.1 jit_solution(2831399158777808173)
XLA Ops:
  0.7 5.3 %enter.1 = (bf16[256,512]{1,0:T(8,128)(2,1)}, f32[4,16,512]{2,1,0:T(8,128)}, f32[2,2,16,8,512]{4,3,2,1,0:T(8,128)}, f32[2,2,16,512]{3,2,1,0:T(8,128)}, bf16[2,2,...) custom-call(bf16[2,128,512]{2,1,0:T(8,128)(2,1)} %tok.7, ...), custom_call_target="tpu_custom_call" | custom-call | tf_op jit(solution)/shard_map/enter/pallas_call | solution.py:94
  6.0 3.0 %collective-permute-start.4 = (bf16[256,512]{1,0:T(8,128)(2,1)}, bf16[256,512]{1,0:T(8,128)(2,1)S(1)}, u32[]{:S(2)}, u32[]{:S(2)}) collective-permute-start(bf16[256,512]{1,0:T(8,128)(2,1)} %get-tuple-element.170), channel_id=1, source_target_pairs={{0,2},{1,3},{2,0},{3,1},{4,6},{5,7},{6,4},{7,5},{8,10},{9,11},{10,... | collective-permute-start | bytes 786440 | tf_op jit(solution)/shard_map/ppermute | solution.py:956
  10.3 1.7 %collective-permute-done.refs_0_ = bf16[2,2,16,512]{3,2,1,0:T(8,128)(2,1)S(1)} collective-permute-done((bf16[2,2,16,512]{3,2,1,0:T(8,128)(2,1)}, bf16[2,2,16,512]{3,2,1,0:T(8,128)(2,1)S(1)}, u32[]{:S(2)}, u32[]{:S(2)}) %collective-permute-start) | collective-permute-done | bytes 65568 | tf_op jit(solution)/shard_map/ppermute | solution.py:956
  12.0 0.9 copy-done
  12.9 0.9 copy-done.13
  14.4 1.6 collective-permute-start.3
  16.1 3.6 %collective-permute-done.3.refs_2_.refs_3_ = bf16[2,2,16,512]{3,2,1,0:T(8,128)(2,1)S(1)} collective-permute-done((bf16[2,2,16,512]{3,2,1,0:T(8,128)(2,1)S(1)}, bf16[2,2,16,512]{3,2,1,0:T(8,128)(2,1)S(1)}, u32[]{:S(2)}, u32[]{:S(2)}) %collective-permute-start.3) | collective-permute-done | bytes 65568 | tf_op jit(solution)/shard_map/ppermute | solution.py:956
  19.8 1.1 collective-permute-done.2.refs_1_.refs_2_
  20.9 3.0 %collective-permute-done.1.refs_0_.refs_1_ = bf16[2,2,16,512]{3,2,1,0:T(8,128)(2,1)S(1)} collective-permute-done((bf16[2,2,16,512]{3,2,1,0:T(8,128)(2,1)S(1)}, bf16[2,2,16,512]{3,2,1,0:T(8,128)(2,1)S(1)}, u32[]{:S(2)}, u32[]{:S(2)}) %collective-permute-start.1) | collective-permute-done | bytes 65568 | tf_op jit(solution)/shard_map/ppermute | solution.py:956
  24.8 1.9 %collective-permute-start.5 = (bf16[2,2,16,512]{3,2,1,0:T(8,128)(2,1)S(1)}, bf16[2,2,16,512]{3,2,1,0:T(8,128)(2,1)S(1)}, u32[]{:S(2)}, u32[]{:S(2)}) collective-permute-start(bf16[2,2,16,512]{3,2,1,0:T(8,128)(2,1)S(1)} %get-tuple-element.171), channel_id=1, source_target_pairs={{0,8},{1,9},{2,10},{3,11},{4,12},{5,13},{6,14},{7,15},{8,0},{9,1},... | collective-permute-start | bytes 196616 | tf_op jit(solution)/shard_map/ppermute | solution.py:956
  26.8 1.5 collective-permute-start.11
  28.3 0.8 collective-permute-done.5.refs_0_.refs_4_
  29.1 1.2 hop.7
  30.4 0.9 collective-permute-done.6.refs_6_
  31.3 1.7 %collective-permute-start.12 = (bf16[512,256]{1,0:T(8,128)(2,1)S(1)}, bf16[512,256]{1,0:T(8,128)(2,1)S(1)}, u32[]{:S(2)}, u32[]{:S(2)}) collective-permute-start(bf16[512,256]{1,0:T(8,128)(2,1)S(1)} %collective-permute-done.6.refs_6_), channel_id=1, source_target_pairs={{0,4},{1,5},{2,6},{3,7},{4,0},{5,1},{6,2},{7,3},{8,12},{9,13},{10,... | collective-permute-start | bytes 786440 | tf_op jit(solution)/shard_map/ppermute | solution.py:956
  33.0 0.8 collective-permute-start.9
  33.8 2.6 %collective-permute-start.10 = (bf16[2,2,16,512]{3,2,1,0:T(8,128)(2,1)S(1)}, bf16[2,2,16,512]{3,2,1,0:T(8,128)(2,1)S(1)}, u32[]{:S(2)}, u32[]{:S(2)}) collective-permute-start(bf16[2,2,16,512]{3,2,1,0:T(8,128)(2,1)S(1)} %get-tuple-element.177), channel_id=1, source_target_pairs={{0,16},{1,17},{2,18},{3,19},{4,20},{5,21},{6,22},{7,23},{8,24},{9,... | collective-permute-start | bytes 196616 | tf_op jit(solution)/shard_map/ppermute | solution.py:956
  36.7 4.0 %collective-permute-done.10.refs_5_ = bf16[2,2,16,512]{3,2,1,0:T(8,128)(2,1)S(1)} collective-permute-done((bf16[2,2,16,512]{3,2,1,0:T(8,128)(2,1)S(1)}, bf16[2,2,16,512]{3,2,1,0:T(8,128)(2,1)S(1)}, u32[]{:S(2)}, u32[]{:S(2)}) %collective-permute-start.10) | collective-permute-done | bytes 65568 | tf_op jit(solution)/shard_map/ppermute | solution.py:956
  42.4 1.2 copy-done.3
  43.6 3.0 %look.1 = (f32[2,2,16,512]{3,2,1,0:T(8,128)S(1)}, f32[256,512]{1,0:T(8,128)S(1)}, bf16[256,512]{1,0:T(8,128)(2,1)S(1)}, f32[256,128]{1,0:T(8,128)S(1)}, f32[2,128,128]{2,1,0:T(8,128)S(1)}) custom-call(s32[5]{0:T(128)S(1)} %pad_add_fusion.ids, bf16[256,512]{1,0:T(8,128)(2,1)S(1)} %copy-done.5, f32[4,16,512]{2,1,0:T(8,128)S(1)} %copy-done.1, ...), custom_call_target="tpu_custom_call" | custom-call | tf_op jit(solution)/shard_map/look/pallas_call | solution.py:94
  47.2 4.1 %mix.1 = (bf16[4,256,256]{2,1,0:T(8,128)(2,1)S(1)}, f32[4,256,256]{2,1,0:T(8,128)S(1)}, f32[4,256,256]{2,1,0:T(8,128)S(1)}, f32[4,256,256]{2,1,0:T(8,128)S(1)}, ...) custom-call(s32[5]{0:T(128)S(1)} %pad_add_fusion.ids, ...), custom_call_target="tpu_custom_call" | custom-call | tf_op jit(solution)/shard_map/mix/pallas_call | solution.py:94
  51.5 1.5 collective-permute-done.20.refs_5_
  53.7 5.1 %ffn.1 = (bf16[256,512]{1,0:T(8,128)(2,1)}, bf16[2,512,512]{2,1,0:T(8,128)(2,1)S(1)}, bf16[2,512,512]{2,1,0:T(8,128)(2,1)S(1)}, bf16[256,1024]{1,0:T(8,128)(2,1)...) custom-call(s32[5]{0:T(128)S(1)} %pad_add_fusion.ids, bf16[2,128,512]{2,1,0:T(8,128)(2,1)S(1)} %copy-done.2, ...), custom_call_target="tpu_custom_call" | custom-call | tf_op jit(solution)/shard_map/ffn/pallas_call | solution.py:94
  59.0 1.7 %gates.1 = (bf16[2,512,512]{2,1,0:T(8,128)(2,1)S(1)}, bf16[2,512,512]{2,1,0:T(8,128)(2,1)S(1)}) custom-call(s32[5]{0:T(128)S(1)} %pad_add_fusion.ids, bf16[256,512]{1,0:T(8,128)(2,1)S(1)} %get-tuple-element.181.mixed, bf16[4,256,256]{2,1,0:T(8,128)(2,1)S(1)} %get-tuple-element.200.gated, bf16[256,1024]{1,0:T(8,128)(2,1)S(1)} %get-tuple-element.208.grad_hu), custom_call_target="tpu_custom_call" | custom-call | tf_op jit(solution)/shard_map/gates/pallas_call | solution.py:94
  61.5 0.9 fold.9
  62.4 1.1 collective-permute-start.23
  63.5 0.9 fold.10
  64.4 1.8 %collective-permute-start.24 = (bf16[2,256,512]{2,1,0:T(8,128)(2,1)S(1)}, bf16[2,256,512]{2,1,0:T(8,128)(2,1)S(1)}, u32[]{:S(2)}, u32[]{:S(2)}) collective-permute-start(bf16[2,256,512]{2,1,0:T(8,128)(2,1)S(1)} %get-tuple-element.221), channel_id=1, source_target_pairs={{0,4},{1,5},{2,6},{3,7},{4,0},{5,1},{6,2},{7,3},{8,12},{9,13},{10,... | collective-permute-start | bytes 1572872 | tf_op jit(solution)/shard_map/ppermute | solution.py:956
  66.2 6.6 %back.1 = (bf16[2,512,512]{2,1,0:T(8,128)(2,1)S(1)}, bf16[2,512,512]{2,1,0:T(8,128)(2,1)S(1)}, f32[4,256,128]{2,1,0:T(8,128)S(1)}, f32[256,512]{1,0:T(8,128)S(1)...) custom-call(s32[5]{0:T(128)S(1)} %pad_add_fusion.ids, ...), custom_call_target="tpu_custom_call" | custom-call | tf_op jit(solution)/shard_map/back/pallas_call | solution.py:94
  72.8 3.6 %collective-permute-done.23.refs_1_ = bf16[1,512,512]{2,1,0:T(8,128)(2,1)S(1)} collective-permute-done((bf16[1,512,512]{2,1,0:T(8,128)(2,1)S(1)}, bf16[1,512,512]{2,1,0:T(8,128)(2,1)S(1)}, u32[]{:S(2)}, u32[]{:S(2)}) %collective-permute-start.23) | collective-permute-done | bytes 524320 | tf_op jit(solution)/shard_map/ppermute | solution.py:956
  76.4 0.7 fold.11
  77.1 1.4 collective-permute-done.24.refs_1_
  78.5 0.7 fold.12
  79.3 1.6 %collective-permute-start.26 = (bf16[1,256,512]{2,1,0:T(8,128)(2,1)S(1)}, bf16[1,256,512]{2,1,0:T(8,128)(2,1)S(1)}, u32[]{:S(2)}, u32[]{:S(2)}) collective-permute-start(bf16[1,256,512]{2,1,0:T(8,128)(2,1)S(1)} %get-tuple-element.237), channel_id=1, source_target_pairs={{0,4},{1,5},{2,6},{3,7},{4,0},{5,1},{6,2},{7,3},{8,12},{9,13},{10,... | collective-permute-start | bytes 786440 | tf_op jit(solution)/shard_map/ppermute | solution.py:956
  80.9 1.2 collective-permute-start.27
  82.2 1.0 fold.13
  83.1 4.4 %sums.1 = (f32[96,512]{1,0:T(8,128)S(1)}, f32[96,512]{1,0:T(8,128)S(1)}) custom-call(s32[5]{0:T(128)S(1)} %pad_add_fusion.ids, bf16[2,128,512]{2,1,0:T(8,128)(2,1)S(1)} %copy-done.2, bf16[256,512]{1,0:T(8,128)(2,1)S(1)} %copy-done.5, f32[4,256,128]{2,1,0:T(8,128)S(1)} %get-tuple-element.282.grad_skip, f32[256,512]{1,0:T(8,128)S(1)} %get-tuple-element.230.grad_normed, ...), custom_call_target="tpu_custom_call" | custom-call | tf_op jit(solution)/shard_map/sums/pallas_call | solution.py:94
  87.5 0.9 collective-permute-start.30
  88.4 1.7 %collective-permute-start.31 = (bf16[2,256,256]{2,1,0:T(8,128)(2,1)S(1)}, bf16[2,256,256]{2,1,0:T(8,128)(2,1)S(1)}, u32[]{:S(2)}, u32[]{:S(2)}) collective-permute-start(bf16[2,256,256]{2,1,0:T(8,128)(2,1)S(1)} %get-tuple-element.247), channel_id=1, source_target_pairs={{0,4},{1,5},{2,6},{3,7},{4,0},{5,1},{6,2},{7,3},{8,12},{9,13},{10,... | collective-permute-start | bytes 786440 | tf_op jit(solution)/shard_map/ppermute | solution.py:956
  90.2 0.7 fold.14
  90.9 0.7 collective-permute-start.32
  92.1 1.0 collective-permute-done.28.other.refs_0_
  93.7 2.0 %collective-permute-done.30.refs_1_ = bf16[1,512,256]{2,1,0:T(8,128)(2,1)S(1)} collective-permute-done((bf16[1,512,256]{2,1,0:T(8,128)(2,1)S(1)}, bf16[1,512,256]{2,1,0:T(8,128)(2,1)S(1)}, u32[]{:S(2)}, u32[]{:S(2)}) %collective-permute-start.30) | collective-permute-done | bytes 262176 | tf_op jit(solution)/shard_map/ppermute | solution.py:956
  95.7 0.7 collective-permute-done.31.refs_3_
  96.5 0.7 fold.15
  97.2 1.5 collective-permute-done.32.refs_1_
  99.3 2.4 %collective-permute-start.34 = (bf16[2,64,512]{2,1,0:T(8,128)(2,1)S(1)}, bf16[2,64,512]{2,1,0:T(8,128)(2,1)S(1)}, u32[]{:S(2)}, u32[]{:S(2)}) collective-permute-start(bf16[2,64,512]{2,1,0:T(8,128)(2,1)S(1)} %get-tuple-element.257), channel_id=1, source_target_pairs={{0,16},{1,17},{2,18},{3,19},{4,20},{5,21},{6,22},{7,23},{8,24},{9,... | collective-permute-start | bytes 393224 | tf_op jit(solution)/shard_map/ppermute | solution.py:956
  101.7 0.8 collective-permute-start.33
  103.0 1.0 collective-permute-start.37
  104.0 2.1 %collective-permute-done.33.other.refs_1_ = bf16[80,512]{1,0:T(8,128)(2,1)S(1)} collective-permute-done((bf16[80,512]{1,0:T(8,128)(2,1)S(1)}, bf16[80,512]{1,0:T(8,128)(2,1)S(1)}, u32[]{:S(2)}, u32[]{:S(2)}) %collective-permute-start.33) | collective-permute-done | bytes 81952 | tf_op jit(solution)/shard_map/ppermute | solution.py:956
  108.3 0.8 collective-permute-start.35
  109.1 3.6 %collective-permute-done.35.other.refs_2_ = bf16[80,512]{1,0:T(8,128)(2,1)S(1)} collective-permute-done((bf16[80,512]{1,0:T(8,128)(2,1)S(1)}, bf16[80,512]{1,0:T(8,128)(2,1)S(1)}, u32[]{:S(2)}, u32[]{:S(2)}) %collective-permute-start.35) | collective-permute-done | bytes 81952 | tf_op jit(solution)/shard_map/ppermute | solution.py:956
  113.5 3.6 %collective-permute-start.39 = (bf16[208,512]{1,0:T(8,128)(2,1)S(1)}, bf16[208,512]{1,0:T(8,128)(2,1)S(1)}, u32[]{:S(2)}, u32[]{:S(2)}) collective-permute-start(bf16[208,512]{1,0:T(8,128)(2,1)S(1)} %get-tuple-element.268.sent), channel_id=1, source_target_pairs={{0,8},{1,9},{2,10},{3,11},{4,12},{5,13},{6,14},{7,15},{8,0},{9,1},... | collective-permute-start | bytes 638984 | tf_op jit(solution)/shard_map/ppermute | solution.py:956
  117.7 7.1 %collective-permute-done.39.other.refs_3_ = bf16[208,512]{1,0:T(8,128)(2,1)S(1)} collective-permute-done((bf16[208,512]{1,0:T(8,128)(2,1)S(1)}, bf16[208,512]{1,0:T(8,128)(2,1)S(1)}, u32[]{:S(2)}, u32[]{:S(2)}) %collective-permute-start.39) | collective-permute-done | bytes 213024 | tf_op jit(solution)/shard_map/ppermute | solution.py:956
  125.5 2.4 %collective-permute-done.40.other = bf16[2,128,512]{2,1,0:T(8,128)(2,1)S(1)} collective-permute-done((bf16[2,128,512]{2,1,0:T(8,128)(2,1)S(1)}, bf16[2,128,512]{2,1,0:T(8,128)(2,1)S(1)}, u32[]{:S(2)}, u32[]{:S(2)}) %collective-permute-start.40) | collective-permute-done | bytes 262176 | tf_op jit(solution)/shard_map/ppermute | solution.py:956
  129.1 5.3 %collective-permute-done.41.other.refs_4_ = bf16[144,512]{1,0:T(8,128)(2,1)S(1)} collective-permute-done((bf16[144,512]{1,0:T(8,128)(2,1)S(1)}, bf16[144,512]{1,0:T(8,128)(2,1)S(1)}, u32[]{:S(2)}, u32[]{:S(2)}) %collective-permute-start.41) | collective-permute-done | bytes 147488 | tf_op jit(solution)/shard_map/ppermute | solution.py:956
  135.1 5.2 %collective-permute-done.42.other = bf16[1,64,512]{2,1,0:T(8,128)(2,1)S(1)} collective-permute-done((bf16[1,64,512]{2,1,0:T(8,128)(2,1)S(1)}, bf16[1,64,512]{2,1,0:T(8,128)(2,1)S(1)}, u32[]{:S(2)}, u32[]{:S(2)}) %collective-permute-start.42) | collective-permute-done | bytes 65568 | tf_op jit(solution)/shard_map/ppermute | solution.py:956
  140.8 0.9 collective-permute-start.43
  141.8 4.0 %collective-permute-done.44.other = bf16[1,128,512]{2,1,0:T(8,128)(2,1)S(1)} collective-permute-done((bf16[1,128,512]{2,1,0:T(8,128)(2,1)S(1)}, bf16[1,128,512]{2,1,0:T(8,128)(2,1)S(1)}, u32[]{:S(2)}, u32[]{:S(2)}) %collective-permute-start.44) | collective-permute-done | bytes 131104 | tf_op jit(solution)/shard_map/ppermute | solution.py:956
  147.5 1.4 collective-permute-done.45.other
  148.9 1.3 finish.1
  150.3 3.3 %leave.1 = bf16[2,128,512]{2,1,0:T(8,128)(2,1)} custom-call(s32[5]{0:T(128)S(1)} %pad_add_fusion.ids, bf16[2,128,512]{2,1,0:T(8,128)(2,1)S(1)} %copy-done.2, f32[4,16,512]{2,1,0:T(8,128)S(1)} %copy-done.1, f32[4,256,128]{2,1,0:T(8,128)S(1)} %get-tuple-element.282.grad_skip, f32[256,512]{1,0:T(8,128)S(1)} %get-tuple-element.230.grad_normed, ...), custom_call_target="tpu_custom_call" | custom-call | tf_op jit(solution)/shard_map/leave/pallas_call | solution.py:94
  153.5 2.0 %unpack.2 = (f32[512,256]{1,0:T(8,128)}, f32[256,512]{1,0:T(8,128)}, f32[128,512]{1,0:T(8,128)}, f32[128,512]{1,0:T(8,128)}, f32[256,512]{1,0:T(8,128)}) custom-call(s32[5]{0:T(128)S(1)} %pad_add_fusion.ids, bf16[2,256,512]{2,1,0:T(8,128)(2,1)S(1)} %join.5.refs_0_, bf16[2,256,512]{2,1,0:T(8,128)(2,1)S(1)} %collective-permute-done.46.refs_1_), custom_call_target="tpu_custom_call" | custom-call | tf_op jit(solution)/shard_map/unpack/pallas_call | solution.py:94
  155.5 1.6 unpack.3
  (108 shorter events, 17.9 us)
Async XLA Ops:
  6.0 18.6 %collective-permute-start.4 = (bf16[256,512]{1,0:T(8,128)(2,1)}, bf16[256,512]{1,0:T(8,128)(2,1)S(1)}, u32[]{:S(2)}, u32[]{:S(2)}) collective-permute-start(bf16[256,512]{1,0:T(8,128)(2,1)} %get-tuple-element.170), channel_id=1, source_target_pairs={{0,2},{1,3},{2,0},{3,1},{4,6},{5,7},{6,4},{7,5},{8,10},{9,11},{10,... | collective-permute-start | bytes 786440 | tf_op jit(solution)/shard_map/ppermute | solution.py:956
  9.0 22.2 %collective-permute-start.7 = (bf16[512,512]{1,0:T(8,128)(2,1)}, bf16[512,512]{1,0:T(8,128)(2,1)S(1)}, u32[]{:S(2)}, u32[]{:S(2)}) collective-permute-start(bf16[512,512]{1,0:T(8,128)(2,1)} %get-tuple-element.175.refs_0_), channel_id=1, source_target_pairs={{0,1},{1,0},{2,3},{3,2},{4,5},{5,4},{6,7},{7,6},{8,9},{9,8},{10,11... | collective-permute-start | bytes 1572872 | tf_op jit(solution)/shard_map/ppermute | solution.py:956
  9.0 22.2 %collective-permute-start.8 = (bf16[512,512]{1,0:T(8,128)(2,1)}, bf16[512,512]{1,0:T(8,128)(2,1)S(1)}, u32[]{:S(2)}, u32[]{:S(2)}) collective-permute-start(bf16[512,512]{1,0:T(8,128)(2,1)} %get-tuple-element.176.refs_1_), channel_id=1, source_target_pairs={{0,1},{1,0},{2,3},{3,2},{4,5},{5,4},{6,7},{7,6},{8,9},{9,8},{10,11... | collective-permute-start | bytes 1572872 | tf_op jit(solution)/shard_map/ppermute | solution.py:956
  9.5 2.5 %collective-permute-start = (bf16[2,2,16,512]{3,2,1,0:T(8,128)(2,1)}, bf16[2,2,16,512]{3,2,1,0:T(8,128)(2,1)S(1)}, u32[]{:S(2)}, u32[]{:S(2)}) collective-permute-start(bf16[2,2,16,512]{3,2,1,0:T(8,128)(2,1)} %get-tuple-element.165), channel_id=1, source_target_pairs={{0,1},{1,0},{2,3},{3,2},{4,5},{5,4},{6,7},{7,6},{8,9},{9,8},{10,11... | collective-permute-start | bytes 196616 | tf_op jit(solution)/shard_map/ppermute | solution.py:956
  12.0 0.9 copy-start
  12.9 0.9 copy-start.13
  13.8 27.9 %copy-start.9 = (bf16[512,512]{1,0:T(8,128)(2,1)S(1)}, bf16[512,512]{1,0:T(8,128)(2,1)}, u32[]{:S(2)}) copy-start(bf16[512,512]{1,0:T(8,128)(2,1)} %get-tuple-element.189.refs_0_) | copy-start | bytes 1572868
  14.4 5.3 %collective-permute-start.3 = (bf16[2,2,16,512]{3,2,1,0:T(8,128)(2,1)S(1)}, bf16[2,2,16,512]{3,2,1,0:T(8,128)(2,1)S(1)}, u32[]{:S(2)}, u32[]{:S(2)}) collective-permute-start(bf16[2,2,16,512]{3,2,1,0:T(8,128)(2,1)S(1)} %get-tuple-element.167), channel_id=1, source_target_pairs={{0,6},{1,7},{2,4},{3,5},{4,2},{5,3},{6,0},{7,1},{8,14},{9,15},{10,... | collective-permute-start | bytes 196616 | tf_op jit(solution)/shard_map/ppermute | solution.py:956
  16.0 4.9 %collective-permute-start.2 = (bf16[2,2,16,512]{3,2,1,0:T(8,128)(2,1)S(1)}, bf16[2,2,16,512]{3,2,1,0:T(8,128)(2,1)S(1)}, u32[]{:S(2)}, u32[]{:S(2)}) collective-permute-start(bf16[2,2,16,512]{3,2,1,0:T(8,128)(2,1)S(1)} %get-tuple-element.167), channel_id=1, source_target_pairs={{0,4},{1,5},{2,6},{3,7},{4,0},{5,1},{6,2},{7,3},{8,12},{9,13},{10,... | collective-permute-start | bytes 196616 | tf_op jit(solution)/shard_map/ppermute | solution.py:956
  19.7 4.3 %collective-permute-start.1 = (bf16[2,2,16,512]{3,2,1,0:T(8,128)(2,1)S(1)}, bf16[2,2,16,512]{3,2,1,0:T(8,128)(2,1)S(1)}, u32[]{:S(2)}, u32[]{:S(2)}) collective-permute-start(bf16[2,2,16,512]{3,2,1,0:T(8,128)(2,1)S(1)} %get-tuple-element.167), channel_id=1, source_target_pairs={{0,2},{1,3},{2,0},{3,1},{4,6},{5,7},{6,4},{7,5},{8,10},{9,11},{10,... | collective-permute-start | bytes 196616 | tf_op jit(solution)/shard_map/ppermute | solution.py:956
  23.9 17.8 %copy-start.5 = (bf16[256,512]{1,0:T(8,128)(2,1)S(1)}, bf16[256,512]{1,0:T(8,128)(2,1)}, u32[]{:S(2)}) copy-start(bf16[256,512]{1,0:T(8,128)(2,1)} %get-tuple-element.179.normed) | copy-start | bytes 786436
  24.6 6.6 %collective-permute-start.6 = (bf16[512,256]{1,0:T(8,128)(2,1)}, bf16[512,256]{1,0:T(8,128)(2,1)S(1)}, u32[]{:S(2)}, u32[]{:S(2)}) collective-permute-start(bf16[512,256]{1,0:T(8,128)(2,1)} %get-tuple-element.174), channel_id=1, source_target_pairs={{0,2},{1,3},{2,0},{3,1},{4,6},{5,7},{6,4},{7,5},{8,10},{9,11},{10,... | collective-permute-start | bytes 786440 | tf_op jit(solution)/shard_map/ppermute | solution.py:956
  24.8 4.3 %collective-permute-start.5 = (bf16[2,2,16,512]{3,2,1,0:T(8,128)(2,1)S(1)}, bf16[2,2,16,512]{3,2,1,0:T(8,128)(2,1)S(1)}, u32[]{:S(2)}, u32[]{:S(2)}) collective-permute-start(bf16[2,2,16,512]{3,2,1,0:T(8,128)(2,1)S(1)} %get-tuple-element.171), channel_id=1, source_target_pairs={{0,8},{1,9},{2,10},{3,11},{4,12},{5,13},{6,14},{7,15},{8,0},{9,1},... | collective-permute-start | bytes 196616 | tf_op jit(solution)/shard_map/ppermute | solution.py:956
  26.8 9.7 %collective-permute-start.11 = (bf16[256,512]{1,0:T(8,128)(2,1)S(1)}, bf16[256,512]{1,0:T(8,128)(2,1)S(1)}, u32[]{:S(2)}, u32[]{:S(2)}) collective-permute-start(bf16[256,512]{1,0:T(8,128)(2,1)S(1)} %collective-permute-done.4.refs_4_), channel_id=1, source_target_pairs={{0,4},{1,5},{2,6},{3,7},{4,0},{5,1},{6,2},{7,3},{8,12},{9,13},{10,... | collective-permute-start | bytes 786440 | tf_op jit(solution)/shard_map/ppermute | solution.py:956
  29.1 12.6 %copy-start.1 = (f32[4,16,512]{2,1,0:T(8,128)S(1)}, f32[4,16,512]{2,1,0:T(8,128)}, u32[]{:S(2)}) copy-start(f32[4,16,512]{2,1,0:T(8,128)} %get-tuple-element.163.par) | copy-start | bytes 393220
  29.1 12.6 %copy-start.8 = (bf16[512,128]{1,0:T(8,128)(2,1)S(1)}, bf16[512,128]{1,0:T(8,128)(2,1)}, u32[]{:S(2)}) copy-start(bf16[512,128]{1,0:T(8,128)(2,1)} %wsh.3) | copy-start | bytes 393220
  31.3 9.4 %collective-permute-start.12 = (bf16[512,256]{1,0:T(8,128)(2,1)S(1)}, bf16[512,256]{1,0:T(8,128)(2,1)S(1)}, u32[]{:S(2)}, u32[]{:S(2)}) collective-permute-start(bf16[512,256]{1,0:T(8,128)(2,1)S(1)} %collective-permute-done.6.refs_6_), channel_id=1, source_target_pairs={{0,4},{1,5},{2,6},{3,7},{4,0},{5,1},{6,2},{7,3},{8,12},{9,13},{10,... | collective-permute-start | bytes 786440 | tf_op jit(solution)/shard_map/ppermute | solution.py:956
  33.0 8.1 %collective-permute-start.9 = (bf16[256,512]{1,0:T(8,128)(2,1)}, bf16[256,512]{1,0:T(8,128)(2,1)S(1)}, u32[]{:S(2)}, u32[]{:S(2)}) collective-permute-start(bf16[256,512]{1,0:T(8,128)(2,1)} %get-tuple-element.178), channel_id=1, source_target_pairs={{0,2},{1,3},{2,0},{3,1},{4,6},{5,7},{6,4},{7,5},{8,10},{9,11},{10,... | collective-permute-start | bytes 786440 | tf_op jit(solution)/shard_map/ppermute | solution.py:956
  33.8 7.8 %collective-permute-start.13 = (bf16[256,512]{1,0:T(8,128)(2,1)S(1)}, bf16[256,512]{1,0:T(8,128)(2,1)S(1)}, u32[]{:S(2)}, u32[]{:S(2)}) collective-permute-start(bf16[256,512]{1,0:T(8,128)(2,1)S(1)} %collective-permute-done.4.refs_4_), channel_id=1, source_target_pairs={{0,1},{1,0},{2,3},{3,2},{4,5},{5,4},{6,7},{7,6},{8,9},{9,8},{10,11... | collective-permute-start | bytes 786440 | tf_op jit(solution)/shard_map/ppermute | solution.py:956
  33.8 6.8 %collective-permute-start.10 = (bf16[2,2,16,512]{3,2,1,0:T(8,128)(2,1)S(1)}, bf16[2,2,16,512]{3,2,1,0:T(8,128)(2,1)S(1)}, u32[]{:S(2)}, u32[]{:S(2)}) collective-permute-start(bf16[2,2,16,512]{3,2,1,0:T(8,128)(2,1)S(1)} %get-tuple-element.177), channel_id=1, source_target_pairs={{0,16},{1,17},{2,18},{3,19},{4,20},{5,21},{6,22},{7,23},{8,24},{9,... | collective-permute-start | bytes 196616 | tf_op jit(solution)/shard_map/ppermute | solution.py:956
  36.4 10.2 %collective-permute-start.15 = (bf16[512,256]{1,0:T(8,128)(2,1)S(1)}, bf16[512,256]{1,0:T(8,128)(2,1)S(1)}, u32[]{:S(2)}, u32[]{:S(2)}) collective-permute-start(bf16[512,256]{1,0:T(8,128)(2,1)S(1)} %collective-permute-done.6.refs_6_), channel_id=1, source_target_pairs={{0,1},{1,0},{2,3},{3,2},{4,5},{5,4},{6,7},{7,6},{8,9},{9,8},{10,11... | collective-permute-start | bytes 786440 | tf_op jit(solution)/shard_map/ppermute | solution.py:956
  40.6 6.5 %collective-permute-start.14 = (bf16[256,512]{1,0:T(8,128)(2,1)S(1)}, bf16[256,512]{1,0:T(8,128)(2,1)S(1)}, u32[]{:S(2)}, u32[]{:S(2)}) collective-permute-start(bf16[256,512]{1,0:T(8,128)(2,1)S(1)} %collective-permute-done.11.refs_5_), channel_id=1, source_target_pairs={{0,1},{1,0},{2,3},{3,2},{4,5},{5,4},{6,7},{7,6},{8,9},{9,8},{10,11... | collective-permute-start | bytes 786440 | tf_op jit(solution)/shard_map/ppermute | solution.py:956
  40.6 6.5 %collective-permute-start.16 = (bf16[512,256]{1,0:T(8,128)(2,1)S(1)}, bf16[512,256]{1,0:T(8,128)(2,1)S(1)}, u32[]{:S(2)}, u32[]{:S(2)}) collective-permute-start(bf16[512,256]{1,0:T(8,128)(2,1)S(1)} %collective-permute-done.12.refs_7_), channel_id=1, source_target_pairs={{0,1},{1,0},{2,3},{3,2},{4,5},{5,4},{6,7},{7,6},{8,9},{9,8},{10,11... | collective-permute-start | bytes 786440 | tf_op jit(solution)/shard_map/ppermute | solution.py:956
  41.2 10.2 %collective-permute-start.18 = (bf16[256,512]{1,0:T(8,128)(2,1)S(1)}, bf16[256,512]{1,0:T(8,128)(2,1)S(1)}, u32[]{:S(2)}, u32[]{:S(2)}) collective-permute-start(bf16[256,512]{1,0:T(8,128)(2,1)S(1)} %collective-permute-done.9.refs_2_), channel_id=1, source_target_pairs={{0,4},{1,5},{2,6},{3,7},{4,0},{5,1},{6,2},{7,3},{8,12},{9,13},{10,... | collective-permute-start | bytes 786440 | tf_op jit(solution)/shard_map/ppermute | solution.py:956
  41.7 9.8 %collective-permute-start.17 = (bf16[512,512]{1,0:T(8,128)(2,1)S(1)}, bf16[512,512]{1,0:T(8,128)(2,1)S(1)}, u32[]{:S(2)}, u32[]{:S(2)}) collective-permute-start(bf16[512,512]{1,0:T(8,128)(2,1)S(1)} %copy-done.9), channel_id=1, source_target_pairs={{0,1},{1,0},{2,3},{3,2},{4,5},{5,4},{6,7},{7,6},{8,9},{9,8},{10,11... | collective-permute-start | bytes 1572872 | tf_op jit(solution)/shard_map/ppermute | solution.py:956
  41.7 0.7 copy-start.15
  42.4 1.2 copy-start.3
  43.6 3.6 %copy-start.2 = (bf16[2,128,512]{2,1,0:T(8,128)(2,1)S(1)}, bf16[2,128,512]{2,1,0:T(8,128)(2,1)}, u32[]{:S(2)}) copy-start(bf16[2,128,512]{2,1,0:T(8,128)(2,1)} %tok.7) | copy-start | bytes 786436
  43.6 3.6 %copy-start.6 = (bf16[512,512]{1,0:T(8,128)(2,1)S(1)}, bf16[512,512]{1,0:T(8,128)(2,1)}, u32[]{:S(2)}) copy-start(bf16[512,512]{1,0:T(8,128)(2,1)} %get-tuple-element.175.refs_0_) | copy-start | bytes 1572868
  43.6 3.6 %copy-start.7 = (bf16[512,512]{1,0:T(8,128)(2,1)S(1)}, bf16[512,512]{1,0:T(8,128)(2,1)}, u32[]{:S(2)}) copy-start(bf16[512,512]{1,0:T(8,128)(2,1)} %get-tuple-element.176.refs_1_) | copy-start | bytes 1572868
  46.6 4.9 %collective-permute-start.19 = (bf16[256,512]{1,0:T(8,128)(2,1)S(1)}, bf16[256,512]{1,0:T(8,128)(2,1)S(1)}, u32[]{:S(2)}, u32[]{:S(2)}) collective-permute-start(bf16[256,512]{1,0:T(8,128)(2,1)S(1)} %collective-permute-done.9.refs_2_), channel_id=1, source_target_pairs={{0,1},{1,0},{2,3},{3,2},{4,5},{5,4},{6,7},{7,6},{8,9},{9,8},{10,11... | collective-permute-start | bytes 786440 | tf_op jit(solution)/shard_map/ppermute | solution.py:956
  47.2 5.8 %copy-start.10 = (bf16[2,128,512]{2,1,0:T(8,128)(2,1)S(1)}, bf16[2,128,512]{2,1,0:T(8,128)(2,1)}, u32[]{:S(2)}) copy-start(bf16[2,128,512]{2,1,0:T(8,128)(2,1)} %cot.1) | copy-start | bytes 786436
  51.4 1.6 %collective-permute-start.20 = (bf16[256,512]{1,0:T(8,128)(2,1)S(1)}, bf16[256,512]{1,0:T(8,128)(2,1)S(1)}, u32[]{:S(2)}, u32[]{:S(2)}) collective-permute-start(bf16[256,512]{1,0:T(8,128)(2,1)S(1)} %collective-permute-done.18.refs_3_), channel_id=1, source_target_pairs={{0,1},{1,0},{2,3},{3,2},{4,5},{5,4},{6,7},{7,6},{8,9},{9,8},{10,11... | collective-permute-start | bytes 786440 | tf_op jit(solution)/shard_map/ppermute | solution.py:956
  58.8 2.7 %collective-permute-start.22 = (bf16[2,512,512]{2,1,0:T(8,128)(2,1)S(1)}, bf16[2,512,512]{2,1,0:T(8,128)(2,1)S(1)}, u32[]{:S(2)}, u32[]{:S(2)}) collective-permute-start(bf16[2,512,512]{2,1,0:T(8,128)(2,1)S(1)} %get-tuple-element.204), channel_id=1, source_target_pairs={{0,1},{1,0},{2,3},{3,2},{4,5},{5,4},{6,7},{7,6},{8,9},{9,8},{10,11... | collective-permute-start | bytes 3145736 | tf_op jit(solution)/shard_map/ppermute | solution.py:956
  60.7 2.8 %collective-permute-start.21 = (bf16[2,512,512]{2,1,0:T(8,128)(2,1)S(1)}, bf16[2,512,512]{2,1,0:T(8,128)(2,1)S(1)}, u32[]{:S(2)}, u32[]{:S(2)}) collective-permute-start(bf16[2,512,512]{2,1,0:T(8,128)(2,1)S(1)} %get-tuple-element.202), channel_id=1, source_target_pairs={{0,1},{1,0},{2,3},{3,2},{4,5},{5,4},{6,7},{7,6},{8,9},{9,8},{10,11... | collective-permute-start | bytes 3145736 | tf_op jit(solution)/shard_map/ppermute | solution.py:956
  62.4 14.0 %collective-permute-start.23 = (bf16[1,512,512]{2,1,0:T(8,128)(2,1)S(1)}, bf16[1,512,512]{2,1,0:T(8,128)(2,1)S(1)}, u32[]{:S(2)}, u32[]{:S(2)}) collective-permute-start(bf16[1,512,512]{2,1,0:T(8,128)(2,1)S(1)} %get-tuple-element.218), channel_id=1, source_target_pairs={{0,2},{1,3},{2,0},{3,1},{4,6},{5,7},{6,4},{7,5},{8,10},{9,11},{10,... | collective-permute-start | bytes 1572872 | tf_op jit(solution)/shard_map/ppermute | solution.py:956
  64.4 14.2 %collective-permute-start.24 = (bf16[2,256,512]{2,1,0:T(8,128)(2,1)S(1)}, bf16[2,256,512]{2,1,0:T(8,128)(2,1)S(1)}, u32[]{:S(2)}, u32[]{:S(2)}) collective-permute-start(bf16[2,256,512]{2,1,0:T(8,128)(2,1)S(1)} %get-tuple-element.221), channel_id=1, source_target_pairs={{0,4},{1,5},{2,6},{3,7},{4,0},{5,1},{6,2},{7,3},{8,12},{9,13},{10,... | collective-permute-start | bytes 1572872 | tf_op jit(solution)/shard_map/ppermute | solution.py:956
  79.3 2.9 %collective-permute-start.25 = (bf16[2,512,512]{2,1,0:T(8,128)(2,1)S(1)}, bf16[2,512,512]{2,1,0:T(8,128)(2,1)S(1)}, u32[]{:S(2)}, u32[]{:S(2)}) collective-permute-start(bf16[2,512,512]{2,1,0:T(8,128)(2,1)S(1)} %get-tuple-element.227), channel_id=1, source_target_pairs={{0,1},{1,0},{2,3},{3,2},{4,5},{5,4},{6,7},{7,6},{8,9},{9,8},{10,11... | collective-permute-start | bytes 3145736 | tf_op jit(solution)/shard_map/ppermute | solution.py:956
  79.3 10.8 %collective-permute-start.26 = (bf16[1,256,512]{2,1,0:T(8,128)(2,1)S(1)}, bf16[1,256,512]{2,1,0:T(8,128)(2,1)S(1)}, u32[]{:S(2)}, u32[]{:S(2)}) collective-permute-start(bf16[1,256,512]{2,1,0:T(8,128)(2,1)S(1)} %get-tuple-element.237), channel_id=1, source_target_pairs={{0,4},{1,5},{2,6},{3,7},{4,0},{5,1},{6,2},{7,3},{8,12},{9,13},{10,... | collective-permute-start | bytes 786440 | tf_op jit(solution)/shard_map/ppermute | solution.py:956
  80.9 2.2 %copy-start.4 = (f32[2,2,16,8,512]{4,3,2,1,0:T(8,128)S(1)}, f32[2,2,16,8,512]{4,3,2,1,0:T(8,128)}, u32[]{:S(2)}) copy-start(f32[2,2,16,8,512]{4,3,2,1,0:T(8,128)} %get-tuple-element.180.before) | copy-start | bytes 3145732
  80.9 9.2 %collective-permute-start.27 = (bf16[1,256,512]{2,1,0:T(8,128)(2,1)S(1)}, bf16[1,256,512]{2,1,0:T(8,128)(2,1)S(1)}, u32[]{:S(2)}, u32[]{:S(2)}) collective-permute-start(bf16[1,256,512]{2,1,0:T(8,128)(2,1)S(1)} %get-tuple-element.238), channel_id=1, source_target_pairs={{0,2},{1,3},{2,0},{3,1},{4,6},{5,7},{6,4},{7,5},{8,10},{9,11},{10,... | collective-permute-start | bytes 786440 | tf_op jit(solution)/shard_map/ppermute | solution.py:956
  87.5 8.2 %collective-permute-start.30 = (bf16[1,512,256]{2,1,0:T(8,128)(2,1)S(1)}, bf16[1,512,256]{2,1,0:T(8,128)(2,1)S(1)}, u32[]{:S(2)}, u32[]{:S(2)}) collective-permute-start(bf16[1,512,256]{2,1,0:T(8,128)(2,1)S(1)} %get-tuple-element.245), channel_id=1, source_target_pairs={{0,2},{1,3},{2,0},{3,1},{4,6},{5,7},{6,4},{7,5},{8,10},{9,11},{10,... | collective-permute-start | bytes 786440 | tf_op jit(solution)/shard_map/ppermute | solution.py:956
  88.4 8.1 %collective-permute-start.31 = (bf16[2,256,256]{2,1,0:T(8,128)(2,1)S(1)}, bf16[2,256,256]{2,1,0:T(8,128)(2,1)S(1)}, u32[]{:S(2)}, u32[]{:S(2)}) collective-permute-start(bf16[2,256,256]{2,1,0:T(8,128)(2,1)S(1)} %get-tuple-element.247), channel_id=1, source_target_pairs={{0,4},{1,5},{2,6},{3,7},{4,0},{5,1},{6,2},{7,3},{8,12},{9,13},{10,... | collective-permute-start | bytes 786440 | tf_op jit(solution)/shard_map/ppermute | solution.py:956
  90.9 7.9 %collective-permute-start.32 = (bf16[2,128,512]{2,1,0:T(8,128)(2,1)S(1)}, bf16[2,128,512]{2,1,0:T(8,128)(2,1)S(1)}, u32[]{:S(2)}, u32[]{:S(2)}) collective-permute-start(bf16[2,128,512]{2,1,0:T(8,128)(2,1)S(1)} %get-tuple-element.250), channel_id=1, source_target_pairs={{0,8},{1,9},{2,10},{3,11},{4,12},{5,13},{6,14},{7,15},{8,0},{9,1},... | collective-permute-start | bytes 786440 | tf_op jit(solution)/shard_map/ppermute | solution.py:956
  91.6 1.5 collective-permute-start.29
  91.6 1.5 collective-permute-start.28
  99.3 7.8 %collective-permute-start.34 = (bf16[2,64,512]{2,1,0:T(8,128)(2,1)S(1)}, bf16[2,64,512]{2,1,0:T(8,128)(2,1)S(1)}, u32[]{:S(2)}, u32[]{:S(2)}) collective-permute-start(bf16[2,64,512]{2,1,0:T(8,128)(2,1)S(1)} %get-tuple-element.257), channel_id=1, source_target_pairs={{0,16},{1,17},{2,18},{3,19},{4,20},{5,21},{6,22},{7,23},{8,24},{9,... | collective-permute-start | bytes 393224 | tf_op jit(solution)/shard_map/ppermute | solution.py:956
  101.7 4.5 %collective-permute-start.33 = (bf16[80,512]{1,0:T(8,128)(2,1)S(1)}, bf16[80,512]{1,0:T(8,128)(2,1)S(1)}, u32[]{:S(2)}, u32[]{:S(2)}) collective-permute-start(bf16[80,512]{1,0:T(8,128)(2,1)S(1)} %get-tuple-element.243.sent), channel_id=1, source_target_pairs={{0,2},{1,3},{2,0},{3,1},{4,6},{5,7},{6,4},{7,5},{8,10},{9,11},{10,... | collective-permute-start | bytes 245768 | tf_op jit(solution)/shard_map/ppermute | solution.py:956
  102.5 10.2 %collective-permute-start.36 = (bf16[1,256,256]{2,1,0:T(8,128)(2,1)S(1)}, bf16[1,256,256]{2,1,0:T(8,128)(2,1)S(1)}, u32[]{:S(2)}, u32[]{:S(2)}) collective-permute-start(bf16[1,256,256]{2,1,0:T(8,128)(2,1)S(1)} %get-tuple-element.260), channel_id=1, source_target_pairs={{0,4},{1,5},{2,6},{3,7},{4,0},{5,1},{6,2},{7,3},{8,12},{9,13},{10,... | collective-permute-start | bytes 393224 | tf_op jit(solution)/shard_map/ppermute | solution.py:956
  103.0 9.7 %collective-permute-start.37 = (bf16[1,256,256]{2,1,0:T(8,128)(2,1)S(1)}, bf16[1,256,256]{2,1,0:T(8,128)(2,1)S(1)}, u32[]{:S(2)}, u32[]{:S(2)}) collective-permute-start(bf16[1,256,256]{2,1,0:T(8,128)(2,1)S(1)} %get-tuple-element.262), channel_id=1, source_target_pairs={{0,2},{1,3},{2,0},{3,1},{4,6},{5,7},{6,4},{7,5},{8,10},{9,11},{10,... | collective-permute-start | bytes 393224 | tf_op jit(solution)/shard_map/ppermute | solution.py:956
  107.8 9.3 %collective-permute-start.38 = (bf16[2,64,512]{2,1,0:T(8,128)(2,1)S(1)}, bf16[2,64,512]{2,1,0:T(8,128)(2,1)S(1)}, u32[]{:S(2)}, u32[]{:S(2)}) collective-permute-start(bf16[2,64,512]{2,1,0:T(8,128)(2,1)S(1)} %fold.17.mine), channel_id=1, source_target_pairs={{0,16},{1,17},{2,18},{3,19},{4,20},{5,21},{6,22},{7,23},{8,24},{9,... | collective-permute-start | bytes 393224 | tf_op jit(solution)/shard_map/ppermute | solution.py:956
  108.3 4.4 %collective-permute-start.35 = (bf16[80,512]{1,0:T(8,128)(2,1)S(1)}, bf16[80,512]{1,0:T(8,128)(2,1)S(1)}, u32[]{:S(2)}, u32[]{:S(2)}) collective-permute-start(bf16[80,512]{1,0:T(8,128)(2,1)S(1)} %get-tuple-element.255.sent), channel_id=1, source_target_pairs={{0,4},{1,5},{2,6},{3,7},{4,0},{5,1},{6,2},{7,3},{8,12},{9,13},{10,... | collective-permute-start | bytes 245768 | tf_op jit(solution)/shard_map/ppermute | solution.py:956
  113.5 11.4 %collective-permute-start.39 = (bf16[208,512]{1,0:T(8,128)(2,1)S(1)}, bf16[208,512]{1,0:T(8,128)(2,1)S(1)}, u32[]{:S(2)}, u32[]{:S(2)}) collective-permute-start(bf16[208,512]{1,0:T(8,128)(2,1)S(1)} %get-tuple-element.268.sent), channel_id=1, source_target_pairs={{0,8},{1,9},{2,10},{3,11},{4,12},{5,13},{6,14},{7,15},{8,0},{9,1},... | collective-permute-start | bytes 638984 | tf_op jit(solution)/shard_map/ppermute | solution.py:956
  117.6 10.2 %collective-permute-start.40 = (bf16[2,128,512]{2,1,0:T(8,128)(2,1)S(1)}, bf16[2,128,512]{2,1,0:T(8,128)(2,1)S(1)}, u32[]{:S(2)}, u32[]{:S(2)}) collective-permute-start(bf16[2,128,512]{2,1,0:T(8,128)(2,1)S(1)} %join.4.mine), channel_id=1, source_target_pairs={{0,8},{1,9},{2,10},{3,11},{4,12},{5,13},{6,14},{7,15},{8,0},{9,1},... | collective-permute-start | bytes 786440 | tf_op jit(solution)/shard_map/ppermute | solution.py:956
  125.4 9.0 %collective-permute-start.41 = (bf16[144,512]{1,0:T(8,128)(2,1)S(1)}, bf16[144,512]{1,0:T(8,128)(2,1)S(1)}, u32[]{:S(2)}, u32[]{:S(2)}) collective-permute-start(bf16[144,512]{1,0:T(8,128)(2,1)S(1)} %get-tuple-element.274.sent), channel_id=1, source_target_pairs={{0,16},{1,17},{2,18},{3,19},{4,20},{5,21},{6,22},{7,23},{8,24},{9,... | collective-permute-start | bytes 442376 | tf_op jit(solution)/shard_map/ppermute | solution.py:956
  128.4 25.1 %collective-permute-start.46 = (bf16[2,256,512]{2,1,0:T(8,128)(2,1)S(1)}, bf16[2,256,512]{2,1,0:T(8,128)(2,1)S(1)}, u32[]{:S(2)}, u32[]{:S(2)}) collective-permute-start(bf16[2,256,512]{2,1,0:T(8,128)(2,1)S(1)} %join.5.refs_0_), channel_id=1, source_target_pairs={{0,4},{1,5},{2,6},{3,7},{4,0},{5,1},{6,2},{7,3},{8,12},{9,13},{10,... | collective-permute-start | bytes 1572872 | tf_op jit(solution)/shard_map/ppermute | solution.py:956
  135.0 5.2 %collective-permute-start.42 = (bf16[1,64,512]{2,1,0:T(8,128)(2,1)S(1)}, bf16[1,64,512]{2,1,0:T(8,128)(2,1)S(1)}, u32[]{:S(2)}, u32[]{:S(2)}) collective-permute-start(bf16[1,64,512]{2,1,0:T(8,128)(2,1)S(1)} %bitcast.38), channel_id=1, source_target_pairs={{0,16},{1,17},{2,18},{3,19},{4,20},{5,21},{6,22},{7,23},{8,24},{9,... | collective-permute-start | bytes 196616 | tf_op jit(solution)/shard_map/ppermute | solution.py:956
  140.8 5.0 %collective-permute-start.44 = (bf16[1,128,512]{2,1,0:T(8,128)(2,1)S(1)}, bf16[1,128,512]{2,1,0:T(8,128)(2,1)S(1)}, u32[]{:S(2)}, u32[]{:S(2)}) collective-permute-start(bf16[1,128,512]{2,1,0:T(8,128)(2,1)S(1)} %join.6.mine), channel_id=1, source_target_pairs={{0,8},{1,9},{2,10},{3,11},{4,12},{5,13},{6,14},{7,15},{8,0},{9,1},... | collective-permute-start | bytes 393224 | tf_op jit(solution)/shard_map/ppermute | solution.py:956
  140.8 6.0 %collective-permute-start.43 = (f32[48,512]{1,0:T(8,128)S(1)}, f32[48,512]{1,0:T(8,128)S(1)}, u32[]{:S(2)}, u32[]{:S(2)}) collective-permute-start(f32[48,512]{1,0:T(8,128)S(1)} %get-tuple-element.278.mine), channel_id=1, source_target_pairs={{0,2},{1,3},{2,0},{3,1},{4,6},{5,7},{6,4},{7,5},{8,10},{9,11},{10,... | collective-permute-start | bytes 294920 | tf_op jit(solution)/shard_map/ppermute | solution.py:956
  146.4 2.5 %copy-start.11 = (f32[512,16]{0,1:T(8,128)S(1)}, f32[512,16]{0,1:T(8,128)}, u32[]{:S(2)}) copy-start(f32[512,16]{0,1:T(8,128)} %param.24) | copy-start | bytes 98308
  146.4 2.5 %copy-start.12 = (f32[512,16]{0,1:T(8,128)S(1)}, f32[512,16]{0,1:T(8,128)}, u32[]{:S(2)}) copy-start(f32[512,16]{0,1:T(8,128)} %param.25) | copy-start | bytes 98308
  146.4 2.5 %copy-start.14 = (f32[512]{0:T(512)S(1)}, f32[512]{0:T(512)}, u32[]{:S(2)}) copy-start(f32[512]{0:T(512)} %param.23) | copy-start | bytes 6148
  146.4 9.1 %collective-permute-start.47 = (bf16[1,256,512]{2,1,0:T(8,128)(2,1)S(1)}, bf16[1,256,512]{2,1,0:T(8,128)(2,1)S(1)}, u32[]{:S(2)}, u32[]{:S(2)}) collective-permute-start(bf16[1,256,512]{2,1,0:T(8,128)(2,1)S(1)} %join.7.refs_0_), channel_id=1, source_target_pairs={{0,4},{1,5},{2,6},{3,7},{4,0},{5,1},{6,2},{7,3},{8,12},{9,13},{10,... | collective-permute-start | bytes 786440 | tf_op jit(solution)/shard_map/ppermute | solution.py:956
  147.4 1.5 collective-permute-start.45
  (5 other events, 3.3 us)

commit v3 on v2

--- a/solution.py
+++ b/solution.py
@@ -90,7 +90,31 @@
     return jnp.concatenate([ref[b, rows, :] for b in range(BLOCKS)], axis=1)
 
 
+class Here:
+    def __init__(self, seqs, lengths):
+        self.seqs, self.lengths = seqs, lengths
+
+    def __getitem__(self, i):
+        if i == 0:
+            return lax.axis_index("tp")
+        if i == 1:
+            return lax.axis_index("seq")
+        if i == 2:
+            index = lax.axis_index("seq") * lax.axis_size("tp") + lax.axis_index("tp")
+            return index if self.seqs > 1 else jnp.right_shift(index, 1)
+        return self.lengths[i - 3 if self.seqs > 1 else jnp.bitwise_and(lax.axis_index("tp"), 1)]
+
+
 def call(body, out, scratch, operands, specs, name, limit=2, outs=None):
+    place = operands[0]
+    if isinstance(place, Here):
+        kernel = body
+        if place.lengths is None:
+            operands, specs = operands[1:], specs[1:]
+            body = lambda *refs: kernel(place, *refs)
+        else:
+            operands = (place.lengths, *operands[1:])
+            body = lambda lengths, *refs: kernel(Here(place.seqs, lengths), *refs)
     return pl.pallas_call(
         body,
         out_shape=out,
@@ -98,7 +122,7 @@
         out_specs=outs or jax.tree.map(lambda _: VMEM, out),
         scratch_shapes=scratch,
         name=name,
-        compiler_params=pltpu.CompilerParams(vmem_limit_bytes=limit * 1024 * 1024),
+        compiler_params=pltpu.CompilerParams(vmem_limit_bytes=int(limit * 1024 * 1024)),
     )(*operands)
 
 
@@ -108,39 +132,14 @@
 
 def enter_kernel(seqs, *refs):
     far, refs = refs[:5], refs[5:]
-    w_value, w_reset, w_hidden, w_update, u_hidden, w_in, w_out = refs[:7]
-    normed, par, before, ends, low, p1, p2, p3, h1, h2, h3 = refs[7:18]
-    tok, gain, rate, beta, eta, nf, tab, sems = refs[18:]
-    copies = []
-
-    def add(source, target):
-        copies.append(pltpu.make_async_copy(source, target, sems.at[len(copies)]))
-
-    for pair in zip(far, (tok, gain, rate, beta, eta)):
-        add(*pair)
-    vb, nb, cut = w_value.shape[1], w_hidden.shape[0], D // 2
-    at = pl.ds(pl.multiple_of(jnp.bitwise_and(lax.axis_index("seq"), 1) * cut, cut), cut)
-    for i, w in enumerate((w_value, w_reset)):
-        lane = pl.ds(i * vb, vb)
-        add(w.at[at, :], h1.at[:, lane])
-        add(w, p1.at[:, lane])
-    top = 0
-    for w in (w_hidden, w_update, u_hidden):
-        row = pl.ds(top, w.shape[0])
-        add(w.at[:, at], h2.at[row, :])
-        add(w, p2.at[row, :])
-        top += w.shape[0]
-    add(w_in.at[at, :], h3.at[:, pl.ds(0, vb)])
-    add(w_in, p3.at[:, pl.ds(0, vb)])
-    for k in range(D // vb):
-        row = pl.ds(k * vb, vb)
-        add(w_out.at[:, row], p3.at[row, pl.ds(vb, vb)])
-        if k < cut // vb:
-            first = pl.multiple_of(jnp.bitwise_and(lax.axis_index("seq"), 1) * cut + k * vb, vb)
-            add(w_out.at[:, pl.ds(first, vb)], h3.at[row, pl.ds(vb, vb)])
+    normed, par, before, ends, low, tok, gain, rate, beta, eta, nf, tab, sems = refs
+    copies = [
+        pltpu.make_async_copy(a, b, sems.at[i])
+        for i, (a, b) in enumerate(zip(far, (tok, gain, rate, beta, eta)))
+    ]
     for c in copies:
         c.start()
-    for c in copies[:5]:
+    for c in copies:
         c.wait()
     r = rate[...]
     d = 1.0 - r
@@ -189,13 +188,59 @@
                     a = a + qm * sa
                 before[0, s, j0 + j, :, lane] = jnp.where(place >= 1, pltpu.roll(a, 1, 0), 0.0)
                 before[1, s, j0 + j, :, lane] = jnp.where(place >= 1, pltpu.roll(b, 1, 0), 0.0)
-                ends[0, s, j0 + j : j0 + j + 1, lane] = a[PIECES - 1 :]
-                ends[1, s, j0 + j : j0 + j + 1, lane] = b[PIECES - 1 :]
+                ends[2 * s, j0 + j : j0 + j + 1, lane] = a[PIECES - 1 :]
+                ends[2 * s + 1, j0 + j : j0 + j + 1, lane] = b[PIECES - 1 :]
         return carry
 
     lax.fori_loop(0, seqs * BLOCKS, body, 0)
-    low[...] = ends[...].astype(BF16)
-    for c in copies[5:]:
+    low[...] = ends[: 2 * seqs].astype(BF16)
+    ends[2 * seqs] = par[1]
+
+
+def first_half_kernel(w_value, w_reset, h1, sems):
+    vb, cut = w_value.shape[1], D // 2
+    at = pl.ds(pl.multiple_of(jnp.bitwise_and(lax.axis_index("seq"), 1) * cut, cut), cut)
+    copies = [
+        pltpu.make_async_copy(w.at[at, :], h1.at[:, pl.ds(i * vb, vb)], sems.at[i])
+        for i, w in enumerate((w_value, w_reset))
+    ]
+    for c in copies:
+        c.start()
+    for c in copies:
+        c.wait()
+
+
+def pack_kernel(
+    w_value, w_reset, w_hidden, w_update, u_hidden, w_in, w_out, p1, p2, p3, h2, h3, sems
+):
+    copies = []
+
+    def add(source, target):
+        copies.append(pltpu.make_async_copy(source, target, sems.at[len(copies)]))
+
+    vb, cut = w_value.shape[1], D // 2
+    upper = jnp.bitwise_and(lax.axis_index("seq"), 1) * cut
+    at = pl.ds(pl.multiple_of(upper, cut), cut)
+    for i, w in enumerate((w_value, w_reset)):
+        add(w, p1.at[:, pl.ds(i * vb, vb)])
+    far = jnp.bitwise_and(jnp.right_shift(lax.axis_index("seq"), far_shift()), 1) * cut
+    top = 0
+    for w in (w_hidden, w_update, u_hidden):
+        row = pl.ds(top, w.shape[0])
+        add(w.at[:, pl.ds(pl.multiple_of(far, cut), cut)], h2.at[row, :])
+        add(w, p2.at[row, :])
+        top += w.shape[0]
+    add(w_in.at[at, :], h3.at[:, pl.ds(0, vb)])
+    add(w_in, p3.at[:, pl.ds(0, vb)])
+    for k in range(D // vb):
+        row = pl.ds(k * vb, vb)
+        add(w_out.at[:, row], p3.at[row, pl.ds(vb, vb)])
+        if k < cut // vb:
+            lane = pl.ds(pl.multiple_of(upper + k * vb, vb), vb)
+            add(w_out.at[:, lane], h3.at[row, pl.ds(vb, vb)])
+    for c in copies:
+        c.start()
+    for c in copies:
         c.wait()
 
 
@@ -213,9 +258,14 @@
     return near, far, refs[top * second :]
 
 
+def far_shift():
+    return (lax.axis_size("seq").bit_length() - 1) // 2
+
+
 def gate_copies(tp, ids, near, far, w1, w2, sems):
     top, cut = tp // 2, D // 2
-    upper = jnp.bitwise_and(ids[1], 1)
+    first = jnp.bitwise_and(ids[1], 1)
+    second = jnp.bitwise_and(jnp.right_shift(ids[1], far_shift()), 1)
     copies = []
 
     def add(source, target):
@@ -225,10 +275,10 @@
         add(near[r][0], w1.at[r])
         add(near[r][1], w2.at[r])
         mine1, other1, mine2, other2 = far[r]
-        for part1, part2, at in ((mine1, mine2, upper), (other1, other2, 1 - upper)):
-            at = pl.ds(pl.multiple_of(at * cut, cut), cut)
-            add(part1, w1.at[top + r, at, :])
-            add(part2, w2.at[top + r, :, at])
+        for part, at in ((mine1, first), (other1, 1 - first)):
+            add(part, w1.at[top + r, pl.ds(pl.multiple_of(at * cut, cut), cut), :])
+        for part, at in ((mine2, second), (other2, 1 - second)):
+            add(part, w2.at[top + r, :, pl.ds(pl.multiple_of(at * cut, cut), cut)])
     for c in copies:
         c.start()
     return copies
@@ -259,8 +309,8 @@
             end = jnp.left_shift(jnp.bitwise_xor(jnp.right_shift(place, shift), k) + 1, shift)
             off = (place - end).astype(F32) * float(CH)
             power = jnp.where(place >= end, jnp.exp(jnp.maximum(off, 0.0) * logd), 0.0)
-            oa = got[0, s].astype(F32) * power
-            b = b + got[1, s].astype(F32) * power + off * oa * dinv
+            oa = got[2 * s].astype(F32) * power
+            b = b + got[2 * s + 1].astype(F32) * power + off * oa * dinv
             a = a + oa
         st_in[0, s] = a
         st_in[1, s] = b
@@ -447,12 +497,12 @@
 def back_kernel(
     seqs, tp,
     ids, normed, mixed, skip_pre, shared_pre, prob, values, value_pre, reset_pre, attended,
-    grad_hu, par, wsh, qg, kg, *refs,
+    grad_hu, par, wsh, qg, kg, tok, before, st_in, skip, grad_gain2, *refs,
 ):
     near, far, refs = take_weights(refs, tp, 2, 4)
     (
-        keep1, send1, grad_skip, grad_normed, after, ends, grad_wsh, misc,
-        w1, w2, whu, gm, gp, tab, sems,
+        keep1, send1, grad_skip, grad_normed, after, ends, sums_keep, sums_send,
+        w1, w2, whu, gm, gp, tab, grad_wsh, misc, table, nf, pw, sems,
     ) = refs
     vb = values.shape[2]
     nb = D // tp
@@ -556,11 +606,14 @@
         return carry
 
     lax.fori_loop(0, seqs * BLOCKS, body, 0)
-
-
-def sums_kernel(
-    seqs,
-    ids, tok, normed, grad_skip, grad_normed, par, before, st_in, skip, gain2_row, misc, grad_wsh,
+    small_sums(
+        seqs, ids, tok, normed, grad_skip, grad_normed, par, before, st_in, skip, grad_gain2, misc,
+        grad_wsh, sums_keep, sums_send, table, nf, pw,
+    )
+
+
+def small_sums(
+    seqs, ids, tok, normed, grad_skip, grad_normed, par, before, st_in, skip, gain2_row, misc, grad_wsh,
     keep, send, table, nf, pw,
 ):
     put_rows(nf, slice(None), normed[...].astype(F32))
@@ -709,25 +762,23 @@
         ).astype(BF16)
 
 
-def hop_kernel(seqs, shift, count, ids, par, state, *refs):
+def hop_kernel(seqs, shift, count, ids, state, *refs):
     others, (total, low) = refs[: count - 1], refs[count - 1 :]
     mine = jnp.bitwise_and(jnp.right_shift(ids[2], shift), count - 1)
-    logd = par[1]
-    sums = [[None, None] for _ in range(seqs)]
+    logd = state[2 * seqs]
+    total[2 * seqs] = logd
+    sums = [None] * (2 * seqs)
     for k in range(count):
         after = (count - 1 - jnp.bitwise_xor(mine, k)).astype(F32) * float(CH << shift)
         power = jnp.exp(after * logd)
         slope = after * jnp.exp((after - 1.0) * logd)
-        for s in range(seqs):
-            a, b = (state[0, s], state[1, s]) if k == 0 else (
-                others[k - 1][0, s].astype(F32), others[k - 1][1, s].astype(F32)
-            )
-            a, b = power * a, power * b + slope * a
-            sums[s] = [a, b] if k == 0 else [sums[s][0] + a, sums[s][1] + b]
-    for s in range(seqs):
-        for i in range(2):
-            total[i, s] = sums[s][i]
-            low[i, s] = sums[s][i].astype(BF16)
+        for i in range(0, 2 * seqs, 2):
+            part = (state if k == 0 else others[k - 1])[i : i + 2].astype(F32)
+            a, b = power * part[0], power * part[1] + slope * part[0]
+            sums[i : i + 2] = [a, b] if k == 0 else [sums[i] + a, sums[i + 1] + b]
+    for i in range(2 * seqs):
+        total[i] = sums[i]
+        low[i] = sums[i].astype(BF16)
 
 
 def put_wide(ref, top, value):
@@ -873,23 +924,25 @@
 
 
 def ride_kernel(
-    seqs, level, split, halved, top, jobs, cut, last, ids, par, own, kept, sent, other, *refs
+    seqs, level, split, halved, top, jobs, cut, high, last, ids, par, own, kept, sent, other, *refs
 ):
     count = 1 + max(p for job in jobs for p in job[0])
     parts, refs = refs[:count], refs[count:]
+    out = payload = None
     if last:
         keep, kept_out = refs
-        out = payload = None
-        halves = ((0, keep, None),)
+        halves = ((0, keep),)
+    elif cut is None:
+        kept_out, out, payload = refs
+        halves = ((0, payload),)
     else:
         keep, kept_out, out, payload = refs
-        halves = ((0, keep, cut), (1, payload, cut))
-    high = keep.shape[0]
+        halves = ((0, keep), (1, payload))
     for picks, width, at in jobs:
-        own_parts = [other if p < 0 else parts[p] for p in picks]
-        for k, target, where in halves:
-            start = 0 if where is None else split_rows(2 * high, where, ids[1], k)[0]
-            add_rows(own_parts, start, high, target, 0, 0, width, at)
+        chosen = [other if p == -1 else sent if p == -2 else parts[p] for p in picks]
+        for k, target in halves:
+            start = 0 if cut is None else split_rows(2 * high, cut, ids[1], k)[0]
+            add_rows(chosen, start, high, target, 0, 0, width, at)
     chain_hop(
         seqs, level, split, halved, top, ids, par, own, kept, sent, other, out, kept_out, payload,
         high,
@@ -1012,14 +1065,12 @@
     w_out,
 ):
     part = lax.axis_index("tp")
-    place = lax.axis_index("seq")
     tp = lax.axis_size("tp")
     seq = lax.axis_size("seq")
     all_seqs, local_rows, _ = tokens.shape
     vb = w_value.shape[1]
     nb = D // tp
-    index = place * tp + part
-    ybits = (seq.bit_length() - 1) // 2
+    ybits = far_shift()
     traded = local_rows < CH
     lower = part % 2 == 0
 
@@ -1041,18 +1092,13 @@
     if traded:
         assert all_seqs == 2 and 2 * local_rows == CH
         seqs = 1
-        stretch = index // 2
-        lengths = jnp.where(lower, valid_lengths[0], valid_lengths[1])[None]
     else:
         assert local_rows == CH
         seqs = all_seqs
-        stretch = index
-        lengths = valid_lengths
     rows = seqs * CH
-    ids = jnp.concatenate([jnp.stack([part, place, stretch]), lengths]).astype(jnp.int32)
+    ids, ids_lengths = Here(seqs, None), Here(seqs, valid_lengths.astype(jnp.int32))
     masks = bits_of(tp * seq)[int(traded) :]
     levels = len(masks)
-    upper_y = has(place, 1)
 
     tok = trade(tokens)
     cot = trade(cotangent)
@@ -1065,20 +1111,14 @@
     top = tp // 2
     weights = (w_value, w_reset, w_hidden, w_update, u_hidden, w_in, w_out)
     rows2 = 2 * nb + vb
-    normed, par, before, ends, low, pack1, pack2, pack3, half1, half2, half3 = call(
+    normed, par, before, ends, low = call(
         functools.partial(enter_kernel, seqs),
         (
             shape((rows, D), BF16),
             shape((4, NDIM, D)),
             shape((2, seqs, NDIM, PIECES, D)),
-            shape((2, seqs, NDIM, D)),
-            shape((2, seqs, NDIM, D), BF16),
-            shape((D, 2 * vb), BF16),
-            shape((rows2, D), BF16),
-            shape((D, 2 * vb), BF16),
-            shape((D // 2, 2 * vb), BF16),
-            shape((rows2, D // 2), BF16),
-            shape((D // 2, 2 * vb), BF16),
+            shape((2 * seqs + 1, NDIM, D)),
+            shape((2 * seqs, NDIM, D), BF16),
         ),
         [
             pltpu.VMEM((seqs, CH, D), BF16),
@@ -1088,30 +1128,54 @@
             pltpu.VMEM((NDIM, D), F32),
             pltpu.VMEM((BLOCKS, rows, LANES), F32),
             pltpu.VMEM((6, NDIM, D), F32),
-            pltpu.SemaphoreType.DMA((17 + 2 * (D // vb),)),
+            pltpu.SemaphoreType.DMA((5,)),
         ],
-        (tok, gain1, rate, beta, ema_eta.T, *weights),
-        [ANY] * 12,
+        (tok, gain1, rate, beta, ema_eta.T),
+        [ANY] * 5,
         "enter",
-        limit=60,
-        outs=(pl.BlockSpec(),) * 11,
-    )
-
+        limit=58.96,
+    )
     start = 1 - int(traded)
     groups = [(0, 1)] * start + [(start, 2)] + [(i, 1) for i in range(start + 2, levels)]
     hops = []
-    state = ends
+    (half1,) = call(
+        first_half_kernel,
+        (shape((D // 2, 2 * vb), BF16),),
+        [pltpu.SemaphoreType.DMA((2,))],
+        (w_value, w_reset),
+        [ANY] * 2,
+        "half",
+        limit=60,
+        outs=(pl.BlockSpec(),),
+    )
+    mine1 = swap(half1, top)
+    state, low = ends, after(low, mine1)
     for i, (shift, bits) in enumerate(groups):
         if i == start:
-            mine1 = swap(half1, top)
-            near_gates = spread_out([pack1, pack2], tp)
+            pack1, pack2, pack3, half2, half3 = call(
+                pack_kernel,
+                (
+                    shape((D, 2 * vb), BF16),
+                    shape((rows2, D), BF16),
+                    shape((D, 2 * vb), BF16),
+                    shape((rows2, D // 2), BF16),
+                    shape((D // 2, 2 * vb), BF16),
+                ),
+                [pltpu.SemaphoreType.DMA((10 + 3 * D // vb // 2,))],
+                lax.optimization_barrier((*weights, low))[:-1],
+                [ANY] * 7,
+                "pack",
+                limit=60,
+                outs=(pl.BlockSpec(),) * 5,
+            )
         if i == start + 1:
-            low = after(low, mine1)
             mine2 = swap(after(half2, low), top)
             other1 = swap(after(mine1, low), tp)
+            near_gates = spread_out([after(pack1, low), after(pack2, low)], tp)
         if i == start + 2:
-            low = after(low, mine2, *near_gates[-1])
+            low = after(low, mine2, other1, *near_gates[-1])
             mine3 = swap(after(half3, low), top)
+            other2 = swap(after(mine2, low), tp << ybits)
             near_feeds = spread_out([after(pack3, low)], tp)
         got = []
         for k in range(1, 1 << bits):
@@ -1120,10 +1184,10 @@
         if i + 1 < len(groups):
             state, low = call(
                 functools.partial(hop_kernel, seqs, shift, 1 << bits),
-                (shape((2, seqs, NDIM, D)), shape((2, seqs, NDIM, D), BF16)),
+                (shape((2 * seqs + 1, NDIM, D)), shape((2 * seqs, NDIM, D), BF16)),
                 [],
-                (ids, par, state, *got),
-                [SMEM] + [VMEM] * (2 + len(got)),
+                (ids, state, *got),
+                [SMEM] + [VMEM] * (1 + len(got)),
                 "hop",
             )
     st_in, skip_pre, mixed, shared_pre, prob = call(
@@ -1141,16 +1205,15 @@
             pltpu.VMEM((NDIM, PIECES, D), F32),
         ],
         (
-            ids, after(normed, mine3), par, before, skip, w_shared, qg, kg, rb,
+            ids_lengths, after(normed, mine3), par, before, skip, w_shared, qg, kg, rb,
             *[h[2] for h in hops],
         ),
         [SMEM] + [VMEM] * (8 + len(hops)),
         "look",
         limit=10,
     )
-    other2 = swap(after(mine2, low), tp)
-    far_gates = spread_out([mine1, other1, mine2, other2], tp)
-    other3 = swap(after(mine3, *got), tp)
+    far_gates = spread_out([mine1, after(other1, prob), mine2, after(other2, prob)], tp)
+    other3 = swap(mine3, tp)
     gates = [w for group in near_gates + far_gates for w in group]
 
     values, value_pre, reset_pre, attended, gated, hidden_pre, update_pre, middle = call(
@@ -1171,13 +1234,13 @@
             pltpu.VMEM((D, 2 * D), BF16),
             pltpu.SemaphoreType.DMA((3 * tp,)),
         ],
-        (ids, tok, normed, mixed, prob, *gates),
+        (ids, tok, normed, after(mixed, other3), prob, *gates),
         [SMEM] + [VMEM] * 4 + [ANY] * len(gates),
         "mix",
         limit=10,
     )
 
-    far_feeds = spread_out([mine3, after(other3, middle)], tp)
+    far_feeds = spread_out([mine3, other3], tp)
     feeds = [w for group in near_feeds + far_feeds for w in group]
     out, keep3, send3, grad_hu, resid, grad_gain2 = call(
         functools.partial(ffn_kernel, seqs, tp),
@@ -1197,7 +1260,7 @@
             pltpu.VMEM((rows, D), F32),
             pltpu.SemaphoreType.DMA((3 * tp // 2,)),
         ],
-        (ids, tok, cot, middle, hidden_pre, update_pre, gain2, *feeds),
+        (ids_lengths, tok, cot, middle, hidden_pre, update_pre, gain2, *feeds),
         [SMEM] + [VMEM] * 6 + [ANY] * len(feeds),
         "ffn",
         limit=10,
@@ -1256,19 +1319,21 @@
     g2 = cut_y([keep2, after(got2, g3[0])], chunk)
     g2 = over_y(g2)
 
+    count = Z + SMALL_ROWS
+    count += -count % (16 * tp)
     (
-        keep1, send1, grad_skip, grad_normed, behind, back_ends, grad_wsh, misc,
+        keep1, send1, grad_skip, grad_normed, behind, back_ends, sums_keep, sums_send,
     ) = call(
         functools.partial(back_kernel, seqs, tp),
         (
-            shape((half, D, 2 * vb), BF16),
-            shape((half, D, 2 * vb), BF16),
+            shape(chunk, BF16),
+            shape(chunk, BF16),
             shape((BLOCKS, rows, LANES)),
             shape((rows, D)),
             shape((seqs, NDIM, PIECES, D)),
             shape((seqs, NDIM, D)),
-            shape((D, Z)),
-            shape((1, D)),
+            shape((count // 2, D)),
+            shape((count // 2, D)),
         ),
         [
             pltpu.VMEM((tp, D, 2 * vb), BF16),
@@ -1277,23 +1342,29 @@
             pltpu.VMEM((rows, D), F32),
             pltpu.VMEM((seqs, CH, CH), F32),
             pltpu.VMEM((3, NDIM, D), F32),
+            pltpu.VMEM((D, Z), F32),
+            pltpu.VMEM((1, D), F32),
+            pltpu.VMEM((count, D), F32),
+            pltpu.VMEM((BLOCKS, rows, LANES), F32),
+            pltpu.VMEM((NDIM, PIECES, D), F32),
             pltpu.SemaphoreType.DMA((3 * tp,)),
         ],
         (
             ids, normed, mixed, skip_pre, shared_pre, prob, values, value_pre, reset_pre, attended,
-            after(grad_hu, g2[0]), par, w_shared, qg, kg, *gates,
+            after(grad_hu, g2[0]), par, w_shared, qg, kg, tok, before, st_in, skip, grad_gain2,
+            *gates,
         ),
-        [SMEM] + [VMEM] * 14 + [ANY] * len(gates),
+        [SMEM] + [VMEM] * 19 + [ANY] * len(gates),
         "back",
-        limit=10,
+        limit=12,
     )
 
     g3 = cut_y([after(g3[0], send1)] + g3[1:], (1, D, wide))
     g2 = cut_tp([after(g2[0], g3[0])] + g2[1:], (half, D // yn, wide))
-    keep1, send1, grad_skip, grad_normed, behind, back_ends, grad_wsh, misc, _ = (
-        lax.optimization_barrier(
-            (keep1, send1, grad_skip, grad_normed, behind, back_ends, grad_wsh, misc, g2[0])
-        )
+    (
+        keep1, send1, grad_skip, grad_normed, behind, back_ends, sums_keep, sums_send, _,
+    ) = lax.optimization_barrier(
+        (keep1, send1, grad_skip, grad_normed, behind, back_ends, sums_keep, sums_send, g2[0])
     )
     adjoint = back_ends.reshape(seqs * NDIM, D)
     last[0] = g2[0]
@@ -1301,6 +1372,7 @@
     g2 = over_tp(g2)
     got1 = swap(send1, 1)
     got_adjoint = adjoint if traded else swap(adjoint, 1)
+    got_sums = swap(sums_send, 1)
     done = {}
 
     def first_chunks():
@@ -1313,8 +1385,8 @@
                 (g2, 0, wide, zcuts[0], [(0, 1, 0), (1, 1, 0)]),
             ],
         )
-        for cut in zcuts[1:]:
-            other = over_z(send, zcuts[zcuts.index(cut) - 1])
+        for i, cut in enumerate(zcuts[1:-1]):
+            other = over_z(send, zcuts[i])
             yield keep
             high //= 2
             keep, send = fold(
@@ -1322,10 +1394,15 @@
                 [(2, high, wide)] * 2,
                 [([now(keep), other], 0, wide, cut, [(0, 0, 0), (1, 0, 0)])],
             )
-        other = over_z(send, zcuts[-1])
+        other = over_z(send, zcuts[-2])
         yield keep
-        (total,) = fold(ids, [keep.shape], [([now(keep), other], 0, wide, None, [(0, 0, 0)])])
-        for cut in reversed(zcuts):
+        total = keep
+        for cut in zcuts[-1:] + [None]:
+            (total,) = fold(ids, [keep.shape], [([now(total), other], 0, wide, None, [(0, 0, 0)])])
+            if cut:
+                other = over_z(total, cut)
+                yield total
+        for cut in reversed(zcuts[:-1]):
             other = over_z(total, cut)
             yield total
             total = join(ids, now(total), other, cut)
@@ -1341,6 +1418,29 @@
         yield done["first"][0]
 
     def second_chunk():
+        small_high = count // 4
+        ad_rows = seqs * NDIM
+
+        def payload_rows():
+            return (ad_rows + small_high) * runs
+
+        own, kept, payload = call(
+            functools.partial(first_back_hop, seqs, not traded),
+            (
+                shape((ad_rows, D)),
+                shape((small_high, D)),
+                shape((payload_rows(), wide), BF16),
+            ),
+            [],
+            (ids, par, now(adjoint), got_adjoint, sums_keep, got_sums),
+            [SMEM] + [VMEM] * 5,
+            "hop",
+        )
+        got = [] if traded else [(got_adjoint, 0)]
+        level = int(not traded)
+        halved = True
+        other = swap(payload, masks[level])
+        yield payload
         parts = fold(
             ids,
             [(1, D, vb)] * half + [(half, D // yn, vb)] * yn,
@@ -1351,59 +1451,7 @@
         )
         left, right = over_tp(parts[:half]), over_y(parts[half:])
         yield parts[0]
-        count = Z + SMALL_ROWS
-        count += -count % (16 * tp)
-        sums, send = call(
-            functools.partial(sums_kernel, seqs),
-            (shape((count // 2, D)), shape((count // 2, D))),
-            [
-                pltpu.VMEM((count, D), F32),
-                pltpu.VMEM((BLOCKS, rows, LANES), F32),
-                pltpu.VMEM((NDIM, PIECES, D), F32),
-            ],
-            (
-                ids, tok, normed, now(grad_skip), grad_normed, par, before, st_in, skip, grad_gain2,
-                misc, grad_wsh,
-            ),
-            [SMEM] + [VMEM] * 11,
-            "sums",
-            limit=10,
-        )
-        got_sums = swap(send, 1)
-        yield sums
-        small_high = count // 4
-        ad_rows = seqs * NDIM
-
-        def payload_rows():
-            return (ad_rows + small_high) * runs
-
-        own, kept, payload = call(
-            functools.partial(first_back_hop, seqs, not traded),
-            (
-                shape((ad_rows, D)),
-                shape((small_high, D)),
-                shape((payload_rows(), wide), BF16),
-            ),
-            [],
-            (ids, par, now(adjoint), got_adjoint, sums, got_sums),
-            [SMEM] + [VMEM] * 5,
-            "hop",
-        )
-        got = [] if traded else [(got_adjoint, 0)]
-        level = int(not traded)
-        halved = True
-        other = swap(payload, masks[level])
-        yield payload
-        parts = fold(
-            ids,
-            [(1, D // yn, vb)] * (yn + half),
-            [
-                ([now(left[0])] + left[1:], 0, vb, cut_of_y, [(k, 0, 0) for k in range(yn)]),
-                (right, 0, vb, "tp", [(yn + k, 0, 0) for k in range(half)]),
-            ],
-        )
-        left, right = over_y(parts[:yn]), over_tp(parts[yn:])
-        yield parts[0]
+        crossed = False
         while level + 1 < levels - len(zcuts):
             got.append((other, 0))
             split = 2 * masks[level] if 2 * masks[level] < tp else 0
@@ -1424,6 +1472,19 @@
             level += 1
             other = swap(payload, masks[level])
             yield payload
+            if crossed:
+                continue
+            crossed = True
+            parts = fold(
+                ids,
+                [(1, D // yn, vb)] * (yn + half),
+                [
+                    ([now(left[0])] + left[1:], 0, vb, cut_of_y, [(k, 0, 0) for k in range(yn)]),
+                    (right, 0, vb, "tp", [(yn + k, 0, 0) for k in range(half)]),
+                ],
+            )
+            left, right = over_y(parts[:yn]), over_tp(parts[yn:])
+            yield parts[0]
         high = D // yn
         top = 0
         flat = [p.reshape(p.shape[1:]) for p in left + right]
@@ -1431,15 +1492,16 @@
             (tuple(range(len(left))), vb, 0),
             (tuple(range(len(left), len(flat))), vb, vb),
         ]
-        for cut in zcuts:
+        for cut in zcuts[:-1] + [None]:
             got.append((other, top))
-            high //= 2
-            keep, kept, own, payload = call(
+            high = high // 2 if cut else high
+            kept_chunk = [shape((high, wide), BF16)] if cut else []
+            *flat, kept, own, payload = call(
                 functools.partial(
-                    ride_kernel, seqs, level, 0, halved, top, jobs, cut, False
+                    ride_kernel, seqs, level, 0, halved, top, jobs, cut, high, False
                 ),
                 (
-                    shape((high, wide), BF16),
+                    *kept_chunk,
                     shape((small_high, D)),
                     shape((ad_rows, D)),
                     shape((high + payload_rows(), wide), BF16),
@@ -1452,13 +1514,12 @@
             halved = False
             level += 1
             top = high
-            flat = [keep]
-            jobs = [((0, -1), wide, 0)]
+            jobs = [((0 if cut else -2, -1), wide, 0)]
             other = swap(payload, masks[level])
-            yield keep
+            yield payload
         got.append((other, top))
         total, kept = call(
-            functools.partial(ride_kernel, seqs, level, 0, False, top, jobs, None, True),
+            functools.partial(ride_kernel, seqs, level, 0, False, top, jobs, None, high, True),
             (shape((high, wide), BF16), shape((small_high, D))),
             [],
             (ids, par, now(own), kept, payload, other, *flat),
@@ -1468,22 +1529,43 @@
         bits = list(reversed(bits_of(tp)))
         total = total[None]
         far = swap(kept, bits[0])
-        for i, cut in enumerate(reversed(zcuts)):
-            other = over_z(total, cut)
-            yield total
-            total = join(ids, now(total), other, cut)
-            if i + 1 < len(bits):
-                (kept,) = call(
-                    functools.partial(pair_kernel, bits[i]),
-                    (shape((2 * kept.shape[0], D)),),
-                    [],
-                    (ids, after(kept, total), far),
-                    [SMEM, VMEM, VMEM],
-                    "pair",
-                )
-                far = swap(kept, bits[i + 1])
+        other = over_z(total, zcuts[-2])
+        yield total
+        (done["tokens"],) = call(
+            functools.partial(leave_kernel, seqs, [at for _, at in got]),
+            (shape((seqs, CH, D), BF16),),
+            [
+                pltpu.VMEM((seqs, NDIM, D), F32),
+                pltpu.VMEM((NDIM, PIECES, D), F32),
+                pltpu.VMEM((BLOCKS, rows, LANES), F32),
+            ],
+            (
+                ids, tok, par, now(grad_skip), grad_normed, behind, resid, gain1, skip,
+                *[g for g, _ in got],
+            ),
+            [SMEM] + [VMEM] * (8 + levels),
+            "leave",
+            limit=10,
+        )
+        yield done["tokens"]
+        for i in range(len(zcuts) - 2, -1, -1):
+            total = join(ids, now(total), other, zcuts[i])
+            if i:
+                other = over_z(total, zcuts[i - 1])
+                yield total
         pieces = over_y([total] * yn)
         yield total
+        for i in range(len(bits) - 1):
+            (kept,) = call(
+                functools.partial(pair_kernel, bits[i]),
+                (shape((2 * kept.shape[0], D)),),
+                [],
+                (ids, now(kept), far),
+                [SMEM, VMEM, VMEM],
+                "pair",
+            )
+            far = swap(kept, bits[i + 1])
+            yield kept
         done["small"] = call(
             finish_kernel,
             (
@@ -1503,30 +1585,14 @@
             [SMEM] + [VMEM] * 6,
             "finish",
         )
-        (done["tokens"],) = call(
-            functools.partial(leave_kernel, seqs, [at for _, at in got]),
-            (shape((seqs, CH, D), BF16),),
-            [
-                pltpu.VMEM((seqs, NDIM, D), F32),
-                pltpu.VMEM((NDIM, PIECES, D), F32),
-                pltpu.VMEM((BLOCKS, rows, LANES), F32),
-            ],
-            (
-                ids, tok, par, after(grad_skip, done["small"][0]), grad_normed, behind, resid,
-                gain1, skip, *[g for g, _ in got],
-            ),
-            [SMEM] + [VMEM] * (8 + levels),
-            "leave",
-            limit=10,
-        )
-        yield done["tokens"]
+        yield done["small"][0]
         done["second"] = unpack(
             unpack_sides, cut_of_y, ids, [now(pieces[0])] + pieces[1:], [(D, vb), (D, vb)]
         )
         yield done["second"][0]
 
     walks = {"f": first_chunks(), "s": second_chunk()}
-    order = "s s f s s f s f s f s f s s s s f s".replace(" ", "")
+    order = "sssfsfsfsfsssssfs"
 
     def advance(name):
         try:

time: 157 us -> 140 us (0.89)
  Pallas kernels: 53.5 us -> 41.2 us
  local copies, waits for them, and re-layouts: 5.06 us -> 2.26 us
  waiting for transfers between devices: 59 us -> 56.3 us
    pallas_call x33 -> x32, Pallas kernels: 53.5 us -> 41.2 us  [call(): pl.pallas_call(body, out_shape=out, in_specs=specs, out_specs=outs or jax...]
    unnamed x42 -> x38, local copies, waits for them, and re-layouts: 5.06 us -> 2.26 us
    ppermute x48 -> x46, waiting for transfers between devices: 59 us -> 56.3 us  [swap(): return lax.ppermute(value, BOTH, [(i, i ^ mask) for i in range(count)])]
    ppermute x48 -> x46, starting transfers between devices: 38.4 us -> 38.4 us  [swap(): return lax.ppermute(value, BOTH, [(i, i ^ mask) for i in range(count)])]
  transfers between devices with their start and end apart: 48 -> 46, of which waited for: 24 -> 26; matrix products, arithmetic and copies ran while one was open for 0% -> 0% of each run, Pallas kernels for 26% -> 23%
where the time goes in v3:
time: 140 us; the launch traced here: 139 us
  waiting for transfers between devices  56.3 us (40%)
  Pallas kernels  41.2 us (29%)
  starting transfers between devices  38.4 us (27%)
  local copies, waits for them, and re-layouts  2.26 us (2%)
    ppermute x46, waiting for transfers between devices, swap(): return lax.ppermute(value, BOTH, [(i, i ^ mask) for i in range(count)])  56.3 us
    pallas_call x32, Pallas kernels, call(): pl.pallas_call(body, out_shape=out, in_specs=specs, out_specs=outs or jax...  41.2 us
    ppermute x46, starting transfers between devices, swap(): return lax.ppermute(value, BOTH, [(i, i ^ mask) for i in range(count)])  38.4 us
  transfers between devices with their start and end apart: 46, of which 26 were waited for; matrix products, arithmetic and copies ran while one was open for 0% of the time, Pallas kernels for 23%

profile of v3, /device:TPU:0, one launch (start us, length us, event | category | flops | bytes accessed | tf_op | source)
XLA Modules:
  0.0 139.3 jit_solution(10487366019660746241)
XLA Ops:
  0.7 1.7 %half.1 = bf16[256,512]{1,0:T(8,128)(2,1)} custom-call(bf16[512,256]{1,0:T(8,128)(2,1)} %w_value.2, bf16[512,256]{1,0:T(8,128)(2,1)} %w_reset.2), custom_call_target="tpu_custom_call" | custom-call | tf_op jit(solution)/shard_map/half/pallas_call | solution.py:118
  2.4 3.0 %collective-permute-start = (bf16[256,512]{1,0:T(8,128)(2,1)}, bf16[256,512]{1,0:T(8,128)(2,1)S(1)}, u32[]{:S(2)}, u32[]{:S(2)}) collective-permute-start(bf16[256,512]{1,0:T(8,128)(2,1)} %half.1), channel_id=1, source_target_pairs={{0,2},{1,3},{2,0},{3,1},{4,6},{5,7},{6,4},{7,5},{8,10},{9,11},{10,... | collective-permute-start | bytes 786440 | tf_op jit(solution)/shard_map/ppermute | solution.py:1009
  5.4 4.3 %enter.1 = (bf16[256,512]{1,0:T(8,128)(2,1)}, f32[4,16,512]{2,1,0:T(8,128)}, f32[2,2,16,8,512]{4,3,2,1,0:T(8,128)}, f32[5,16,512]{2,1,0:T(8,128)}, bf16[4,16,512]{2,1,0:T(8,128)(2,1)}) custom-call(bf16[2,128,512]{2,1,0:T(8,128)(2,1)} %refs_0_.7, f32[1,512]{1,0:T(1,128)} %bitcast.37, f32[16,512]{1,0:T(8,128)} %bitcast.31, f32[16,512]{1,0:T(8,128)} %bitcast.33, ...), custom_call_target="tpu_custom_call" | custom-call | tf_op jit(solution)/shard_map/enter/pallas_call | solution.py:118
  9.7 2.2 %collective-permute-done.refs_8_.refs_23_ = bf16[256,512]{1,0:T(8,128)(2,1)S(1)} collective-permute-done((bf16[256,512]{1,0:T(8,128)(2,1)}, bf16[256,512]{1,0:T(8,128)(2,1)S(1)}, u32[]{:S(2)}, u32[]{:S(2)}) %collective-permute-start) | collective-permute-done | bytes 262176 | tf_op jit(solution)/shard_map/ppermute | solution.py:1009
  11.9 1.5 %collective-permute-done.1.refs_1_.refs_8_ = bf16[4,16,512]{2,1,0:T(8,128)(2,1)S(1)} collective-permute-done((bf16[4,16,512]{2,1,0:T(8,128)(2,1)}, bf16[4,16,512]{2,1,0:T(8,128)(2,1)S(1)}, u32[]{:S(2)}, u32[]{:S(2)}) %collective-permute-start.1) | collective-permute-done | bytes 65568 | tf_op jit(solution)/shard_map/ppermute | solution.py:1009
  13.3 0.9 copy-done.9
  14.3 2.8 %collective-permute-start.4 = (bf16[4,16,512]{2,1,0:T(8,128)(2,1)S(1)}, bf16[4,16,512]{2,1,0:T(8,128)(2,1)S(1)}, u32[]{:S(2)}, u32[]{:S(2)}) collective-permute-start(bf16[4,16,512]{2,1,0:T(8,128)(2,1)S(1)} %get-tuple-element.166), channel_id=1, source_target_pairs={{0,6},{1,7},{2,4},{3,5},{4,2},{5,3},{6,0},{7,1},{8,14},{9,15},{10,... | collective-permute-start | bytes 196616 | tf_op jit(solution)/shard_map/ppermute | solution.py:1009
  17.9 2.9 %pack.1 = (bf16[512,512]{1,0:T(8,128)(2,1)}, bf16[512,512]{1,0:T(8,128)(2,1)}, bf16[512,512]{1,0:T(8,128)(2,1)}, bf16[512,256]{1,0:T(8,128)(2,1)}, bf16[256,512]{1,0:T(8,128)(2,1)}) custom-call(bf16[512,256]{1,0:T(8,128)(2,1)} %w_value.2, bf16[512,256]{1,0:T(8,128)(2,1)} %w_reset.2, bf16[128,512]{1,0:T(8,128)(2,1)} %w_hidden, bf16[128,512]{1,0:T(8,128)(2,1)} %w_update, ...), custom_call_target="tpu_custom_call" | custom-call | tf_op jit(solution)/shard_map/pack/pallas_call | solution.py:118
  22.6 1.5 %collective-permute-start.7 = (bf16[256,512]{1,0:T(8,128)(2,1)S(1)}, bf16[256,512]{1,0:T(8,128)(2,1)S(1)}, u32[]{:S(2)}, u32[]{:S(2)}) collective-permute-start(bf16[256,512]{1,0:T(8,128)(2,1)S(1)} %collective-permute-done.refs_8_.refs_23_), channel_id=1, source_target_pairs={{0,4},{1,5},{2,6},{3,7},{4,0},{5,1},{6,2},{7,3},{8,12},{9,13},{10,... | collective-permute-start | bytes 786440 | tf_op jit(solution)/shard_map/ppermute | solution.py:1009
  24.1 0.7 collective-permute-start.6
  24.8 1.6 %collective-permute-start.5 = (bf16[4,16,512]{2,1,0:T(8,128)(2,1)S(1)}, bf16[4,16,512]{2,1,0:T(8,128)(2,1)S(1)}, u32[]{:S(2)}, u32[]{:S(2)}) collective-permute-start(bf16[4,16,512]{2,1,0:T(8,128)(2,1)S(1)} %get-tuple-element.177), channel_id=1, source_target_pairs={{0,8},{1,9},{2,10},{3,11},{4,12},{5,13},{6,14},{7,15},{8,0},{9,1},... | collective-permute-start | bytes 196616 | tf_op jit(solution)/shard_map/ppermute | solution.py:1009
  26.4 2.7 %collective-permute-done.5.refs_1_.refs_12_ = bf16[4,16,512]{2,1,0:T(8,128)(2,1)S(1)} collective-permute-done((bf16[4,16,512]{2,1,0:T(8,128)(2,1)S(1)}, bf16[4,16,512]{2,1,0:T(8,128)(2,1)S(1)}, u32[]{:S(2)}, u32[]{:S(2)}) %collective-permute-start.5) | collective-permute-done | bytes 65568 | tf_op jit(solution)/shard_map/ppermute | solution.py:1009
  29.1 0.7 hop.7
  29.8 1.0 collective-permute-done.7.refs_9_.refs_24_
  30.9 1.4 %collective-permute-done.6.refs_10_.refs_25_ = bf16[512,256]{1,0:T(8,128)(2,1)S(1)} collective-permute-done((bf16[512,256]{1,0:T(8,128)(2,1)}, bf16[512,256]{1,0:T(8,128)(2,1)S(1)}, u32[]{:S(2)}, u32[]{:S(2)}) %collective-permute-start.6) | collective-permute-done | bytes 262176 | tf_op jit(solution)/shard_map/ppermute | solution.py:1009
  32.3 0.7 collective-permute-start.10
  33.1 2.6 %collective-permute-start.11 = (bf16[4,16,512]{2,1,0:T(8,128)(2,1)S(1)}, bf16[4,16,512]{2,1,0:T(8,128)(2,1)S(1)}, u32[]{:S(2)}, u32[]{:S(2)}) collective-permute-start(bf16[4,16,512]{2,1,0:T(8,128)(2,1)S(1)} %get-tuple-element.186), channel_id=1, source_target_pairs={{0,16},{1,17},{2,18},{3,19},{4,20},{5,21},{6,22},{7,23},{8,24},{9,... | collective-permute-start | bytes 196616 | tf_op jit(solution)/shard_map/ppermute | solution.py:1009
  35.7 1.6 %collective-permute-start.13 = (bf16[512,256]{1,0:T(8,128)(2,1)S(1)}, bf16[512,256]{1,0:T(8,128)(2,1)S(1)}, u32[]{:S(2)}, u32[]{:S(2)}) collective-permute-start(bf16[512,256]{1,0:T(8,128)(2,1)S(1)} %collective-permute-done.6.refs_10_.refs_25_), channel_id=1, source_target_pairs={{0,8},{1,9},{2,10},{3,11},{4,12},{5,13},{6,14},{7,15},{8,0},{9,1},... | collective-permute-start | bytes 786440 | tf_op jit(solution)/shard_map/ppermute | solution.py:1009
  37.7 1.9 %collective-permute-done.10.refs_8_ = bf16[256,512]{1,0:T(8,128)(2,1)S(1)} collective-permute-done((bf16[256,512]{1,0:T(8,128)(2,1)}, bf16[256,512]{1,0:T(8,128)(2,1)S(1)}, u32[]{:S(2)}, u32[]{:S(2)}) %collective-permute-start.10) | collective-permute-done | bytes 262176 | tf_op jit(solution)/shard_map/ppermute | solution.py:1009
  40.3 0.6 copy-done.13
  40.9 3.0 %look.1 = (f32[2,2,16,512]{3,2,1,0:T(8,128)S(1)}, f32[256,512]{1,0:T(8,128)S(1)}, bf16[256,512]{1,0:T(8,128)(2,1)S(1)}, f32[256,128]{1,0:T(8,128)S(1)}, f32[2,128,128]{2,1,0:T(8,128)S(1)}) custom-call(s32[2]{0:T(128)S(1)} %copy-done.15, bf16[256,512]{1,0:T(8,128)(2,1)S(1)} %copy-done.3, f32[4,16,512]{2,1,0:T(8,128)S(1)} %copy-done, ...), custom_call_target="tpu_custom_call" | custom-call | tf_op jit(solution)/shard_map/look/pallas_call | solution.py:118
  44.0 0.6 collective-permute-start.15
  45.1 1.0 collective-permute-done.12.refs_9_
  46.1 3.6 %mix.1 = (bf16[4,256,256]{2,1,0:T(8,128)(2,1)S(1)}, f32[4,256,256]{2,1,0:T(8,128)S(1)}, f32[4,256,256]{2,1,0:T(8,128)S(1)}, f32[4,256,256]{2,1,0:T(8,128)S(1)}, ...) custom-call(bf16[2,128,512]{2,1,0:T(8,128)(2,1)S(1)} %copy-done.1, ...), custom_call_target="tpu_custom_call" | custom-call | tf_op jit(solution)/shard_map/mix/pallas_call | solution.py:118
  49.8 0.7 copy-done.14
  50.4 5.2 %ffn.1 = (bf16[256,512]{1,0:T(8,128)(2,1)}, bf16[2,512,512]{2,1,0:T(8,128)(2,1)S(1)}, bf16[2,512,512]{2,1,0:T(8,128)(2,1)S(1)}, bf16[256,1024]{1,0:T(8,128)(2,1)...) custom-call(s32[2]{0:T(128)S(1)} %copy-done.15, bf16[2,128,512]{2,1,0:T(8,128)(2,1)S(1)} %copy-done.1, ...), custom_call_target="tpu_custom_call" | custom-call | tf_op jit(solution)/shard_map/ffn/pallas_call | solution.py:118
  56.2 1.1 gates.1
  57.4 1.1 collective-permute-done.22.refs_1_
  58.8 1.3 collective-permute-start.23
  60.4 1.4 %collective-permute-start.24 = (bf16[2,256,512]{2,1,0:T(8,128)(2,1)S(1)}, bf16[2,256,512]{2,1,0:T(8,128)(2,1)S(1)}, u32[]{:S(2)}, u32[]{:S(2)}) collective-permute-start(bf16[2,256,512]{2,1,0:T(8,128)(2,1)S(1)} %get-tuple-element.233), channel_id=1, source_target_pairs={{0,4},{1,5},{2,6},{3,7},{4,0},{5,1},{6,2},{7,3},{8,12},{9,13},{10,... | collective-permute-start | bytes 1572872 | tf_op jit(solution)/shard_map/ppermute | solution.py:1009
  61.8 9.8 %back.1 = (bf16[2,512,512]{2,1,0:T(8,128)(2,1)S(1)}, bf16[2,512,512]{2,1,0:T(8,128)(2,1)S(1)}, f32[4,256,128]{2,1,0:T(8,128)S(1)}, f32[256,512]{1,0:T(8,128)S(1)...) custom-call(bf16[256,512]{1,0:T(8,128)(2,1)S(1)} %copy-done.3, ...), custom_call_target="tpu_custom_call" | custom-call | tf_op jit(solution)/shard_map/back/pallas_call | solution.py:118
  71.6 1.4 %collective-permute-done.23.refs_1_ = bf16[1,512,512]{2,1,0:T(8,128)(2,1)S(1)} collective-permute-done((bf16[1,512,512]{2,1,0:T(8,128)(2,1)S(1)}, bf16[1,512,512]{2,1,0:T(8,128)(2,1)S(1)}, u32[]{:S(2)}, u32[]{:S(2)}) %collective-permute-start.23) | collective-permute-done | bytes 524320 | tf_op jit(solution)/shard_map/ppermute | solution.py:1009
  73.2 1.3 collective-permute-done.24.refs_1_
  75.5 1.4 collective-permute-start.29
  76.9 0.7 collective-permute-start.30
  77.6 1.3 collective-permute-done.25.refs_2_.refs_8_
  78.9 1.4 collective-permute-start.28
  80.7 5.9 %collective-permute-done.28.refs_4_.refs_9_ = bf16[80,512]{1,0:T(8,128)(2,1)S(1)} collective-permute-done((bf16[80,512]{1,0:T(8,128)(2,1)S(1)}, bf16[80,512]{1,0:T(8,128)(2,1)S(1)}, u32[]{:S(2)}, u32[]{:S(2)}) %collective-permute-start.28) | collective-permute-done | bytes 81952 | tf_op jit(solution)/shard_map/ppermute | solution.py:1009
  86.7 0.8 collective-permute-start.31
  87.5 1.1 collective-permute-start.32
  88.8 1.2 collective-permute-start.33
  90.0 3.9 %collective-permute-done.31.refs_1_ = bf16[1,512,256]{2,1,0:T(8,128)(2,1)S(1)} collective-permute-done((bf16[1,512,256]{2,1,0:T(8,128)(2,1)S(1)}, bf16[1,512,256]{2,1,0:T(8,128)(2,1)S(1)}, u32[]{:S(2)}, u32[]{:S(2)}) %collective-permute-start.31) | collective-permute-done | bytes 262176 | tf_op jit(solution)/shard_map/ppermute | solution.py:1009
  94.5 0.9 collective-permute-done.33.refs_1_
  95.5 2.2 %collective-permute-start.37 = (bf16[2,128,512]{2,1,0:T(8,128)(2,1)S(1)}, bf16[2,128,512]{2,1,0:T(8,128)(2,1)S(1)}, u32[]{:S(2)}, u32[]{:S(2)}) collective-permute-start(bf16[2,128,512]{2,1,0:T(8,128)(2,1)S(1)} %fold.16.refs_0_), channel_id=1, source_target_pairs={{0,16},{1,17},{2,18},{3,19},{4,20},{5,21},{6,22},{7,23},{8,24},{9,... | collective-permute-start | bytes 786440 | tf_op jit(solution)/shard_map/ppermute | solution.py:1009
  97.7 1.4 %collective-permute-start.35 = (bf16[1,256,256]{2,1,0:T(8,128)(2,1)S(1)}, bf16[1,256,256]{2,1,0:T(8,128)(2,1)S(1)}, u32[]{:S(2)}, u32[]{:S(2)}) collective-permute-start(bf16[1,256,256]{2,1,0:T(8,128)(2,1)S(1)} %get-tuple-element.263), channel_id=1, source_target_pairs={{0,4},{1,5},{2,6},{3,7},{4,0},{5,1},{6,2},{7,3},{8,12},{9,13},{10,... | collective-permute-start | bytes 393224 | tf_op jit(solution)/shard_map/ppermute | solution.py:1009
  99.1 1.3 collective-permute-start.36
  100.4 0.6 collective-permute-start.34
  101.0 3.8 %collective-permute-done.34.refs_4_.refs_10_ = bf16[80,512]{1,0:T(8,128)(2,1)S(1)} collective-permute-done((bf16[80,512]{1,0:T(8,128)(2,1)S(1)}, bf16[80,512]{1,0:T(8,128)(2,1)S(1)}, u32[]{:S(2)}, u32[]{:S(2)}) %collective-permute-start.34) | collective-permute-done | bytes 81952 | tf_op jit(solution)/shard_map/ppermute | solution.py:1009
  105.0 1.6 %collective-permute-start.38 = (bf16[208,512]{1,0:T(8,128)(2,1)S(1)}, bf16[208,512]{1,0:T(8,128)(2,1)S(1)}, u32[]{:S(2)}, u32[]{:S(2)}) collective-permute-start(bf16[208,512]{1,0:T(8,128)(2,1)S(1)} %get-tuple-element.267.refs_3_), channel_id=1, source_target_pairs={{0,8},{1,9},{2,10},{3,11},{4,12},{5,13},{6,14},{7,15},{8,0},{9,1},... | collective-permute-start | bytes 638984 | tf_op jit(solution)/shard_map/ppermute | solution.py:1009
  106.6 1.2 collective-permute-done.37.refs_1_
  108.1 5.1 %collective-permute-done.38.refs_4_.refs_11_ = bf16[208,512]{1,0:T(8,128)(2,1)S(1)} collective-permute-done((bf16[208,512]{1,0:T(8,128)(2,1)S(1)}, bf16[208,512]{1,0:T(8,128)(2,1)S(1)}, u32[]{:S(2)}, u32[]{:S(2)}) %collective-permute-start.38) | collective-permute-done | bytes 213024 | tf_op jit(solution)/shard_map/ppermute | solution.py:1009
  113.4 6.4 %collective-permute-done.39.refs_1_ = bf16[2,128,512]{2,1,0:T(8,128)(2,1)S(1)} collective-permute-done((bf16[2,128,512]{2,1,0:T(8,128)(2,1)S(1)}, bf16[2,128,512]{2,1,0:T(8,128)(2,1)S(1)}, u32[]{:S(2)}, u32[]{:S(2)}) %collective-permute-start.39) | collective-permute-done | bytes 262176 | tf_op jit(solution)/shard_map/ppermute | solution.py:1009
  119.9 0.9 collective-permute-start.44
  120.8 2.9 %collective-permute-done.40.refs_4_.refs_12_ = bf16[208,512]{1,0:T(8,128)(2,1)S(1)} collective-permute-done((bf16[208,512]{1,0:T(8,128)(2,1)S(1)}, bf16[208,512]{1,0:T(8,128)(2,1)S(1)}, u32[]{:S(2)}, u32[]{:S(2)}) %collective-permute-start.40) | collective-permute-done | bytes 213024 | tf_op jit(solution)/shard_map/ppermute | solution.py:1009
  123.9 0.7 collective-permute-start.42
  124.6 2.8 %leave.1 = bf16[2,128,512]{2,1,0:T(8,128)(2,1)} custom-call(bf16[2,128,512]{2,1,0:T(8,128)(2,1)S(1)} %copy-done.1, f32[4,16,512]{2,1,0:T(8,128)S(1)} %copy-done, f32[4,256,128]{2,1,0:T(8,128)S(1)} %get-tuple-element.278.refs_2_, f32[256,512]{1,0:T(8,128)S(1)} %get-tuple-element.279.refs_3_, f32[2,16,8,512]{3,2,1,0:T(8,128)S(1)} %get-tuple-element.280.refs_4_, ...), custom_call_target="tpu_custom_call" | custom-call | tf_op jit(solution)/shard_map/leave/pallas_call | solution.py:118
  127.4 1.4 %collective-permute-done.41.refs_1_ = bf16[1,128,512]{2,1,0:T(8,128)(2,1)S(1)} collective-permute-done((bf16[1,128,512]{2,1,0:T(8,128)(2,1)S(1)}, bf16[1,128,512]{2,1,0:T(8,128)(2,1)S(1)}, u32[]{:S(2)}, u32[]{:S(2)}) %collective-permute-start.41) | collective-permute-done | bytes 131104 | tf_op jit(solution)/shard_map/ppermute | solution.py:1009
  128.9 0.7 collective-permute-start.45
  129.7 1.4 %collective-permute-done.43.refs_5_ = f32[96,512]{1,0:T(8,128)S(1)} collective-permute-done((f32[96,512]{1,0:T(8,128)S(1)}, f32[96,512]{1,0:T(8,128)S(1)}, u32[]{:S(2)}, u32[]{:S(2)}) %collective-permute-start.43) | collective-permute-done | bytes 196640 | tf_op jit(solution)/shard_map/ppermute | solution.py:1009
  131.1 0.8 finish.1
  131.9 2.9 %collective-permute-done.44.refs_1_ = bf16[2,256,512]{2,1,0:T(8,128)(2,1)S(1)} collective-permute-done((bf16[2,256,512]{2,1,0:T(8,128)(2,1)S(1)}, bf16[2,256,512]{2,1,0:T(8,128)(2,1)S(1)}, u32[]{:S(2)}, u32[]{:S(2)}) %collective-permute-start.44) | collective-permute-done | bytes 524320 | tf_op jit(solution)/shard_map/ppermute | solution.py:1009
  134.8 1.5 %unpack.2 = (f32[512,256]{1,0:T(8,128)}, f32[256,512]{1,0:T(8,128)}, f32[128,512]{1,0:T(8,128)}, f32[128,512]{1,0:T(8,128)}, f32[256,512]{1,0:T(8,128)}) custom-call(bf16[2,256,512]{2,1,0:T(8,128)(2,1)S(1)} %join.2.refs_0_, bf16[2,256,512]{2,1,0:T(8,128)(2,1)S(1)} %collective-permute-done.44.refs_1_), custom_call_target="tpu_custom_call" | custom-call | tf_op jit(solution)/shard_map/unpack/pallas_call | solution.py:118
  136.3 2.0 %collective-permute-done.45.refs_1_ = bf16[1,256,512]{2,1,0:T(8,128)(2,1)S(1)} collective-permute-done((bf16[1,256,512]{2,1,0:T(8,128)(2,1)S(1)}, bf16[1,256,512]{2,1,0:T(8,128)(2,1)S(1)}, u32[]{:S(2)}, u32[]{:S(2)}) %collective-permute-start.45) | collective-permute-done | bytes 262176 | tf_op jit(solution)/shard_map/ppermute | solution.py:1009
  138.3 1.0 unpack.3
  (98 shorter events, 8.9 us)
Async XLA Ops:
  2.4 9.5 %collective-permute-start = (bf16[256,512]{1,0:T(8,128)(2,1)}, bf16[256,512]{1,0:T(8,128)(2,1)S(1)}, u32[]{:S(2)}, u32[]{:S(2)}) collective-permute-start(bf16[256,512]{1,0:T(8,128)(2,1)} %half.1), channel_id=1, source_target_pairs={{0,2},{1,3},{2,0},{3,1},{4,6},{5,7},{6,4},{7,5},{8,10},{9,11},{10,... | collective-permute-start | bytes 786440 | tf_op jit(solution)/shard_map/ppermute | solution.py:1009
  11.9 1.5 %collective-permute-start.1 = (bf16[4,16,512]{2,1,0:T(8,128)(2,1)}, bf16[4,16,512]{2,1,0:T(8,128)(2,1)S(1)}, u32[]{:S(2)}, u32[]{:S(2)}) collective-permute-start(bf16[4,16,512]{2,1,0:T(8,128)(2,1)} %get-tuple-element.165), channel_id=1, source_target_pairs={{0,1},{1,0},{2,3},{3,2},{4,5},{5,4},{6,7},{7,6},{8,9},{9,8},{10,11... | collective-permute-start | bytes 196616 | tf_op jit(solution)/shard_map/ppermute | solution.py:1009
  13.3 0.9 copy-start.9
  14.3 25.9 %copy-start.2 = (f32[2,2,16,8,512]{4,3,2,1,0:T(8,128)S(1)}, f32[2,2,16,8,512]{4,3,2,1,0:T(8,128)}, u32[]{:S(2)}) copy-start(f32[2,2,16,8,512]{4,3,2,1,0:T(8,128)} %get-tuple-element.190.refs_2_.refs_15_) | copy-start | bytes 3145732
  14.3 6.5 %collective-permute-start.4 = (bf16[4,16,512]{2,1,0:T(8,128)(2,1)S(1)}, bf16[4,16,512]{2,1,0:T(8,128)(2,1)S(1)}, u32[]{:S(2)}, u32[]{:S(2)}) collective-permute-start(bf16[4,16,512]{2,1,0:T(8,128)(2,1)S(1)} %get-tuple-element.166), channel_id=1, source_target_pairs={{0,6},{1,7},{2,4},{3,5},{4,2},{5,3},{6,0},{7,1},{8,14},{9,15},{10,... | collective-permute-start | bytes 196616 | tf_op jit(solution)/shard_map/ppermute | solution.py:1009
  17.1 4.3 %collective-permute-start.3 = (bf16[4,16,512]{2,1,0:T(8,128)(2,1)S(1)}, bf16[4,16,512]{2,1,0:T(8,128)(2,1)S(1)}, u32[]{:S(2)}, u32[]{:S(2)}) collective-permute-start(bf16[4,16,512]{2,1,0:T(8,128)(2,1)S(1)} %get-tuple-element.166), channel_id=1, source_target_pairs={{0,4},{1,5},{2,6},{3,7},{4,0},{5,1},{6,2},{7,3},{8,12},{9,13},{10,... | collective-permute-start | bytes 196616 | tf_op jit(solution)/shard_map/ppermute | solution.py:1009
  17.6 4.3 %collective-permute-start.2 = (bf16[4,16,512]{2,1,0:T(8,128)(2,1)S(1)}, bf16[4,16,512]{2,1,0:T(8,128)(2,1)S(1)}, u32[]{:S(2)}, u32[]{:S(2)}) collective-permute-start(bf16[4,16,512]{2,1,0:T(8,128)(2,1)S(1)} %get-tuple-element.166), channel_id=1, source_target_pairs={{0,2},{1,3},{2,0},{3,1},{4,6},{5,7},{6,4},{7,5},{8,10},{9,11},{10,... | collective-permute-start | bytes 196616 | tf_op jit(solution)/shard_map/ppermute | solution.py:1009
  21.9 18.4 %copy-start.3 = (bf16[256,512]{1,0:T(8,128)(2,1)S(1)}, bf16[256,512]{1,0:T(8,128)(2,1)}, u32[]{:S(2)}) copy-start(bf16[256,512]{1,0:T(8,128)(2,1)} %get-tuple-element.188.refs_0_.refs_1_) | copy-start | bytes 786436
  21.9 18.4 %copy-start.6 = (bf16[512,128]{1,0:T(8,128)(2,1)S(1)}, bf16[512,128]{1,0:T(8,128)(2,1)}, u32[]{:S(2)}) copy-start(bf16[512,128]{1,0:T(8,128)(2,1)} %refs_11_.1) | copy-start | bytes 393220
  22.0 18.3 %copy-start = (f32[4,16,512]{2,1,0:T(8,128)S(1)}, f32[4,16,512]{2,1,0:T(8,128)}, u32[]{:S(2)}) copy-start(f32[4,16,512]{2,1,0:T(8,128)} %get-tuple-element.189.refs_1_.refs_10_.refs_0_) | copy-start | bytes 393220
  22.0 10.3 %collective-permute-start.9 = (bf16[512,512]{1,0:T(8,128)(2,1)}, bf16[512,512]{1,0:T(8,128)(2,1)S(1)}, u32[]{:S(2)}, u32[]{:S(2)}) collective-permute-start(bf16[512,512]{1,0:T(8,128)(2,1)} %get-tuple-element.185.refs_5_.refs_20_), channel_id=1, source_target_pairs={{0,1},{1,0},{2,3},{3,2},{4,5},{5,4},{6,7},{7,6},{8,9},{9,8},{10,11... | collective-permute-start | bytes 1572872 | tf_op jit(solution)/shard_map/ppermute | solution.py:1009
  22.1 10.2 %collective-permute-start.8 = (bf16[512,512]{1,0:T(8,128)(2,1)}, bf16[512,512]{1,0:T(8,128)(2,1)S(1)}, u32[]{:S(2)}, u32[]{:S(2)}) collective-permute-start(bf16[512,512]{1,0:T(8,128)(2,1)} %get-tuple-element.183.refs_4_.refs_19_), channel_id=1, source_target_pairs={{0,1},{1,0},{2,3},{3,2},{4,5},{5,4},{6,7},{7,6},{8,9},{9,8},{10,11... | collective-permute-start | bytes 1572872 | tf_op jit(solution)/shard_map/ppermute | solution.py:1009
  22.6 8.3 %collective-permute-start.7 = (bf16[256,512]{1,0:T(8,128)(2,1)S(1)}, bf16[256,512]{1,0:T(8,128)(2,1)S(1)}, u32[]{:S(2)}, u32[]{:S(2)}) collective-permute-start(bf16[256,512]{1,0:T(8,128)(2,1)S(1)} %collective-permute-done.refs_8_.refs_23_), channel_id=1, source_target_pairs={{0,4},{1,5},{2,6},{3,7},{4,0},{5,1},{6,2},{7,3},{8,12},{9,13},{10,... | collective-permute-start | bytes 786440 | tf_op jit(solution)/shard_map/ppermute | solution.py:1009
  24.1 8.2 %collective-permute-start.6 = (bf16[512,256]{1,0:T(8,128)(2,1)}, bf16[512,256]{1,0:T(8,128)(2,1)S(1)}, u32[]{:S(2)}, u32[]{:S(2)}) collective-permute-start(bf16[512,256]{1,0:T(8,128)(2,1)} %get-tuple-element.180), channel_id=1, source_target_pairs={{0,2},{1,3},{2,0},{3,1},{4,6},{5,7},{6,4},{7,5},{8,10},{9,11},{10,... | collective-permute-start | bytes 786440 | tf_op jit(solution)/shard_map/ppermute | solution.py:1009
  24.8 4.3 %collective-permute-start.5 = (bf16[4,16,512]{2,1,0:T(8,128)(2,1)S(1)}, bf16[4,16,512]{2,1,0:T(8,128)(2,1)S(1)}, u32[]{:S(2)}, u32[]{:S(2)}) collective-permute-start(bf16[4,16,512]{2,1,0:T(8,128)(2,1)S(1)} %get-tuple-element.177), channel_id=1, source_target_pairs={{0,8},{1,9},{2,10},{3,11},{4,12},{5,13},{6,14},{7,15},{8,0},{9,1},... | collective-permute-start | bytes 196616 | tf_op jit(solution)/shard_map/ppermute | solution.py:1009
  29.1 11.2 %copy-start.18 = (f32[128]{0:T(128)S(1)}, f32[128]{0:T(128)}, u32[]{:S(2)}) copy-start(f32[128]{0:T(128)} %param.31) | copy-start | bytes 1540
  32.3 7.3 %collective-permute-start.10 = (bf16[256,512]{1,0:T(8,128)(2,1)}, bf16[256,512]{1,0:T(8,128)(2,1)S(1)}, u32[]{:S(2)}, u32[]{:S(2)}) collective-permute-start(bf16[256,512]{1,0:T(8,128)(2,1)} %get-tuple-element.187), channel_id=1, source_target_pairs={{0,2},{1,3},{2,0},{3,1},{4,6},{5,7},{6,4},{7,5},{8,10},{9,11},{10,... | collective-permute-start | bytes 786440 | tf_op jit(solution)/shard_map/ppermute | solution.py:1009
  33.1 7.1 %collective-permute-start.11 = (bf16[4,16,512]{2,1,0:T(8,128)(2,1)S(1)}, bf16[4,16,512]{2,1,0:T(8,128)(2,1)S(1)}, u32[]{:S(2)}, u32[]{:S(2)}) collective-permute-start(bf16[4,16,512]{2,1,0:T(8,128)(2,1)S(1)} %get-tuple-element.186), channel_id=1, source_target_pairs={{0,16},{1,17},{2,18},{3,19},{4,20},{5,21},{6,22},{7,23},{8,24},{9,... | collective-permute-start | bytes 196616 | tf_op jit(solution)/shard_map/ppermute | solution.py:1009
  35.7 8.3 %collective-permute-start.13 = (bf16[512,256]{1,0:T(8,128)(2,1)S(1)}, bf16[512,256]{1,0:T(8,128)(2,1)S(1)}, u32[]{:S(2)}, u32[]{:S(2)}) collective-permute-start(bf16[512,256]{1,0:T(8,128)(2,1)S(1)} %collective-permute-done.6.refs_10_.refs_25_), channel_id=1, source_target_pairs={{0,8},{1,9},{2,10},{3,11},{4,12},{5,13},{6,14},{7,15},{8,0},{9,1},... | collective-permute-start | bytes 786440 | tf_op jit(solution)/shard_map/ppermute | solution.py:1009
  37.2 7.3 %collective-permute-start.14 = (bf16[256,512]{1,0:T(8,128)(2,1)S(1)}, bf16[256,512]{1,0:T(8,128)(2,1)S(1)}, u32[]{:S(2)}, u32[]{:S(2)}) collective-permute-start(bf16[256,512]{1,0:T(8,128)(2,1)S(1)} %collective-permute-done.refs_8_.refs_23_), channel_id=1, source_target_pairs={{0,1},{1,0},{2,3},{3,2},{4,5},{5,4},{6,7},{7,6},{8,9},{9,8},{10,11... | collective-permute-start | bytes 786440 | tf_op jit(solution)/shard_map/ppermute | solution.py:1009
  37.2 7.4 %collective-permute-start.16 = (bf16[512,256]{1,0:T(8,128)(2,1)S(1)}, bf16[512,256]{1,0:T(8,128)(2,1)S(1)}, u32[]{:S(2)}, u32[]{:S(2)}) collective-permute-start(bf16[512,256]{1,0:T(8,128)(2,1)S(1)} %collective-permute-done.6.refs_10_.refs_25_), channel_id=1, source_target_pairs={{0,1},{1,0},{2,3},{3,2},{4,5},{5,4},{6,7},{7,6},{8,9},{9,8},{10,11... | collective-permute-start | bytes 786440 | tf_op jit(solution)/shard_map/ppermute | solution.py:1009
  39.7 6.4 %collective-permute-start.12 = (bf16[256,512]{1,0:T(8,128)(2,1)S(1)}, bf16[256,512]{1,0:T(8,128)(2,1)S(1)}, u32[]{:S(2)}, u32[]{:S(2)}) collective-permute-start(bf16[256,512]{1,0:T(8,128)(2,1)S(1)} %collective-permute-done.10.refs_8_), channel_id=1, source_target_pairs={{0,4},{1,5},{2,6},{3,7},{4,0},{5,1},{6,2},{7,3},{8,12},{9,13},{10,... | collective-permute-start | bytes 786440 | tf_op jit(solution)/shard_map/ppermute | solution.py:1009
  40.2 9.5 %collective-permute-start.18 = (bf16[512,512]{1,0:T(8,128)(2,1)}, bf16[512,512]{1,0:T(8,128)(2,1)S(1)}, u32[]{:S(2)}, u32[]{:S(2)}) collective-permute-start(bf16[512,512]{1,0:T(8,128)(2,1)} %get-tuple-element.201.refs_6_), channel_id=1, source_target_pairs={{0,1},{1,0},{2,3},{3,2},{4,5},{5,4},{6,7},{7,6},{8,9},{9,8},{10,11... | collective-permute-start | bytes 1572872 | tf_op jit(solution)/shard_map/ppermute | solution.py:1009
  40.2 0.7 copy-start.13
  40.2 0.7 copy-start.15
  40.2 0.7 copy-start.17
  40.9 5.2 %copy-start.1 = (bf16[2,128,512]{2,1,0:T(8,128)(2,1)S(1)}, bf16[2,128,512]{2,1,0:T(8,128)(2,1)}, u32[]{:S(2)}) copy-start(bf16[2,128,512]{2,1,0:T(8,128)(2,1)} %refs_0_.7) | copy-start | bytes 786436
  40.9 5.2 %copy-start.4 = (bf16[512,512]{1,0:T(8,128)(2,1)S(1)}, bf16[512,512]{1,0:T(8,128)(2,1)}, u32[]{:S(2)}) copy-start(bf16[512,512]{1,0:T(8,128)(2,1)} %get-tuple-element.183.refs_4_.refs_19_) | copy-start | bytes 1572868
  40.9 5.2 %copy-start.5 = (bf16[512,512]{1,0:T(8,128)(2,1)S(1)}, bf16[512,512]{1,0:T(8,128)(2,1)}, u32[]{:S(2)}) copy-start(bf16[512,512]{1,0:T(8,128)(2,1)} %get-tuple-element.185.refs_5_.refs_20_) | copy-start | bytes 1572868
  44.0 2.1 %collective-permute-start.15 = (bf16[256,512]{1,0:T(8,128)(2,1)S(1)}, bf16[256,512]{1,0:T(8,128)(2,1)S(1)}, u32[]{:S(2)}, u32[]{:S(2)}) collective-permute-start(bf16[256,512]{1,0:T(8,128)(2,1)S(1)} %collective-permute-done.7.refs_9_.refs_24_), channel_id=1, source_target_pairs={{0,1},{1,0},{2,3},{3,2},{4,5},{5,4},{6,7},{7,6},{8,9},{9,8},{10,11... | collective-permute-start | bytes 786440 | tf_op jit(solution)/shard_map/ppermute | solution.py:1009
  44.5 1.5 %collective-permute-start.17 = (bf16[512,256]{1,0:T(8,128)(2,1)S(1)}, bf16[512,256]{1,0:T(8,128)(2,1)S(1)}, u32[]{:S(2)}, u32[]{:S(2)}) collective-permute-start(bf16[512,256]{1,0:T(8,128)(2,1)S(1)} %collective-permute-done.13.refs_11_.refs_26_), channel_id=1, source_target_pairs={{0,1},{1,0},{2,3},{3,2},{4,5},{5,4},{6,7},{7,6},{8,9},{9,8},{10,11... | collective-permute-start | bytes 786440 | tf_op jit(solution)/shard_map/ppermute | solution.py:1009
  44.6 5.1 %collective-permute-start.19 = (bf16[256,512]{1,0:T(8,128)(2,1)S(1)}, bf16[256,512]{1,0:T(8,128)(2,1)S(1)}, u32[]{:S(2)}, u32[]{:S(2)}) collective-permute-start(bf16[256,512]{1,0:T(8,128)(2,1)S(1)} %collective-permute-done.10.refs_8_), channel_id=1, source_target_pairs={{0,1},{1,0},{2,3},{3,2},{4,5},{5,4},{6,7},{7,6},{8,9},{9,8},{10,11... | collective-permute-start | bytes 786440 | tf_op jit(solution)/shard_map/ppermute | solution.py:1009
  46.0 3.7 %collective-permute-start.20 = (bf16[256,512]{1,0:T(8,128)(2,1)S(1)}, bf16[256,512]{1,0:T(8,128)(2,1)S(1)}, u32[]{:S(2)}, u32[]{:S(2)}) collective-permute-start(bf16[256,512]{1,0:T(8,128)(2,1)S(1)} %collective-permute-done.12.refs_9_), channel_id=1, source_target_pairs={{0,1},{1,0},{2,3},{3,2},{4,5},{5,4},{6,7},{7,6},{8,9},{9,8},{10,11... | collective-permute-start | bytes 786440 | tf_op jit(solution)/shard_map/ppermute | solution.py:1009
  46.0 3.7 %copy-start.7 = (bf16[512,512]{1,0:T(8,128)(2,1)S(1)}, bf16[512,512]{1,0:T(8,128)(2,1)}, u32[]{:S(2)}) copy-start(bf16[512,512]{1,0:T(8,128)(2,1)} %get-tuple-element.201.refs_6_) | copy-start | bytes 1572868
  46.0 3.7 %copy-start.8 = (bf16[2,128,512]{2,1,0:T(8,128)(2,1)S(1)}, bf16[2,128,512]{2,1,0:T(8,128)(2,1)}, u32[]{:S(2)}) copy-start(bf16[2,128,512]{2,1,0:T(8,128)(2,1)} %refs_1_.1) | copy-start | bytes 786436
  49.7 0.7 copy-start.14
  55.6 2.9 %collective-permute-start.22 = (bf16[2,512,512]{2,1,0:T(8,128)(2,1)S(1)}, bf16[2,512,512]{2,1,0:T(8,128)(2,1)S(1)}, u32[]{:S(2)}, u32[]{:S(2)}) collective-permute-start(bf16[2,512,512]{2,1,0:T(8,128)(2,1)S(1)} %get-tuple-element.214), channel_id=1, source_target_pairs={{0,1},{1,0},{2,3},{3,2},{4,5},{5,4},{6,7},{7,6},{8,9},{9,8},{10,11... | collective-permute-start | bytes 3145736 | tf_op jit(solution)/shard_map/ppermute | solution.py:1009
  57.3 2.8 %collective-permute-start.21 = (bf16[2,512,512]{2,1,0:T(8,128)(2,1)S(1)}, bf16[2,512,512]{2,1,0:T(8,128)(2,1)S(1)}, u32[]{:S(2)}, u32[]{:S(2)}) collective-permute-start(bf16[2,512,512]{2,1,0:T(8,128)(2,1)S(1)} %get-tuple-element.212), channel_id=1, source_target_pairs={{0,1},{1,0},{2,3},{3,2},{4,5},{5,4},{6,7},{7,6},{8,9},{9,8},{10,11... | collective-permute-start | bytes 3145736 | tf_op jit(solution)/shard_map/ppermute | solution.py:1009
  58.8 14.3 %collective-permute-start.23 = (bf16[1,512,512]{2,1,0:T(8,128)(2,1)S(1)}, bf16[1,512,512]{2,1,0:T(8,128)(2,1)S(1)}, u32[]{:S(2)}, u32[]{:S(2)}) collective-permute-start(bf16[1,512,512]{2,1,0:T(8,128)(2,1)S(1)} %get-tuple-element.230), channel_id=1, source_target_pairs={{0,2},{1,3},{2,0},{3,1},{4,6},{5,7},{6,4},{7,5},{8,10},{9,11},{10,... | collective-permute-start | bytes 1572872 | tf_op jit(solution)/shard_map/ppermute | solution.py:1009
  60.4 14.1 %collective-permute-start.24 = (bf16[2,256,512]{2,1,0:T(8,128)(2,1)S(1)}, bf16[2,256,512]{2,1,0:T(8,128)(2,1)S(1)}, u32[]{:S(2)}, u32[]{:S(2)}) collective-permute-start(bf16[2,256,512]{2,1,0:T(8,128)(2,1)S(1)} %get-tuple-element.233), channel_id=1, source_target_pairs={{0,4},{1,5},{2,6},{3,7},{4,0},{5,1},{6,2},{7,3},{8,12},{9,13},{10,... | collective-permute-start | bytes 1572872 | tf_op jit(solution)/shard_map/ppermute | solution.py:1009
  74.9 5.4 %collective-permute-start.27 = (bf16[2,512,512]{2,1,0:T(8,128)(2,1)S(1)}, bf16[2,512,512]{2,1,0:T(8,128)(2,1)S(1)}, u32[]{:S(2)}, u32[]{:S(2)}) collective-permute-start(bf16[2,512,512]{2,1,0:T(8,128)(2,1)S(1)} %get-tuple-element.244), channel_id=1, source_target_pairs={{0,1},{1,0},{2,3},{3,2},{4,5},{5,4},{6,7},{7,6},{8,9},{9,8},{10,11... | collective-permute-start | bytes 3145736 | tf_op jit(solution)/shard_map/ppermute | solution.py:1009
  75.0 3.9 %collective-permute-start.26 = (f32[96,512]{1,0:T(8,128)S(1)}, f32[96,512]{1,0:T(8,128)S(1)}, u32[]{:S(2)}, u32[]{:S(2)}) collective-permute-start(f32[96,512]{1,0:T(8,128)S(1)} %get-tuple-element.239), channel_id=1, source_target_pairs={{0,1},{1,0},{2,3},{3,2},{4,5},{5,4},{6,7},{7,6},{8,9},{9,8},{10,11... | collective-permute-start | bytes 589832 | tf_op jit(solution)/shard_map/ppermute | solution.py:1009
  75.5 13.1 %collective-permute-start.29 = (bf16[1,256,512]{2,1,0:T(8,128)(2,1)S(1)}, bf16[1,256,512]{2,1,0:T(8,128)(2,1)S(1)}, u32[]{:S(2)}, u32[]{:S(2)}) collective-permute-start(bf16[1,256,512]{2,1,0:T(8,128)(2,1)S(1)} %get-tuple-element.251), channel_id=1, source_target_pairs={{0,4},{1,5},{2,6},{3,7},{4,0},{5,1},{6,2},{7,3},{8,12},{9,13},{10,... | collective-permute-start | bytes 786440 | tf_op jit(solution)/shard_map/ppermute | solution.py:1009
  76.9 11.7 %collective-permute-start.30 = (bf16[1,256,512]{2,1,0:T(8,128)(2,1)S(1)}, bf16[1,256,512]{2,1,0:T(8,128)(2,1)S(1)}, u32[]{:S(2)}, u32[]{:S(2)}) collective-permute-start(bf16[1,256,512]{2,1,0:T(8,128)(2,1)S(1)} %get-tuple-element.252), channel_id=1, source_target_pairs={{0,2},{1,3},{2,0},{3,1},{4,6},{5,7},{6,4},{7,5},{8,10},{9,11},{10,... | collective-permute-start | bytes 786440 | tf_op jit(solution)/shard_map/ppermute | solution.py:1009
  77.6 1.3 collective-permute-start.25
  78.9 7.7 %collective-permute-start.28 = (bf16[80,512]{1,0:T(8,128)(2,1)S(1)}, bf16[80,512]{1,0:T(8,128)(2,1)S(1)}, u32[]{:S(2)}, u32[]{:S(2)}) collective-permute-start(bf16[80,512]{1,0:T(8,128)(2,1)S(1)} %get-tuple-element.242.refs_3_), channel_id=1, source_target_pairs={{0,2},{1,3},{2,0},{3,1},{4,6},{5,7},{6,4},{7,5},{8,10},{9,11},{10,... | collective-permute-start | bytes 245768 | tf_op jit(solution)/shard_map/ppermute | solution.py:1009
  86.7 7.2 %collective-permute-start.31 = (bf16[1,512,256]{2,1,0:T(8,128)(2,1)S(1)}, bf16[1,512,256]{2,1,0:T(8,128)(2,1)S(1)}, u32[]{:S(2)}, u32[]{:S(2)}) collective-permute-start(bf16[1,512,256]{2,1,0:T(8,128)(2,1)S(1)} %get-tuple-element.255), channel_id=1, source_target_pairs={{0,2},{1,3},{2,0},{3,1},{4,6},{5,7},{6,4},{7,5},{8,10},{9,11},{10,... | collective-permute-start | bytes 786440 | tf_op jit(solution)/shard_map/ppermute | solution.py:1009
  87.5 6.8 %collective-permute-start.32 = (bf16[2,256,256]{2,1,0:T(8,128)(2,1)S(1)}, bf16[2,256,256]{2,1,0:T(8,128)(2,1)S(1)}, u32[]{:S(2)}, u32[]{:S(2)}) collective-permute-start(bf16[2,256,256]{2,1,0:T(8,128)(2,1)S(1)} %get-tuple-element.257), channel_id=1, source_target_pairs={{0,4},{1,5},{2,6},{3,7},{4,0},{5,1},{6,2},{7,3},{8,12},{9,13},{10,... | collective-permute-start | bytes 786440 | tf_op jit(solution)/shard_map/ppermute | solution.py:1009
  88.8 6.6 %collective-permute-start.33 = (bf16[2,128,512]{2,1,0:T(8,128)(2,1)S(1)}, bf16[2,128,512]{2,1,0:T(8,128)(2,1)S(1)}, u32[]{:S(2)}, u32[]{:S(2)}) collective-permute-start(bf16[2,128,512]{2,1,0:T(8,128)(2,1)S(1)} %get-tuple-element.260), channel_id=1, source_target_pairs={{0,8},{1,9},{2,10},{3,11},{4,12},{5,13},{6,14},{7,15},{8,0},{9,1},... | collective-permute-start | bytes 786440 | tf_op jit(solution)/shard_map/ppermute | solution.py:1009
  95.5 12.3 %collective-permute-start.37 = (bf16[2,128,512]{2,1,0:T(8,128)(2,1)S(1)}, bf16[2,128,512]{2,1,0:T(8,128)(2,1)S(1)}, u32[]{:S(2)}, u32[]{:S(2)}) collective-permute-start(bf16[2,128,512]{2,1,0:T(8,128)(2,1)S(1)} %fold.16.refs_0_), channel_id=1, source_target_pairs={{0,16},{1,17},{2,18},{3,19},{4,20},{5,21},{6,22},{7,23},{8,24},{9,... | collective-permute-start | bytes 786440 | tf_op jit(solution)/shard_map/ppermute | solution.py:1009
  97.7 7.2 %collective-permute-start.35 = (bf16[1,256,256]{2,1,0:T(8,128)(2,1)S(1)}, bf16[1,256,256]{2,1,0:T(8,128)(2,1)S(1)}, u32[]{:S(2)}, u32[]{:S(2)}) collective-permute-start(bf16[1,256,256]{2,1,0:T(8,128)(2,1)S(1)} %get-tuple-element.263), channel_id=1, source_target_pairs={{0,4},{1,5},{2,6},{3,7},{4,0},{5,1},{6,2},{7,3},{8,12},{9,13},{10,... | collective-permute-start | bytes 393224 | tf_op jit(solution)/shard_map/ppermute | solution.py:1009
  99.1 5.8 %collective-permute-start.36 = (bf16[1,256,256]{2,1,0:T(8,128)(2,1)S(1)}, bf16[1,256,256]{2,1,0:T(8,128)(2,1)S(1)}, u32[]{:S(2)}, u32[]{:S(2)}) collective-permute-start(bf16[1,256,256]{2,1,0:T(8,128)(2,1)S(1)} %get-tuple-element.265), channel_id=1, source_target_pairs={{0,2},{1,3},{2,0},{3,1},{4,6},{5,7},{6,4},{7,5},{8,10},{9,11},{10,... | collective-permute-start | bytes 393224 | tf_op jit(solution)/shard_map/ppermute | solution.py:1009
  100.4 4.4 %collective-permute-start.34 = (bf16[80,512]{1,0:T(8,128)(2,1)S(1)}, bf16[80,512]{1,0:T(8,128)(2,1)S(1)}, u32[]{:S(2)}, u32[]{:S(2)}) collective-permute-start(bf16[80,512]{1,0:T(8,128)(2,1)S(1)} %get-tuple-element.249.refs_3_), channel_id=1, source_target_pairs={{0,4},{1,5},{2,6},{3,7},{4,0},{5,1},{6,2},{7,3},{8,12},{9,13},{10,... | collective-permute-start | bytes 245768 | tf_op jit(solution)/shard_map/ppermute | solution.py:1009
  105.0 8.3 %collective-permute-start.38 = (bf16[208,512]{1,0:T(8,128)(2,1)S(1)}, bf16[208,512]{1,0:T(8,128)(2,1)S(1)}, u32[]{:S(2)}, u32[]{:S(2)}) collective-permute-start(bf16[208,512]{1,0:T(8,128)(2,1)S(1)} %get-tuple-element.267.refs_3_), channel_id=1, source_target_pairs={{0,8},{1,9},{2,10},{3,11},{4,12},{5,13},{6,14},{7,15},{8,0},{9,1},... | collective-permute-start | bytes 638984 | tf_op jit(solution)/shard_map/ppermute | solution.py:1009
  107.9 11.9 %collective-permute-start.39 = (bf16[2,128,512]{2,1,0:T(8,128)(2,1)S(1)}, bf16[2,128,512]{2,1,0:T(8,128)(2,1)S(1)}, u32[]{:S(2)}, u32[]{:S(2)}) collective-permute-start(bf16[2,128,512]{2,1,0:T(8,128)(2,1)S(1)} %fold.17.refs_0_), channel_id=1, source_target_pairs={{0,8},{1,9},{2,10},{3,11},{4,12},{5,13},{6,14},{7,15},{8,0},{9,1},... | collective-permute-start | bytes 786440 | tf_op jit(solution)/shard_map/ppermute | solution.py:1009
  113.3 10.4 %collective-permute-start.40 = (bf16[208,512]{1,0:T(8,128)(2,1)S(1)}, bf16[208,512]{1,0:T(8,128)(2,1)S(1)}, u32[]{:S(2)}, u32[]{:S(2)}) collective-permute-start(bf16[208,512]{1,0:T(8,128)(2,1)S(1)} %get-tuple-element.273.refs_3_), channel_id=1, source_target_pairs={{0,16},{1,17},{2,18},{3,19},{4,20},{5,21},{6,22},{7,23},{8,24},{9,... | collective-permute-start | bytes 638984 | tf_op jit(solution)/shard_map/ppermute | solution.py:1009
  119.9 14.9 %collective-permute-start.44 = (bf16[2,256,512]{2,1,0:T(8,128)(2,1)S(1)}, bf16[2,256,512]{2,1,0:T(8,128)(2,1)S(1)}, u32[]{:S(2)}, u32[]{:S(2)}) collective-permute-start(bf16[2,256,512]{2,1,0:T(8,128)(2,1)S(1)} %join.2.refs_0_), channel_id=1, source_target_pairs={{0,4},{1,5},{2,6},{3,7},{4,0},{5,1},{6,2},{7,3},{8,12},{9,13},{10,... | collective-permute-start | bytes 1572872 | tf_op jit(solution)/shard_map/ppermute | solution.py:1009
  123.8 0.8 copy-start.12
  123.8 5.0 %collective-permute-start.41 = (bf16[1,128,512]{2,1,0:T(8,128)(2,1)S(1)}, bf16[1,128,512]{2,1,0:T(8,128)(2,1)S(1)}, u32[]{:S(2)}, u32[]{:S(2)}) collective-permute-start(bf16[1,128,512]{2,1,0:T(8,128)(2,1)S(1)} %bitcast.29), channel_id=1, source_target_pairs={{0,8},{1,9},{2,10},{3,11},{4,12},{5,13},{6,14},{7,15},{8,0},{9,1},... | collective-permute-start | bytes 393224 | tf_op jit(solution)/shard_map/ppermute | solution.py:1009
  123.9 5.8 %collective-permute-start.42 = (f32[48,512]{1,0:T(8,128)S(1)}, f32[48,512]{1,0:T(8,128)S(1)}, u32[]{:S(2)}, u32[]{:S(2)}) collective-permute-start(f32[48,512]{1,0:T(8,128)S(1)} %get-tuple-element.284.refs_0_), channel_id=1, source_target_pairs={{0,2},{1,3},{2,0},{3,1},{4,6},{5,7},{6,4},{7,5},{8,10},{9,11},{10,... | collective-permute-start | bytes 294920 | tf_op jit(solution)/shard_map/ppermute | solution.py:1009
  128.8 2.3 %copy-start.10 = (f32[512,16]{0,1:T(8,128)S(1)}, f32[512,16]{0,1:T(8,128)}, u32[]{:S(2)}) copy-start(f32[512,16]{0,1:T(8,128)} %param.24) | copy-start | bytes 98308
  128.9 2.3 %copy-start.11 = (f32[512,16]{0,1:T(8,128)S(1)}, f32[512,16]{0,1:T(8,128)}, u32[]{:S(2)}) copy-start(f32[512,16]{0,1:T(8,128)} %param.25) | copy-start | bytes 98308
  128.9 9.4 %collective-permute-start.45 = (bf16[1,256,512]{2,1,0:T(8,128)(2,1)S(1)}, bf16[1,256,512]{2,1,0:T(8,128)(2,1)S(1)}, u32[]{:S(2)}, u32[]{:S(2)}) collective-permute-start(bf16[1,256,512]{2,1,0:T(8,128)(2,1)S(1)} %join.3.refs_0_), channel_id=1, source_target_pairs={{0,4},{1,5},{2,6},{3,7},{4,0},{5,1},{6,2},{7,3},{8,12},{9,13},{10,... | collective-permute-start | bytes 786440 | tf_op jit(solution)/shard_map/ppermute | solution.py:1009
  129.6 1.5 %collective-permute-start.43 = (f32[96,512]{1,0:T(8,128)S(1)}, f32[96,512]{1,0:T(8,128)S(1)}, u32[]{:S(2)}, u32[]{:S(2)}) collective-permute-start(f32[96,512]{1,0:T(8,128)S(1)} %pair.1.refs_4_), channel_id=1, source_target_pairs={{0,1},{1,0},{2,3},{3,2},{4,5},{5,4},{6,7},{7,6},{8,9},{9,8},{10,11... | collective-permute-start | bytes 589832 | tf_op jit(solution)/shard_map/ppermute | solution.py:1009
  (1 other events, 0.7 us)

commit v4 on v3

--- a/solution.py
+++ b/solution.py
@@ -128,6 +128,19 @@
 
 def shape(dims, dtype=F32):
     return jax.ShapeDtypeStruct(dims, dtype)
+
+
+def put_low(low, pairs):
+    for i in range(0, len(pairs), 2):
+        high = pairs[i].astype(BF16)
+        low[3 * i // 2] = high
+        low[3 * i // 2 + 1] = (pairs[i] - high.astype(F32)).astype(BF16)
+        low[3 * i // 2 + 2] = pairs[i + 1].astype(BF16)
+
+
+def get_low(low, s):
+    high, rest, slope = (low[3 * s + i].astype(F32) for i in range(3))
+    return high + rest, slope
 
 
 def enter_kernel(seqs, *refs):
@@ -193,8 +206,8 @@
         return carry
 
     lax.fori_loop(0, seqs * BLOCKS, body, 0)
-    low[...] = ends[: 2 * seqs].astype(BF16)
     ends[2 * seqs] = par[1]
+    put_low(low, [ends[i] for i in range(2 * seqs)])
 
 
 def first_half_kernel(w_value, w_reset, h1, sems):
@@ -309,8 +322,8 @@
             end = jnp.left_shift(jnp.bitwise_xor(jnp.right_shift(place, shift), k) + 1, shift)
             off = (place - end).astype(F32) * float(CH)
             power = jnp.where(place >= end, jnp.exp(jnp.maximum(off, 0.0) * logd), 0.0)
-            oa = got[2 * s].astype(F32) * power
-            b = b + got[2 * s + 1].astype(F32) * power + off * oa * dinv
+            oa, ob = (part * power for part in get_low(got, s))
+            b = b + ob + off * oa * dinv
             a = a + oa
         st_in[0, s] = a
         st_in[1, s] = b
@@ -772,13 +785,13 @@
         after = (count - 1 - jnp.bitwise_xor(mine, k)).astype(F32) * float(CH << shift)
         power = jnp.exp(after * logd)
         slope = after * jnp.exp((after - 1.0) * logd)
-        for i in range(0, 2 * seqs, 2):
-            part = (state if k == 0 else others[k - 1])[i : i + 2].astype(F32)
+        for s in range(seqs):
+            part = get_low(others[k - 1], s) if k else (state[2 * s], state[2 * s + 1])
             a, b = power * part[0], power * part[1] + slope * part[0]
-            sums[i : i + 2] = [a, b] if k == 0 else [sums[i] + a, sums[i + 1] + b]
+            sums[2 * s : 2 * s + 2] = [sums[2 * s] + a, sums[2 * s + 1] + b] if k else [a, b]
     for i in range(2 * seqs):
         total[i] = sums[i]
-        low[i] = sums[i].astype(BF16)
+    put_low(low, sums)
 
 
 def put_wide(ref, top, value):
@@ -1118,7 +1131,7 @@
             shape((4, NDIM, D)),
             shape((2, seqs, NDIM, PIECES, D)),
             shape((2 * seqs + 1, NDIM, D)),
-            shape((2 * seqs, NDIM, D), BF16),
+            shape((3 * seqs, NDIM, D), BF16),
         ),
         [
             pltpu.VMEM((seqs, CH, D), BF16),
@@ -1133,7 +1146,7 @@
         (tok, gain1, rate, beta, ema_eta.T),
         [ANY] * 5,
         "enter",
-        limit=58.96,
+        limit=12,
     )
     start = 1 - int(traded)
     groups = [(0, 1)] * start + [(start, 2)] + [(i, 1) for i in range(start + 2, levels)]
@@ -1149,9 +1162,10 @@
         outs=(pl.BlockSpec(),),
     )
     mine1 = swap(half1, top)
-    state, low = ends, after(low, mine1)
+    state = ends
     for i, (shift, bits) in enumerate(groups):
         if i == start:
+            low = after(low, mine1)
             pack1, pack2, pack3, half2, half3 = call(
                 pack_kernel,
                 (
@@ -1184,7 +1198,7 @@
         if i + 1 < len(groups):
             state, low = call(
                 functools.partial(hop_kernel, seqs, shift, 1 << bits),
-                (shape((2 * seqs + 1, NDIM, D)), shape((2 * seqs, NDIM, D), BF16)),
+                (shape((2 * seqs + 1, NDIM, D)), shape((3 * seqs, NDIM, D), BF16)),
                 [],
                 (ids, state, *got),
                 [SMEM] + [VMEM] * (1 + len(got)),
@@ -1376,32 +1390,21 @@
     done = {}
 
     def first_chunks():
-        high = D // yn >> 1
-        keep, send = fold(
-            ids,
-            [(2, high, wide)] * 2,
-            [
-                ([now(g3[0])] + g3[1:], 0, wide, zcuts[0], [(0, 0, 0), (1, 0, 0)]),
-                (g2, 0, wide, zcuts[0], [(0, 1, 0), (1, 1, 0)]),
-            ],
-        )
-        for i, cut in enumerate(zcuts[1:-1]):
-            other = over_z(send, zcuts[i])
+        high = D // yn
+        for i, cut in enumerate(zcuts[:-1] + [None]):
+            high = high // 2 if cut else high
+            pieces = 2 if cut else 1
+            if i:
+                jobs = [([now(keep), other], 0, wide, cut, [(k, 0, 0) for k in range(pieces)])]
+            else:
+                jobs = [
+                    ([now(g3[0])] + g3[1:], 0, wide, cut, [(k, 0, 0) for k in range(pieces)]),
+                    (g2, 0, wide, cut, [(k, 1, 0) for k in range(pieces)]),
+                ]
+            keep, *send = fold(ids, [(2, high, wide)] * pieces, jobs)
+            other = over_z(*send, cut) if cut else over_z(keep, zcuts[-1])
             yield keep
-            high //= 2
-            keep, send = fold(
-                ids,
-                [(2, high, wide)] * 2,
-                [([now(keep), other], 0, wide, cut, [(0, 0, 0), (1, 0, 0)])],
-            )
-        other = over_z(send, zcuts[-2])
-        yield keep
-        total = keep
-        for cut in zcuts[-1:] + [None]:
-            (total,) = fold(ids, [keep.shape], [([now(total), other], 0, wide, None, [(0, 0, 0)])])
-            if cut:
-                other = over_z(total, cut)
-                yield total
+        (total,) = fold(ids, [keep.shape], [([now(keep), other], 0, wide, None, [(0, 0, 0)])])
         for cut in reversed(zcuts[:-1]):
             other = over_z(total, cut)
             yield total
@@ -1529,7 +1532,7 @@
         bits = list(reversed(bits_of(tp)))
         total = total[None]
         far = swap(kept, bits[0])
-        other = over_z(total, zcuts[-2])
+        other = over_z(total, zcuts[-2]) if len(zcuts) > 1 else None
         yield total
         (done["tokens"],) = call(
             functools.partial(leave_kernel, seqs, [at for _, at in got]),

time: 140 us -> 137 us (0.979)
  Pallas kernels: 41.2 us -> 38.9 us
    pallas_call x32, Pallas kernels: 41.2 us -> 38.9 us  [call(): pl.pallas_call(body, out_shape=out, in_specs=specs, out_specs=outs or jax...]
  transfers between devices with their start and end apart: 46 -> 46, of which waited for: 26 -> 26; matrix products, arithmetic and copies ran while one was open for 0% -> 0% of each run, Pallas kernels for 23% -> 22%
where the time goes in v4:
time: 137 us
  waiting for transfers between devices  57.3 us (42%)
  Pallas kernels  38.9 us (28%)
  starting transfers between devices  37.6 us (27%)
  local copies, waits for them, and re-layouts  2.02 us (1%)
    ppermute x46, waiting for transfers between devices, swap(): return lax.ppermute(value, BOTH, [(i, i ^ mask) for i in range(count)])  57.3 us
    pallas_call x32, Pallas kernels, call(): pl.pallas_call(body, out_shape=out, in_specs=specs, out_specs=outs or jax...  38.9 us
    ppermute x46, starting transfers between devices, swap(): return lax.ppermute(value, BOTH, [(i, i ^ mask) for i in range(count)])  37.6 us
  transfers between devices with their start and end apart: 46, of which 26 were waited for; matrix products, arithmetic and copies ran while one was open for 0% of the time, Pallas kernels for 22%

profile of v4, /device:TPU:0, one launch (start us, length us, event | category | flops | bytes accessed | tf_op | source)
XLA Modules:
  0.0 136.9 jit_solution(16873830986212030314)
XLA Ops:
  0.7 1.7 %half.1 = bf16[256,512]{1,0:T(8,128)(2,1)} custom-call(bf16[512,256]{1,0:T(8,128)(2,1)} %w_value.2, bf16[512,256]{1,0:T(8,128)(2,1)} %w_reset.2), custom_call_target="tpu_custom_call" | custom-call | tf_op jit(solution)/shard_map/half/pallas_call | solution.py:118
  2.4 3.0 %collective-permute-start.1 = (bf16[256,512]{1,0:T(8,128)(2,1)}, bf16[256,512]{1,0:T(8,128)(2,1)S(1)}, u32[]{:S(2)}, u32[]{:S(2)}) collective-permute-start(bf16[256,512]{1,0:T(8,128)(2,1)} %half.1), channel_id=1, source_target_pairs={{0,2},{1,3},{2,0},{3,1},{4,6},{5,7},{6,4},{7,5},{8,10},{9,11},{10,... | collective-permute-start | bytes 786440 | tf_op jit(solution)/shard_map/ppermute | solution.py:1022
  5.5 0.7 copy-done.9
  6.1 2.4 %enter.1 = (bf16[256,512]{1,0:T(8,128)(2,1)S(1)}, f32[4,16,512]{2,1,0:T(8,128)S(1)}, f32[2,2,16,8,512]{4,3,2,1,0:T(8,128)S(1)}, f32[5,16,512]{2,1,0:T(8,128)S(1)}, bf16[6,16,512]{2,1,0:T(8,128)(2,1)S(1)}) custom-call(bf16[2,128,512]{2,1,0:T(8,128)(2,1)S(1)} %copy-done, f32[1,512]{1,0:T(1,128)S(1)} %bitcast.38, f32[16,512]{1,0:T(8,128)S(1)} %bitcast.31, ...), custom_call_target="tpu_custom_call" | custom-call | tf_op jit(solution)/shard_map/enter/pallas_call | solution.py:118
  8.6 1.3 collective-permute-done.refs_1_.refs_8_
  10.0 2.0 %collective-permute-done.1.refs_8_.refs_23_ = bf16[256,512]{1,0:T(8,128)(2,1)S(1)} collective-permute-done((bf16[256,512]{1,0:T(8,128)(2,1)}, bf16[256,512]{1,0:T(8,128)(2,1)S(1)}, u32[]{:S(2)}, u32[]{:S(2)}) %collective-permute-start.1) | collective-permute-done | bytes 262176 | tf_op jit(solution)/shard_map/ppermute | solution.py:1022
  12.0 2.7 %collective-permute-start.4 = (bf16[6,16,512]{2,1,0:T(8,128)(2,1)S(1)}, bf16[6,16,512]{2,1,0:T(8,128)(2,1)S(1)}, u32[]{:S(2)}, u32[]{:S(2)}) collective-permute-start(bf16[6,16,512]{2,1,0:T(8,128)(2,1)S(1)} %get-tuple-element.166), channel_id=1, source_target_pairs={{0,6},{1,7},{2,4},{3,5},{4,2},{5,3},{6,0},{7,1},{8,14},{9,15},{10,... | collective-permute-start | bytes 294920 | tf_op jit(solution)/shard_map/ppermute | solution.py:1022
  15.4 2.9 %pack.1 = (bf16[512,512]{1,0:T(8,128)(2,1)}, bf16[512,512]{1,0:T(8,128)(2,1)}, bf16[512,512]{1,0:T(8,128)(2,1)}, bf16[512,256]{1,0:T(8,128)(2,1)}, bf16[256,512]{1,0:T(8,128)(2,1)}) custom-call(bf16[512,256]{1,0:T(8,128)(2,1)} %w_value.2, bf16[512,256]{1,0:T(8,128)(2,1)} %w_reset.2, bf16[128,512]{1,0:T(8,128)(2,1)} %w_hidden, bf16[128,512]{1,0:T(8,128)(2,1)} %w_update, ...), custom_call_target="tpu_custom_call" | custom-call | tf_op jit(solution)/shard_map/pack/pallas_call | solution.py:118
  18.4 0.9 collective-permute-done.3.refs_2_.refs_10_
  20.5 1.5 %collective-permute-start.7 = (bf16[256,512]{1,0:T(8,128)(2,1)S(1)}, bf16[256,512]{1,0:T(8,128)(2,1)S(1)}, u32[]{:S(2)}, u32[]{:S(2)}) collective-permute-start(bf16[256,512]{1,0:T(8,128)(2,1)S(1)} %collective-permute-done.1.refs_8_.refs_23_), channel_id=1, source_target_pairs={{0,4},{1,5},{2,6},{3,7},{4,0},{5,1},{6,2},{7,3},{8,12},{9,13},{10,... | collective-permute-start | bytes 786440 | tf_op jit(solution)/shard_map/ppermute | solution.py:1022
  22.5 1.6 %collective-permute-start.5 = (bf16[6,16,512]{2,1,0:T(8,128)(2,1)S(1)}, bf16[6,16,512]{2,1,0:T(8,128)(2,1)S(1)}, u32[]{:S(2)}, u32[]{:S(2)}) collective-permute-start(bf16[6,16,512]{2,1,0:T(8,128)(2,1)S(1)} %get-tuple-element.177), channel_id=1, source_target_pairs={{0,8},{1,9},{2,10},{3,11},{4,12},{5,13},{6,14},{7,15},{8,0},{9,1},... | collective-permute-start | bytes 294920 | tf_op jit(solution)/shard_map/ppermute | solution.py:1022
  24.1 3.0 %collective-permute-done.5.refs_1_.refs_12_ = bf16[6,16,512]{2,1,0:T(8,128)(2,1)S(1)} collective-permute-done((bf16[6,16,512]{2,1,0:T(8,128)(2,1)S(1)}, bf16[6,16,512]{2,1,0:T(8,128)(2,1)S(1)}, u32[]{:S(2)}, u32[]{:S(2)}) %collective-permute-start.5) | collective-permute-done | bytes 98336 | tf_op jit(solution)/shard_map/ppermute | solution.py:1022
  27.2 0.7 hop.7
  27.9 0.9 collective-permute-done.7.refs_9_.refs_24_
  28.8 1.4 %collective-permute-done.6.refs_10_.refs_25_ = bf16[512,256]{1,0:T(8,128)(2,1)S(1)} collective-permute-done((bf16[512,256]{1,0:T(8,128)(2,1)}, bf16[512,256]{1,0:T(8,128)(2,1)S(1)}, u32[]{:S(2)}, u32[]{:S(2)}) %collective-permute-start.6) | collective-permute-done | bytes 262176 | tf_op jit(solution)/shard_map/ppermute | solution.py:1022
  30.8 2.6 %collective-permute-start.11 = (bf16[6,16,512]{2,1,0:T(8,128)(2,1)S(1)}, bf16[6,16,512]{2,1,0:T(8,128)(2,1)S(1)}, u32[]{:S(2)}, u32[]{:S(2)}) collective-permute-start(bf16[6,16,512]{2,1,0:T(8,128)(2,1)S(1)} %get-tuple-element.186), channel_id=1, source_target_pairs={{0,16},{1,17},{2,18},{3,19},{4,20},{5,21},{6,22},{7,23},{8,24},{9,... | collective-permute-start | bytes 294920 | tf_op jit(solution)/shard_map/ppermute | solution.py:1022
  33.4 1.6 %collective-permute-start.13 = (bf16[512,256]{1,0:T(8,128)(2,1)S(1)}, bf16[512,256]{1,0:T(8,128)(2,1)S(1)}, u32[]{:S(2)}, u32[]{:S(2)}) collective-permute-start(bf16[512,256]{1,0:T(8,128)(2,1)S(1)} %collective-permute-done.6.refs_10_.refs_25_), channel_id=1, source_target_pairs={{0,8},{1,9},{2,10},{3,11},{4,12},{5,13},{6,14},{7,15},{8,0},{9,1},... | collective-permute-start | bytes 786440 | tf_op jit(solution)/shard_map/ppermute | solution.py:1022
  35.4 2.1 %collective-permute-done.10.refs_8_ = bf16[256,512]{1,0:T(8,128)(2,1)S(1)} collective-permute-done((bf16[256,512]{1,0:T(8,128)(2,1)}, bf16[256,512]{1,0:T(8,128)(2,1)S(1)}, u32[]{:S(2)}, u32[]{:S(2)}) %collective-permute-start.10) | collective-permute-done | bytes 262176 | tf_op jit(solution)/shard_map/ppermute | solution.py:1022
  38.2 0.6 copy-done.10
  38.8 3.0 %look.1 = (f32[2,2,16,512]{3,2,1,0:T(8,128)S(1)}, f32[256,512]{1,0:T(8,128)S(1)}, bf16[256,512]{1,0:T(8,128)(2,1)S(1)}, f32[256,128]{1,0:T(8,128)S(1)}, f32[2,128,128]{2,1,0:T(8,128)S(1)}) custom-call(s32[2]{0:T(128)S(1)} %copy-done.12, bf16[256,512]{1,0:T(8,128)(2,1)S(1)} %get-tuple-element.188.refs_0_.refs_1_, ...), custom_call_target="tpu_custom_call" | custom-call | tf_op jit(solution)/shard_map/look/pallas_call | solution.py:118
  41.9 0.6 collective-permute-start.15
  42.9 1.0 collective-permute-done.12.refs_9_
  44.0 3.6 %mix.1 = (bf16[4,256,256]{2,1,0:T(8,128)(2,1)S(1)}, f32[4,256,256]{2,1,0:T(8,128)S(1)}, f32[4,256,256]{2,1,0:T(8,128)S(1)}, f32[4,256,256]{2,1,0:T(8,128)S(1)}, ...) custom-call(bf16[2,128,512]{2,1,0:T(8,128)(2,1)S(1)} %copy-done, ...), custom_call_target="tpu_custom_call" | custom-call | tf_op jit(solution)/shard_map/mix/pallas_call | solution.py:118
  47.6 0.7 copy-done.11
  48.3 5.1 %ffn.1 = (bf16[256,512]{1,0:T(8,128)(2,1)}, bf16[2,512,512]{2,1,0:T(8,128)(2,1)S(1)}, bf16[2,512,512]{2,1,0:T(8,128)(2,1)S(1)}, bf16[256,1024]{1,0:T(8,128)(2,1)...) custom-call(s32[2]{0:T(128)S(1)} %copy-done.12, bf16[2,128,512]{2,1,0:T(8,128)(2,1)S(1)} %copy-done, ...), custom_call_target="tpu_custom_call" | custom-call | tf_op jit(solution)/shard_map/ffn/pallas_call | solution.py:118
  53.4 0.6 collective-permute-start.22
  54.0 1.1 gates.1
  55.2 1.1 collective-permute-done.22.refs_1_
  56.6 1.3 collective-permute-start.23
  58.3 1.4 collective-permute-start.24
  59.6 9.7 %back.1 = (bf16[2,512,512]{2,1,0:T(8,128)(2,1)S(1)}, bf16[2,512,512]{2,1,0:T(8,128)(2,1)S(1)}, f32[4,256,128]{2,1,0:T(8,128)S(1)}, f32[256,512]{1,0:T(8,128)S(1)...) custom-call(bf16[256,512]{1,0:T(8,128)(2,1)S(1)} %get-tuple-element., ...), custom_call_target="tpu_custom_call" | custom-call | tf_op jit(solution)/shard_map/back/pallas_call | solution.py:118
  69.3 1.6 %collective-permute-done.23.refs_1_ = bf16[1,512,512]{2,1,0:T(8,128)(2,1)S(1)} collective-permute-done((bf16[1,512,512]{2,1,0:T(8,128)(2,1)S(1)}, bf16[1,512,512]{2,1,0:T(8,128)(2,1)S(1)}, u32[]{:S(2)}, u32[]{:S(2)}) %collective-permute-start.23) | collective-permute-done | bytes 524320 | tf_op jit(solution)/shard_map/ppermute | solution.py:1022
  71.0 1.3 collective-permute-done.24.refs_1_
  73.1 1.4 %collective-permute-start.29 = (bf16[1,256,512]{2,1,0:T(8,128)(2,1)S(1)}, bf16[1,256,512]{2,1,0:T(8,128)(2,1)S(1)}, u32[]{:S(2)}, u32[]{:S(2)}) collective-permute-start(bf16[1,256,512]{2,1,0:T(8,128)(2,1)S(1)} %get-tuple-element.251), channel_id=1, source_target_pairs={{0,4},{1,5},{2,6},{3,7},{4,0},{5,1},{6,2},{7,3},{8,12},{9,13},{10,... | collective-permute-start | bytes 786440 | tf_op jit(solution)/shard_map/ppermute | solution.py:1022
  74.5 0.6 collective-permute-start.30
  75.1 1.3 collective-permute-done.25.refs_2_.refs_8_
  76.4 1.4 %collective-permute-start.28 = (bf16[80,512]{1,0:T(8,128)(2,1)S(1)}, bf16[80,512]{1,0:T(8,128)(2,1)S(1)}, u32[]{:S(2)}, u32[]{:S(2)}) collective-permute-start(bf16[80,512]{1,0:T(8,128)(2,1)S(1)} %get-tuple-element.242.refs_3_), channel_id=1, source_target_pairs={{0,2},{1,3},{2,0},{3,1},{4,6},{5,7},{6,4},{7,5},{8,10},{9,11},{10,... | collective-permute-start | bytes 245768 | tf_op jit(solution)/shard_map/ppermute | solution.py:1022
  78.3 5.9 %collective-permute-done.28.refs_4_.refs_9_ = bf16[80,512]{1,0:T(8,128)(2,1)S(1)} collective-permute-done((bf16[80,512]{1,0:T(8,128)(2,1)S(1)}, bf16[80,512]{1,0:T(8,128)(2,1)S(1)}, u32[]{:S(2)}, u32[]{:S(2)}) %collective-permute-start.28) | collective-permute-done | bytes 81952 | tf_op jit(solution)/shard_map/ppermute | solution.py:1022
  84.3 0.7 collective-permute-start.31
  85.0 1.2 collective-permute-start.32
  86.4 1.1 collective-permute-start.33
  87.5 4.0 %collective-permute-done.31.refs_1_ = bf16[1,512,256]{2,1,0:T(8,128)(2,1)S(1)} collective-permute-done((bf16[1,512,256]{2,1,0:T(8,128)(2,1)S(1)}, bf16[1,512,256]{2,1,0:T(8,128)(2,1)S(1)}, u32[]{:S(2)}, u32[]{:S(2)}) %collective-permute-start.31) | collective-permute-done | bytes 262176 | tf_op jit(solution)/shard_map/ppermute | solution.py:1022
  92.1 1.0 collective-permute-done.33.refs_1_
  93.2 2.1 %collective-permute-start.37 = (bf16[2,128,512]{2,1,0:T(8,128)(2,1)S(1)}, bf16[2,128,512]{2,1,0:T(8,128)(2,1)S(1)}, u32[]{:S(2)}, u32[]{:S(2)}) collective-permute-start(bf16[2,128,512]{2,1,0:T(8,128)(2,1)S(1)} %fold.16.refs_0_), channel_id=1, source_target_pairs={{0,16},{1,17},{2,18},{3,19},{4,20},{5,21},{6,22},{7,23},{8,24},{9,... | collective-permute-start | bytes 786440 | tf_op jit(solution)/shard_map/ppermute | solution.py:1022
  95.2 1.3 collective-permute-start.35
  96.6 1.4 %collective-permute-start.36 = (bf16[1,256,256]{2,1,0:T(8,128)(2,1)S(1)}, bf16[1,256,256]{2,1,0:T(8,128)(2,1)S(1)}, u32[]{:S(2)}, u32[]{:S(2)}) collective-permute-start(bf16[1,256,256]{2,1,0:T(8,128)(2,1)S(1)} %get-tuple-element.265), channel_id=1, source_target_pairs={{0,2},{1,3},{2,0},{3,1},{4,6},{5,7},{6,4},{7,5},{8,10},{9,11},{10,... | collective-permute-start | bytes 393224 | tf_op jit(solution)/shard_map/ppermute | solution.py:1022
  98.0 0.7 collective-permute-start.34
  98.7 3.8 %collective-permute-done.34.refs_4_.refs_10_ = bf16[80,512]{1,0:T(8,128)(2,1)S(1)} collective-permute-done((bf16[80,512]{1,0:T(8,128)(2,1)S(1)}, bf16[80,512]{1,0:T(8,128)(2,1)S(1)}, u32[]{:S(2)}, u32[]{:S(2)}) %collective-permute-start.34) | collective-permute-done | bytes 81952 | tf_op jit(solution)/shard_map/ppermute | solution.py:1022
  102.6 1.6 %collective-permute-start.38 = (bf16[208,512]{1,0:T(8,128)(2,1)S(1)}, bf16[208,512]{1,0:T(8,128)(2,1)S(1)}, u32[]{:S(2)}, u32[]{:S(2)}) collective-permute-start(bf16[208,512]{1,0:T(8,128)(2,1)S(1)} %get-tuple-element.267.refs_3_), channel_id=1, source_target_pairs={{0,8},{1,9},{2,10},{3,11},{4,12},{5,13},{6,14},{7,15},{8,0},{9,1},... | collective-permute-start | bytes 638984 | tf_op jit(solution)/shard_map/ppermute | solution.py:1022
  104.2 1.3 collective-permute-done.37.refs_1_
  105.7 5.1 %collective-permute-done.38.refs_4_.refs_11_ = bf16[208,512]{1,0:T(8,128)(2,1)S(1)} collective-permute-done((bf16[208,512]{1,0:T(8,128)(2,1)S(1)}, bf16[208,512]{1,0:T(8,128)(2,1)S(1)}, u32[]{:S(2)}, u32[]{:S(2)}) %collective-permute-start.38) | collective-permute-done | bytes 213024 | tf_op jit(solution)/shard_map/ppermute | solution.py:1022
  111.0 6.3 %collective-permute-done.39.refs_1_ = bf16[2,128,512]{2,1,0:T(8,128)(2,1)S(1)} collective-permute-done((bf16[2,128,512]{2,1,0:T(8,128)(2,1)S(1)}, bf16[2,128,512]{2,1,0:T(8,128)(2,1)S(1)}, u32[]{:S(2)}, u32[]{:S(2)}) %collective-permute-start.39) | collective-permute-done | bytes 262176 | tf_op jit(solution)/shard_map/ppermute | solution.py:1022
  117.3 1.0 collective-permute-start.44
  118.4 3.1 %collective-permute-done.40.refs_4_.refs_12_ = bf16[208,512]{1,0:T(8,128)(2,1)S(1)} collective-permute-done((bf16[208,512]{1,0:T(8,128)(2,1)S(1)}, bf16[208,512]{1,0:T(8,128)(2,1)S(1)}, u32[]{:S(2)}, u32[]{:S(2)}) %collective-permute-start.40) | collective-permute-done | bytes 213024 | tf_op jit(solution)/shard_map/ppermute | solution.py:1022
  121.6 0.5 collective-permute-start.42
  122.1 2.7 %leave.1 = bf16[2,128,512]{2,1,0:T(8,128)(2,1)} custom-call(bf16[2,128,512]{2,1,0:T(8,128)(2,1)S(1)} %copy-done, f32[4,16,512]{2,1,0:T(8,128)S(1)} %get-tuple-element.189.refs_1_.refs_10_.refs_0_, f32[4,256,128]{2,1,0:T(8,128)S(1)} %get-tuple-element.278.refs_2_, f32[256,512]{1,0:T(8,128)S(1)} %get-tuple-element.279.refs_3_, ...), custom_call_target="tpu_custom_call" | custom-call | tf_op jit(solution)/shard_map/leave/pallas_call | solution.py:118
  124.9 1.7 %collective-permute-done.41.refs_1_ = bf16[1,128,512]{2,1,0:T(8,128)(2,1)S(1)} collective-permute-done((bf16[1,128,512]{2,1,0:T(8,128)(2,1)S(1)}, bf16[1,128,512]{2,1,0:T(8,128)(2,1)S(1)}, u32[]{:S(2)}, u32[]{:S(2)}) %collective-permute-start.41) | collective-permute-done | bytes 131104 | tf_op jit(solution)/shard_map/ppermute | solution.py:1022
  126.6 0.6 collective-permute-start.45
  127.3 1.4 %collective-permute-done.43.refs_5_ = f32[96,512]{1,0:T(8,128)S(1)} collective-permute-done((f32[96,512]{1,0:T(8,128)S(1)}, f32[96,512]{1,0:T(8,128)S(1)}, u32[]{:S(2)}, u32[]{:S(2)}) %collective-permute-start.43) | collective-permute-done | bytes 196640 | tf_op jit(solution)/shard_map/ppermute | solution.py:1022
  128.7 0.8 finish.1
  129.5 2.8 %collective-permute-done.44.refs_1_ = bf16[2,256,512]{2,1,0:T(8,128)(2,1)S(1)} collective-permute-done((bf16[2,256,512]{2,1,0:T(8,128)(2,1)S(1)}, bf16[2,256,512]{2,1,0:T(8,128)(2,1)S(1)}, u32[]{:S(2)}, u32[]{:S(2)}) %collective-permute-start.44) | collective-permute-done | bytes 524320 | tf_op jit(solution)/shard_map/ppermute | solution.py:1022
  132.3 1.5 %unpack.2 = (f32[512,256]{1,0:T(8,128)}, f32[256,512]{1,0:T(8,128)}, f32[128,512]{1,0:T(8,128)}, f32[128,512]{1,0:T(8,128)}, f32[256,512]{1,0:T(8,128)}) custom-call(bf16[2,256,512]{2,1,0:T(8,128)(2,1)S(1)} %join.2.refs_0_, bf16[2,256,512]{2,1,0:T(8,128)(2,1)S(1)} %collective-permute-done.44.refs_1_), custom_call_target="tpu_custom_call" | custom-call | tf_op jit(solution)/shard_map/unpack/pallas_call | solution.py:118
  133.7 2.1 %collective-permute-done.45.refs_1_ = bf16[1,256,512]{2,1,0:T(8,128)(2,1)S(1)} collective-permute-done((bf16[1,256,512]{2,1,0:T(8,128)(2,1)S(1)}, bf16[1,256,512]{2,1,0:T(8,128)(2,1)S(1)}, u32[]{:S(2)}, u32[]{:S(2)}) %collective-permute-start.45) | collective-permute-done | bytes 262176 | tf_op jit(solution)/shard_map/ppermute | solution.py:1022
  135.9 1.0 unpack.3
  (92 shorter events, 8.5 us)
Async XLA Ops:
  0.7 4.8 %copy-start = (bf16[2,128,512]{2,1,0:T(8,128)(2,1)S(1)}, bf16[2,128,512]{2,1,0:T(8,128)(2,1)}, u32[]{:S(2)}) copy-start(bf16[2,128,512]{2,1,0:T(8,128)(2,1)} %refs_0_.7) | copy-start | bytes 786436
  0.7 4.8 %copy-start.8 = (f32[512,16]{0,1:T(8,128)S(1)}, f32[512,16]{0,1:T(8,128)}, u32[]{:S(2)}) copy-start(f32[512,16]{0,1:T(8,128)} %param.26) | copy-start | bytes 98308
  0.7 4.8 %copy-start.7 = (f32[512,16]{0,1:T(8,128)S(1)}, f32[512,16]{0,1:T(8,128)}, u32[]{:S(2)}) copy-start(f32[512,16]{0,1:T(8,128)} %param.25) | copy-start | bytes 98308
  0.7 4.8 %copy-start.6 = (f32[512,16]{0,1:T(8,128)S(1)}, f32[512,16]{0,1:T(8,128)}, u32[]{:S(2)}) copy-start(f32[512,16]{0,1:T(8,128)} %param.24) | copy-start | bytes 98308
  2.4 9.5 %collective-permute-start.1 = (bf16[256,512]{1,0:T(8,128)(2,1)}, bf16[256,512]{1,0:T(8,128)(2,1)S(1)}, u32[]{:S(2)}, u32[]{:S(2)}) collective-permute-start(bf16[256,512]{1,0:T(8,128)(2,1)} %half.1), channel_id=1, source_target_pairs={{0,2},{1,3},{2,0},{3,1},{4,6},{5,7},{6,4},{7,5},{8,10},{9,11},{10,... | collective-permute-start | bytes 786440 | tf_op jit(solution)/shard_map/ppermute | solution.py:1022
  5.4 0.7 copy-start.9
  8.6 1.4 collective-permute-start
  12.0 6.4 %collective-permute-start.4 = (bf16[6,16,512]{2,1,0:T(8,128)(2,1)S(1)}, bf16[6,16,512]{2,1,0:T(8,128)(2,1)S(1)}, u32[]{:S(2)}, u32[]{:S(2)}) collective-permute-start(bf16[6,16,512]{2,1,0:T(8,128)(2,1)S(1)} %get-tuple-element.166), channel_id=1, source_target_pairs={{0,6},{1,7},{2,4},{3,5},{4,2},{5,3},{6,0},{7,1},{8,14},{9,15},{10,... | collective-permute-start | bytes 294920 | tf_op jit(solution)/shard_map/ppermute | solution.py:1022
  14.7 4.6 %collective-permute-start.3 = (bf16[6,16,512]{2,1,0:T(8,128)(2,1)S(1)}, bf16[6,16,512]{2,1,0:T(8,128)(2,1)S(1)}, u32[]{:S(2)}, u32[]{:S(2)}) collective-permute-start(bf16[6,16,512]{2,1,0:T(8,128)(2,1)S(1)} %get-tuple-element.166), channel_id=1, source_target_pairs={{0,4},{1,5},{2,6},{3,7},{4,0},{5,1},{6,2},{7,3},{8,12},{9,13},{10,... | collective-permute-start | bytes 294920 | tf_op jit(solution)/shard_map/ppermute | solution.py:1022
  15.2 4.6 %collective-permute-start.2 = (bf16[6,16,512]{2,1,0:T(8,128)(2,1)S(1)}, bf16[6,16,512]{2,1,0:T(8,128)(2,1)S(1)}, u32[]{:S(2)}, u32[]{:S(2)}) collective-permute-start(bf16[6,16,512]{2,1,0:T(8,128)(2,1)S(1)} %get-tuple-element.166), channel_id=1, source_target_pairs={{0,2},{1,3},{2,0},{3,1},{4,6},{5,7},{6,4},{7,5},{8,10},{9,11},{10,... | collective-permute-start | bytes 294920 | tf_op jit(solution)/shard_map/ppermute | solution.py:1022
  18.4 19.7 %copy-start.4 = (bf16[512,512]{1,0:T(8,128)(2,1)S(1)}, bf16[512,512]{1,0:T(8,128)(2,1)}, u32[]{:S(2)}) copy-start(bf16[512,512]{1,0:T(8,128)(2,1)} %get-tuple-element.201.refs_6_) | copy-start | bytes 1572868
  19.9 10.3 %collective-permute-start.9 = (bf16[512,512]{1,0:T(8,128)(2,1)}, bf16[512,512]{1,0:T(8,128)(2,1)S(1)}, u32[]{:S(2)}, u32[]{:S(2)}) collective-permute-start(bf16[512,512]{1,0:T(8,128)(2,1)} %get-tuple-element.185.refs_5_.refs_20_), channel_id=1, source_target_pairs={{0,1},{1,0},{2,3},{3,2},{4,5},{5,4},{6,7},{7,6},{8,9},{9,8},{10,11... | collective-permute-start | bytes 1572872 | tf_op jit(solution)/shard_map/ppermute | solution.py:1022
  20.0 10.2 %collective-permute-start.8 = (bf16[512,512]{1,0:T(8,128)(2,1)}, bf16[512,512]{1,0:T(8,128)(2,1)S(1)}, u32[]{:S(2)}, u32[]{:S(2)}) collective-permute-start(bf16[512,512]{1,0:T(8,128)(2,1)} %get-tuple-element.183.refs_4_.refs_19_), channel_id=1, source_target_pairs={{0,1},{1,0},{2,3},{3,2},{4,5},{5,4},{6,7},{7,6},{8,9},{9,8},{10,11... | collective-permute-start | bytes 1572872 | tf_op jit(solution)/shard_map/ppermute | solution.py:1022
  20.5 8.3 %collective-permute-start.7 = (bf16[256,512]{1,0:T(8,128)(2,1)S(1)}, bf16[256,512]{1,0:T(8,128)(2,1)S(1)}, u32[]{:S(2)}, u32[]{:S(2)}) collective-permute-start(bf16[256,512]{1,0:T(8,128)(2,1)S(1)} %collective-permute-done.1.refs_8_.refs_23_), channel_id=1, source_target_pairs={{0,4},{1,5},{2,6},{3,7},{4,0},{5,1},{6,2},{7,3},{8,12},{9,13},{10,... | collective-permute-start | bytes 786440 | tf_op jit(solution)/shard_map/ppermute | solution.py:1022
  22.0 8.2 %collective-permute-start.6 = (bf16[512,256]{1,0:T(8,128)(2,1)}, bf16[512,256]{1,0:T(8,128)(2,1)S(1)}, u32[]{:S(2)}, u32[]{:S(2)}) collective-permute-start(bf16[512,256]{1,0:T(8,128)(2,1)} %get-tuple-element.180), channel_id=1, source_target_pairs={{0,2},{1,3},{2,0},{3,1},{4,6},{5,7},{6,4},{7,5},{8,10},{9,11},{10,... | collective-permute-start | bytes 786440 | tf_op jit(solution)/shard_map/ppermute | solution.py:1022
  22.5 4.6 %collective-permute-start.5 = (bf16[6,16,512]{2,1,0:T(8,128)(2,1)S(1)}, bf16[6,16,512]{2,1,0:T(8,128)(2,1)S(1)}, u32[]{:S(2)}, u32[]{:S(2)}) collective-permute-start(bf16[6,16,512]{2,1,0:T(8,128)(2,1)S(1)} %get-tuple-element.177), channel_id=1, source_target_pairs={{0,8},{1,9},{2,10},{3,11},{4,12},{5,13},{6,14},{7,15},{8,0},{9,1},... | collective-permute-start | bytes 294920 | tf_op jit(solution)/shard_map/ppermute | solution.py:1022
  27.2 11.0 %copy-start.3 = (bf16[512,128]{1,0:T(8,128)(2,1)S(1)}, bf16[512,128]{1,0:T(8,128)(2,1)}, u32[]{:S(2)}) copy-start(bf16[512,128]{1,0:T(8,128)(2,1)} %refs_11_.1) | copy-start | bytes 393220
  27.2 11.0 %copy-start.15 = (f32[128]{0:T(128)S(1)}, f32[128]{0:T(128)}, u32[]{:S(2)}) copy-start(f32[128]{0:T(128)} %param.31) | copy-start | bytes 1540
  30.2 7.3 %collective-permute-start.10 = (bf16[256,512]{1,0:T(8,128)(2,1)}, bf16[256,512]{1,0:T(8,128)(2,1)S(1)}, u32[]{:S(2)}, u32[]{:S(2)}) collective-permute-start(bf16[256,512]{1,0:T(8,128)(2,1)} %get-tuple-element.187), channel_id=1, source_target_pairs={{0,2},{1,3},{2,0},{3,1},{4,6},{5,7},{6,4},{7,5},{8,10},{9,11},{10,... | collective-permute-start | bytes 786440 | tf_op jit(solution)/shard_map/ppermute | solution.py:1022
  30.8 7.3 %collective-permute-start.11 = (bf16[6,16,512]{2,1,0:T(8,128)(2,1)S(1)}, bf16[6,16,512]{2,1,0:T(8,128)(2,1)S(1)}, u32[]{:S(2)}, u32[]{:S(2)}) collective-permute-start(bf16[6,16,512]{2,1,0:T(8,128)(2,1)S(1)} %get-tuple-element.186), channel_id=1, source_target_pairs={{0,16},{1,17},{2,18},{3,19},{4,20},{5,21},{6,22},{7,23},{8,24},{9,... | collective-permute-start | bytes 294920 | tf_op jit(solution)/shard_map/ppermute | solution.py:1022
  33.4 8.5 %collective-permute-start.13 = (bf16[512,256]{1,0:T(8,128)(2,1)S(1)}, bf16[512,256]{1,0:T(8,128)(2,1)S(1)}, u32[]{:S(2)}, u32[]{:S(2)}) collective-permute-start(bf16[512,256]{1,0:T(8,128)(2,1)S(1)} %collective-permute-done.6.refs_10_.refs_25_), channel_id=1, source_target_pairs={{0,8},{1,9},{2,10},{3,11},{4,12},{5,13},{6,14},{7,15},{8,0},{9,1},... | collective-permute-start | bytes 786440 | tf_op jit(solution)/shard_map/ppermute | solution.py:1022
  34.9 7.5 %collective-permute-start.14 = (bf16[256,512]{1,0:T(8,128)(2,1)S(1)}, bf16[256,512]{1,0:T(8,128)(2,1)S(1)}, u32[]{:S(2)}, u32[]{:S(2)}) collective-permute-start(bf16[256,512]{1,0:T(8,128)(2,1)S(1)} %collective-permute-done.1.refs_8_.refs_23_), channel_id=1, source_target_pairs={{0,1},{1,0},{2,3},{3,2},{4,5},{5,4},{6,7},{7,6},{8,9},{9,8},{10,11... | collective-permute-start | bytes 786440 | tf_op jit(solution)/shard_map/ppermute | solution.py:1022
  34.9 7.6 %collective-permute-start.16 = (bf16[512,256]{1,0:T(8,128)(2,1)S(1)}, bf16[512,256]{1,0:T(8,128)(2,1)S(1)}, u32[]{:S(2)}, u32[]{:S(2)}) collective-permute-start(bf16[512,256]{1,0:T(8,128)(2,1)S(1)} %collective-permute-done.6.refs_10_.refs_25_), channel_id=1, source_target_pairs={{0,1},{1,0},{2,3},{3,2},{4,5},{5,4},{6,7},{7,6},{8,9},{9,8},{10,11... | collective-permute-start | bytes 786440 | tf_op jit(solution)/shard_map/ppermute | solution.py:1022
  37.6 6.4 %collective-permute-start.12 = (bf16[256,512]{1,0:T(8,128)(2,1)S(1)}, bf16[256,512]{1,0:T(8,128)(2,1)S(1)}, u32[]{:S(2)}, u32[]{:S(2)}) collective-permute-start(bf16[256,512]{1,0:T(8,128)(2,1)S(1)} %collective-permute-done.10.refs_8_), channel_id=1, source_target_pairs={{0,4},{1,5},{2,6},{3,7},{4,0},{5,1},{6,2},{7,3},{8,12},{9,13},{10,... | collective-permute-start | bytes 786440 | tf_op jit(solution)/shard_map/ppermute | solution.py:1022
  38.1 9.5 %collective-permute-start.18 = (bf16[512,512]{1,0:T(8,128)(2,1)S(1)}, bf16[512,512]{1,0:T(8,128)(2,1)S(1)}, u32[]{:S(2)}, u32[]{:S(2)}) collective-permute-start(bf16[512,512]{1,0:T(8,128)(2,1)S(1)} %copy-done.4), channel_id=1, source_target_pairs={{0,1},{1,0},{2,3},{3,2},{4,5},{5,4},{6,7},{7,6},{8,9},{9,8},{10,11... | collective-permute-start | bytes 1572872 | tf_op jit(solution)/shard_map/ppermute | solution.py:1022
  38.1 0.7 copy-start.10
  38.1 0.7 copy-start.12
  38.1 0.7 copy-start.13
  38.1 0.7 copy-start.14
  38.8 5.2 %copy-start.1 = (bf16[512,512]{1,0:T(8,128)(2,1)S(1)}, bf16[512,512]{1,0:T(8,128)(2,1)}, u32[]{:S(2)}) copy-start(bf16[512,512]{1,0:T(8,128)(2,1)} %get-tuple-element.183.refs_4_.refs_19_) | copy-start | bytes 1572868
  38.8 5.2 %copy-start.2 = (bf16[512,512]{1,0:T(8,128)(2,1)S(1)}, bf16[512,512]{1,0:T(8,128)(2,1)}, u32[]{:S(2)}) copy-start(bf16[512,512]{1,0:T(8,128)(2,1)} %get-tuple-element.185.refs_5_.refs_20_) | copy-start | bytes 1572868
  41.9 2.1 %collective-permute-start.15 = (bf16[256,512]{1,0:T(8,128)(2,1)S(1)}, bf16[256,512]{1,0:T(8,128)(2,1)S(1)}, u32[]{:S(2)}, u32[]{:S(2)}) collective-permute-start(bf16[256,512]{1,0:T(8,128)(2,1)S(1)} %collective-permute-done.7.refs_9_.refs_24_), channel_id=1, source_target_pairs={{0,1},{1,0},{2,3},{3,2},{4,5},{5,4},{6,7},{7,6},{8,9},{9,8},{10,11... | collective-permute-start | bytes 786440 | tf_op jit(solution)/shard_map/ppermute | solution.py:1022
  42.4 1.5 %collective-permute-start.17 = (bf16[512,256]{1,0:T(8,128)(2,1)S(1)}, bf16[512,256]{1,0:T(8,128)(2,1)S(1)}, u32[]{:S(2)}, u32[]{:S(2)}) collective-permute-start(bf16[512,256]{1,0:T(8,128)(2,1)S(1)} %collective-permute-done.13.refs_11_.refs_26_), channel_id=1, source_target_pairs={{0,1},{1,0},{2,3},{3,2},{4,5},{5,4},{6,7},{7,6},{8,9},{9,8},{10,11... | collective-permute-start | bytes 786440 | tf_op jit(solution)/shard_map/ppermute | solution.py:1022
  42.5 5.1 %collective-permute-start.19 = (bf16[256,512]{1,0:T(8,128)(2,1)S(1)}, bf16[256,512]{1,0:T(8,128)(2,1)S(1)}, u32[]{:S(2)}, u32[]{:S(2)}) collective-permute-start(bf16[256,512]{1,0:T(8,128)(2,1)S(1)} %collective-permute-done.10.refs_8_), channel_id=1, source_target_pairs={{0,1},{1,0},{2,3},{3,2},{4,5},{5,4},{6,7},{7,6},{8,9},{9,8},{10,11... | collective-permute-start | bytes 786440 | tf_op jit(solution)/shard_map/ppermute | solution.py:1022
  43.9 3.7 %collective-permute-start.20 = (bf16[256,512]{1,0:T(8,128)(2,1)S(1)}, bf16[256,512]{1,0:T(8,128)(2,1)S(1)}, u32[]{:S(2)}, u32[]{:S(2)}) collective-permute-start(bf16[256,512]{1,0:T(8,128)(2,1)S(1)} %collective-permute-done.12.refs_9_), channel_id=1, source_target_pairs={{0,1},{1,0},{2,3},{3,2},{4,5},{5,4},{6,7},{7,6},{8,9},{9,8},{10,11... | collective-permute-start | bytes 786440 | tf_op jit(solution)/shard_map/ppermute | solution.py:1022
  43.9 3.7 %copy-start.5 = (bf16[2,128,512]{2,1,0:T(8,128)(2,1)S(1)}, bf16[2,128,512]{2,1,0:T(8,128)(2,1)}, u32[]{:S(2)}) copy-start(bf16[2,128,512]{2,1,0:T(8,128)(2,1)} %refs_1_.1) | copy-start | bytes 786436
  47.6 0.7 copy-start.11
  53.4 2.8 %collective-permute-start.22 = (bf16[2,512,512]{2,1,0:T(8,128)(2,1)S(1)}, bf16[2,512,512]{2,1,0:T(8,128)(2,1)S(1)}, u32[]{:S(2)}, u32[]{:S(2)}) collective-permute-start(bf16[2,512,512]{2,1,0:T(8,128)(2,1)S(1)} %get-tuple-element.214), channel_id=1, source_target_pairs={{0,1},{1,0},{2,3},{3,2},{4,5},{5,4},{6,7},{7,6},{8,9},{9,8},{10,11... | collective-permute-start | bytes 3145736 | tf_op jit(solution)/shard_map/ppermute | solution.py:1022
  55.1 2.8 %collective-permute-start.21 = (bf16[2,512,512]{2,1,0:T(8,128)(2,1)S(1)}, bf16[2,512,512]{2,1,0:T(8,128)(2,1)S(1)}, u32[]{:S(2)}, u32[]{:S(2)}) collective-permute-start(bf16[2,512,512]{2,1,0:T(8,128)(2,1)S(1)} %get-tuple-element.212), channel_id=1, source_target_pairs={{0,1},{1,0},{2,3},{3,2},{4,5},{5,4},{6,7},{7,6},{8,9},{9,8},{10,11... | collective-permute-start | bytes 3145736 | tf_op jit(solution)/shard_map/ppermute | solution.py:1022
  56.6 14.3 %collective-permute-start.23 = (bf16[1,512,512]{2,1,0:T(8,128)(2,1)S(1)}, bf16[1,512,512]{2,1,0:T(8,128)(2,1)S(1)}, u32[]{:S(2)}, u32[]{:S(2)}) collective-permute-start(bf16[1,512,512]{2,1,0:T(8,128)(2,1)S(1)} %get-tuple-element.230), channel_id=1, source_target_pairs={{0,2},{1,3},{2,0},{3,1},{4,6},{5,7},{6,4},{7,5},{8,10},{9,11},{10,... | collective-permute-start | bytes 1572872 | tf_op jit(solution)/shard_map/ppermute | solution.py:1022
  58.3 14.1 %collective-permute-start.24 = (bf16[2,256,512]{2,1,0:T(8,128)(2,1)S(1)}, bf16[2,256,512]{2,1,0:T(8,128)(2,1)S(1)}, u32[]{:S(2)}, u32[]{:S(2)}) collective-permute-start(bf16[2,256,512]{2,1,0:T(8,128)(2,1)S(1)} %get-tuple-element.233), channel_id=1, source_target_pairs={{0,4},{1,5},{2,6},{3,7},{4,0},{5,1},{6,2},{7,3},{8,12},{9,13},{10,... | collective-permute-start | bytes 1572872 | tf_op jit(solution)/shard_map/ppermute | solution.py:1022
  72.5 5.3 %collective-permute-start.27 = (bf16[2,512,512]{2,1,0:T(8,128)(2,1)S(1)}, bf16[2,512,512]{2,1,0:T(8,128)(2,1)S(1)}, u32[]{:S(2)}, u32[]{:S(2)}) collective-permute-start(bf16[2,512,512]{2,1,0:T(8,128)(2,1)S(1)} %get-tuple-element.244), channel_id=1, source_target_pairs={{0,1},{1,0},{2,3},{3,2},{4,5},{5,4},{6,7},{7,6},{8,9},{9,8},{10,11... | collective-permute-start | bytes 3145736 | tf_op jit(solution)/shard_map/ppermute | solution.py:1022
  72.6 3.8 %collective-permute-start.26 = (f32[96,512]{1,0:T(8,128)S(1)}, f32[96,512]{1,0:T(8,128)S(1)}, u32[]{:S(2)}, u32[]{:S(2)}) collective-permute-start(f32[96,512]{1,0:T(8,128)S(1)} %get-tuple-element.239), channel_id=1, source_target_pairs={{0,1},{1,0},{2,3},{3,2},{4,5},{5,4},{6,7},{7,6},{8,9},{9,8},{10,11... | collective-permute-start | bytes 589832 | tf_op jit(solution)/shard_map/ppermute | solution.py:1022
  73.1 13.1 %collective-permute-start.29 = (bf16[1,256,512]{2,1,0:T(8,128)(2,1)S(1)}, bf16[1,256,512]{2,1,0:T(8,128)(2,1)S(1)}, u32[]{:S(2)}, u32[]{:S(2)}) collective-permute-start(bf16[1,256,512]{2,1,0:T(8,128)(2,1)S(1)} %get-tuple-element.251), channel_id=1, source_target_pairs={{0,4},{1,5},{2,6},{3,7},{4,0},{5,1},{6,2},{7,3},{8,12},{9,13},{10,... | collective-permute-start | bytes 786440 | tf_op jit(solution)/shard_map/ppermute | solution.py:1022
  74.5 11.8 %collective-permute-start.30 = (bf16[1,256,512]{2,1,0:T(8,128)(2,1)S(1)}, bf16[1,256,512]{2,1,0:T(8,128)(2,1)S(1)}, u32[]{:S(2)}, u32[]{:S(2)}) collective-permute-start(bf16[1,256,512]{2,1,0:T(8,128)(2,1)S(1)} %get-tuple-element.252), channel_id=1, source_target_pairs={{0,2},{1,3},{2,0},{3,1},{4,6},{5,7},{6,4},{7,5},{8,10},{9,11},{10,... | collective-permute-start | bytes 786440 | tf_op jit(solution)/shard_map/ppermute | solution.py:1022
  75.1 1.3 collective-permute-start.25
  76.4 7.8 %collective-permute-start.28 = (bf16[80,512]{1,0:T(8,128)(2,1)S(1)}, bf16[80,512]{1,0:T(8,128)(2,1)S(1)}, u32[]{:S(2)}, u32[]{:S(2)}) collective-permute-start(bf16[80,512]{1,0:T(8,128)(2,1)S(1)} %get-tuple-element.242.refs_3_), channel_id=1, source_target_pairs={{0,2},{1,3},{2,0},{3,1},{4,6},{5,7},{6,4},{7,5},{8,10},{9,11},{10,... | collective-permute-start | bytes 245768 | tf_op jit(solution)/shard_map/ppermute | solution.py:1022
  84.3 7.2 %collective-permute-start.31 = (bf16[1,512,256]{2,1,0:T(8,128)(2,1)S(1)}, bf16[1,512,256]{2,1,0:T(8,128)(2,1)S(1)}, u32[]{:S(2)}, u32[]{:S(2)}) collective-permute-start(bf16[1,512,256]{2,1,0:T(8,128)(2,1)S(1)} %get-tuple-element.255), channel_id=1, source_target_pairs={{0,2},{1,3},{2,0},{3,1},{4,6},{5,7},{6,4},{7,5},{8,10},{9,11},{10,... | collective-permute-start | bytes 786440 | tf_op jit(solution)/shard_map/ppermute | solution.py:1022
  85.0 6.8 %collective-permute-start.32 = (bf16[2,256,256]{2,1,0:T(8,128)(2,1)S(1)}, bf16[2,256,256]{2,1,0:T(8,128)(2,1)S(1)}, u32[]{:S(2)}, u32[]{:S(2)}) collective-permute-start(bf16[2,256,256]{2,1,0:T(8,128)(2,1)S(1)} %get-tuple-element.257), channel_id=1, source_target_pairs={{0,4},{1,5},{2,6},{3,7},{4,0},{5,1},{6,2},{7,3},{8,12},{9,13},{10,... | collective-permute-start | bytes 786440 | tf_op jit(solution)/shard_map/ppermute | solution.py:1022
  86.4 6.6 %collective-permute-start.33 = (bf16[2,128,512]{2,1,0:T(8,128)(2,1)S(1)}, bf16[2,128,512]{2,1,0:T(8,128)(2,1)S(1)}, u32[]{:S(2)}, u32[]{:S(2)}) collective-permute-start(bf16[2,128,512]{2,1,0:T(8,128)(2,1)S(1)} %get-tuple-element.260), channel_id=1, source_target_pairs={{0,8},{1,9},{2,10},{3,11},{4,12},{5,13},{6,14},{7,15},{8,0},{9,1},... | collective-permute-start | bytes 786440 | tf_op jit(solution)/shard_map/ppermute | solution.py:1022
  93.2 12.3 %collective-permute-start.37 = (bf16[2,128,512]{2,1,0:T(8,128)(2,1)S(1)}, bf16[2,128,512]{2,1,0:T(8,128)(2,1)S(1)}, u32[]{:S(2)}, u32[]{:S(2)}) collective-permute-start(bf16[2,128,512]{2,1,0:T(8,128)(2,1)S(1)} %fold.16.refs_0_), channel_id=1, source_target_pairs={{0,16},{1,17},{2,18},{3,19},{4,20},{5,21},{6,22},{7,23},{8,24},{9,... | collective-permute-start | bytes 786440 | tf_op jit(solution)/shard_map/ppermute | solution.py:1022
  95.2 7.2 %collective-permute-start.35 = (bf16[1,256,256]{2,1,0:T(8,128)(2,1)S(1)}, bf16[1,256,256]{2,1,0:T(8,128)(2,1)S(1)}, u32[]{:S(2)}, u32[]{:S(2)}) collective-permute-start(bf16[1,256,256]{2,1,0:T(8,128)(2,1)S(1)} %get-tuple-element.263), channel_id=1, source_target_pairs={{0,4},{1,5},{2,6},{3,7},{4,0},{5,1},{6,2},{7,3},{8,12},{9,13},{10,... | collective-permute-start | bytes 393224 | tf_op jit(solution)/shard_map/ppermute | solution.py:1022
  96.6 5.8 %collective-permute-start.36 = (bf16[1,256,256]{2,1,0:T(8,128)(2,1)S(1)}, bf16[1,256,256]{2,1,0:T(8,128)(2,1)S(1)}, u32[]{:S(2)}, u32[]{:S(2)}) collective-permute-start(bf16[1,256,256]{2,1,0:T(8,128)(2,1)S(1)} %get-tuple-element.265), channel_id=1, source_target_pairs={{0,2},{1,3},{2,0},{3,1},{4,6},{5,7},{6,4},{7,5},{8,10},{9,11},{10,... | collective-permute-start | bytes 393224 | tf_op jit(solution)/shard_map/ppermute | solution.py:1022
  98.0 4.4 %collective-permute-start.34 = (bf16[80,512]{1,0:T(8,128)(2,1)S(1)}, bf16[80,512]{1,0:T(8,128)(2,1)S(1)}, u32[]{:S(2)}, u32[]{:S(2)}) collective-permute-start(bf16[80,512]{1,0:T(8,128)(2,1)S(1)} %get-tuple-element.249.refs_3_), channel_id=1, source_target_pairs={{0,4},{1,5},{2,6},{3,7},{4,0},{5,1},{6,2},{7,3},{8,12},{9,13},{10,... | collective-permute-start | bytes 245768 | tf_op jit(solution)/shard_map/ppermute | solution.py:1022
  102.6 8.3 %collective-permute-start.38 = (bf16[208,512]{1,0:T(8,128)(2,1)S(1)}, bf16[208,512]{1,0:T(8,128)(2,1)S(1)}, u32[]{:S(2)}, u32[]{:S(2)}) collective-permute-start(bf16[208,512]{1,0:T(8,128)(2,1)S(1)} %get-tuple-element.267.refs_3_), channel_id=1, source_target_pairs={{0,8},{1,9},{2,10},{3,11},{4,12},{5,13},{6,14},{7,15},{8,0},{9,1},... | collective-permute-start | bytes 638984 | tf_op jit(solution)/shard_map/ppermute | solution.py:1022
  105.6 11.7 %collective-permute-start.39 = (bf16[2,128,512]{2,1,0:T(8,128)(2,1)S(1)}, bf16[2,128,512]{2,1,0:T(8,128)(2,1)S(1)}, u32[]{:S(2)}, u32[]{:S(2)}) collective-permute-start(bf16[2,128,512]{2,1,0:T(8,128)(2,1)S(1)} %fold.17.refs_0_), channel_id=1, source_target_pairs={{0,8},{1,9},{2,10},{3,11},{4,12},{5,13},{6,14},{7,15},{8,0},{9,1},... | collective-permute-start | bytes 786440 | tf_op jit(solution)/shard_map/ppermute | solution.py:1022
  110.9 10.6 %collective-permute-start.40 = (bf16[208,512]{1,0:T(8,128)(2,1)S(1)}, bf16[208,512]{1,0:T(8,128)(2,1)S(1)}, u32[]{:S(2)}, u32[]{:S(2)}) collective-permute-start(bf16[208,512]{1,0:T(8,128)(2,1)S(1)} %get-tuple-element.273.refs_3_), channel_id=1, source_target_pairs={{0,16},{1,17},{2,18},{3,19},{4,20},{5,21},{6,22},{7,23},{8,24},{9,... | collective-permute-start | bytes 638984 | tf_op jit(solution)/shard_map/ppermute | solution.py:1022
  117.3 14.9 %collective-permute-start.44 = (bf16[2,256,512]{2,1,0:T(8,128)(2,1)S(1)}, bf16[2,256,512]{2,1,0:T(8,128)(2,1)S(1)}, u32[]{:S(2)}, u32[]{:S(2)}) collective-permute-start(bf16[2,256,512]{2,1,0:T(8,128)(2,1)S(1)} %join.2.refs_0_), channel_id=1, source_target_pairs={{0,4},{1,5},{2,6},{3,7},{4,0},{5,1},{6,2},{7,3},{8,12},{9,13},{10,... | collective-permute-start | bytes 1572872 | tf_op jit(solution)/shard_map/ppermute | solution.py:1022
  121.5 5.0 %collective-permute-start.41 = (bf16[1,128,512]{2,1,0:T(8,128)(2,1)S(1)}, bf16[1,128,512]{2,1,0:T(8,128)(2,1)S(1)}, u32[]{:S(2)}, u32[]{:S(2)}) collective-permute-start(bf16[1,128,512]{2,1,0:T(8,128)(2,1)S(1)} %bitcast.29), channel_id=1, source_target_pairs={{0,8},{1,9},{2,10},{3,11},{4,12},{5,13},{6,14},{7,15},{8,0},{9,1},... | collective-permute-start | bytes 393224 | tf_op jit(solution)/shard_map/ppermute | solution.py:1022
  121.6 5.6 %collective-permute-start.42 = (f32[48,512]{1,0:T(8,128)S(1)}, f32[48,512]{1,0:T(8,128)S(1)}, u32[]{:S(2)}, u32[]{:S(2)}) collective-permute-start(f32[48,512]{1,0:T(8,128)S(1)} %get-tuple-element.284.refs_0_), channel_id=1, source_target_pairs={{0,2},{1,3},{2,0},{3,1},{4,6},{5,7},{6,4},{7,5},{8,10},{9,11},{10,... | collective-permute-start | bytes 294920 | tf_op jit(solution)/shard_map/ppermute | solution.py:1022
  126.6 9.3 %collective-permute-start.45 = (bf16[1,256,512]{2,1,0:T(8,128)(2,1)S(1)}, bf16[1,256,512]{2,1,0:T(8,128)(2,1)S(1)}, u32[]{:S(2)}, u32[]{:S(2)}) collective-permute-start(bf16[1,256,512]{2,1,0:T(8,128)(2,1)S(1)} %join.3.refs_0_), channel_id=1, source_target_pairs={{0,4},{1,5},{2,6},{3,7},{4,0},{5,1},{6,2},{7,3},{8,12},{9,13},{10,... | collective-permute-start | bytes 786440 | tf_op jit(solution)/shard_map/ppermute | solution.py:1022
  127.2 1.5 %collective-permute-start.43 = (f32[96,512]{1,0:T(8,128)S(1)}, f32[96,512]{1,0:T(8,128)S(1)}, u32[]{:S(2)}, u32[]{:S(2)}) collective-permute-start(f32[96,512]{1,0:T(8,128)S(1)} %pair.1.refs_4_), channel_id=1, source_target_pairs={{0,1},{1,0},{2,3},{3,2},{4,5},{5,4},{6,7},{7,6},{8,9},{9,8},{10,11... | collective-permute-start | bytes 589832 | tf_op jit(solution)/shard_map/ppermute | solution.py:1022

commit v5 on v4

--- a/solution.py
+++ b/solution.py
@@ -143,13 +143,12 @@
     return high + rest, slope
 
 
-def enter_kernel(seqs, *refs):
-    far, refs = refs[:5], refs[5:]
-    normed, par, before, ends, low, tok, gain, rate, beta, eta, nf, tab, sems = refs
-    copies = [
-        pltpu.make_async_copy(a, b, sems.at[i])
-        for i, (a, b) in enumerate(zip(far, (tok, gain, rate, beta, eta)))
-    ]
+def enter_kernel(seqs, ids, *refs):
+    count = 10
+    far, near, sems = refs[:count], refs[count + 5 : 2 * count + 5], refs[-1]
+    normed, par, before, ends, low = refs[count : count + 5]
+    tok, gain, rate, beta, eta, skip, gain2, qg, kg, rb, nf, tab = refs[count + 5 : -1]
+    copies = [pltpu.make_async_copy(a, b, sems.at[i]) for i, (a, b) in enumerate(zip(far, near))]
     for c in copies:
         c.start()
     for c in copies:
@@ -160,6 +159,12 @@
     par[1] = jnp.log(d)
     par[2] = jnp.sqrt(r * (2.0 - r)) * beta[...]
     par[3] = eta[...]
+    for i, row in enumerate((skip, gain2, gain)):
+        par[4, i : i + 1, :] = row[...]
+    for i, row in enumerate((qg, kg, rb)):
+        par[4, 3:4, i * Z : (i + 1) * Z] = row[...]
+    for s in range(seqs):
+        par[4, 4 + s : 5 + s, :] = jnp.full((1, D), ids[3 + s].astype(F32))
     d2 = d * d
     d4 = d2 * d2
     d8 = d4 * d4
@@ -257,6 +262,11 @@
         c.wait()
 
 
+def vectors(par):
+    whole = [par.at[4, pl.ds(i, 1), :] for i in range(3)]
+    return whole + [par.at[4, pl.ds(3, 1), pl.ds(i * Z, Z)] for i in range(3)]
+
+
 def piece_powers(par, pw):
     k = lax.broadcasted_iota(jnp.int32, (PIECES, D), 0).astype(F32) * PIECE
     for j in range(NDIM):
@@ -279,21 +289,24 @@
     top, cut = tp // 2, D // 2
     first = jnp.bitwise_and(ids[1], 1)
     second = jnp.bitwise_and(jnp.right_shift(ids[1], far_shift()), 1)
-    copies = []
-
-    def add(source, target):
-        copies.append(pltpu.make_async_copy(source, target, sems.at[len(copies)]))
+    copies = [[] for _ in range(tp)]
+
+    def add(r, source, target):
+        at = sems.at[sum(len(c) for c in copies)]
+        copies[r].append(pltpu.make_async_copy(source, target, at))
 
     for r in range(top):
-        add(near[r][0], w1.at[r])
-        add(near[r][1], w2.at[r])
+        add(r, near[r][0], w1.at[r])
+        add(r, near[r][1], w2.at[r])
+    for r in range(top):
         mine1, other1, mine2, other2 = far[r]
         for part, at in ((mine1, first), (other1, 1 - first)):
-            add(part, w1.at[top + r, pl.ds(pl.multiple_of(at * cut, cut), cut), :])
+            add(top + r, part, w1.at[top + r, pl.ds(pl.multiple_of(at * cut, cut), cut), :])
         for part, at in ((mine2, second), (other2, 1 - second)):
-            add(part, w2.at[top + r, :, pl.ds(pl.multiple_of(at * cut, cut), cut)])
-    for c in copies:
-        c.start()
+            add(top + r, part, w2.at[top + r, :, pl.ds(pl.multiple_of(at * cut, cut), cut)])
+    for group in copies:
+        for c in group:
+            c.start()
     return copies
 
 
@@ -306,10 +319,11 @@
 
 
 def look_kernel(
-    seqs, hops, ids, normed, par, before, skip, wsh, qg, kg, rb, *refs
+    seqs, hops, ids, normed, par, before, wsh, *refs
 ):
     recvs, refs = refs[: len(hops)], refs[len(hops) :]
     st_in, skip_pre, mixed, shared_pre, prob, nf, sm, pw = refs
+    skip, _, _, qg, kg, rb = vectors(par)
     place = ids[2]
     put_rows(nf, slice(None), normed[...].astype(F32))
     piece_powers(par, pw)
@@ -368,7 +382,7 @@
     bias = bias_t.T
     for s in range(seqs):
         raw = mm_nt(query[s * CH : (s + 1) * CH], keys[s * CH : (s + 1) * CH]) * Z ** (-0.5)
-        live = (place * CH + s_at) < ids[3 + s]
+        live = (place * CH + s_at).astype(F32) < par[4, 4 + s : 5 + s, :CH]
         allowed = (s_at <= t_at) & (live | (s_at == t_at))
         masked = jnp.where(allowed, raw + bias, -1e30)
         top = jnp.max(masked, axis=-1, keepdims=True)
@@ -385,14 +399,9 @@
     vb = values.shape[2]
     nb = D // tp
     copies = gate_copies(tp, ids, near, far, w1, w2, sems)
-    for c in copies:
-        c.wait()
-    gate_rows(tp, ids[0], w2, whu)
-    hu = mm(mixed[...], whu[...])
-    hidden_pre[...] = hu[:, :D]
-    update_pre[...] = hu[:, D:]
-
-    def block(r, carry):
+    for r in range(tp):
+        for c in copies[r]:
+            c.wait()
         vp = mm(normed[...], w1[r, :, :vb])
         value_pre[r] = vp
         v = silu(vp).astype(BF16)
@@ -404,10 +413,12 @@
             att = mm(prob[s].astype(BF16), v[s * CH : (s + 1) * CH])
             attended[r, rows_of(s), :] = att
             gated[r, rows_of(s), :] = (gate[s * CH : (s + 1) * CH] * att).astype(BF16)
-        hidden_pre[...] += mm(gated[r], w2[r, pl.ds(2 * nb, vb), :])
-        return carry
-
-    lax.fori_loop(0, tp, block, 0)
+        part = mm(gated[r], w2[r, pl.ds(2 * nb, vb), :])
+        hidden_pre[...] = hidden_pre[...] + part if r else part
+    gate_rows(tp, ids[0], w2, whu)
+    hu = mm(mixed[...], whu[...])
+    hidden_pre[...] += hu[:, :D]
+    update_pre[...] = hu[:, D:]
     for s in range(seqs):
         x = tok[s].astype(F32)
         middle[rows_of(s), :] = x + sigmoid(update_pre[rows_of(s), :]) * (
@@ -415,7 +426,8 @@
         )
 
 
-def ffn_kernel(seqs, tp, ids, tok, cot, middle, hidden_pre, update_pre, gain2, *refs):
+def ffn_kernel(seqs, tp, ids, tok, cot, middle, hidden_pre, update_pre, par, *refs):
+    gain2 = vectors(par)[1]
     near, far, refs = take_weights(refs, tp, 1, 2)
     (
         out, keep, send, grad_hu, resid, grad_gain2,
@@ -425,31 +437,36 @@
     top, half = tp // 2, D // 2
     cuts = D // vb
     upper = jnp.bitwise_and(ids[1], 1)
-    copies = []
-
-    def add(source, target):
-        copies.append(pltpu.make_async_copy(source, target, sems.at[len(copies)]))
+    copies = [[] for _ in range(tp)]
+
+    def add(r, source, target):
+        at = sems.at[sum(len(c) for c in copies)]
+        copies[r].append(pltpu.make_async_copy(source, target, at))
 
     for r in range(top):
-        add(near[r][0], w3.at[r])
+        add(r, near[r][0], w3.at[r])
+    for r in range(top):
         for part, at in zip(far[r], (upper, 1 - upper)):
-            add(part, w3.at[top + r, pl.ds(pl.multiple_of(at * half, half), half), :])
-    for c in copies:
-        c.start()
+            row = pl.ds(pl.multiple_of(at * half, half), half)
+            add(top + r, part, w3.at[top + r, row, :])
+    for group in copies:
+        for c in group:
+            c.start()
     place = ids[2]
     xhat, scale = normalized(middle[...])
     n2[...] = (xhat * gain2[...]).astype(BF16)
-    at = lax.broadcasted_iota(jnp.int32, (CH, D), 0) + place * CH
+    at = (lax.broadcasted_iota(jnp.int32, (CH, D), 0) + place * CH).astype(F32)
     for s in range(seqs):
-        lg[rows_of(s), :] = jnp.where(at < ids[3 + s], cot[s].astype(F32), 0.0).astype(BF16)
+        lg[rows_of(s), :] = jnp.where(
+            at < par[4, 4 + s : 5 + s, :], cot[s].astype(F32), 0.0
+        ).astype(BF16)
     acc[...] = jnp.zeros_like(acc)
     gn2[...] = jnp.zeros_like(gn2)
-    for c in copies:
-        c.wait()
-
-    def block(h, carry):
+    for h in range(tp // 2):
         for odd in range(2):
             r = 2 * h + odd
+            for c in copies[r]:
+                c.wait()
             grads = (keep, send)[odd]
             pre = mm(n2[...], w3[r, :, :vb])
             inner = silu(pre).astype(BF16)
@@ -466,9 +483,6 @@
             gwo = mm_tn(inner, lg[...]).astype(BF16)
             for k in range(cuts):
                 grads[h, k * vb : (k + 1) * vb, vb:] = gwo[:, k * vb : (k + 1) * vb]
-        return carry
-
-    lax.fori_loop(0, tp // 2, block, 0)
     mid = middle[...]
     out[...] = (mid + acc[...]).astype(BF16)
     grad = gn2[...]
@@ -510,8 +524,9 @@
 def back_kernel(
     seqs, tp,
     ids, normed, mixed, skip_pre, shared_pre, prob, values, value_pre, reset_pre, attended,
-    grad_hu, par, wsh, qg, kg, tok, before, st_in, skip, grad_gain2, *refs,
+    grad_hu, par, wsh, tok, before, st_in, grad_gain2, *refs,
 ):
+    skip, _, _, qg, kg, _ = vectors(par)
     near, far, refs = take_weights(refs, tp, 2, 4)
     (
         keep1, send1, grad_skip, grad_normed, after, ends, sums_keep, sums_send,
@@ -523,8 +538,9 @@
     copies = gate_copies(tp, ids, near, far, w1, w2, sems)
     gp[...] = jnp.zeros_like(gp)
     grad_normed[...] = jnp.zeros_like(grad_normed)
-    for c in copies:
-        c.wait()
+    for group in copies:
+        for c in group:
+            c.wait()
     gate_rows(tp, me, w2, whu)
     gm[...] = mm_nt(grad_hu[...], whu[...])
 
@@ -695,10 +711,11 @@
 
 
 def finish_kernel(
-    ids, par, rate, beta, gain, mine, other,
+    ids, par, rate, beta, mine, other,
     grad_gain, grad_rate, grad_beta, grad_eta, grad_skip, grad_wsh, grad_qg, grad_kg, grad_rb,
     grad_gain2, table,
 ):
+    gain = vectors(par)[2]
     pair_kernel(1, ids, mine, other, table)
     count = D // (D // Z)
     for k in range(D // Z):
@@ -722,11 +739,12 @@
 
 
 def leave_kernel(
-    seqs, tops, ids, tok, par, grad_skip, grad_normed, behind, resid, gain, skip, *refs
+    seqs, tops, ids, tok, par, grad_skip, grad_normed, behind, resid, *refs
 ):
     levels = len(tops)
     recvs, refs = refs[:levels], refs[levels:]
     grad_tokens, ad_in, pw, sm = refs
+    skip, _, gain = vectors(par)[:3]
     place = ids[2]
     logd = par[1]
     gots = [get_wide(recvs[k], tops[k], seqs * NDIM) for k in range(levels)]
@@ -836,6 +854,7 @@
 def chain_hop(seqs, level, split, halved, top, ids, par, own, kept, sent, other, out, keep, payload, base):
     rows = seqs * NDIM
     lanes = D // other.shape[1]
+    small_base = 0 if payload is None else base + rows * (D // payload.shape[1])
     if out is not None:
         join_adjoint(seqs, level, ids, par, own, get_wide(other, top, rows), out)
         put_wide(payload, base, out[...])
@@ -845,13 +864,13 @@
         got = get_wide(other, top + rows * lanes, 2 * half)
         first, second = kept[:half, :] + got[:half], kept[half:, :] + got[half:]
         keep[...] = jnp.where(upper, second, first)
-        put_wide(payload, base + rows * lanes, jnp.where(upper, first, second))
+        put_wide(payload, small_base, jnp.where(upper, first, second))
     else:
         mine = kept[...] if halved else get_wide(sent, top + rows * lanes, half)
         total = mine + get_wide(other, top + rows * lanes, half)
         keep[...] = total
         if payload is not None:
-            put_wide(payload, base + rows * lanes, total)
+            put_wide(payload, small_base, total)
 
 
 def back_hop(seqs, level, split, halved, ids, par, own, kept, sent, other, out, keep, payload):
@@ -934,6 +953,41 @@
         [SMEM, VMEM, VMEM],
         "join",
     )[0]
+
+
+def start_kernel(
+    seqs, bits, ids, par, own, other, sums, got, keep1, got1, out, keep, left, payload, right, send
+):
+    vb = keep1.shape[2] // 2
+    for b, target in enumerate((left, payload)):
+        add_rows([keep1.at[b], got1.at[b]], 0, D, target, 0, 0, vb, 0)
+    for k, target in enumerate((right, send)):
+        start, high = split_rows(D, (0, bits), ids[1], k)
+        for b in range(2):
+            add_rows([keep1.at[b], got1.at[b]], start, high, target.at[b], 0, vb, vb, 0)
+    join_adjoint(seqs, 0, ids, par, own, other[...], out)
+    rows, half = seqs * NDIM, keep.shape[0]
+    put_wide(payload, D, out[...])
+    upper = jnp.where(jnp.bitwise_and(ids[0], 2) > 0, half, 0)
+    mine = pl.ds(pl.multiple_of(upper, 8), half)
+    theirs = pl.ds(pl.multiple_of(half - upper, 8), half)
+    keep[...] = sums[mine, :] + got[mine, :]
+    put_wide(payload, D + rows * (D // vb), sums[theirs, :] + got[theirs, :])
+
+
+def cross_kernel(
+    seqs, bits, ids, par, own, kept, sent, other, left, right, got, out, keep, left_out, payload,
+    right_out, send,
+):
+    vb = left.shape[1]
+    for k, target in enumerate((left_out, payload)):
+        start, high = split_rows(D, (0, bits), ids[1], k)
+        add_rows([left, other], start, high, target, 0, 0, vb, 0)
+    for b, target in enumerate((right_out, send)):
+        add_rows([right.at[b], got.at[b]], 0, high, target, 0, 0, vb, 0)
+    chain_hop(
+        seqs, 1, 0, True, D, ids, par, own, kept, sent, other, out, keep, payload, high
+    )
 
 
 def ride_kernel(
@@ -1128,7 +1182,7 @@
         functools.partial(enter_kernel, seqs),
         (
             shape((rows, D), BF16),
-            shape((4, NDIM, D)),
+            shape((5, NDIM, D)),
             shape((2, seqs, NDIM, PIECES, D)),
             shape((2 * seqs + 1, NDIM, D)),
             shape((3 * seqs, NDIM, D), BF16),
@@ -1139,12 +1193,17 @@
             pltpu.VMEM((NDIM, D), F32),
             pltpu.VMEM((NDIM, D), F32),
             pltpu.VMEM((NDIM, D), F32),
+            pltpu.VMEM((1, D), F32),
+            pltpu.VMEM((1, D), F32),
+            pltpu.VMEM((1, Z), F32),
+            pltpu.VMEM((1, Z), F32),
+            pltpu.VMEM((1, Z), F32),
             pltpu.VMEM((BLOCKS, rows, LANES), F32),
             pltpu.VMEM((6, NDIM, D), F32),
-            pltpu.SemaphoreType.DMA((5,)),
+            pltpu.SemaphoreType.DMA((10,)),
         ],
-        (tok, gain1, rate, beta, ema_eta.T),
-        [ANY] * 5,
+        (ids_lengths, tok, gain1, rate, beta, ema_eta.T, skip, gain2, qg, kg, rb),
+        [SMEM] + [ANY] * 10,
         "enter",
         limit=12,
     )
@@ -1219,10 +1278,10 @@
             pltpu.VMEM((NDIM, PIECES, D), F32),
         ],
         (
-            ids_lengths, after(normed, mine3), par, before, skip, w_shared, qg, kg, rb,
+            ids, after(normed, mine3), par, before, w_shared,
             *[h[2] for h in hops],
         ),
-        [SMEM] + [VMEM] * (8 + len(hops)),
+        [SMEM] + [VMEM] * (4 + len(hops)),
         "look",
         limit=10,
     )
@@ -1274,7 +1333,7 @@
             pltpu.VMEM((rows, D), F32),
             pltpu.SemaphoreType.DMA((3 * tp // 2,)),
         ],
-        (ids_lengths, tok, cot, middle, hidden_pre, update_pre, gain2, *feeds),
+        (ids, tok, cot, middle, hidden_pre, update_pre, par, *feeds),
         [SMEM] + [VMEM] * 6 + [ANY] * len(feeds),
         "ffn",
         limit=10,
@@ -1365,10 +1424,10 @@
         ],
         (
             ids, normed, mixed, skip_pre, shared_pre, prob, values, value_pre, reset_pre, attended,
-            after(grad_hu, g2[0]), par, w_shared, qg, kg, tok, before, st_in, skip, grad_gain2,
+            after(grad_hu, g2[0]), par, w_shared, tok, before, st_in, grad_gain2,
             *gates,
         ),
-        [SMEM] + [VMEM] * 19 + [ANY] * len(gates),
+        [SMEM] + [VMEM] * 16 + [ANY] * len(gates),
         "back",
         limit=12,
     )
@@ -1427,74 +1486,116 @@
         def payload_rows():
             return (ad_rows + small_high) * runs
 
-        own, kept, payload = call(
-            functools.partial(first_back_hop, seqs, not traded),
-            (
-                shape((ad_rows, D)),
-                shape((small_high, D)),
-                shape((payload_rows(), wide), BF16),
-            ),
-            [],
-            (ids, par, now(adjoint), got_adjoint, sums_keep, got_sums),
-            [SMEM] + [VMEM] * 5,
-            "hop",
-        )
-        got = [] if traded else [(got_adjoint, 0)]
-        level = int(not traded)
-        halved = True
-        other = swap(payload, masks[level])
-        yield payload
-        parts = fold(
-            ids,
-            [(1, D, vb)] * half + [(half, D // yn, vb)] * yn,
-            [
-                ([now(keep1), got1], 0, vb, "tp", [(k, 0, 0) for k in range(half)]),
-                ([keep1, got1], vb, vb, cut_of_y, [(half + k, 0, 0) for k in range(yn)]),
-            ],
-        )
-        left, right = over_tp(parts[:half]), over_y(parts[half:])
-        yield parts[0]
-        crossed = False
-        while level + 1 < levels - len(zcuts):
-            got.append((other, 0))
-            split = 2 * masks[level] if 2 * masks[level] < tp else 0
-            small_high = small_high // 2 if split else small_high
+        together = half == 2 and yn == 2 and not traded
+        if together:
+            lanes = D // vb
+            own, kept, left, payload, right, send = call(
+                functools.partial(start_kernel, seqs, ybits),
+                (
+                    shape((ad_rows, D)),
+                    shape((small_high, D)),
+                    shape((D, vb), BF16),
+                    shape((D + (ad_rows + small_high) * lanes, vb), BF16),
+                    shape((2, D // 2, vb), BF16),
+                    shape((2, D // 2, vb), BF16),
+                ),
+                [],
+                (ids, par, now(adjoint), got_adjoint, sums_keep, got_sums, keep1, got1),
+                [SMEM] + [VMEM] * 7,
+                "start",
+            )
+            other, got_right = swap(payload, 2), swap(send, tp)
+            got = [(got_adjoint, 0), (other, D)]
+            yield payload
+            own, kept, left, payload, right, send = call(
+                functools.partial(cross_kernel, seqs, ybits),
+                (
+                    shape((ad_rows, D)),
+                    shape((small_high, D)),
+                    shape((D // 2, vb), BF16),
+                    shape((D // 2 + (ad_rows + small_high) * lanes, vb), BF16),
+                    shape((D // 2, vb), BF16),
+                    shape((D // 2, vb), BF16),
+                ),
+                [],
+                (ids, par, now(own), kept, payload, other, left, right, got_right),
+                [SMEM] + [VMEM] * 8,
+                "cross",
+            )
+            other, got_right = swap(payload, tp), swap(send, 2)
+            level, top, halved = 2, D // 2, False
+            flat = [left, right, got_right]
+            jobs = [((0, -1), vb, 0), ((1, 2), vb, vb)]
+            yield payload
+        else:
             own, kept, payload = call(
-                functools.partial(back_hop, seqs, level, split, halved),
+                functools.partial(first_back_hop, seqs, not traded),
                 (
                     shape((ad_rows, D)),
                     shape((small_high, D)),
                     shape((payload_rows(), wide), BF16),
                 ),
                 [],
-                (ids, par, now(own), kept, payload, other),
+                (ids, par, now(adjoint), got_adjoint, sums_keep, got_sums),
                 [SMEM] + [VMEM] * 5,
                 "hop",
             )
-            halved = bool(split)
-            level += 1
+            got = [] if traded else [(got_adjoint, 0)]
+            level = int(not traded)
+            halved = True
             other = swap(payload, masks[level])
             yield payload
-            if crossed:
-                continue
-            crossed = True
             parts = fold(
                 ids,
-                [(1, D // yn, vb)] * (yn + half),
+                [(1, D, vb)] * half + [(half, D // yn, vb)] * yn,
                 [
-                    ([now(left[0])] + left[1:], 0, vb, cut_of_y, [(k, 0, 0) for k in range(yn)]),
-                    (right, 0, vb, "tp", [(yn + k, 0, 0) for k in range(half)]),
+                    ([now(keep1), got1], 0, vb, "tp", [(k, 0, 0) for k in range(half)]),
+                    ([keep1, got1], vb, vb, cut_of_y, [(half + k, 0, 0) for k in range(yn)]),
                 ],
             )
-            left, right = over_y(parts[:yn]), over_tp(parts[yn:])
+            left, right = over_tp(parts[:half]), over_y(parts[half:])
             yield parts[0]
+            crossed = False
+            while level + 1 < levels - len(zcuts):
+                got.append((other, 0))
+                split = 2 * masks[level] if 2 * masks[level] < tp else 0
+                small_high = small_high // 2 if split else small_high
+                own, kept, payload = call(
+                    functools.partial(back_hop, seqs, level, split, halved),
+                    (
+                        shape((ad_rows, D)),
+                        shape((small_high, D)),
+                        shape((payload_rows(), wide), BF16),
+                    ),
+                    [],
+                    (ids, par, now(own), kept, payload, other),
+                    [SMEM] + [VMEM] * 5,
+                    "hop",
+                )
+                halved = bool(split)
+                level += 1
+                other = swap(payload, masks[level])
+                yield payload
+                if crossed:
+                    continue
+                crossed = True
+                parts = fold(
+                    ids,
+                    [(1, D // yn, vb)] * (yn + half),
+                    [
+                        ([now(left[0])] + left[1:], 0, vb, cut_of_y, [(k, 0, 0) for k in range(yn)]),
+                        (right, 0, vb, "tp", [(yn + k, 0, 0) for k in range(half)]),
+                    ],
+                )
+                left, right = over_y(parts[:yn]), over_tp(parts[yn:])
+                yield parts[0]
+            top = 0
+            flat = [p.reshape(p.shape[1:]) for p in left + right]
+            jobs = [
+                (tuple(range(len(left))), vb, 0),
+                (tuple(range(len(left), len(flat))), vb, vb),
+            ]
         high = D // yn
-        top = 0
-        flat = [p.reshape(p.shape[1:]) for p in left + right]
-        jobs = [
-            (tuple(range(len(left))), vb, 0),
-            (tuple(range(len(left), len(flat))), vb, vb),
-        ]
         for cut in zcuts[:-1] + [None]:
             got.append((other, top))
             high = high // 2 if cut else high
@@ -1543,10 +1644,10 @@
                 pltpu.VMEM((BLOCKS, rows, LANES), F32),
             ],
             (
-                ids, tok, par, now(grad_skip), grad_normed, behind, resid, gain1, skip,
+                ids, tok, par, now(grad_skip), grad_normed, behind, resid,
                 *[g for g, _ in got],
             ),
-            [SMEM] + [VMEM] * (8 + levels),
+            [SMEM] + [VMEM] * (6 + levels),
             "leave",
             limit=10,
         )
@@ -1584,8 +1685,8 @@
                 shape((1, D)),
             ),
             [pltpu.VMEM((count, D), F32)],
-            (ids, par, rate, beta, gain1, now(kept), far),
-            [SMEM] + [VMEM] * 6,
+            (ids, par, rate, beta, now(kept), far),
+            [SMEM] + [VMEM] * 5,
             "finish",
         )
         yield done["small"][0]
@@ -1595,7 +1696,7 @@
         yield done["second"][0]
 
     walks = {"f": first_chunks(), "s": second_chunk()}
-    order = "sssfsfsfsfsssssfs"
+    order = "sfsfssffssssfss"
 
     def advance(name):
         try:

time: 137 us -> 133 us (0.971)
  waiting for transfers between devices: 57.3 us -> 52 us
  starting transfers between devices: 37.6 us -> 42 us
  Pallas kernels: 38.9 us -> 37.1 us
    ppermute x46 -> x44, waiting for transfers between devices: 57.3 us -> 52 us  [swap(): return lax.ppermute(value, BOTH, [(i, i ^ mask) for i in range(count)])]
    ppermute x46 -> x44, starting transfers between devices: 37.6 us -> 42 us  [swap(): return lax.ppermute(value, BOTH, [(i, i ^ mask) for i in range(count)])]
    pallas_call x32 -> x30, Pallas kernels: 38.9 us -> 37.1 us  [call(): pl.pallas_call(body, out_shape=out, in_specs=specs, out_specs=outs or jax...]
  transfers between devices with their start and end apart: 46 -> 44, of which waited for: 26 -> 23; matrix products, arithmetic and copies ran while one was open for 0% -> 0% of each run, Pallas kernels for 22% -> 23%
where the time goes in v5:
time: 133 us
  waiting for transfers between devices  52 us (39%)
  starting transfers between devices  42 us (32%)
  Pallas kernels  37.1 us (28%)
    ppermute x44, waiting for transfers between devices, swap(): return lax.ppermute(value, BOTH, [(i, i ^ mask) for i in range(count)])  52 us
    ppermute x44, starting transfers between devices, swap(): return lax.ppermute(value, BOTH, [(i, i ^ mask) for i in range(count)])  42 us
    pallas_call x30, Pallas kernels, call(): pl.pallas_call(body, out_shape=out, in_specs=specs, out_specs=outs or jax...  37.1 us
  transfers between devices with their start and end apart: 44, of which 23 were waited for; matrix products, arithmetic and copies ran while one was open for 0% of the time, Pallas kernels for 23%

profile of v5, /device:TPU:0, one launch (start us, length us, event | category | flops | bytes accessed | tf_op | source)
XLA Modules:
  0.0 133.0 jit_solution(5448185286567513911)
XLA Ops:
  0.7 1.7 %half.1 = bf16[256,512]{1,0:T(8,128)(2,1)} custom-call(bf16[512,256]{1,0:T(8,128)(2,1)} %w_value.2, bf16[512,256]{1,0:T(8,128)(2,1)} %w_reset.2), custom_call_target="tpu_custom_call" | custom-call | tf_op jit(solution)/shard_map/half/pallas_call | solution.py:118
  2.4 3.0 %collective-permute-start.1 = (bf16[256,512]{1,0:T(8,128)(2,1)}, bf16[256,512]{1,0:T(8,128)(2,1)S(1)}, u32[]{:S(2)}, u32[]{:S(2)}) collective-permute-start(bf16[256,512]{1,0:T(8,128)(2,1)} %half.1), channel_id=1, source_target_pairs={{0,2},{1,3},{2,0},{3,1},{4,6},{5,7},{6,4},{7,5},{8,10},{9,11},{10,... | collective-permute-start | bytes 786440 | tf_op jit(solution)/shard_map/ppermute | solution.py:1076
  5.5 0.6 copy-done.11
  6.2 3.0 %enter.1 = (bf16[256,512]{1,0:T(8,128)(2,1)S(1)}, f32[5,16,512]{2,1,0:T(8,128)S(1)}, f32[2,2,16,8,512]{4,3,2,1,0:T(8,128)S(1)}, f32[5,16,512]{2,1,0:T(8,128)S(1)}, bf16[6,16,512]{2,1,0:T(8,128)(2,1)S(1)}) custom-call(s32[2]{0:T(128)S(1)} %copy-done.12, bf16[2,128,512]{2,1,0:T(8,128)(2,1)S(1)} %copy-done, f32[1,512]{1,0:T(1,128)S(1)} %bitcast.30, ...), custom_call_target="tpu_custom_call" | custom-call | tf_op jit(solution)/shard_map/enter/pallas_call | solution.py:118
  9.3 1.3 collective-permute-done.refs_1_.refs_4_
  10.7 1.3 collective-permute-done.1.refs_8_.refs_20_
  12.0 2.7 %collective-permute-start.4 = (bf16[6,16,512]{2,1,0:T(8,128)(2,1)S(1)}, bf16[6,16,512]{2,1,0:T(8,128)(2,1)S(1)}, u32[]{:S(2)}, u32[]{:S(2)}) collective-permute-start(bf16[6,16,512]{2,1,0:T(8,128)(2,1)S(1)} %get-tuple-element.162), channel_id=1, source_target_pairs={{0,6},{1,7},{2,4},{3,5},{4,2},{5,3},{6,0},{7,1},{8,14},{9,15},{10,... | collective-permute-start | bytes 294920 | tf_op jit(solution)/shard_map/ppermute | solution.py:1076
  14.7 0.5 collective-permute-start.3
  15.4 2.9 %pack.1 = (bf16[512,512]{1,0:T(8,128)(2,1)}, bf16[512,512]{1,0:T(8,128)(2,1)}, bf16[512,512]{1,0:T(8,128)(2,1)}, bf16[512,256]{1,0:T(8,128)(2,1)}, bf16[256,512]{1,0:T(8,128)(2,1)}) custom-call(bf16[512,256]{1,0:T(8,128)(2,1)} %w_value.2, bf16[512,256]{1,0:T(8,128)(2,1)} %w_reset.2, bf16[128,512]{1,0:T(8,128)(2,1)} %w_hidden, bf16[128,512]{1,0:T(8,128)(2,1)} %w_update, ...), custom_call_target="tpu_custom_call" | custom-call | tf_op jit(solution)/shard_map/pack/pallas_call | solution.py:118
  18.4 0.9 collective-permute-done.3.refs_2_.refs_6_
  19.3 0.5 collective-permute-done.2.refs_1_.refs_5_
  20.5 1.5 %collective-permute-start.7 = (bf16[256,512]{1,0:T(8,128)(2,1)S(1)}, bf16[256,512]{1,0:T(8,128)(2,1)S(1)}, u32[]{:S(2)}, u32[]{:S(2)}) collective-permute-start(bf16[256,512]{1,0:T(8,128)(2,1)S(1)} %collective-permute-done.1.refs_8_.refs_20_), channel_id=1, source_target_pairs={{0,4},{1,5},{2,6},{3,7},{4,0},{5,1},{6,2},{7,3},{8,12},{9,13},{10,... | collective-permute-start | bytes 786440 | tf_op jit(solution)/shard_map/ppermute | solution.py:1076
  22.0 0.5 collective-permute-start.6
  22.5 1.6 %collective-permute-start.5 = (bf16[6,16,512]{2,1,0:T(8,128)(2,1)S(1)}, bf16[6,16,512]{2,1,0:T(8,128)(2,1)S(1)}, u32[]{:S(2)}, u32[]{:S(2)}) collective-permute-start(bf16[6,16,512]{2,1,0:T(8,128)(2,1)S(1)} %get-tuple-element.173), channel_id=1, source_target_pairs={{0,8},{1,9},{2,10},{3,11},{4,12},{5,13},{6,14},{7,15},{8,0},{9,1},... | collective-permute-start | bytes 294920 | tf_op jit(solution)/shard_map/ppermute | solution.py:1076
  24.1 3.0 %collective-permute-done.5.refs_1_.refs_8_ = bf16[6,16,512]{2,1,0:T(8,128)(2,1)S(1)} collective-permute-done((bf16[6,16,512]{2,1,0:T(8,128)(2,1)S(1)}, bf16[6,16,512]{2,1,0:T(8,128)(2,1)S(1)}, u32[]{:S(2)}, u32[]{:S(2)}) %collective-permute-start.5) | collective-permute-done | bytes 98336 | tf_op jit(solution)/shard_map/ppermute | solution.py:1076
  27.2 0.7 hop.5
  27.9 0.9 collective-permute-done.7.refs_9_.refs_21_
  28.8 1.4 %collective-permute-done.6.refs_10_.refs_22_ = bf16[512,256]{1,0:T(8,128)(2,1)S(1)} collective-permute-done((bf16[512,256]{1,0:T(8,128)(2,1)}, bf16[512,256]{1,0:T(8,128)(2,1)S(1)}, u32[]{:S(2)}, u32[]{:S(2)}) %collective-permute-start.6) | collective-permute-done | bytes 262176 | tf_op jit(solution)/shard_map/ppermute | solution.py:1076
  30.2 0.5 collective-permute-start.10
  30.8 2.6 %collective-permute-start.11 = (bf16[6,16,512]{2,1,0:T(8,128)(2,1)S(1)}, bf16[6,16,512]{2,1,0:T(8,128)(2,1)S(1)}, u32[]{:S(2)}, u32[]{:S(2)}) collective-permute-start(bf16[6,16,512]{2,1,0:T(8,128)(2,1)S(1)} %get-tuple-element.182), channel_id=1, source_target_pairs={{0,16},{1,17},{2,18},{3,19},{4,20},{5,21},{6,22},{7,23},{8,24},{9,... | collective-permute-start | bytes 294920 | tf_op jit(solution)/shard_map/ppermute | solution.py:1076
  33.3 1.6 %collective-permute-start.13 = (bf16[512,256]{1,0:T(8,128)(2,1)S(1)}, bf16[512,256]{1,0:T(8,128)(2,1)S(1)}, u32[]{:S(2)}, u32[]{:S(2)}) collective-permute-start(bf16[512,256]{1,0:T(8,128)(2,1)S(1)} %collective-permute-done.6.refs_10_.refs_22_), channel_id=1, source_target_pairs={{0,8},{1,9},{2,10},{3,11},{4,12},{5,13},{6,14},{7,15},{8,0},{9,1},... | collective-permute-start | bytes 786440 | tf_op jit(solution)/shard_map/ppermute | solution.py:1076
  34.9 0.5 collective-permute-start.16
  35.4 2.1 %collective-permute-done.10.refs_8_ = bf16[256,512]{1,0:T(8,128)(2,1)S(1)} collective-permute-done((bf16[256,512]{1,0:T(8,128)(2,1)}, bf16[256,512]{1,0:T(8,128)(2,1)S(1)}, u32[]{:S(2)}, u32[]{:S(2)}) %collective-permute-start.10) | collective-permute-done | bytes 262176 | tf_op jit(solution)/shard_map/ppermute | solution.py:1076
  37.6 0.5 collective-permute-start.12
  38.1 2.4 %look.1 = (f32[2,2,16,512]{3,2,1,0:T(8,128)S(1)}, f32[256,512]{1,0:T(8,128)S(1)}, bf16[256,512]{1,0:T(8,128)(2,1)S(1)}, f32[256,128]{1,0:T(8,128)S(1)}, f32[2,128,128]{2,1,0:T(8,128)S(1)}) custom-call(bf16[256,512]{1,0:T(8,128)(2,1)S(1)} %get-tuple-element.184.refs_0_.refs_1_, f32[5,16,512]{2,1,0:T(8,128)S(1)} %get-tuple-element.185.refs_1_.refs_5_.refs_10_.refs_0_, ...), custom_call_target="tpu_custom_call" | custom-call | tf_op jit(solution)/shard_map/look/pallas_call | solution.py:118
  41.6 2.3 %collective-permute-done.12.refs_9_ = bf16[256,512]{1,0:T(8,128)(2,1)S(1)} collective-permute-done((bf16[256,512]{1,0:T(8,128)(2,1)S(1)}, bf16[256,512]{1,0:T(8,128)(2,1)S(1)}, u32[]{:S(2)}, u32[]{:S(2)}) %collective-permute-start.12) | collective-permute-done | bytes 262176 | tf_op jit(solution)/shard_map/ppermute | solution.py:1076
  44.0 2.9 %mix.1 = (bf16[4,256,256]{2,1,0:T(8,128)(2,1)S(1)}, f32[4,256,256]{2,1,0:T(8,128)S(1)}, f32[4,256,256]{2,1,0:T(8,128)S(1)}, f32[4,256,256]{2,1,0:T(8,128)S(1)}, ...) custom-call(bf16[2,128,512]{2,1,0:T(8,128)(2,1)S(1)} %copy-done, ...), custom_call_target="tpu_custom_call" | custom-call | tf_op jit(solution)/shard_map/mix/pallas_call | solution.py:118
  46.9 4.1 %ffn.1 = (bf16[256,512]{1,0:T(8,128)(2,1)}, bf16[2,512,512]{2,1,0:T(8,128)(2,1)S(1)}, bf16[2,512,512]{2,1,0:T(8,128)(2,1)S(1)}, bf16[256,1024]{1,0:T(8,128)(2,1)...) custom-call(bf16[2,128,512]{2,1,0:T(8,128)(2,1)S(1)} %copy-done, bf16[2,128,512]{2,1,0:T(8,128)(2,1)S(1)} %copy-done.5, ...), custom_call_target="tpu_custom_call" | custom-call | tf_op jit(solution)/shard_map/ffn/pallas_call | solution.py:118
  51.0 0.6 collective-permute-start.22
  51.5 1.1 gates.1
  52.8 1.1 collective-permute-done.22.refs_1_
  54.2 1.3 collective-permute-start.23
  55.8 0.6 collective-permute-start.24
  56.4 9.8 %back.1 = (bf16[2,512,512]{2,1,0:T(8,128)(2,1)S(1)}, bf16[2,512,512]{2,1,0:T(8,128)(2,1)S(1)}, f32[4,256,128]{2,1,0:T(8,128)S(1)}, f32[256,512]{1,0:T(8,128)S(1)...) custom-call(bf16[256,512]{1,0:T(8,128)(2,1)S(1)} %get-tuple-element., ...), custom_call_target="tpu_custom_call" | custom-call | tf_op jit(solution)/shard_map/back/pallas_call | solution.py:118
  66.2 2.2 %collective-permute-done.23.refs_1_ = bf16[1,512,512]{2,1,0:T(8,128)(2,1)S(1)} collective-permute-done((bf16[1,512,512]{2,1,0:T(8,128)(2,1)S(1)}, bf16[1,512,512]{2,1,0:T(8,128)(2,1)S(1)}, u32[]{:S(2)}, u32[]{:S(2)}) %collective-permute-start.23) | collective-permute-done | bytes 524320 | tf_op jit(solution)/shard_map/ppermute | solution.py:1076
  68.6 1.3 %collective-permute-done.24.refs_1_ = bf16[2,256,512]{2,1,0:T(8,128)(2,1)S(1)} collective-permute-done((bf16[2,256,512]{2,1,0:T(8,128)(2,1)S(1)}, bf16[2,256,512]{2,1,0:T(8,128)(2,1)S(1)}, u32[]{:S(2)}, u32[]{:S(2)}) %collective-permute-start.24) | collective-permute-done | bytes 524320 | tf_op jit(solution)/shard_map/ppermute | solution.py:1076
  70.8 0.5 collective-permute-start.28
  71.3 1.2 collective-permute-start.29
  72.5 0.7 collective-permute-done.25.refs_2_.refs_6_
  73.7 1.3 collective-permute-start.30
  74.9 0.5 collective-permute-start.31
  75.5 4.4 %collective-permute-done.28.refs_1_ = bf16[1,256,512]{2,1,0:T(8,128)(2,1)S(1)} collective-permute-done((bf16[1,256,512]{2,1,0:T(8,128)(2,1)S(1)}, bf16[1,256,512]{2,1,0:T(8,128)(2,1)S(1)}, u32[]{:S(2)}, u32[]{:S(2)}) %collective-permute-start.28) | collective-permute-done | bytes 262176 | tf_op jit(solution)/shard_map/ppermute | solution.py:1076
  79.9 0.6 collective-permute-done.29.refs_3_
  80.6 1.6 %collective-permute-start.32 = (bf16[2,128,512]{2,1,0:T(8,128)(2,1)S(1)}, bf16[2,128,512]{2,1,0:T(8,128)(2,1)S(1)}, u32[]{:S(2)}, u32[]{:S(2)}) collective-permute-start(bf16[2,128,512]{2,1,0:T(8,128)(2,1)S(1)} %get-tuple-element.252), channel_id=1, source_target_pairs={{0,8},{1,9},{2,10},{3,11},{4,12},{5,13},{6,14},{7,15},{8,0},{9,1},... | collective-permute-start | bytes 786440 | tf_op jit(solution)/shard_map/ppermute | solution.py:1076
  82.2 2.8 %collective-permute-done.31.refs_7_ = bf16[2,256,256]{2,1,0:T(8,128)(2,1)S(1)} collective-permute-done((bf16[2,256,256]{2,1,0:T(8,128)(2,1)S(1)}, bf16[2,256,256]{2,1,0:T(8,128)(2,1)S(1)}, u32[]{:S(2)}, u32[]{:S(2)}) %collective-permute-start.31) | collective-permute-done | bytes 262176 | tf_op jit(solution)/shard_map/ppermute | solution.py:1076
  85.0 2.0 %collective-permute-done.30.refs_4_.refs_7_ = bf16[672,256]{1,0:T(8,128)(2,1)S(1)} collective-permute-done((bf16[672,256]{1,0:T(8,128)(2,1)S(1)}, bf16[672,256]{1,0:T(8,128)(2,1)S(1)}, u32[]{:S(2)}, u32[]{:S(2)}) %collective-permute-start.30) | collective-permute-done | bytes 344096 | tf_op jit(solution)/shard_map/ppermute | solution.py:1076
  87.3 1.6 %collective-permute-start.33 = (bf16[416,256]{1,0:T(8,128)(2,1)S(1)}, bf16[416,256]{1,0:T(8,128)(2,1)S(1)}, u32[]{:S(2)}, u32[]{:S(2)}) collective-permute-start(bf16[416,256]{1,0:T(8,128)(2,1)S(1)} %get-tuple-element.250.refs_3_), channel_id=1, source_target_pairs={{0,4},{1,5},{2,6},{3,7},{4,0},{5,1},{6,2},{7,3},{8,12},{9,13},{10,... | collective-permute-start | bytes 638984 | tf_op jit(solution)/shard_map/ppermute | solution.py:1076
  88.8 1.2 collective-permute-start.34
  90.1 2.1 %collective-permute-start.36 = (bf16[2,128,512]{2,1,0:T(8,128)(2,1)S(1)}, bf16[2,128,512]{2,1,0:T(8,128)(2,1)S(1)}, u32[]{:S(2)}, u32[]{:S(2)}) collective-permute-start(bf16[2,128,512]{2,1,0:T(8,128)(2,1)S(1)} %fold.12.refs_0_), channel_id=1, source_target_pairs={{0,16},{1,17},{2,18},{3,19},{4,20},{5,21},{6,22},{7,23},{8,24},{9,... | collective-permute-start | bytes 786440 | tf_op jit(solution)/shard_map/ppermute | solution.py:1076
  92.2 1.6 %collective-permute-done.34.refs_7_ = bf16[256,256]{1,0:T(8,128)(2,1)S(1)} collective-permute-done((bf16[256,256]{1,0:T(8,128)(2,1)S(1)}, bf16[256,256]{1,0:T(8,128)(2,1)S(1)}, u32[]{:S(2)}, u32[]{:S(2)}) %collective-permute-start.34) | collective-permute-done | bytes 131104 | tf_op jit(solution)/shard_map/ppermute | solution.py:1076
  94.0 1.6 %collective-permute-start.35 = (bf16[208,512]{1,0:T(8,128)(2,1)S(1)}, bf16[208,512]{1,0:T(8,128)(2,1)S(1)}, u32[]{:S(2)}, u32[]{:S(2)}) collective-permute-start(bf16[208,512]{1,0:T(8,128)(2,1)S(1)} %get-tuple-element.259.refs_3_), channel_id=1, source_target_pairs={{0,8},{1,9},{2,10},{3,11},{4,12},{5,13},{6,14},{7,15},{8,0},{9,1},... | collective-permute-start | bytes 638984 | tf_op jit(solution)/shard_map/ppermute | solution.py:1076
  95.6 9.2 %collective-permute-done.35.refs_4_.refs_9_ = bf16[208,512]{1,0:T(8,128)(2,1)S(1)} collective-permute-done((bf16[208,512]{1,0:T(8,128)(2,1)S(1)}, bf16[208,512]{1,0:T(8,128)(2,1)S(1)}, u32[]{:S(2)}, u32[]{:S(2)}) %collective-permute-start.35) | collective-permute-done | bytes 213024 | tf_op jit(solution)/shard_map/ppermute | solution.py:1076
  105.0 4.5 %collective-permute-start.38 = (bf16[208,512]{1,0:T(8,128)(2,1)S(1)}, bf16[208,512]{1,0:T(8,128)(2,1)S(1)}, u32[]{:S(2)}, u32[]{:S(2)}) collective-permute-start(bf16[208,512]{1,0:T(8,128)(2,1)S(1)} %get-tuple-element.264.refs_3_), channel_id=1, source_target_pairs={{0,16},{1,17},{2,18},{3,19},{4,20},{5,21},{6,22},{7,23},{8,24},{9,... | collective-permute-start | bytes 638984 | tf_op jit(solution)/shard_map/ppermute | solution.py:1076
  109.5 6.6 %collective-permute-done.37.refs_1_ = bf16[2,128,512]{2,1,0:T(8,128)(2,1)S(1)} collective-permute-done((bf16[2,128,512]{2,1,0:T(8,128)(2,1)S(1)}, bf16[2,128,512]{2,1,0:T(8,128)(2,1)S(1)}, u32[]{:S(2)}, u32[]{:S(2)}) %collective-permute-start.37) | collective-permute-done | bytes 262176 | tf_op jit(solution)/shard_map/ppermute | solution.py:1076
  116.2 1.2 collective-permute-start.41
  117.5 1.8 %collective-permute-start.39 = (bf16[1,128,512]{2,1,0:T(8,128)(2,1)S(1)}, bf16[1,128,512]{2,1,0:T(8,128)(2,1)S(1)}, u32[]{:S(2)}, u32[]{:S(2)}) collective-permute-start(bf16[1,128,512]{2,1,0:T(8,128)(2,1)S(1)} %bitcast.25), channel_id=1, source_target_pairs={{0,8},{1,9},{2,10},{3,11},{4,12},{5,13},{6,14},{7,15},{8,0},{9,1},... | collective-permute-start | bytes 393224 | tf_op jit(solution)/shard_map/ppermute | solution.py:1076
  119.3 0.6 collective-permute-start.40
  119.9 2.6 %leave.1 = bf16[2,128,512]{2,1,0:T(8,128)(2,1)} custom-call(bf16[2,128,512]{2,1,0:T(8,128)(2,1)S(1)} %copy-done, f32[5,16,512]{2,1,0:T(8,128)S(1)} %get-tuple-element.185.refs_1_.refs_5_.refs_10_.refs_0_, f32[4,256,128]{2,1,0:T(8,128)S(1)} %get-tuple-element.270.refs_2_, f32[256,512]{1,0:T(8,128)S(1)} %get-tuple-element.271.refs_3_, ...), custom_call_target="tpu_custom_call" | custom-call | tf_op jit(solution)/shard_map/leave/pallas_call | solution.py:118
  122.6 1.7 %collective-permute-start.43 = (bf16[1,256,512]{2,1,0:T(8,128)(2,1)S(1)}, bf16[1,256,512]{2,1,0:T(8,128)(2,1)S(1)}, u32[]{:S(2)}, u32[]{:S(2)}) collective-permute-start(bf16[1,256,512]{2,1,0:T(8,128)(2,1)S(1)} %join.3.refs_0_), channel_id=1, source_target_pairs={{0,4},{1,5},{2,6},{3,7},{4,0},{5,1},{6,2},{7,3},{8,12},{9,13},{10,... | collective-permute-start | bytes 786440 | tf_op jit(solution)/shard_map/ppermute | solution.py:1076
  124.4 4.7 %collective-permute-done.41.refs_1_ = bf16[2,256,512]{2,1,0:T(8,128)(2,1)S(1)} collective-permute-done((bf16[2,256,512]{2,1,0:T(8,128)(2,1)S(1)}, bf16[2,256,512]{2,1,0:T(8,128)(2,1)S(1)}, u32[]{:S(2)}, u32[]{:S(2)}) %collective-permute-start.41) | collective-permute-done | bytes 524320 | tf_op jit(solution)/shard_map/ppermute | solution.py:1076
  129.1 1.5 %unpack.2 = (f32[512,256]{1,0:T(8,128)}, f32[256,512]{1,0:T(8,128)}, f32[128,512]{1,0:T(8,128)}, f32[128,512]{1,0:T(8,128)}, f32[256,512]{1,0:T(8,128)}) custom-call(bf16[2,256,512]{2,1,0:T(8,128)(2,1)S(1)} %join.2.refs_0_, bf16[2,256,512]{2,1,0:T(8,128)(2,1)S(1)} %collective-permute-done.41.refs_1_), custom_call_target="tpu_custom_call" | custom-call | tf_op jit(solution)/shard_map/unpack/pallas_call | solution.py:118
  130.6 0.8 finish.1
  131.4 0.5 collective-permute-done.43.refs_1_
  131.9 1.0 unpack.3
  (86 shorter events, 5.5 us)
Async XLA Ops:
  0.7 4.8 %copy-start = (bf16[2,128,512]{2,1,0:T(8,128)(2,1)S(1)}, bf16[2,128,512]{2,1,0:T(8,128)(2,1)}, u32[]{:S(2)}) copy-start(bf16[2,128,512]{2,1,0:T(8,128)(2,1)} %refs_0_.7) | copy-start | bytes 786436
  0.7 4.8 %copy-start.6 = (f32[512,16]{0,1:T(8,128)S(1)}, f32[512,16]{0,1:T(8,128)}, u32[]{:S(2)}) copy-start(f32[512,16]{0,1:T(8,128)} %param.24) | copy-start | bytes 98308
  0.7 4.8 %copy-start.7 = (f32[512,16]{0,1:T(8,128)S(1)}, f32[512,16]{0,1:T(8,128)}, u32[]{:S(2)}) copy-start(f32[512,16]{0,1:T(8,128)} %param.25) | copy-start | bytes 98308
  0.7 4.8 %copy-start.8 = (f32[512,16]{0,1:T(8,128)S(1)}, f32[512,16]{0,1:T(8,128)}, u32[]{:S(2)}) copy-start(f32[512,16]{0,1:T(8,128)} %param.26) | copy-start | bytes 98308
  2.4 9.5 %collective-permute-start.1 = (bf16[256,512]{1,0:T(8,128)(2,1)}, bf16[256,512]{1,0:T(8,128)(2,1)S(1)}, u32[]{:S(2)}, u32[]{:S(2)}) collective-permute-start(bf16[256,512]{1,0:T(8,128)(2,1)} %half.1), channel_id=1, source_target_pairs={{0,2},{1,3},{2,0},{3,1},{4,6},{5,7},{6,4},{7,5},{8,10},{9,11},{10,... | collective-permute-start | bytes 786440 | tf_op jit(solution)/shard_map/ppermute | solution.py:1076
  5.4 0.7 copy-start.11
  5.4 0.7 copy-start.15
  5.4 0.7 copy-start.10
  5.4 0.7 copy-start.9
  5.5 0.7 copy-start.12
  5.5 0.7 copy-start.13
  5.5 0.7 copy-start.14
  9.2 1.4 %collective-permute-start = (bf16[6,16,512]{2,1,0:T(8,128)(2,1)S(1)}, bf16[6,16,512]{2,1,0:T(8,128)(2,1)S(1)}, u32[]{:S(2)}, u32[]{:S(2)}) collective-permute-start(bf16[6,16,512]{2,1,0:T(8,128)(2,1)S(1)} %get-tuple-element.160), channel_id=1, source_target_pairs={{0,1},{1,0},{2,3},{3,2},{4,5},{5,4},{6,7},{7,6},{8,9},{9,8},{10,11... | collective-permute-start | bytes 294920 | tf_op jit(solution)/shard_map/ppermute | solution.py:1076
  12.0 6.4 %collective-permute-start.4 = (bf16[6,16,512]{2,1,0:T(8,128)(2,1)S(1)}, bf16[6,16,512]{2,1,0:T(8,128)(2,1)S(1)}, u32[]{:S(2)}, u32[]{:S(2)}) collective-permute-start(bf16[6,16,512]{2,1,0:T(8,128)(2,1)S(1)} %get-tuple-element.162), channel_id=1, source_target_pairs={{0,6},{1,7},{2,4},{3,5},{4,2},{5,3},{6,0},{7,1},{8,14},{9,15},{10,... | collective-permute-start | bytes 294920 | tf_op jit(solution)/shard_map/ppermute | solution.py:1076
  14.7 4.6 %collective-permute-start.3 = (bf16[6,16,512]{2,1,0:T(8,128)(2,1)S(1)}, bf16[6,16,512]{2,1,0:T(8,128)(2,1)S(1)}, u32[]{:S(2)}, u32[]{:S(2)}) collective-permute-start(bf16[6,16,512]{2,1,0:T(8,128)(2,1)S(1)} %get-tuple-element.162), channel_id=1, source_target_pairs={{0,4},{1,5},{2,6},{3,7},{4,0},{5,1},{6,2},{7,3},{8,12},{9,13},{10,... | collective-permute-start | bytes 294920 | tf_op jit(solution)/shard_map/ppermute | solution.py:1076
  15.2 4.6 %collective-permute-start.2 = (bf16[6,16,512]{2,1,0:T(8,128)(2,1)S(1)}, bf16[6,16,512]{2,1,0:T(8,128)(2,1)S(1)}, u32[]{:S(2)}, u32[]{:S(2)}) collective-permute-start(bf16[6,16,512]{2,1,0:T(8,128)(2,1)S(1)} %get-tuple-element.162), channel_id=1, source_target_pairs={{0,2},{1,3},{2,0},{3,1},{4,6},{5,7},{6,4},{7,5},{8,10},{9,11},{10,... | collective-permute-start | bytes 294920 | tf_op jit(solution)/shard_map/ppermute | solution.py:1076
  18.4 19.7 %copy-start.4 = (bf16[512,512]{1,0:T(8,128)(2,1)S(1)}, bf16[512,512]{1,0:T(8,128)(2,1)}, u32[]{:S(2)}) copy-start(bf16[512,512]{1,0:T(8,128)(2,1)} %get-tuple-element.197.refs_6_) | copy-start | bytes 1572868
  19.9 10.3 %collective-permute-start.9 = (bf16[512,512]{1,0:T(8,128)(2,1)}, bf16[512,512]{1,0:T(8,128)(2,1)S(1)}, u32[]{:S(2)}, u32[]{:S(2)}) collective-permute-start(bf16[512,512]{1,0:T(8,128)(2,1)} %get-tuple-element.181.refs_5_.refs_17_), channel_id=1, source_target_pairs={{0,1},{1,0},{2,3},{3,2},{4,5},{5,4},{6,7},{7,6},{8,9},{9,8},{10,11... | collective-permute-start | bytes 1572872 | tf_op jit(solution)/shard_map/ppermute | solution.py:1076
  20.0 10.2 %collective-permute-start.8 = (bf16[512,512]{1,0:T(8,128)(2,1)}, bf16[512,512]{1,0:T(8,128)(2,1)S(1)}, u32[]{:S(2)}, u32[]{:S(2)}) collective-permute-start(bf16[512,512]{1,0:T(8,128)(2,1)} %get-tuple-element.179.refs_4_.refs_16_), channel_id=1, source_target_pairs={{0,1},{1,0},{2,3},{3,2},{4,5},{5,4},{6,7},{7,6},{8,9},{9,8},{10,11... | collective-permute-start | bytes 1572872 | tf_op jit(solution)/shard_map/ppermute | solution.py:1076
  20.5 8.3 %collective-permute-start.7 = (bf16[256,512]{1,0:T(8,128)(2,1)S(1)}, bf16[256,512]{1,0:T(8,128)(2,1)S(1)}, u32[]{:S(2)}, u32[]{:S(2)}) collective-permute-start(bf16[256,512]{1,0:T(8,128)(2,1)S(1)} %collective-permute-done.1.refs_8_.refs_20_), channel_id=1, source_target_pairs={{0,4},{1,5},{2,6},{3,7},{4,0},{5,1},{6,2},{7,3},{8,12},{9,13},{10,... | collective-permute-start | bytes 786440 | tf_op jit(solution)/shard_map/ppermute | solution.py:1076
  22.0 8.2 %collective-permute-start.6 = (bf16[512,256]{1,0:T(8,128)(2,1)}, bf16[512,256]{1,0:T(8,128)(2,1)S(1)}, u32[]{:S(2)}, u32[]{:S(2)}) collective-permute-start(bf16[512,256]{1,0:T(8,128)(2,1)} %get-tuple-element.176), channel_id=1, source_target_pairs={{0,2},{1,3},{2,0},{3,1},{4,6},{5,7},{6,4},{7,5},{8,10},{9,11},{10,... | collective-permute-start | bytes 786440 | tf_op jit(solution)/shard_map/ppermute | solution.py:1076
  22.5 4.6 %collective-permute-start.5 = (bf16[6,16,512]{2,1,0:T(8,128)(2,1)S(1)}, bf16[6,16,512]{2,1,0:T(8,128)(2,1)S(1)}, u32[]{:S(2)}, u32[]{:S(2)}) collective-permute-start(bf16[6,16,512]{2,1,0:T(8,128)(2,1)S(1)} %get-tuple-element.173), channel_id=1, source_target_pairs={{0,8},{1,9},{2,10},{3,11},{4,12},{5,13},{6,14},{7,15},{8,0},{9,1},... | collective-permute-start | bytes 294920 | tf_op jit(solution)/shard_map/ppermute | solution.py:1076
  27.1 10.9 %copy-start.3 = (bf16[512,128]{1,0:T(8,128)(2,1)S(1)}, bf16[512,128]{1,0:T(8,128)(2,1)}, u32[]{:S(2)}) copy-start(bf16[512,128]{1,0:T(8,128)(2,1)} %refs_11_.1) | copy-start | bytes 393220
  30.2 7.3 %collective-permute-start.10 = (bf16[256,512]{1,0:T(8,128)(2,1)}, bf16[256,512]{1,0:T(8,128)(2,1)S(1)}, u32[]{:S(2)}, u32[]{:S(2)}) collective-permute-start(bf16[256,512]{1,0:T(8,128)(2,1)} %get-tuple-element.183), channel_id=1, source_target_pairs={{0,2},{1,3},{2,0},{3,1},{4,6},{5,7},{6,4},{7,5},{8,10},{9,11},{10,... | collective-permute-start | bytes 786440 | tf_op jit(solution)/shard_map/ppermute | solution.py:1076
  30.8 7.3 %collective-permute-start.11 = (bf16[6,16,512]{2,1,0:T(8,128)(2,1)S(1)}, bf16[6,16,512]{2,1,0:T(8,128)(2,1)S(1)}, u32[]{:S(2)}, u32[]{:S(2)}) collective-permute-start(bf16[6,16,512]{2,1,0:T(8,128)(2,1)S(1)} %get-tuple-element.182), channel_id=1, source_target_pairs={{0,16},{1,17},{2,18},{3,19},{4,20},{5,21},{6,22},{7,23},{8,24},{9,... | collective-permute-start | bytes 294920 | tf_op jit(solution)/shard_map/ppermute | solution.py:1076
  33.3 7.6 %collective-permute-start.13 = (bf16[512,256]{1,0:T(8,128)(2,1)S(1)}, bf16[512,256]{1,0:T(8,128)(2,1)S(1)}, u32[]{:S(2)}, u32[]{:S(2)}) collective-permute-start(bf16[512,256]{1,0:T(8,128)(2,1)S(1)} %collective-permute-done.6.refs_10_.refs_22_), channel_id=1, source_target_pairs={{0,8},{1,9},{2,10},{3,11},{4,12},{5,13},{6,14},{7,15},{8,0},{9,1},... | collective-permute-start | bytes 786440 | tf_op jit(solution)/shard_map/ppermute | solution.py:1076
  34.9 6.2 %collective-permute-start.14 = (bf16[256,512]{1,0:T(8,128)(2,1)S(1)}, bf16[256,512]{1,0:T(8,128)(2,1)S(1)}, u32[]{:S(2)}, u32[]{:S(2)}) collective-permute-start(bf16[256,512]{1,0:T(8,128)(2,1)S(1)} %collective-permute-done.1.refs_8_.refs_20_), channel_id=1, source_target_pairs={{0,1},{1,0},{2,3},{3,2},{4,5},{5,4},{6,7},{7,6},{8,9},{9,8},{10,11... | collective-permute-start | bytes 786440 | tf_op jit(solution)/shard_map/ppermute | solution.py:1076
  34.9 6.6 %collective-permute-start.16 = (bf16[512,256]{1,0:T(8,128)(2,1)S(1)}, bf16[512,256]{1,0:T(8,128)(2,1)S(1)}, u32[]{:S(2)}, u32[]{:S(2)}) collective-permute-start(bf16[512,256]{1,0:T(8,128)(2,1)S(1)} %collective-permute-done.6.refs_10_.refs_22_), channel_id=1, source_target_pairs={{0,1},{1,0},{2,3},{3,2},{4,5},{5,4},{6,7},{7,6},{8,9},{9,8},{10,11... | collective-permute-start | bytes 786440 | tf_op jit(solution)/shard_map/ppermute | solution.py:1076
  37.6 6.4 %collective-permute-start.12 = (bf16[256,512]{1,0:T(8,128)(2,1)S(1)}, bf16[256,512]{1,0:T(8,128)(2,1)S(1)}, u32[]{:S(2)}, u32[]{:S(2)}) collective-permute-start(bf16[256,512]{1,0:T(8,128)(2,1)S(1)} %collective-permute-done.10.refs_8_), channel_id=1, source_target_pairs={{0,4},{1,5},{2,6},{3,7},{4,0},{5,1},{6,2},{7,3},{8,12},{9,13},{10,... | collective-permute-start | bytes 786440 | tf_op jit(solution)/shard_map/ppermute | solution.py:1076
  38.1 8.8 %collective-permute-start.18 = (bf16[512,512]{1,0:T(8,128)(2,1)S(1)}, bf16[512,512]{1,0:T(8,128)(2,1)S(1)}, u32[]{:S(2)}, u32[]{:S(2)}) collective-permute-start(bf16[512,512]{1,0:T(8,128)(2,1)S(1)} %copy-done.4), channel_id=1, source_target_pairs={{0,1},{1,0},{2,3},{3,2},{4,5},{5,4},{6,7},{7,6},{8,9},{9,8},{10,11... | collective-permute-start | bytes 1572872 | tf_op jit(solution)/shard_map/ppermute | solution.py:1076
  38.1 5.9 %copy-start.1 = (bf16[512,512]{1,0:T(8,128)(2,1)S(1)}, bf16[512,512]{1,0:T(8,128)(2,1)}, u32[]{:S(2)}) copy-start(bf16[512,512]{1,0:T(8,128)(2,1)} %get-tuple-element.179.refs_4_.refs_16_) | copy-start | bytes 1572868
  38.1 5.9 %copy-start.2 = (bf16[512,512]{1,0:T(8,128)(2,1)S(1)}, bf16[512,512]{1,0:T(8,128)(2,1)}, u32[]{:S(2)}) copy-start(bf16[512,512]{1,0:T(8,128)(2,1)} %get-tuple-element.181.refs_5_.refs_17_) | copy-start | bytes 1572868
  41.0 3.0 %collective-permute-start.15 = (bf16[256,512]{1,0:T(8,128)(2,1)S(1)}, bf16[256,512]{1,0:T(8,128)(2,1)S(1)}, u32[]{:S(2)}, u32[]{:S(2)}) collective-permute-start(bf16[256,512]{1,0:T(8,128)(2,1)S(1)} %collective-permute-done.7.refs_9_.refs_21_), channel_id=1, source_target_pairs={{0,1},{1,0},{2,3},{3,2},{4,5},{5,4},{6,7},{7,6},{8,9},{9,8},{10,11... | collective-permute-start | bytes 786440 | tf_op jit(solution)/shard_map/ppermute | solution.py:1076
  41.1 2.8 %collective-permute-start.17 = (bf16[512,256]{1,0:T(8,128)(2,1)S(1)}, bf16[512,256]{1,0:T(8,128)(2,1)S(1)}, u32[]{:S(2)}, u32[]{:S(2)}) collective-permute-start(bf16[512,256]{1,0:T(8,128)(2,1)S(1)} %collective-permute-done.13.refs_11_.refs_23_), channel_id=1, source_target_pairs={{0,1},{1,0},{2,3},{3,2},{4,5},{5,4},{6,7},{7,6},{8,9},{9,8},{10,11... | collective-permute-start | bytes 786440 | tf_op jit(solution)/shard_map/ppermute | solution.py:1076
  41.5 5.4 %collective-permute-start.19 = (bf16[256,512]{1,0:T(8,128)(2,1)S(1)}, bf16[256,512]{1,0:T(8,128)(2,1)S(1)}, u32[]{:S(2)}, u32[]{:S(2)}) collective-permute-start(bf16[256,512]{1,0:T(8,128)(2,1)S(1)} %collective-permute-done.10.refs_8_), channel_id=1, source_target_pairs={{0,1},{1,0},{2,3},{3,2},{4,5},{5,4},{6,7},{7,6},{8,9},{9,8},{10,11... | collective-permute-start | bytes 786440 | tf_op jit(solution)/shard_map/ppermute | solution.py:1076
  43.9 2.9 %collective-permute-start.20 = (bf16[256,512]{1,0:T(8,128)(2,1)S(1)}, bf16[256,512]{1,0:T(8,128)(2,1)S(1)}, u32[]{:S(2)}, u32[]{:S(2)}) collective-permute-start(bf16[256,512]{1,0:T(8,128)(2,1)S(1)} %collective-permute-done.12.refs_9_), channel_id=1, source_target_pairs={{0,1},{1,0},{2,3},{3,2},{4,5},{5,4},{6,7},{7,6},{8,9},{9,8},{10,11... | collective-permute-start | bytes 786440 | tf_op jit(solution)/shard_map/ppermute | solution.py:1076
  43.9 2.9 %copy-start.5 = (bf16[2,128,512]{2,1,0:T(8,128)(2,1)S(1)}, bf16[2,128,512]{2,1,0:T(8,128)(2,1)}, u32[]{:S(2)}) copy-start(bf16[2,128,512]{2,1,0:T(8,128)(2,1)} %refs_1_.1) | copy-start | bytes 786436
  51.0 2.9 %collective-permute-start.22 = (bf16[2,512,512]{2,1,0:T(8,128)(2,1)S(1)}, bf16[2,512,512]{2,1,0:T(8,128)(2,1)S(1)}, u32[]{:S(2)}, u32[]{:S(2)}) collective-permute-start(bf16[2,512,512]{2,1,0:T(8,128)(2,1)S(1)} %get-tuple-element.210), channel_id=1, source_target_pairs={{0,1},{1,0},{2,3},{3,2},{4,5},{5,4},{6,7},{7,6},{8,9},{9,8},{10,11... | collective-permute-start | bytes 3145736 | tf_op jit(solution)/shard_map/ppermute | solution.py:1076
  52.7 2.8 %collective-permute-start.21 = (bf16[2,512,512]{2,1,0:T(8,128)(2,1)S(1)}, bf16[2,512,512]{2,1,0:T(8,128)(2,1)S(1)}, u32[]{:S(2)}, u32[]{:S(2)}) collective-permute-start(bf16[2,512,512]{2,1,0:T(8,128)(2,1)S(1)} %get-tuple-element.208), channel_id=1, source_target_pairs={{0,1},{1,0},{2,3},{3,2},{4,5},{5,4},{6,7},{7,6},{8,9},{9,8},{10,11... | collective-permute-start | bytes 3145736 | tf_op jit(solution)/shard_map/ppermute | solution.py:1076
  54.2 14.3 %collective-permute-start.23 = (bf16[1,512,512]{2,1,0:T(8,128)(2,1)S(1)}, bf16[1,512,512]{2,1,0:T(8,128)(2,1)S(1)}, u32[]{:S(2)}, u32[]{:S(2)}) collective-permute-start(bf16[1,512,512]{2,1,0:T(8,128)(2,1)S(1)} %get-tuple-element.226), channel_id=1, source_target_pairs={{0,2},{1,3},{2,0},{3,1},{4,6},{5,7},{6,4},{7,5},{8,10},{9,11},{10,... | collective-permute-start | bytes 1572872 | tf_op jit(solution)/shard_map/ppermute | solution.py:1076
  55.8 14.1 %collective-permute-start.24 = (bf16[2,256,512]{2,1,0:T(8,128)(2,1)S(1)}, bf16[2,256,512]{2,1,0:T(8,128)(2,1)S(1)}, u32[]{:S(2)}, u32[]{:S(2)}) collective-permute-start(bf16[2,256,512]{2,1,0:T(8,128)(2,1)S(1)} %get-tuple-element.229), channel_id=1, source_target_pairs={{0,4},{1,5},{2,6},{3,7},{4,0},{5,1},{6,2},{7,3},{8,12},{9,13},{10,... | collective-permute-start | bytes 1572872 | tf_op jit(solution)/shard_map/ppermute | solution.py:1076
  70.1 3.1 %collective-permute-start.27 = (bf16[2,512,512]{2,1,0:T(8,128)(2,1)S(1)}, bf16[2,512,512]{2,1,0:T(8,128)(2,1)S(1)}, u32[]{:S(2)}, u32[]{:S(2)}) collective-permute-start(bf16[2,512,512]{2,1,0:T(8,128)(2,1)S(1)} %get-tuple-element.237), channel_id=1, source_target_pairs={{0,1},{1,0},{2,3},{3,2},{4,5},{5,4},{6,7},{7,6},{8,9},{9,8},{10,11... | collective-permute-start | bytes 3145736 | tf_op jit(solution)/shard_map/ppermute | solution.py:1076
  70.2 3.0 %collective-permute-start.26 = (f32[96,512]{1,0:T(8,128)S(1)}, f32[96,512]{1,0:T(8,128)S(1)}, u32[]{:S(2)}, u32[]{:S(2)}) collective-permute-start(f32[96,512]{1,0:T(8,128)S(1)} %get-tuple-element.235), channel_id=1, source_target_pairs={{0,1},{1,0},{2,3},{3,2},{4,5},{5,4},{6,7},{7,6},{8,9},{9,8},{10,11... | collective-permute-start | bytes 589832 | tf_op jit(solution)/shard_map/ppermute | solution.py:1076
  70.7 2.5 %collective-permute-start.25 = (f32[32,512]{1,0:T(8,128)S(1)}, f32[32,512]{1,0:T(8,128)S(1)}, u32[]{:S(2)}, u32[]{:S(2)}) collective-permute-start(f32[32,512]{1,0:T(8,128)S(1)} %bitcast.27), channel_id=1, source_target_pairs={{0,1},{1,0},{2,3},{3,2},{4,5},{5,4},{6,7},{7,6},{8,9},{9,8},{10,11... | collective-permute-start | bytes 196616 | tf_op jit(solution)/shard_map/ppermute | solution.py:1076
  70.8 9.1 %collective-permute-start.28 = (bf16[1,256,512]{2,1,0:T(8,128)(2,1)S(1)}, bf16[1,256,512]{2,1,0:T(8,128)(2,1)S(1)}, u32[]{:S(2)}, u32[]{:S(2)}) collective-permute-start(bf16[1,256,512]{2,1,0:T(8,128)(2,1)S(1)} %get-tuple-element.241), channel_id=1, source_target_pairs={{0,4},{1,5},{2,6},{3,7},{4,0},{5,1},{6,2},{7,3},{8,12},{9,13},{10,... | collective-permute-start | bytes 786440 | tf_op jit(solution)/shard_map/ppermute | solution.py:1076
  71.3 9.2 %collective-permute-start.29 = (bf16[1,256,512]{2,1,0:T(8,128)(2,1)S(1)}, bf16[1,256,512]{2,1,0:T(8,128)(2,1)S(1)}, u32[]{:S(2)}, u32[]{:S(2)}) collective-permute-start(bf16[1,256,512]{2,1,0:T(8,128)(2,1)S(1)} %get-tuple-element.242), channel_id=1, source_target_pairs={{0,2},{1,3},{2,0},{3,1},{4,6},{5,7},{6,4},{7,5},{8,10},{9,11},{10,... | collective-permute-start | bytes 786440 | tf_op jit(solution)/shard_map/ppermute | solution.py:1076
  73.7 13.3 %collective-permute-start.30 = (bf16[672,256]{1,0:T(8,128)(2,1)S(1)}, bf16[672,256]{1,0:T(8,128)(2,1)S(1)}, u32[]{:S(2)}, u32[]{:S(2)}) collective-permute-start(bf16[672,256]{1,0:T(8,128)(2,1)S(1)} %get-tuple-element.239.refs_3_), channel_id=1, source_target_pairs={{0,2},{1,3},{2,0},{3,1},{4,6},{5,7},{6,4},{7,5},{8,10},{9,11},{10,... | collective-permute-start | bytes 1032200 | tf_op jit(solution)/shard_map/ppermute | solution.py:1076
  74.9 10.1 %collective-permute-start.31 = (bf16[2,256,256]{2,1,0:T(8,128)(2,1)S(1)}, bf16[2,256,256]{2,1,0:T(8,128)(2,1)S(1)}, u32[]{:S(2)}, u32[]{:S(2)}) collective-permute-start(bf16[2,256,256]{2,1,0:T(8,128)(2,1)S(1)} %get-tuple-element.248), channel_id=1, source_target_pairs={{0,4},{1,5},{2,6},{3,7},{4,0},{5,1},{6,2},{7,3},{8,12},{9,13},{10,... | collective-permute-start | bytes 786440 | tf_op jit(solution)/shard_map/ppermute | solution.py:1076
  80.6 9.5 %collective-permute-start.32 = (bf16[2,128,512]{2,1,0:T(8,128)(2,1)S(1)}, bf16[2,128,512]{2,1,0:T(8,128)(2,1)S(1)}, u32[]{:S(2)}, u32[]{:S(2)}) collective-permute-start(bf16[2,128,512]{2,1,0:T(8,128)(2,1)S(1)} %get-tuple-element.252), channel_id=1, source_target_pairs={{0,8},{1,9},{2,10},{3,11},{4,12},{5,13},{6,14},{7,15},{8,0},{9,1},... | collective-permute-start | bytes 786440 | tf_op jit(solution)/shard_map/ppermute | solution.py:1076
  87.3 6.6 %collective-permute-start.33 = (bf16[416,256]{1,0:T(8,128)(2,1)S(1)}, bf16[416,256]{1,0:T(8,128)(2,1)S(1)}, u32[]{:S(2)}, u32[]{:S(2)}) collective-permute-start(bf16[416,256]{1,0:T(8,128)(2,1)S(1)} %get-tuple-element.250.refs_3_), channel_id=1, source_target_pairs={{0,4},{1,5},{2,6},{3,7},{4,0},{5,1},{6,2},{7,3},{8,12},{9,13},{10,... | collective-permute-start | bytes 638984 | tf_op jit(solution)/shard_map/ppermute | solution.py:1076
  88.8 5.0 %collective-permute-start.34 = (bf16[256,256]{1,0:T(8,128)(2,1)S(1)}, bf16[256,256]{1,0:T(8,128)(2,1)S(1)}, u32[]{:S(2)}, u32[]{:S(2)}) collective-permute-start(bf16[256,256]{1,0:T(8,128)(2,1)S(1)} %get-tuple-element.257), channel_id=1, source_target_pairs={{0,2},{1,3},{2,0},{3,1},{4,6},{5,7},{6,4},{7,5},{8,10},{9,11},{10,... | collective-permute-start | bytes 393224 | tf_op jit(solution)/shard_map/ppermute | solution.py:1076
  90.1 14.7 %collective-permute-start.36 = (bf16[2,128,512]{2,1,0:T(8,128)(2,1)S(1)}, bf16[2,128,512]{2,1,0:T(8,128)(2,1)S(1)}, u32[]{:S(2)}, u32[]{:S(2)}) collective-permute-start(bf16[2,128,512]{2,1,0:T(8,128)(2,1)S(1)} %fold.12.refs_0_), channel_id=1, source_target_pairs={{0,16},{1,17},{2,18},{3,19},{4,20},{5,21},{6,22},{7,23},{8,24},{9,... | collective-permute-start | bytes 786440 | tf_op jit(solution)/shard_map/ppermute | solution.py:1076
  94.0 10.8 %collective-permute-start.35 = (bf16[208,512]{1,0:T(8,128)(2,1)S(1)}, bf16[208,512]{1,0:T(8,128)(2,1)S(1)}, u32[]{:S(2)}, u32[]{:S(2)}) collective-permute-start(bf16[208,512]{1,0:T(8,128)(2,1)S(1)} %get-tuple-element.259.refs_3_), channel_id=1, source_target_pairs={{0,8},{1,9},{2,10},{3,11},{4,12},{5,13},{6,14},{7,15},{8,0},{9,1},... | collective-permute-start | bytes 638984 | tf_op jit(solution)/shard_map/ppermute | solution.py:1076
  104.9 11.2 %collective-permute-start.37 = (bf16[2,128,512]{2,1,0:T(8,128)(2,1)S(1)}, bf16[2,128,512]{2,1,0:T(8,128)(2,1)S(1)}, u32[]{:S(2)}, u32[]{:S(2)}) collective-permute-start(bf16[2,128,512]{2,1,0:T(8,128)(2,1)S(1)} %fold.13.refs_0_), channel_id=1, source_target_pairs={{0,8},{1,9},{2,10},{3,11},{4,12},{5,13},{6,14},{7,15},{8,0},{9,1},... | collective-permute-start | bytes 786440 | tf_op jit(solution)/shard_map/ppermute | solution.py:1076
  105.0 12.4 %collective-permute-start.38 = (bf16[208,512]{1,0:T(8,128)(2,1)S(1)}, bf16[208,512]{1,0:T(8,128)(2,1)S(1)}, u32[]{:S(2)}, u32[]{:S(2)}) collective-permute-start(bf16[208,512]{1,0:T(8,128)(2,1)S(1)} %get-tuple-element.264.refs_3_), channel_id=1, source_target_pairs={{0,16},{1,17},{2,18},{3,19},{4,20},{5,21},{6,22},{7,23},{8,24},{9,... | collective-permute-start | bytes 638984 | tf_op jit(solution)/shard_map/ppermute | solution.py:1076
  116.2 12.9 %collective-permute-start.41 = (bf16[2,256,512]{2,1,0:T(8,128)(2,1)S(1)}, bf16[2,256,512]{2,1,0:T(8,128)(2,1)S(1)}, u32[]{:S(2)}, u32[]{:S(2)}) collective-permute-start(bf16[2,256,512]{2,1,0:T(8,128)(2,1)S(1)} %join.2.refs_0_), channel_id=1, source_target_pairs={{0,4},{1,5},{2,6},{3,7},{4,0},{5,1},{6,2},{7,3},{8,12},{9,13},{10,... | collective-permute-start | bytes 1572872 | tf_op jit(solution)/shard_map/ppermute | solution.py:1076
  117.5 5.1 %collective-permute-start.39 = (bf16[1,128,512]{2,1,0:T(8,128)(2,1)S(1)}, bf16[1,128,512]{2,1,0:T(8,128)(2,1)S(1)}, u32[]{:S(2)}, u32[]{:S(2)}) collective-permute-start(bf16[1,128,512]{2,1,0:T(8,128)(2,1)S(1)} %bitcast.25), channel_id=1, source_target_pairs={{0,8},{1,9},{2,10},{3,11},{4,12},{5,13},{6,14},{7,15},{8,0},{9,1},... | collective-permute-start | bytes 393224 | tf_op jit(solution)/shard_map/ppermute | solution.py:1076
  119.3 5.0 %collective-permute-start.40 = (f32[48,512]{1,0:T(8,128)S(1)}, f32[48,512]{1,0:T(8,128)S(1)}, u32[]{:S(2)}, u32[]{:S(2)}) collective-permute-start(f32[48,512]{1,0:T(8,128)S(1)} %get-tuple-element.276.refs_0_), channel_id=1, source_target_pairs={{0,2},{1,3},{2,0},{3,1},{4,6},{5,7},{6,4},{7,5},{8,10},{9,11},{10,... | collective-permute-start | bytes 294920 | tf_op jit(solution)/shard_map/ppermute | solution.py:1076
  122.6 9.3 %collective-permute-start.43 = (bf16[1,256,512]{2,1,0:T(8,128)(2,1)S(1)}, bf16[1,256,512]{2,1,0:T(8,128)(2,1)S(1)}, u32[]{:S(2)}, u32[]{:S(2)}) collective-permute-start(bf16[1,256,512]{2,1,0:T(8,128)(2,1)S(1)} %join.3.refs_0_), channel_id=1, source_target_pairs={{0,4},{1,5},{2,6},{3,7},{4,0},{5,1},{6,2},{7,3},{8,12},{9,13},{10,... | collective-permute-start | bytes 786440 | tf_op jit(solution)/shard_map/ppermute | solution.py:1076
  124.4 6.3 %collective-permute-start.42 = (f32[96,512]{1,0:T(8,128)S(1)}, f32[96,512]{1,0:T(8,128)S(1)}, u32[]{:S(2)}, u32[]{:S(2)}) collective-permute-start(f32[96,512]{1,0:T(8,128)S(1)} %pair.1.refs_3_), channel_id=1, source_target_pairs={{0,1},{1,0},{2,3},{3,2},{4,5},{5,4},{6,7},{7,6},{8,9},{9,8},{10,11... | collective-permute-start | bytes 589832 | tf_op jit(solution)/shard_map/ppermute | solution.py:1076

commit v6 on v5

--- a/solution.py
+++ b/solution.py
@@ -639,6 +639,8 @@
         seqs, ids, tok, normed, grad_skip, grad_normed, par, before, st_in, skip, grad_gain2, misc,
         grad_wsh, sums_keep, sums_send, table, nf, pw,
     )
+    for s in range(seqs):
+        sums_send[pl.ds(sums_keep.shape[0] + s * NDIM, NDIM), :] = ends[s]
 
 
 def small_sums(
@@ -700,7 +702,7 @@
     half = keep.shape[0]
     mine = jnp.bitwise_and(ids[0], 1) * half
     keep[...] = table[pl.ds(pl.multiple_of(mine, 8), half), :]
-    send[...] = table[pl.ds(pl.multiple_of(half - mine, 8), half), :]
+    send[pl.ds(0, half), :] = table[pl.ds(pl.multiple_of(half - mine, 8), half), :]
 
 
 def pair_kernel(bit, ids, mine, other, out):
@@ -825,11 +827,11 @@
     return jnp.concatenate(runs, axis=1) if len(runs) > 1 else runs[0]
 
 
-def first_back_hop(seqs, joins, ids, par, own, other, sums, got, out, keep, payload):
+def first_back_hop(seqs, joins, ids, par, own, sums, got, out, keep, payload):
     rows = seqs * NDIM
     fold_lanes = D // payload.shape[1]
     if joins:
-        join_adjoint(seqs, 0, ids, par, own, other[...], out)
+        join_adjoint(seqs, 0, ids, par, own, got[pl.ds(sums.shape[0], rows), :], out)
     else:
         out[...] = own[...]
     put_wide(payload, 0, out[...])
@@ -956,7 +958,7 @@
 
 
 def start_kernel(
-    seqs, bits, ids, par, own, other, sums, got, keep1, got1, out, keep, left, payload, right, send
+    seqs, bits, ids, par, own, sums, got, keep1, got1, out, keep, left, payload, right, send
 ):
     vb = keep1.shape[2] // 2
     for b, target in enumerate((left, payload)):
@@ -965,8 +967,8 @@
         start, high = split_rows(D, (0, bits), ids[1], k)
         for b in range(2):
             add_rows([keep1.at[b], got1.at[b]], start, high, target.at[b], 0, vb, vb, 0)
-    join_adjoint(seqs, 0, ids, par, own, other[...], out)
     rows, half = seqs * NDIM, keep.shape[0]
+    join_adjoint(seqs, 0, ids, par, own, got[pl.ds(2 * half, rows), :], out)
     put_wide(payload, D, out[...])
     upper = jnp.where(jnp.bitwise_and(ids[0], 2) > 0, half, 0)
     mine = pl.ds(pl.multiple_of(upper, 8), half)
@@ -1406,7 +1408,7 @@
             shape((seqs, NDIM, PIECES, D)),
             shape((seqs, NDIM, D)),
             shape((count // 2, D)),
-            shape((count // 2, D)),
+            shape((count // 2 + seqs * NDIM, D)),
         ),
         [
             pltpu.VMEM((tp, D, 2 * vb), BF16),
@@ -1444,7 +1446,6 @@
     g3 = over_y(g3)
     g2 = over_tp(g2)
     got1 = swap(send1, 1)
-    got_adjoint = adjoint if traded else swap(adjoint, 1)
     got_sums = swap(sums_send, 1)
     done = {}
 
@@ -1500,12 +1501,12 @@
                     shape((2, D // 2, vb), BF16),
                 ),
                 [],
-                (ids, par, now(adjoint), got_adjoint, sums_keep, got_sums, keep1, got1),
-                [SMEM] + [VMEM] * 7,
+                (ids, par, now(adjoint), sums_keep, got_sums, keep1, got1),
+                [SMEM] + [VMEM] * 6,
                 "start",
             )
             other, got_right = swap(payload, 2), swap(send, tp)
-            got = [(got_adjoint, 0), (other, D)]
+            got = [(got_sums, count // 2), (other, D)]
             yield payload
             own, kept, left, payload, right, send = call(
                 functools.partial(cross_kernel, seqs, ybits),
@@ -1536,11 +1537,11 @@
                     shape((payload_rows(), wide), BF16),
                 ),
                 [],
-                (ids, par, now(adjoint), got_adjoint, sums_keep, got_sums),
-                [SMEM] + [VMEM] * 5,
+                (ids, par, now(adjoint), sums_keep, got_sums),
+                [SMEM] + [VMEM] * 4,
                 "hop",
             )
-            got = [] if traded else [(got_adjoint, 0)]
+            got = [] if traded else [(got_sums, count // 2)]
             level = int(not traded)
             halved = True
             other = swap(payload, masks[level])

time: 133 us -> 132 us (level)
    ppermute x44 -> x43, starting transfers between devices: 42 us -> 41 us  [swap(): return lax.ppermute(value, BOTH, [(i, i ^ mask) for i in range(count)])]
    ppermute x44 -> x43, waiting for transfers between devices: 52 us -> 52.3 us  [swap(): return lax.ppermute(value, BOTH, [(i, i ^ mask) for i in range(count)])]
  transfers between devices with their start and end apart: 44 -> 43, of which waited for: 23 -> 23; matrix products, arithmetic and copies ran while one was open for 0% -> 0% of each run, Pallas kernels for 23% -> 23%
where the time goes in v6:
time: 132 us
  waiting for transfers between devices  52.3 us (40%)
  starting transfers between devices  41 us (31%)
  Pallas kernels  37.1 us (28%)
    ppermute x43, waiting for transfers between devices, swap(): return lax.ppermute(value, BOTH, [(i, i ^ mask) for i in range(count)])  52.3 us
    ppermute x43, starting transfers between devices, swap(): return lax.ppermute(value, BOTH, [(i, i ^ mask) for i in range(count)])  41 us
    pallas_call x30, Pallas kernels, call(): pl.pallas_call(body, out_shape=out, in_specs=specs, out_specs=outs or jax...  37.1 us
  transfers between devices with their start and end apart: 43, of which 23 were waited for; matrix products, arithmetic and copies ran while one was open for 0% of the time, Pallas kernels for 23%

profile of v6, /device:TPU:0, one launch (start us, length us, event | category | flops | bytes accessed | tf_op | source)
XLA Modules:
  0.0 132.3 jit_solution(8083234942645288567)
XLA Ops:
  0.7 1.7 %half.1 = bf16[256,512]{1,0:T(8,128)(2,1)} custom-call(bf16[512,256]{1,0:T(8,128)(2,1)} %w_value.2, bf16[512,256]{1,0:T(8,128)(2,1)} %w_reset.2), custom_call_target="tpu_custom_call" | custom-call | tf_op jit(solution)/shard_map/half/pallas_call | solution.py:118
  2.4 3.0 %collective-permute-start.1 = (bf16[256,512]{1,0:T(8,128)(2,1)}, bf16[256,512]{1,0:T(8,128)(2,1)S(1)}, u32[]{:S(2)}, u32[]{:S(2)}) collective-permute-start(bf16[256,512]{1,0:T(8,128)(2,1)} %half.1), channel_id=1, source_target_pairs={{0,2},{1,3},{2,0},{3,1},{4,6},{5,7},{6,4},{7,5},{8,10},{9,11},{10,... | collective-permute-start | bytes 786440 | tf_op jit(solution)/shard_map/ppermute | solution.py:1078
  5.5 0.6 copy-done.11
  6.2 3.0 %enter.1 = (bf16[256,512]{1,0:T(8,128)(2,1)S(1)}, f32[5,16,512]{2,1,0:T(8,128)S(1)}, f32[2,2,16,8,512]{4,3,2,1,0:T(8,128)S(1)}, f32[5,16,512]{2,1,0:T(8,128)S(1)}, bf16[6,16,512]{2,1,0:T(8,128)(2,1)S(1)}) custom-call(s32[2]{0:T(128)S(1)} %copy-done.12, bf16[2,128,512]{2,1,0:T(8,128)(2,1)S(1)} %copy-done, f32[1,512]{1,0:T(1,128)S(1)} %bitcast.29, ...), custom_call_target="tpu_custom_call" | custom-call | tf_op jit(solution)/shard_map/enter/pallas_call | solution.py:118
  9.3 1.3 collective-permute-done.refs_1_.refs_4_
  10.7 1.3 collective-permute-done.1.refs_8_.refs_20_
  12.0 2.7 %collective-permute-start.4 = (bf16[6,16,512]{2,1,0:T(8,128)(2,1)S(1)}, bf16[6,16,512]{2,1,0:T(8,128)(2,1)S(1)}, u32[]{:S(2)}, u32[]{:S(2)}) collective-permute-start(bf16[6,16,512]{2,1,0:T(8,128)(2,1)S(1)} %get-tuple-element.162), channel_id=1, source_target_pairs={{0,6},{1,7},{2,4},{3,5},{4,2},{5,3},{6,0},{7,1},{8,14},{9,15},{10,... | collective-permute-start | bytes 294920 | tf_op jit(solution)/shard_map/ppermute | solution.py:1078
  14.7 0.5 collective-permute-start.3
  15.4 2.9 %pack.1 = (bf16[512,512]{1,0:T(8,128)(2,1)}, bf16[512,512]{1,0:T(8,128)(2,1)}, bf16[512,512]{1,0:T(8,128)(2,1)}, bf16[512,256]{1,0:T(8,128)(2,1)}, bf16[256,512]{1,0:T(8,128)(2,1)}) custom-call(bf16[512,256]{1,0:T(8,128)(2,1)} %w_value.2, bf16[512,256]{1,0:T(8,128)(2,1)} %w_reset.2, bf16[128,512]{1,0:T(8,128)(2,1)} %w_hidden, bf16[128,512]{1,0:T(8,128)(2,1)} %w_update, ...), custom_call_target="tpu_custom_call" | custom-call | tf_op jit(solution)/shard_map/pack/pallas_call | solution.py:118
  18.4 0.9 collective-permute-done.3.refs_2_.refs_6_
  19.3 0.5 collective-permute-done.2.refs_1_.refs_5_
  20.5 1.5 %collective-permute-start.7 = (bf16[256,512]{1,0:T(8,128)(2,1)S(1)}, bf16[256,512]{1,0:T(8,128)(2,1)S(1)}, u32[]{:S(2)}, u32[]{:S(2)}) collective-permute-start(bf16[256,512]{1,0:T(8,128)(2,1)S(1)} %collective-permute-done.1.refs_8_.refs_20_), channel_id=1, source_target_pairs={{0,4},{1,5},{2,6},{3,7},{4,0},{5,1},{6,2},{7,3},{8,12},{9,13},{10,... | collective-permute-start | bytes 786440 | tf_op jit(solution)/shard_map/ppermute | solution.py:1078
  22.0 0.5 collective-permute-start.6
  22.5 1.6 %collective-permute-start.5 = (bf16[6,16,512]{2,1,0:T(8,128)(2,1)S(1)}, bf16[6,16,512]{2,1,0:T(8,128)(2,1)S(1)}, u32[]{:S(2)}, u32[]{:S(2)}) collective-permute-start(bf16[6,16,512]{2,1,0:T(8,128)(2,1)S(1)} %get-tuple-element.173), channel_id=1, source_target_pairs={{0,8},{1,9},{2,10},{3,11},{4,12},{5,13},{6,14},{7,15},{8,0},{9,1},... | collective-permute-start | bytes 294920 | tf_op jit(solution)/shard_map/ppermute | solution.py:1078
  24.1 3.0 %collective-permute-done.5.refs_1_.refs_8_ = bf16[6,16,512]{2,1,0:T(8,128)(2,1)S(1)} collective-permute-done((bf16[6,16,512]{2,1,0:T(8,128)(2,1)S(1)}, bf16[6,16,512]{2,1,0:T(8,128)(2,1)S(1)}, u32[]{:S(2)}, u32[]{:S(2)}) %collective-permute-start.5) | collective-permute-done | bytes 98336 | tf_op jit(solution)/shard_map/ppermute | solution.py:1078
  27.2 0.7 hop.5
  27.9 0.9 collective-permute-done.7.refs_9_.refs_21_
  28.8 1.4 %collective-permute-done.6.refs_10_.refs_22_ = bf16[512,256]{1,0:T(8,128)(2,1)S(1)} collective-permute-done((bf16[512,256]{1,0:T(8,128)(2,1)}, bf16[512,256]{1,0:T(8,128)(2,1)S(1)}, u32[]{:S(2)}, u32[]{:S(2)}) %collective-permute-start.6) | collective-permute-done | bytes 262176 | tf_op jit(solution)/shard_map/ppermute | solution.py:1078
  30.2 0.5 collective-permute-start.10
  30.8 2.6 %collective-permute-start.11 = (bf16[6,16,512]{2,1,0:T(8,128)(2,1)S(1)}, bf16[6,16,512]{2,1,0:T(8,128)(2,1)S(1)}, u32[]{:S(2)}, u32[]{:S(2)}) collective-permute-start(bf16[6,16,512]{2,1,0:T(8,128)(2,1)S(1)} %get-tuple-element.182), channel_id=1, source_target_pairs={{0,16},{1,17},{2,18},{3,19},{4,20},{5,21},{6,22},{7,23},{8,24},{9,... | collective-permute-start | bytes 294920 | tf_op jit(solution)/shard_map/ppermute | solution.py:1078
  33.3 1.6 %collective-permute-start.13 = (bf16[512,256]{1,0:T(8,128)(2,1)S(1)}, bf16[512,256]{1,0:T(8,128)(2,1)S(1)}, u32[]{:S(2)}, u32[]{:S(2)}) collective-permute-start(bf16[512,256]{1,0:T(8,128)(2,1)S(1)} %collective-permute-done.6.refs_10_.refs_22_), channel_id=1, source_target_pairs={{0,8},{1,9},{2,10},{3,11},{4,12},{5,13},{6,14},{7,15},{8,0},{9,1},... | collective-permute-start | bytes 786440 | tf_op jit(solution)/shard_map/ppermute | solution.py:1078
  34.9 0.5 collective-permute-start.16
  35.4 2.1 %collective-permute-done.10.refs_8_ = bf16[256,512]{1,0:T(8,128)(2,1)S(1)} collective-permute-done((bf16[256,512]{1,0:T(8,128)(2,1)}, bf16[256,512]{1,0:T(8,128)(2,1)S(1)}, u32[]{:S(2)}, u32[]{:S(2)}) %collective-permute-start.10) | collective-permute-done | bytes 262176 | tf_op jit(solution)/shard_map/ppermute | solution.py:1078
  37.6 0.5 collective-permute-start.12
  38.1 2.4 %look.1 = (f32[2,2,16,512]{3,2,1,0:T(8,128)S(1)}, f32[256,512]{1,0:T(8,128)S(1)}, bf16[256,512]{1,0:T(8,128)(2,1)S(1)}, f32[256,128]{1,0:T(8,128)S(1)}, f32[2,128,128]{2,1,0:T(8,128)S(1)}) custom-call(bf16[256,512]{1,0:T(8,128)(2,1)S(1)} %get-tuple-element.184.refs_0_.refs_1_, f32[5,16,512]{2,1,0:T(8,128)S(1)} %get-tuple-element.185.refs_1_.refs_5_.refs_10_.refs_0_, ...), custom_call_target="tpu_custom_call" | custom-call | tf_op jit(solution)/shard_map/look/pallas_call | solution.py:118
  41.6 2.3 %collective-permute-done.12.refs_9_ = bf16[256,512]{1,0:T(8,128)(2,1)S(1)} collective-permute-done((bf16[256,512]{1,0:T(8,128)(2,1)S(1)}, bf16[256,512]{1,0:T(8,128)(2,1)S(1)}, u32[]{:S(2)}, u32[]{:S(2)}) %collective-permute-start.12) | collective-permute-done | bytes 262176 | tf_op jit(solution)/shard_map/ppermute | solution.py:1078
  44.0 2.9 %mix.1 = (bf16[4,256,256]{2,1,0:T(8,128)(2,1)S(1)}, f32[4,256,256]{2,1,0:T(8,128)S(1)}, f32[4,256,256]{2,1,0:T(8,128)S(1)}, f32[4,256,256]{2,1,0:T(8,128)S(1)}, ...) custom-call(bf16[2,128,512]{2,1,0:T(8,128)(2,1)S(1)} %copy-done, ...), custom_call_target="tpu_custom_call" | custom-call | tf_op jit(solution)/shard_map/mix/pallas_call | solution.py:118
  46.9 4.1 %ffn.1 = (bf16[256,512]{1,0:T(8,128)(2,1)}, bf16[2,512,512]{2,1,0:T(8,128)(2,1)S(1)}, bf16[2,512,512]{2,1,0:T(8,128)(2,1)S(1)}, bf16[256,1024]{1,0:T(8,128)(2,1)...) custom-call(bf16[2,128,512]{2,1,0:T(8,128)(2,1)S(1)} %copy-done, bf16[2,128,512]{2,1,0:T(8,128)(2,1)S(1)} %copy-done.5, ...), custom_call_target="tpu_custom_call" | custom-call | tf_op jit(solution)/shard_map/ffn/pallas_call | solution.py:118
  51.0 0.6 collective-permute-start.22
  51.5 1.1 gates.1
  52.8 1.1 collective-permute-done.22.refs_1_
  54.2 1.3 collective-permute-start.23
  55.8 0.6 collective-permute-start.24
  56.4 9.8 %back.1 = (bf16[2,512,512]{2,1,0:T(8,128)(2,1)S(1)}, bf16[2,512,512]{2,1,0:T(8,128)(2,1)S(1)}, f32[4,256,128]{2,1,0:T(8,128)S(1)}, f32[256,512]{1,0:T(8,128)S(1)...) custom-call(bf16[256,512]{1,0:T(8,128)(2,1)S(1)} %get-tuple-element., ...), custom_call_target="tpu_custom_call" | custom-call | tf_op jit(solution)/shard_map/back/pallas_call | solution.py:118
  66.2 2.2 %collective-permute-done.23.refs_1_ = bf16[1,512,512]{2,1,0:T(8,128)(2,1)S(1)} collective-permute-done((bf16[1,512,512]{2,1,0:T(8,128)(2,1)S(1)}, bf16[1,512,512]{2,1,0:T(8,128)(2,1)S(1)}, u32[]{:S(2)}, u32[]{:S(2)}) %collective-permute-start.23) | collective-permute-done | bytes 524320 | tf_op jit(solution)/shard_map/ppermute | solution.py:1078
  68.6 1.3 %collective-permute-done.24.refs_1_ = bf16[2,256,512]{2,1,0:T(8,128)(2,1)S(1)} collective-permute-done((bf16[2,256,512]{2,1,0:T(8,128)(2,1)S(1)}, bf16[2,256,512]{2,1,0:T(8,128)(2,1)S(1)}, u32[]{:S(2)}, u32[]{:S(2)}) %collective-permute-start.24) | collective-permute-done | bytes 524320 | tf_op jit(solution)/shard_map/ppermute | solution.py:1078
  70.7 0.5 collective-permute-start.27
  71.2 1.2 collective-permute-start.28
  72.4 0.8 collective-permute-done.25.refs_3_.refs_6_
  73.7 1.3 collective-permute-start.29
  74.9 0.5 collective-permute-start.30
  75.4 4.4 %collective-permute-done.27.refs_1_ = bf16[1,256,512]{2,1,0:T(8,128)(2,1)S(1)} collective-permute-done((bf16[1,256,512]{2,1,0:T(8,128)(2,1)S(1)}, bf16[1,256,512]{2,1,0:T(8,128)(2,1)S(1)}, u32[]{:S(2)}, u32[]{:S(2)}) %collective-permute-start.27) | collective-permute-done | bytes 262176 | tf_op jit(solution)/shard_map/ppermute | solution.py:1078
  79.8 0.5 collective-permute-done.28.refs_3_
  80.6 1.6 %collective-permute-start.31 = (bf16[2,128,512]{2,1,0:T(8,128)(2,1)S(1)}, bf16[2,128,512]{2,1,0:T(8,128)(2,1)S(1)}, u32[]{:S(2)}, u32[]{:S(2)}) collective-permute-start(bf16[2,128,512]{2,1,0:T(8,128)(2,1)S(1)} %get-tuple-element.252), channel_id=1, source_target_pairs={{0,8},{1,9},{2,10},{3,11},{4,12},{5,13},{6,14},{7,15},{8,0},{9,1},... | collective-permute-start | bytes 786440 | tf_op jit(solution)/shard_map/ppermute | solution.py:1078
  82.2 2.4 %collective-permute-done.30.refs_7_ = bf16[2,256,256]{2,1,0:T(8,128)(2,1)S(1)} collective-permute-done((bf16[2,256,256]{2,1,0:T(8,128)(2,1)S(1)}, bf16[2,256,256]{2,1,0:T(8,128)(2,1)S(1)}, u32[]{:S(2)}, u32[]{:S(2)}) %collective-permute-start.30) | collective-permute-done | bytes 262176 | tf_op jit(solution)/shard_map/ppermute | solution.py:1078
  84.6 2.0 %collective-permute-done.29.refs_4_.refs_7_ = bf16[672,256]{1,0:T(8,128)(2,1)S(1)} collective-permute-done((bf16[672,256]{1,0:T(8,128)(2,1)S(1)}, bf16[672,256]{1,0:T(8,128)(2,1)S(1)}, u32[]{:S(2)}, u32[]{:S(2)}) %collective-permute-start.29) | collective-permute-done | bytes 344096 | tf_op jit(solution)/shard_map/ppermute | solution.py:1078
  86.8 1.6 %collective-permute-start.32 = (bf16[416,256]{1,0:T(8,128)(2,1)S(1)}, bf16[416,256]{1,0:T(8,128)(2,1)S(1)}, u32[]{:S(2)}, u32[]{:S(2)}) collective-permute-start(bf16[416,256]{1,0:T(8,128)(2,1)S(1)} %get-tuple-element.250.refs_3_), channel_id=1, source_target_pairs={{0,4},{1,5},{2,6},{3,7},{4,0},{5,1},{6,2},{7,3},{8,12},{9,13},{10,... | collective-permute-start | bytes 638984 | tf_op jit(solution)/shard_map/ppermute | solution.py:1078
  88.4 1.2 collective-permute-start.33
  89.7 2.1 %collective-permute-start.35 = (bf16[2,128,512]{2,1,0:T(8,128)(2,1)S(1)}, bf16[2,128,512]{2,1,0:T(8,128)(2,1)S(1)}, u32[]{:S(2)}, u32[]{:S(2)}) collective-permute-start(bf16[2,128,512]{2,1,0:T(8,128)(2,1)S(1)} %fold.12.refs_0_), channel_id=1, source_target_pairs={{0,16},{1,17},{2,18},{3,19},{4,20},{5,21},{6,22},{7,23},{8,24},{9,... | collective-permute-start | bytes 786440 | tf_op jit(solution)/shard_map/ppermute | solution.py:1078
  91.8 1.6 %collective-permute-done.33.refs_7_ = bf16[256,256]{1,0:T(8,128)(2,1)S(1)} collective-permute-done((bf16[256,256]{1,0:T(8,128)(2,1)S(1)}, bf16[256,256]{1,0:T(8,128)(2,1)S(1)}, u32[]{:S(2)}, u32[]{:S(2)}) %collective-permute-start.33) | collective-permute-done | bytes 131104 | tf_op jit(solution)/shard_map/ppermute | solution.py:1078
  93.5 1.6 %collective-permute-start.34 = (bf16[208,512]{1,0:T(8,128)(2,1)S(1)}, bf16[208,512]{1,0:T(8,128)(2,1)S(1)}, u32[]{:S(2)}, u32[]{:S(2)}) collective-permute-start(bf16[208,512]{1,0:T(8,128)(2,1)S(1)} %get-tuple-element.259.refs_3_), channel_id=1, source_target_pairs={{0,8},{1,9},{2,10},{3,11},{4,12},{5,13},{6,14},{7,15},{8,0},{9,1},... | collective-permute-start | bytes 638984 | tf_op jit(solution)/shard_map/ppermute | solution.py:1078
  95.1 8.8 %collective-permute-done.34.refs_4_.refs_9_ = bf16[208,512]{1,0:T(8,128)(2,1)S(1)} collective-permute-done((bf16[208,512]{1,0:T(8,128)(2,1)S(1)}, bf16[208,512]{1,0:T(8,128)(2,1)S(1)}, u32[]{:S(2)}, u32[]{:S(2)}) %collective-permute-start.34) | collective-permute-done | bytes 213024 | tf_op jit(solution)/shard_map/ppermute | solution.py:1078
  104.2 4.2 %collective-permute-start.37 = (bf16[208,512]{1,0:T(8,128)(2,1)S(1)}, bf16[208,512]{1,0:T(8,128)(2,1)S(1)}, u32[]{:S(2)}, u32[]{:S(2)}) collective-permute-start(bf16[208,512]{1,0:T(8,128)(2,1)S(1)} %get-tuple-element.264.refs_3_), channel_id=1, source_target_pairs={{0,16},{1,17},{2,18},{3,19},{4,20},{5,21},{6,22},{7,23},{8,24},{9,... | collective-permute-start | bytes 638984 | tf_op jit(solution)/shard_map/ppermute | solution.py:1078
  108.4 6.9 %collective-permute-done.36.refs_1_ = bf16[2,128,512]{2,1,0:T(8,128)(2,1)S(1)} collective-permute-done((bf16[2,128,512]{2,1,0:T(8,128)(2,1)S(1)}, bf16[2,128,512]{2,1,0:T(8,128)(2,1)S(1)}, u32[]{:S(2)}, u32[]{:S(2)}) %collective-permute-start.36) | collective-permute-done | bytes 262176 | tf_op jit(solution)/shard_map/ppermute | solution.py:1078
  115.4 1.0 collective-permute-start.40
  116.4 1.6 %collective-permute-start.38 = (bf16[1,128,512]{2,1,0:T(8,128)(2,1)S(1)}, bf16[1,128,512]{2,1,0:T(8,128)(2,1)S(1)}, u32[]{:S(2)}, u32[]{:S(2)}) collective-permute-start(bf16[1,128,512]{2,1,0:T(8,128)(2,1)S(1)} %bitcast.25), channel_id=1, source_target_pairs={{0,8},{1,9},{2,10},{3,11},{4,12},{5,13},{6,14},{7,15},{8,0},{9,1},... | collective-permute-start | bytes 393224 | tf_op jit(solution)/shard_map/ppermute | solution.py:1078
  118.0 1.1 collective-permute-start.39
  119.1 2.6 %leave.1 = bf16[2,128,512]{2,1,0:T(8,128)(2,1)} custom-call(bf16[2,128,512]{2,1,0:T(8,128)(2,1)S(1)} %copy-done, f32[5,16,512]{2,1,0:T(8,128)S(1)} %get-tuple-element.185.refs_1_.refs_5_.refs_10_.refs_0_, f32[4,256,128]{2,1,0:T(8,128)S(1)} %get-tuple-element.270.refs_2_, f32[256,512]{1,0:T(8,128)S(1)} %get-tuple-element.271.refs_3_, ...), custom_call_target="tpu_custom_call" | custom-call | tf_op jit(solution)/shard_map/leave/pallas_call | solution.py:118
  121.7 1.1 collective-permute-start.42
  122.9 5.5 %collective-permute-done.40.refs_1_ = bf16[2,256,512]{2,1,0:T(8,128)(2,1)S(1)} collective-permute-done((bf16[2,256,512]{2,1,0:T(8,128)(2,1)S(1)}, bf16[2,256,512]{2,1,0:T(8,128)(2,1)S(1)}, u32[]{:S(2)}, u32[]{:S(2)}) %collective-permute-start.40) | collective-permute-done | bytes 524320 | tf_op jit(solution)/shard_map/ppermute | solution.py:1078
  128.4 1.5 %unpack.2 = (f32[512,256]{1,0:T(8,128)}, f32[256,512]{1,0:T(8,128)}, f32[128,512]{1,0:T(8,128)}, f32[128,512]{1,0:T(8,128)}, f32[256,512]{1,0:T(8,128)}) custom-call(bf16[2,256,512]{2,1,0:T(8,128)(2,1)S(1)} %join.2.refs_0_, bf16[2,256,512]{2,1,0:T(8,128)(2,1)S(1)} %collective-permute-done.40.refs_1_), custom_call_target="tpu_custom_call" | custom-call | tf_op jit(solution)/shard_map/unpack/pallas_call | solution.py:118
  129.9 0.8 finish.1
  130.7 0.5 collective-permute-done.42.refs_1_
  131.2 1.0 unpack.3
  (84 shorter events, 5.4 us)
Async XLA Ops:
  0.7 4.8 %copy-start = (bf16[2,128,512]{2,1,0:T(8,128)(2,1)S(1)}, bf16[2,128,512]{2,1,0:T(8,128)(2,1)}, u32[]{:S(2)}) copy-start(bf16[2,128,512]{2,1,0:T(8,128)(2,1)} %refs_0_.7) | copy-start | bytes 786436
  0.7 4.8 %copy-start.6 = (f32[512,16]{0,1:T(8,128)S(1)}, f32[512,16]{0,1:T(8,128)}, u32[]{:S(2)}) copy-start(f32[512,16]{0,1:T(8,128)} %param.24) | copy-start | bytes 98308
  0.7 4.8 %copy-start.7 = (f32[512,16]{0,1:T(8,128)S(1)}, f32[512,16]{0,1:T(8,128)}, u32[]{:S(2)}) copy-start(f32[512,16]{0,1:T(8,128)} %param.25) | copy-start | bytes 98308
  0.7 4.8 %copy-start.8 = (f32[512,16]{0,1:T(8,128)S(1)}, f32[512,16]{0,1:T(8,128)}, u32[]{:S(2)}) copy-start(f32[512,16]{0,1:T(8,128)} %param.26) | copy-start | bytes 98308
  2.4 9.5 %collective-permute-start.1 = (bf16[256,512]{1,0:T(8,128)(2,1)}, bf16[256,512]{1,0:T(8,128)(2,1)S(1)}, u32[]{:S(2)}, u32[]{:S(2)}) collective-permute-start(bf16[256,512]{1,0:T(8,128)(2,1)} %half.1), channel_id=1, source_target_pairs={{0,2},{1,3},{2,0},{3,1},{4,6},{5,7},{6,4},{7,5},{8,10},{9,11},{10,... | collective-permute-start | bytes 786440 | tf_op jit(solution)/shard_map/ppermute | solution.py:1078
  5.4 0.7 copy-start.11
  5.4 0.7 copy-start.15
  5.4 0.7 copy-start.10
  5.4 0.7 copy-start.9
  5.5 0.7 copy-start.12
  5.5 0.7 copy-start.13
  5.5 0.7 copy-start.14
  9.2 1.4 %collective-permute-start = (bf16[6,16,512]{2,1,0:T(8,128)(2,1)S(1)}, bf16[6,16,512]{2,1,0:T(8,128)(2,1)S(1)}, u32[]{:S(2)}, u32[]{:S(2)}) collective-permute-start(bf16[6,16,512]{2,1,0:T(8,128)(2,1)S(1)} %get-tuple-element.160), channel_id=1, source_target_pairs={{0,1},{1,0},{2,3},{3,2},{4,5},{5,4},{6,7},{7,6},{8,9},{9,8},{10,11... | collective-permute-start | bytes 294920 | tf_op jit(solution)/shard_map/ppermute | solution.py:1078
  12.0 6.4 %collective-permute-start.4 = (bf16[6,16,512]{2,1,0:T(8,128)(2,1)S(1)}, bf16[6,16,512]{2,1,0:T(8,128)(2,1)S(1)}, u32[]{:S(2)}, u32[]{:S(2)}) collective-permute-start(bf16[6,16,512]{2,1,0:T(8,128)(2,1)S(1)} %get-tuple-element.162), channel_id=1, source_target_pairs={{0,6},{1,7},{2,4},{3,5},{4,2},{5,3},{6,0},{7,1},{8,14},{9,15},{10,... | collective-permute-start | bytes 294920 | tf_op jit(solution)/shard_map/ppermute | solution.py:1078
  14.7 4.6 %collective-permute-start.3 = (bf16[6,16,512]{2,1,0:T(8,128)(2,1)S(1)}, bf16[6,16,512]{2,1,0:T(8,128)(2,1)S(1)}, u32[]{:S(2)}, u32[]{:S(2)}) collective-permute-start(bf16[6,16,512]{2,1,0:T(8,128)(2,1)S(1)} %get-tuple-element.162), channel_id=1, source_target_pairs={{0,4},{1,5},{2,6},{3,7},{4,0},{5,1},{6,2},{7,3},{8,12},{9,13},{10,... | collective-permute-start | bytes 294920 | tf_op jit(solution)/shard_map/ppermute | solution.py:1078
  15.2 4.6 %collective-permute-start.2 = (bf16[6,16,512]{2,1,0:T(8,128)(2,1)S(1)}, bf16[6,16,512]{2,1,0:T(8,128)(2,1)S(1)}, u32[]{:S(2)}, u32[]{:S(2)}) collective-permute-start(bf16[6,16,512]{2,1,0:T(8,128)(2,1)S(1)} %get-tuple-element.162), channel_id=1, source_target_pairs={{0,2},{1,3},{2,0},{3,1},{4,6},{5,7},{6,4},{7,5},{8,10},{9,11},{10,... | collective-permute-start | bytes 294920 | tf_op jit(solution)/shard_map/ppermute | solution.py:1078
  18.4 19.7 %copy-start.4 = (bf16[512,512]{1,0:T(8,128)(2,1)S(1)}, bf16[512,512]{1,0:T(8,128)(2,1)}, u32[]{:S(2)}) copy-start(bf16[512,512]{1,0:T(8,128)(2,1)} %get-tuple-element.197.refs_6_) | copy-start | bytes 1572868
  19.9 10.3 %collective-permute-start.9 = (bf16[512,512]{1,0:T(8,128)(2,1)}, bf16[512,512]{1,0:T(8,128)(2,1)S(1)}, u32[]{:S(2)}, u32[]{:S(2)}) collective-permute-start(bf16[512,512]{1,0:T(8,128)(2,1)} %get-tuple-element.181.refs_5_.refs_17_), channel_id=1, source_target_pairs={{0,1},{1,0},{2,3},{3,2},{4,5},{5,4},{6,7},{7,6},{8,9},{9,8},{10,11... | collective-permute-start | bytes 1572872 | tf_op jit(solution)/shard_map/ppermute | solution.py:1078
  20.0 10.2 %collective-permute-start.8 = (bf16[512,512]{1,0:T(8,128)(2,1)}, bf16[512,512]{1,0:T(8,128)(2,1)S(1)}, u32[]{:S(2)}, u32[]{:S(2)}) collective-permute-start(bf16[512,512]{1,0:T(8,128)(2,1)} %get-tuple-element.179.refs_4_.refs_16_), channel_id=1, source_target_pairs={{0,1},{1,0},{2,3},{3,2},{4,5},{5,4},{6,7},{7,6},{8,9},{9,8},{10,11... | collective-permute-start | bytes 1572872 | tf_op jit(solution)/shard_map/ppermute | solution.py:1078
  20.5 8.3 %collective-permute-start.7 = (bf16[256,512]{1,0:T(8,128)(2,1)S(1)}, bf16[256,512]{1,0:T(8,128)(2,1)S(1)}, u32[]{:S(2)}, u32[]{:S(2)}) collective-permute-start(bf16[256,512]{1,0:T(8,128)(2,1)S(1)} %collective-permute-done.1.refs_8_.refs_20_), channel_id=1, source_target_pairs={{0,4},{1,5},{2,6},{3,7},{4,0},{5,1},{6,2},{7,3},{8,12},{9,13},{10,... | collective-permute-start | bytes 786440 | tf_op jit(solution)/shard_map/ppermute | solution.py:1078
  22.0 8.2 %collective-permute-start.6 = (bf16[512,256]{1,0:T(8,128)(2,1)}, bf16[512,256]{1,0:T(8,128)(2,1)S(1)}, u32[]{:S(2)}, u32[]{:S(2)}) collective-permute-start(bf16[512,256]{1,0:T(8,128)(2,1)} %get-tuple-element.176), channel_id=1, source_target_pairs={{0,2},{1,3},{2,0},{3,1},{4,6},{5,7},{6,4},{7,5},{8,10},{9,11},{10,... | collective-permute-start | bytes 786440 | tf_op jit(solution)/shard_map/ppermute | solution.py:1078
  22.5 4.6 %collective-permute-start.5 = (bf16[6,16,512]{2,1,0:T(8,128)(2,1)S(1)}, bf16[6,16,512]{2,1,0:T(8,128)(2,1)S(1)}, u32[]{:S(2)}, u32[]{:S(2)}) collective-permute-start(bf16[6,16,512]{2,1,0:T(8,128)(2,1)S(1)} %get-tuple-element.173), channel_id=1, source_target_pairs={{0,8},{1,9},{2,10},{3,11},{4,12},{5,13},{6,14},{7,15},{8,0},{9,1},... | collective-permute-start | bytes 294920 | tf_op jit(solution)/shard_map/ppermute | solution.py:1078
  27.1 10.9 %copy-start.3 = (bf16[512,128]{1,0:T(8,128)(2,1)S(1)}, bf16[512,128]{1,0:T(8,128)(2,1)}, u32[]{:S(2)}) copy-start(bf16[512,128]{1,0:T(8,128)(2,1)} %refs_11_.1) | copy-start | bytes 393220
  30.2 7.3 %collective-permute-start.10 = (bf16[256,512]{1,0:T(8,128)(2,1)}, bf16[256,512]{1,0:T(8,128)(2,1)S(1)}, u32[]{:S(2)}, u32[]{:S(2)}) collective-permute-start(bf16[256,512]{1,0:T(8,128)(2,1)} %get-tuple-element.183), channel_id=1, source_target_pairs={{0,2},{1,3},{2,0},{3,1},{4,6},{5,7},{6,4},{7,5},{8,10},{9,11},{10,... | collective-permute-start | bytes 786440 | tf_op jit(solution)/shard_map/ppermute | solution.py:1078
  30.8 7.3 %collective-permute-start.11 = (bf16[6,16,512]{2,1,0:T(8,128)(2,1)S(1)}, bf16[6,16,512]{2,1,0:T(8,128)(2,1)S(1)}, u32[]{:S(2)}, u32[]{:S(2)}) collective-permute-start(bf16[6,16,512]{2,1,0:T(8,128)(2,1)S(1)} %get-tuple-element.182), channel_id=1, source_target_pairs={{0,16},{1,17},{2,18},{3,19},{4,20},{5,21},{6,22},{7,23},{8,24},{9,... | collective-permute-start | bytes 294920 | tf_op jit(solution)/shard_map/ppermute | solution.py:1078
  33.3 7.6 %collective-permute-start.13 = (bf16[512,256]{1,0:T(8,128)(2,1)S(1)}, bf16[512,256]{1,0:T(8,128)(2,1)S(1)}, u32[]{:S(2)}, u32[]{:S(2)}) collective-permute-start(bf16[512,256]{1,0:T(8,128)(2,1)S(1)} %collective-permute-done.6.refs_10_.refs_22_), channel_id=1, source_target_pairs={{0,8},{1,9},{2,10},{3,11},{4,12},{5,13},{6,14},{7,15},{8,0},{9,1},... | collective-permute-start | bytes 786440 | tf_op jit(solution)/shard_map/ppermute | solution.py:1078
  34.9 6.2 %collective-permute-start.14 = (bf16[256,512]{1,0:T(8,128)(2,1)S(1)}, bf16[256,512]{1,0:T(8,128)(2,1)S(1)}, u32[]{:S(2)}, u32[]{:S(2)}) collective-permute-start(bf16[256,512]{1,0:T(8,128)(2,1)S(1)} %collective-permute-done.1.refs_8_.refs_20_), channel_id=1, source_target_pairs={{0,1},{1,0},{2,3},{3,2},{4,5},{5,4},{6,7},{7,6},{8,9},{9,8},{10,11... | collective-permute-start | bytes 786440 | tf_op jit(solution)/shard_map/ppermute | solution.py:1078
  34.9 6.6 %collective-permute-start.16 = (bf16[512,256]{1,0:T(8,128)(2,1)S(1)}, bf16[512,256]{1,0:T(8,128)(2,1)S(1)}, u32[]{:S(2)}, u32[]{:S(2)}) collective-permute-start(bf16[512,256]{1,0:T(8,128)(2,1)S(1)} %collective-permute-done.6.refs_10_.refs_22_), channel_id=1, source_target_pairs={{0,1},{1,0},{2,3},{3,2},{4,5},{5,4},{6,7},{7,6},{8,9},{9,8},{10,11... | collective-permute-start | bytes 786440 | tf_op jit(solution)/shard_map/ppermute | solution.py:1078
  37.6 6.4 %collective-permute-start.12 = (bf16[256,512]{1,0:T(8,128)(2,1)S(1)}, bf16[256,512]{1,0:T(8,128)(2,1)S(1)}, u32[]{:S(2)}, u32[]{:S(2)}) collective-permute-start(bf16[256,512]{1,0:T(8,128)(2,1)S(1)} %collective-permute-done.10.refs_8_), channel_id=1, source_target_pairs={{0,4},{1,5},{2,6},{3,7},{4,0},{5,1},{6,2},{7,3},{8,12},{9,13},{10,... | collective-permute-start | bytes 786440 | tf_op jit(solution)/shard_map/ppermute | solution.py:1078
  38.1 8.8 %collective-permute-start.18 = (bf16[512,512]{1,0:T(8,128)(2,1)S(1)}, bf16[512,512]{1,0:T(8,128)(2,1)S(1)}, u32[]{:S(2)}, u32[]{:S(2)}) collective-permute-start(bf16[512,512]{1,0:T(8,128)(2,1)S(1)} %copy-done.4), channel_id=1, source_target_pairs={{0,1},{1,0},{2,3},{3,2},{4,5},{5,4},{6,7},{7,6},{8,9},{9,8},{10,11... | collective-permute-start | bytes 1572872 | tf_op jit(solution)/shard_map/ppermute | solution.py:1078
  38.1 5.9 %copy-start.1 = (bf16[512,512]{1,0:T(8,128)(2,1)S(1)}, bf16[512,512]{1,0:T(8,128)(2,1)}, u32[]{:S(2)}) copy-start(bf16[512,512]{1,0:T(8,128)(2,1)} %get-tuple-element.179.refs_4_.refs_16_) | copy-start | bytes 1572868
  38.1 5.9 %copy-start.2 = (bf16[512,512]{1,0:T(8,128)(2,1)S(1)}, bf16[512,512]{1,0:T(8,128)(2,1)}, u32[]{:S(2)}) copy-start(bf16[512,512]{1,0:T(8,128)(2,1)} %get-tuple-element.181.refs_5_.refs_17_) | copy-start | bytes 1572868
  41.0 3.0 %collective-permute-start.15 = (bf16[256,512]{1,0:T(8,128)(2,1)S(1)}, bf16[256,512]{1,0:T(8,128)(2,1)S(1)}, u32[]{:S(2)}, u32[]{:S(2)}) collective-permute-start(bf16[256,512]{1,0:T(8,128)(2,1)S(1)} %collective-permute-done.7.refs_9_.refs_21_), channel_id=1, source_target_pairs={{0,1},{1,0},{2,3},{3,2},{4,5},{5,4},{6,7},{7,6},{8,9},{9,8},{10,11... | collective-permute-start | bytes 786440 | tf_op jit(solution)/shard_map/ppermute | solution.py:1078
  41.1 2.8 %collective-permute-start.17 = (bf16[512,256]{1,0:T(8,128)(2,1)S(1)}, bf16[512,256]{1,0:T(8,128)(2,1)S(1)}, u32[]{:S(2)}, u32[]{:S(2)}) collective-permute-start(bf16[512,256]{1,0:T(8,128)(2,1)S(1)} %collective-permute-done.13.refs_11_.refs_23_), channel_id=1, source_target_pairs={{0,1},{1,0},{2,3},{3,2},{4,5},{5,4},{6,7},{7,6},{8,9},{9,8},{10,11... | collective-permute-start | bytes 786440 | tf_op jit(solution)/shard_map/ppermute | solution.py:1078
  41.5 5.4 %collective-permute-start.19 = (bf16[256,512]{1,0:T(8,128)(2,1)S(1)}, bf16[256,512]{1,0:T(8,128)(2,1)S(1)}, u32[]{:S(2)}, u32[]{:S(2)}) collective-permute-start(bf16[256,512]{1,0:T(8,128)(2,1)S(1)} %collective-permute-done.10.refs_8_), channel_id=1, source_target_pairs={{0,1},{1,0},{2,3},{3,2},{4,5},{5,4},{6,7},{7,6},{8,9},{9,8},{10,11... | collective-permute-start | bytes 786440 | tf_op jit(solution)/shard_map/ppermute | solution.py:1078
  43.9 2.9 %collective-permute-start.20 = (bf16[256,512]{1,0:T(8,128)(2,1)S(1)}, bf16[256,512]{1,0:T(8,128)(2,1)S(1)}, u32[]{:S(2)}, u32[]{:S(2)}) collective-permute-start(bf16[256,512]{1,0:T(8,128)(2,1)S(1)} %collective-permute-done.12.refs_9_), channel_id=1, source_target_pairs={{0,1},{1,0},{2,3},{3,2},{4,5},{5,4},{6,7},{7,6},{8,9},{9,8},{10,11... | collective-permute-start | bytes 786440 | tf_op jit(solution)/shard_map/ppermute | solution.py:1078
  43.9 2.9 %copy-start.5 = (bf16[2,128,512]{2,1,0:T(8,128)(2,1)S(1)}, bf16[2,128,512]{2,1,0:T(8,128)(2,1)}, u32[]{:S(2)}) copy-start(bf16[2,128,512]{2,1,0:T(8,128)(2,1)} %refs_1_.1) | copy-start | bytes 786436
  51.0 2.9 %collective-permute-start.22 = (bf16[2,512,512]{2,1,0:T(8,128)(2,1)S(1)}, bf16[2,512,512]{2,1,0:T(8,128)(2,1)S(1)}, u32[]{:S(2)}, u32[]{:S(2)}) collective-permute-start(bf16[2,512,512]{2,1,0:T(8,128)(2,1)S(1)} %get-tuple-element.210), channel_id=1, source_target_pairs={{0,1},{1,0},{2,3},{3,2},{4,5},{5,4},{6,7},{7,6},{8,9},{9,8},{10,11... | collective-permute-start | bytes 3145736 | tf_op jit(solution)/shard_map/ppermute | solution.py:1078
  52.7 2.8 %collective-permute-start.21 = (bf16[2,512,512]{2,1,0:T(8,128)(2,1)S(1)}, bf16[2,512,512]{2,1,0:T(8,128)(2,1)S(1)}, u32[]{:S(2)}, u32[]{:S(2)}) collective-permute-start(bf16[2,512,512]{2,1,0:T(8,128)(2,1)S(1)} %get-tuple-element.208), channel_id=1, source_target_pairs={{0,1},{1,0},{2,3},{3,2},{4,5},{5,4},{6,7},{7,6},{8,9},{9,8},{10,11... | collective-permute-start | bytes 3145736 | tf_op jit(solution)/shard_map/ppermute | solution.py:1078
  54.2 14.3 %collective-permute-start.23 = (bf16[1,512,512]{2,1,0:T(8,128)(2,1)S(1)}, bf16[1,512,512]{2,1,0:T(8,128)(2,1)S(1)}, u32[]{:S(2)}, u32[]{:S(2)}) collective-permute-start(bf16[1,512,512]{2,1,0:T(8,128)(2,1)S(1)} %get-tuple-element.226), channel_id=1, source_target_pairs={{0,2},{1,3},{2,0},{3,1},{4,6},{5,7},{6,4},{7,5},{8,10},{9,11},{10,... | collective-permute-start | bytes 1572872 | tf_op jit(solution)/shard_map/ppermute | solution.py:1078
  55.8 14.1 %collective-permute-start.24 = (bf16[2,256,512]{2,1,0:T(8,128)(2,1)S(1)}, bf16[2,256,512]{2,1,0:T(8,128)(2,1)S(1)}, u32[]{:S(2)}, u32[]{:S(2)}) collective-permute-start(bf16[2,256,512]{2,1,0:T(8,128)(2,1)S(1)} %get-tuple-element.229), channel_id=1, source_target_pairs={{0,4},{1,5},{2,6},{3,7},{4,0},{5,1},{6,2},{7,3},{8,12},{9,13},{10,... | collective-permute-start | bytes 1572872 | tf_op jit(solution)/shard_map/ppermute | solution.py:1078
  70.1 3.1 %collective-permute-start.26 = (bf16[2,512,512]{2,1,0:T(8,128)(2,1)S(1)}, bf16[2,512,512]{2,1,0:T(8,128)(2,1)S(1)}, u32[]{:S(2)}, u32[]{:S(2)}) collective-permute-start(bf16[2,512,512]{2,1,0:T(8,128)(2,1)S(1)} %get-tuple-element.237), channel_id=1, source_target_pairs={{0,1},{1,0},{2,3},{3,2},{4,5},{5,4},{6,7},{7,6},{8,9},{9,8},{10,11... | collective-permute-start | bytes 3145736 | tf_op jit(solution)/shard_map/ppermute | solution.py:1078
  70.2 3.0 %collective-permute-start.25 = (f32[128,512]{1,0:T(8,128)S(1)}, f32[128,512]{1,0:T(8,128)S(1)}, u32[]{:S(2)}, u32[]{:S(2)}) collective-permute-start(f32[128,512]{1,0:T(8,128)S(1)} %get-tuple-element.235), channel_id=1, source_target_pairs={{0,1},{1,0},{2,3},{3,2},{4,5},{5,4},{6,7},{7,6},{8,9},{9,8},{10,11... | collective-permute-start | bytes 786440 | tf_op jit(solution)/shard_map/ppermute | solution.py:1078
  70.7 9.2 %collective-permute-start.27 = (bf16[1,256,512]{2,1,0:T(8,128)(2,1)S(1)}, bf16[1,256,512]{2,1,0:T(8,128)(2,1)S(1)}, u32[]{:S(2)}, u32[]{:S(2)}) collective-permute-start(bf16[1,256,512]{2,1,0:T(8,128)(2,1)S(1)} %get-tuple-element.241), channel_id=1, source_target_pairs={{0,4},{1,5},{2,6},{3,7},{4,0},{5,1},{6,2},{7,3},{8,12},{9,13},{10,... | collective-permute-start | bytes 786440 | tf_op jit(solution)/shard_map/ppermute | solution.py:1078
  71.2 9.2 %collective-permute-start.28 = (bf16[1,256,512]{2,1,0:T(8,128)(2,1)S(1)}, bf16[1,256,512]{2,1,0:T(8,128)(2,1)S(1)}, u32[]{:S(2)}, u32[]{:S(2)}) collective-permute-start(bf16[1,256,512]{2,1,0:T(8,128)(2,1)S(1)} %get-tuple-element.242), channel_id=1, source_target_pairs={{0,2},{1,3},{2,0},{3,1},{4,6},{5,7},{6,4},{7,5},{8,10},{9,11},{10,... | collective-permute-start | bytes 786440 | tf_op jit(solution)/shard_map/ppermute | solution.py:1078
  73.7 12.9 %collective-permute-start.29 = (bf16[672,256]{1,0:T(8,128)(2,1)S(1)}, bf16[672,256]{1,0:T(8,128)(2,1)S(1)}, u32[]{:S(2)}, u32[]{:S(2)}) collective-permute-start(bf16[672,256]{1,0:T(8,128)(2,1)S(1)} %get-tuple-element.239.refs_3_), channel_id=1, source_target_pairs={{0,2},{1,3},{2,0},{3,1},{4,6},{5,7},{6,4},{7,5},{8,10},{9,11},{10,... | collective-permute-start | bytes 1032200 | tf_op jit(solution)/shard_map/ppermute | solution.py:1078
  74.9 9.6 %collective-permute-start.30 = (bf16[2,256,256]{2,1,0:T(8,128)(2,1)S(1)}, bf16[2,256,256]{2,1,0:T(8,128)(2,1)S(1)}, u32[]{:S(2)}, u32[]{:S(2)}) collective-permute-start(bf16[2,256,256]{2,1,0:T(8,128)(2,1)S(1)} %get-tuple-element.248), channel_id=1, source_target_pairs={{0,4},{1,5},{2,6},{3,7},{4,0},{5,1},{6,2},{7,3},{8,12},{9,13},{10,... | collective-permute-start | bytes 786440 | tf_op jit(solution)/shard_map/ppermute | solution.py:1078
  80.6 9.0 %collective-permute-start.31 = (bf16[2,128,512]{2,1,0:T(8,128)(2,1)S(1)}, bf16[2,128,512]{2,1,0:T(8,128)(2,1)S(1)}, u32[]{:S(2)}, u32[]{:S(2)}) collective-permute-start(bf16[2,128,512]{2,1,0:T(8,128)(2,1)S(1)} %get-tuple-element.252), channel_id=1, source_target_pairs={{0,8},{1,9},{2,10},{3,11},{4,12},{5,13},{6,14},{7,15},{8,0},{9,1},... | collective-permute-start | bytes 786440 | tf_op jit(solution)/shard_map/ppermute | solution.py:1078
  86.8 6.6 %collective-permute-start.32 = (bf16[416,256]{1,0:T(8,128)(2,1)S(1)}, bf16[416,256]{1,0:T(8,128)(2,1)S(1)}, u32[]{:S(2)}, u32[]{:S(2)}) collective-permute-start(bf16[416,256]{1,0:T(8,128)(2,1)S(1)} %get-tuple-element.250.refs_3_), channel_id=1, source_target_pairs={{0,4},{1,5},{2,6},{3,7},{4,0},{5,1},{6,2},{7,3},{8,12},{9,13},{10,... | collective-permute-start | bytes 638984 | tf_op jit(solution)/shard_map/ppermute | solution.py:1078
  88.4 5.0 %collective-permute-start.33 = (bf16[256,256]{1,0:T(8,128)(2,1)S(1)}, bf16[256,256]{1,0:T(8,128)(2,1)S(1)}, u32[]{:S(2)}, u32[]{:S(2)}) collective-permute-start(bf16[256,256]{1,0:T(8,128)(2,1)S(1)} %get-tuple-element.257), channel_id=1, source_target_pairs={{0,2},{1,3},{2,0},{3,1},{4,6},{5,7},{6,4},{7,5},{8,10},{9,11},{10,... | collective-permute-start | bytes 393224 | tf_op jit(solution)/shard_map/ppermute | solution.py:1078
  89.7 14.4 %collective-permute-start.35 = (bf16[2,128,512]{2,1,0:T(8,128)(2,1)S(1)}, bf16[2,128,512]{2,1,0:T(8,128)(2,1)S(1)}, u32[]{:S(2)}, u32[]{:S(2)}) collective-permute-start(bf16[2,128,512]{2,1,0:T(8,128)(2,1)S(1)} %fold.12.refs_0_), channel_id=1, source_target_pairs={{0,16},{1,17},{2,18},{3,19},{4,20},{5,21},{6,22},{7,23},{8,24},{9,... | collective-permute-start | bytes 786440 | tf_op jit(solution)/shard_map/ppermute | solution.py:1078
  93.5 10.5 %collective-permute-start.34 = (bf16[208,512]{1,0:T(8,128)(2,1)S(1)}, bf16[208,512]{1,0:T(8,128)(2,1)S(1)}, u32[]{:S(2)}, u32[]{:S(2)}) collective-permute-start(bf16[208,512]{1,0:T(8,128)(2,1)S(1)} %get-tuple-element.259.refs_3_), channel_id=1, source_target_pairs={{0,8},{1,9},{2,10},{3,11},{4,12},{5,13},{6,14},{7,15},{8,0},{9,1},... | collective-permute-start | bytes 638984 | tf_op jit(solution)/shard_map/ppermute | solution.py:1078
  104.2 11.1 %collective-permute-start.36 = (bf16[2,128,512]{2,1,0:T(8,128)(2,1)S(1)}, bf16[2,128,512]{2,1,0:T(8,128)(2,1)S(1)}, u32[]{:S(2)}, u32[]{:S(2)}) collective-permute-start(bf16[2,128,512]{2,1,0:T(8,128)(2,1)S(1)} %fold.13.refs_0_), channel_id=1, source_target_pairs={{0,8},{1,9},{2,10},{3,11},{4,12},{5,13},{6,14},{7,15},{8,0},{9,1},... | collective-permute-start | bytes 786440 | tf_op jit(solution)/shard_map/ppermute | solution.py:1078
  104.2 12.1 %collective-permute-start.37 = (bf16[208,512]{1,0:T(8,128)(2,1)S(1)}, bf16[208,512]{1,0:T(8,128)(2,1)S(1)}, u32[]{:S(2)}, u32[]{:S(2)}) collective-permute-start(bf16[208,512]{1,0:T(8,128)(2,1)S(1)} %get-tuple-element.264.refs_3_), channel_id=1, source_target_pairs={{0,16},{1,17},{2,18},{3,19},{4,20},{5,21},{6,22},{7,23},{8,24},{9,... | collective-permute-start | bytes 638984 | tf_op jit(solution)/shard_map/ppermute | solution.py:1078
  115.4 13.1 %collective-permute-start.40 = (bf16[2,256,512]{2,1,0:T(8,128)(2,1)S(1)}, bf16[2,256,512]{2,1,0:T(8,128)(2,1)S(1)}, u32[]{:S(2)}, u32[]{:S(2)}) collective-permute-start(bf16[2,256,512]{2,1,0:T(8,128)(2,1)S(1)} %join.2.refs_0_), channel_id=1, source_target_pairs={{0,4},{1,5},{2,6},{3,7},{4,0},{5,1},{6,2},{7,3},{8,12},{9,13},{10,... | collective-permute-start | bytes 1572872 | tf_op jit(solution)/shard_map/ppermute | solution.py:1078
  116.4 5.3 %collective-permute-start.38 = (bf16[1,128,512]{2,1,0:T(8,128)(2,1)S(1)}, bf16[1,128,512]{2,1,0:T(8,128)(2,1)S(1)}, u32[]{:S(2)}, u32[]{:S(2)}) collective-permute-start(bf16[1,128,512]{2,1,0:T(8,128)(2,1)S(1)} %bitcast.25), channel_id=1, source_target_pairs={{0,8},{1,9},{2,10},{3,11},{4,12},{5,13},{6,14},{7,15},{8,0},{9,1},... | collective-permute-start | bytes 393224 | tf_op jit(solution)/shard_map/ppermute | solution.py:1078
  118.0 4.8 %collective-permute-start.39 = (f32[48,512]{1,0:T(8,128)S(1)}, f32[48,512]{1,0:T(8,128)S(1)}, u32[]{:S(2)}, u32[]{:S(2)}) collective-permute-start(f32[48,512]{1,0:T(8,128)S(1)} %get-tuple-element.276.refs_0_), channel_id=1, source_target_pairs={{0,2},{1,3},{2,0},{3,1},{4,6},{5,7},{6,4},{7,5},{8,10},{9,11},{10,... | collective-permute-start | bytes 294920 | tf_op jit(solution)/shard_map/ppermute | solution.py:1078
  121.7 9.5 %collective-permute-start.42 = (bf16[1,256,512]{2,1,0:T(8,128)(2,1)S(1)}, bf16[1,256,512]{2,1,0:T(8,128)(2,1)S(1)}, u32[]{:S(2)}, u32[]{:S(2)}) collective-permute-start(bf16[1,256,512]{2,1,0:T(8,128)(2,1)S(1)} %join.3.refs_0_), channel_id=1, source_target_pairs={{0,4},{1,5},{2,6},{3,7},{4,0},{5,1},{6,2},{7,3},{8,12},{9,13},{10,... | collective-permute-start | bytes 786440 | tf_op jit(solution)/shard_map/ppermute | solution.py:1078
  122.9 7.0 %collective-permute-start.41 = (f32[96,512]{1,0:T(8,128)S(1)}, f32[96,512]{1,0:T(8,128)S(1)}, u32[]{:S(2)}, u32[]{:S(2)}) collective-permute-start(f32[96,512]{1,0:T(8,128)S(1)} %pair.1.refs_3_), channel_id=1, source_target_pairs={{0,1},{1,0},{2,3},{3,2},{4,5},{5,4},{6,7},{7,6},{8,9},{9,8},{10,11... | collective-permute-start | bytes 589832 | tf_op jit(solution)/shard_map/ppermute | solution.py:1078

commit v7 on v6

--- a/solution.py
+++ b/solution.py
@@ -213,19 +213,6 @@
     lax.fori_loop(0, seqs * BLOCKS, body, 0)
     ends[2 * seqs] = par[1]
     put_low(low, [ends[i] for i in range(2 * seqs)])
-
-
-def first_half_kernel(w_value, w_reset, h1, sems):
-    vb, cut = w_value.shape[1], D // 2
-    at = pl.ds(pl.multiple_of(jnp.bitwise_and(lax.axis_index("seq"), 1) * cut, cut), cut)
-    copies = [
-        pltpu.make_async_copy(w.at[at, :], h1.at[:, pl.ds(i * vb, vb)], sems.at[i])
-        for i, w in enumerate((w_value, w_reset))
-    ]
-    for c in copies:
-        c.start()
-    for c in copies:
-        c.wait()
 
 
 def pack_kernel(
@@ -1212,16 +1199,8 @@
     start = 1 - int(traded)
     groups = [(0, 1)] * start + [(start, 2)] + [(i, 1) for i in range(start + 2, levels)]
     hops = []
-    (half1,) = call(
-        first_half_kernel,
-        (shape((D // 2, 2 * vb), BF16),),
-        [pltpu.SemaphoreType.DMA((2,))],
-        (w_value, w_reset),
-        [ANY] * 2,
-        "half",
-        limit=60,
-        outs=(pl.BlockSpec(),),
-    )
+    first_half = has(lax.axis_index("seq"), 1)
+    half1 = jnp.concatenate([half_of(w, first_half) for w in (w_value, w_reset)], axis=1)
     mine1 = swap(half1, top)
     state = ends
     for i, (shift, bits) in enumerate(groups):

time: 132 us -> 132 us (level)
  Pallas kernels: 37.1 us -> 35.7 us
    pallas_call x30 -> x29, Pallas kernels: 37.1 us -> 35.7 us  [call(): pl.pallas_call(body, out_shape=out, in_specs=specs, out_specs=outs or jax...]
where the time goes in v7:
time: 132 us; the launch traced here: 131 us
  waiting for transfers between devices  51.9 us (39%)
  starting transfers between devices  41 us (31%)
  Pallas kernels  35.7 us (27%)
  local copies, waits for them, and re-layouts  1.72 us (1%)
    ppermute x43, waiting for transfers between devices, swap(): return lax.ppermute(value, BOTH, [(i, i ^ mask) for i in range(count)])  51.9 us
    ppermute x43, starting transfers between devices, swap(): return lax.ppermute(value, BOTH, [(i, i ^ mask) for i in range(count)])  41 us
    pallas_call x29, Pallas kernels, call(): pl.pallas_call(body, out_shape=out, in_specs=specs, out_specs=outs or jax...  35.7 us
  transfers between devices with their start and end apart: 43, of which 23 were waited for; matrix products, arithmetic and copies ran while one was open for 0% of the time, Pallas kernels for 23%

profile of v7, /device:TPU:0, one launch (start us, length us, event | category | flops | bytes accessed | tf_op | source)
XLA Modules:
  0.0 131.4 jit_solution(1384703212872498021)
XLA Ops:
  0.7 1.0 constant_dynamic-slice_fusion
  1.7 3.0 %collective-permute-start.1 = (bf16[256,512]{1,0:T(8,128)(2,1)S(1)}, bf16[256,512]{1,0:T(8,128)(2,1)S(1)}, u32[]{:S(2)}, u32[]{:S(2)}) collective-permute-start(bf16[256,512]{1,0:T(8,128)(2,1)S(1)} %pad_maximum_fusion), channel_id=1, source_target_pairs={{0,2},{1,3},{2,0},{3,1},{4,6},{5,7},{6,4},{7,5},{8,10},{9,11},{10,... | collective-permute-start | bytes 786440 | tf_op jit(solution)/shard_map/ppermute | solution.py:1065
  4.8 0.6 copy-done.11
  5.5 3.0 %enter.1 = (bf16[256,512]{1,0:T(8,128)(2,1)S(1)}, f32[5,16,512]{2,1,0:T(8,128)S(1)}, f32[2,2,16,8,512]{4,3,2,1,0:T(8,128)S(1)}, f32[5,16,512]{2,1,0:T(8,128)S(1)}, bf16[6,16,512]{2,1,0:T(8,128)(2,1)S(1)}) custom-call(s32[2]{0:T(128)S(1)} %copy-done.12, bf16[2,128,512]{2,1,0:T(8,128)(2,1)S(1)} %copy-done, f32[1,512]{1,0:T(1,128)S(1)} %bitcast.29, ...), custom_call_target="tpu_custom_call" | custom-call | tf_op jit(solution)/shard_map/enter/pallas_call | solution.py:118
  8.6 1.3 collective-permute-done.refs_1_.refs_4_
  10.0 1.1 collective-permute-done.1.refs_8_.refs_20_
  11.0 2.7 %collective-permute-start.4 = (bf16[6,16,512]{2,1,0:T(8,128)(2,1)S(1)}, bf16[6,16,512]{2,1,0:T(8,128)(2,1)S(1)}, u32[]{:S(2)}, u32[]{:S(2)}) collective-permute-start(bf16[6,16,512]{2,1,0:T(8,128)(2,1)S(1)} %get-tuple-element.162), channel_id=1, source_target_pairs={{0,6},{1,7},{2,4},{3,5},{4,2},{5,3},{6,0},{7,1},{8,14},{9,15},{10,... | collective-permute-start | bytes 294920 | tf_op jit(solution)/shard_map/ppermute | solution.py:1065
  13.7 0.5 collective-permute-start.3
  14.5 2.9 %pack.1 = (bf16[512,512]{1,0:T(8,128)(2,1)}, bf16[512,512]{1,0:T(8,128)(2,1)}, bf16[512,512]{1,0:T(8,128)(2,1)}, bf16[512,256]{1,0:T(8,128)(2,1)}, bf16[256,512]{1,0:T(8,128)(2,1)}) custom-call(bf16[512,256]{1,0:T(8,128)(2,1)} %w_value, bf16[512,256]{1,0:T(8,128)(2,1)} %w_reset, bf16[128,512]{1,0:T(8,128)(2,1)} %w_hidden, bf16[128,512]{1,0:T(8,128)(2,1)} %w_update, ...), custom_call_target="tpu_custom_call" | custom-call | tf_op jit(solution)/shard_map/pack/pallas_call | solution.py:118
  17.5 0.9 collective-permute-done.3.refs_2_.refs_6_
  18.4 0.5 collective-permute-done.2.refs_1_.refs_5_
  19.6 1.5 %collective-permute-start.7 = (bf16[256,512]{1,0:T(8,128)(2,1)S(1)}, bf16[256,512]{1,0:T(8,128)(2,1)S(1)}, u32[]{:S(2)}, u32[]{:S(2)}) collective-permute-start(bf16[256,512]{1,0:T(8,128)(2,1)S(1)} %collective-permute-done.1.refs_8_.refs_20_), channel_id=1, source_target_pairs={{0,4},{1,5},{2,6},{3,7},{4,0},{5,1},{6,2},{7,3},{8,12},{9,13},{10,... | collective-permute-start | bytes 786440 | tf_op jit(solution)/shard_map/ppermute | solution.py:1065
  21.1 0.5 collective-permute-start.6
  21.6 1.6 %collective-permute-start.5 = (bf16[6,16,512]{2,1,0:T(8,128)(2,1)S(1)}, bf16[6,16,512]{2,1,0:T(8,128)(2,1)S(1)}, u32[]{:S(2)}, u32[]{:S(2)}) collective-permute-start(bf16[6,16,512]{2,1,0:T(8,128)(2,1)S(1)} %get-tuple-element.173), channel_id=1, source_target_pairs={{0,8},{1,9},{2,10},{3,11},{4,12},{5,13},{6,14},{7,15},{8,0},{9,1},... | collective-permute-start | bytes 294920 | tf_op jit(solution)/shard_map/ppermute | solution.py:1065
  23.2 3.0 %collective-permute-done.5.refs_1_.refs_8_ = bf16[6,16,512]{2,1,0:T(8,128)(2,1)S(1)} collective-permute-done((bf16[6,16,512]{2,1,0:T(8,128)(2,1)S(1)}, bf16[6,16,512]{2,1,0:T(8,128)(2,1)S(1)}, u32[]{:S(2)}, u32[]{:S(2)}) %collective-permute-start.5) | collective-permute-done | bytes 98336 | tf_op jit(solution)/shard_map/ppermute | solution.py:1065
  26.2 0.7 hop.5
  27.0 0.9 collective-permute-done.7.refs_9_.refs_21_
  27.9 1.4 %collective-permute-done.6.refs_10_.refs_22_ = bf16[512,256]{1,0:T(8,128)(2,1)S(1)} collective-permute-done((bf16[512,256]{1,0:T(8,128)(2,1)}, bf16[512,256]{1,0:T(8,128)(2,1)S(1)}, u32[]{:S(2)}, u32[]{:S(2)}) %collective-permute-start.6) | collective-permute-done | bytes 262176 | tf_op jit(solution)/shard_map/ppermute | solution.py:1065
  29.3 0.5 collective-permute-start.10
  29.8 2.6 %collective-permute-start.11 = (bf16[6,16,512]{2,1,0:T(8,128)(2,1)S(1)}, bf16[6,16,512]{2,1,0:T(8,128)(2,1)S(1)}, u32[]{:S(2)}, u32[]{:S(2)}) collective-permute-start(bf16[6,16,512]{2,1,0:T(8,128)(2,1)S(1)} %get-tuple-element.182), channel_id=1, source_target_pairs={{0,16},{1,17},{2,18},{3,19},{4,20},{5,21},{6,22},{7,23},{8,24},{9,... | collective-permute-start | bytes 294920 | tf_op jit(solution)/shard_map/ppermute | solution.py:1065
  32.4 1.6 %collective-permute-start.13 = (bf16[512,256]{1,0:T(8,128)(2,1)S(1)}, bf16[512,256]{1,0:T(8,128)(2,1)S(1)}, u32[]{:S(2)}, u32[]{:S(2)}) collective-permute-start(bf16[512,256]{1,0:T(8,128)(2,1)S(1)} %collective-permute-done.6.refs_10_.refs_22_), channel_id=1, source_target_pairs={{0,8},{1,9},{2,10},{3,11},{4,12},{5,13},{6,14},{7,15},{8,0},{9,1},... | collective-permute-start | bytes 786440 | tf_op jit(solution)/shard_map/ppermute | solution.py:1065
  34.0 0.5 collective-permute-start.16
  34.5 2.1 %collective-permute-done.10.refs_8_ = bf16[256,512]{1,0:T(8,128)(2,1)S(1)} collective-permute-done((bf16[256,512]{1,0:T(8,128)(2,1)}, bf16[256,512]{1,0:T(8,128)(2,1)S(1)}, u32[]{:S(2)}, u32[]{:S(2)}) %collective-permute-start.10) | collective-permute-done | bytes 262176 | tf_op jit(solution)/shard_map/ppermute | solution.py:1065
  36.7 0.5 collective-permute-start.12
  37.2 2.4 %look.1 = (f32[2,2,16,512]{3,2,1,0:T(8,128)S(1)}, f32[256,512]{1,0:T(8,128)S(1)}, bf16[256,512]{1,0:T(8,128)(2,1)S(1)}, f32[256,128]{1,0:T(8,128)S(1)}, f32[2,128,128]{2,1,0:T(8,128)S(1)}) custom-call(bf16[256,512]{1,0:T(8,128)(2,1)S(1)} %get-tuple-element.184.refs_0_.refs_1_, f32[5,16,512]{2,1,0:T(8,128)S(1)} %get-tuple-element.185.refs_1_.refs_5_.refs_10_.refs_0_, ...), custom_call_target="tpu_custom_call" | custom-call | tf_op jit(solution)/shard_map/look/pallas_call | solution.py:118
  40.7 2.3 %collective-permute-done.12.refs_9_ = bf16[256,512]{1,0:T(8,128)(2,1)S(1)} collective-permute-done((bf16[256,512]{1,0:T(8,128)(2,1)S(1)}, bf16[256,512]{1,0:T(8,128)(2,1)S(1)}, u32[]{:S(2)}, u32[]{:S(2)}) %collective-permute-start.12) | collective-permute-done | bytes 262176 | tf_op jit(solution)/shard_map/ppermute | solution.py:1065
  43.1 2.9 %mix.1 = (bf16[4,256,256]{2,1,0:T(8,128)(2,1)S(1)}, f32[4,256,256]{2,1,0:T(8,128)S(1)}, f32[4,256,256]{2,1,0:T(8,128)S(1)}, f32[4,256,256]{2,1,0:T(8,128)S(1)}, ...) custom-call(bf16[2,128,512]{2,1,0:T(8,128)(2,1)S(1)} %copy-done, ...), custom_call_target="tpu_custom_call" | custom-call | tf_op jit(solution)/shard_map/mix/pallas_call | solution.py:118
  46.0 4.1 %ffn.1 = (bf16[256,512]{1,0:T(8,128)(2,1)}, bf16[2,512,512]{2,1,0:T(8,128)(2,1)S(1)}, bf16[2,512,512]{2,1,0:T(8,128)(2,1)S(1)}, bf16[256,1024]{1,0:T(8,128)(2,1)...) custom-call(bf16[2,128,512]{2,1,0:T(8,128)(2,1)S(1)} %copy-done, bf16[2,128,512]{2,1,0:T(8,128)(2,1)S(1)} %copy-done.5, ...), custom_call_target="tpu_custom_call" | custom-call | tf_op jit(solution)/shard_map/ffn/pallas_call | solution.py:118
  50.1 0.6 collective-permute-start.22
  50.7 1.1 gates.1
  51.9 1.1 collective-permute-done.22.refs_1_
  53.3 1.3 collective-permute-start.23
  54.9 0.6 collective-permute-start.24
  55.5 9.9 %back.1 = (bf16[2,512,512]{2,1,0:T(8,128)(2,1)S(1)}, bf16[2,512,512]{2,1,0:T(8,128)(2,1)S(1)}, f32[4,256,128]{2,1,0:T(8,128)S(1)}, f32[256,512]{1,0:T(8,128)S(1)...) custom-call(bf16[256,512]{1,0:T(8,128)(2,1)S(1)} %get-tuple-element., ...), custom_call_target="tpu_custom_call" | custom-call | tf_op jit(solution)/shard_map/back/pallas_call | solution.py:118
  65.4 2.1 %collective-permute-done.23.refs_1_ = bf16[1,512,512]{2,1,0:T(8,128)(2,1)S(1)} collective-permute-done((bf16[1,512,512]{2,1,0:T(8,128)(2,1)S(1)}, bf16[1,512,512]{2,1,0:T(8,128)(2,1)S(1)}, u32[]{:S(2)}, u32[]{:S(2)}) %collective-permute-start.23) | collective-permute-done | bytes 524320 | tf_op jit(solution)/shard_map/ppermute | solution.py:1065
  67.7 1.3 %collective-permute-done.24.refs_1_ = bf16[2,256,512]{2,1,0:T(8,128)(2,1)S(1)} collective-permute-done((bf16[2,256,512]{2,1,0:T(8,128)(2,1)S(1)}, bf16[2,256,512]{2,1,0:T(8,128)(2,1)S(1)}, u32[]{:S(2)}, u32[]{:S(2)}) %collective-permute-start.24) | collective-permute-done | bytes 524320 | tf_op jit(solution)/shard_map/ppermute | solution.py:1065
  69.8 0.5 collective-permute-start.27
  70.3 1.2 collective-permute-start.28
  71.5 0.8 collective-permute-done.25.refs_3_.refs_6_
  72.8 1.3 collective-permute-start.29
  74.1 0.5 collective-permute-start.30
  74.6 4.4 %collective-permute-done.27.refs_1_ = bf16[1,256,512]{2,1,0:T(8,128)(2,1)S(1)} collective-permute-done((bf16[1,256,512]{2,1,0:T(8,128)(2,1)S(1)}, bf16[1,256,512]{2,1,0:T(8,128)(2,1)S(1)}, u32[]{:S(2)}, u32[]{:S(2)}) %collective-permute-start.27) | collective-permute-done | bytes 262176 | tf_op jit(solution)/shard_map/ppermute | solution.py:1065
  79.0 0.5 collective-permute-done.28.refs_3_
  79.7 1.6 %collective-permute-start.31 = (bf16[2,128,512]{2,1,0:T(8,128)(2,1)S(1)}, bf16[2,128,512]{2,1,0:T(8,128)(2,1)S(1)}, u32[]{:S(2)}, u32[]{:S(2)}) collective-permute-start(bf16[2,128,512]{2,1,0:T(8,128)(2,1)S(1)} %get-tuple-element.252), channel_id=1, source_target_pairs={{0,8},{1,9},{2,10},{3,11},{4,12},{5,13},{6,14},{7,15},{8,0},{9,1},... | collective-permute-start | bytes 786440 | tf_op jit(solution)/shard_map/ppermute | solution.py:1065
  81.3 2.4 %collective-permute-done.30.refs_7_ = bf16[2,256,256]{2,1,0:T(8,128)(2,1)S(1)} collective-permute-done((bf16[2,256,256]{2,1,0:T(8,128)(2,1)S(1)}, bf16[2,256,256]{2,1,0:T(8,128)(2,1)S(1)}, u32[]{:S(2)}, u32[]{:S(2)}) %collective-permute-start.30) | collective-permute-done | bytes 262176 | tf_op jit(solution)/shard_map/ppermute | solution.py:1065
  83.7 2.0 %collective-permute-done.29.refs_4_.refs_7_ = bf16[672,256]{1,0:T(8,128)(2,1)S(1)} collective-permute-done((bf16[672,256]{1,0:T(8,128)(2,1)S(1)}, bf16[672,256]{1,0:T(8,128)(2,1)S(1)}, u32[]{:S(2)}, u32[]{:S(2)}) %collective-permute-start.29) | collective-permute-done | bytes 344096 | tf_op jit(solution)/shard_map/ppermute | solution.py:1065
  85.9 1.6 %collective-permute-start.32 = (bf16[416,256]{1,0:T(8,128)(2,1)S(1)}, bf16[416,256]{1,0:T(8,128)(2,1)S(1)}, u32[]{:S(2)}, u32[]{:S(2)}) collective-permute-start(bf16[416,256]{1,0:T(8,128)(2,1)S(1)} %get-tuple-element.250.refs_3_), channel_id=1, source_target_pairs={{0,4},{1,5},{2,6},{3,7},{4,0},{5,1},{6,2},{7,3},{8,12},{9,13},{10,... | collective-permute-start | bytes 638984 | tf_op jit(solution)/shard_map/ppermute | solution.py:1065
  87.5 1.2 collective-permute-start.33
  88.8 2.1 %collective-permute-start.35 = (bf16[2,128,512]{2,1,0:T(8,128)(2,1)S(1)}, bf16[2,128,512]{2,1,0:T(8,128)(2,1)S(1)}, u32[]{:S(2)}, u32[]{:S(2)}) collective-permute-start(bf16[2,128,512]{2,1,0:T(8,128)(2,1)S(1)} %fold.12.refs_0_), channel_id=1, source_target_pairs={{0,16},{1,17},{2,18},{3,19},{4,20},{5,21},{6,22},{7,23},{8,24},{9,... | collective-permute-start | bytes 786440 | tf_op jit(solution)/shard_map/ppermute | solution.py:1065
  90.9 1.6 %collective-permute-done.33.refs_7_ = bf16[256,256]{1,0:T(8,128)(2,1)S(1)} collective-permute-done((bf16[256,256]{1,0:T(8,128)(2,1)S(1)}, bf16[256,256]{1,0:T(8,128)(2,1)S(1)}, u32[]{:S(2)}, u32[]{:S(2)}) %collective-permute-start.33) | collective-permute-done | bytes 131104 | tf_op jit(solution)/shard_map/ppermute | solution.py:1065
  92.6 1.6 %collective-permute-start.34 = (bf16[208,512]{1,0:T(8,128)(2,1)S(1)}, bf16[208,512]{1,0:T(8,128)(2,1)S(1)}, u32[]{:S(2)}, u32[]{:S(2)}) collective-permute-start(bf16[208,512]{1,0:T(8,128)(2,1)S(1)} %get-tuple-element.259.refs_3_), channel_id=1, source_target_pairs={{0,8},{1,9},{2,10},{3,11},{4,12},{5,13},{6,14},{7,15},{8,0},{9,1},... | collective-permute-start | bytes 638984 | tf_op jit(solution)/shard_map/ppermute | solution.py:1065
  94.3 8.8 %collective-permute-done.34.refs_4_.refs_9_ = bf16[208,512]{1,0:T(8,128)(2,1)S(1)} collective-permute-done((bf16[208,512]{1,0:T(8,128)(2,1)S(1)}, bf16[208,512]{1,0:T(8,128)(2,1)S(1)}, u32[]{:S(2)}, u32[]{:S(2)}) %collective-permute-start.34) | collective-permute-done | bytes 213024 | tf_op jit(solution)/shard_map/ppermute | solution.py:1065
  103.4 4.2 %collective-permute-start.37 = (bf16[208,512]{1,0:T(8,128)(2,1)S(1)}, bf16[208,512]{1,0:T(8,128)(2,1)S(1)}, u32[]{:S(2)}, u32[]{:S(2)}) collective-permute-start(bf16[208,512]{1,0:T(8,128)(2,1)S(1)} %get-tuple-element.264.refs_3_), channel_id=1, source_target_pairs={{0,16},{1,17},{2,18},{3,19},{4,20},{5,21},{6,22},{7,23},{8,24},{9,... | collective-permute-start | bytes 638984 | tf_op jit(solution)/shard_map/ppermute | solution.py:1065
  107.6 6.9 %collective-permute-done.36.refs_1_ = bf16[2,128,512]{2,1,0:T(8,128)(2,1)S(1)} collective-permute-done((bf16[2,128,512]{2,1,0:T(8,128)(2,1)S(1)}, bf16[2,128,512]{2,1,0:T(8,128)(2,1)S(1)}, u32[]{:S(2)}, u32[]{:S(2)}) %collective-permute-start.36) | collective-permute-done | bytes 262176 | tf_op jit(solution)/shard_map/ppermute | solution.py:1065
  114.5 1.0 collective-permute-start.40
  115.5 1.6 %collective-permute-start.38 = (bf16[1,128,512]{2,1,0:T(8,128)(2,1)S(1)}, bf16[1,128,512]{2,1,0:T(8,128)(2,1)S(1)}, u32[]{:S(2)}, u32[]{:S(2)}) collective-permute-start(bf16[1,128,512]{2,1,0:T(8,128)(2,1)S(1)} %bitcast.25), channel_id=1, source_target_pairs={{0,8},{1,9},{2,10},{3,11},{4,12},{5,13},{6,14},{7,15},{8,0},{9,1},... | collective-permute-start | bytes 393224 | tf_op jit(solution)/shard_map/ppermute | solution.py:1065
  117.1 1.1 collective-permute-start.39
  118.2 2.7 %leave.1 = bf16[2,128,512]{2,1,0:T(8,128)(2,1)} custom-call(bf16[2,128,512]{2,1,0:T(8,128)(2,1)S(1)} %copy-done, f32[5,16,512]{2,1,0:T(8,128)S(1)} %get-tuple-element.185.refs_1_.refs_5_.refs_10_.refs_0_, f32[4,256,128]{2,1,0:T(8,128)S(1)} %get-tuple-element.270.refs_2_, f32[256,512]{1,0:T(8,128)S(1)} %get-tuple-element.271.refs_3_, ...), custom_call_target="tpu_custom_call" | custom-call | tf_op jit(solution)/shard_map/leave/pallas_call | solution.py:118
  120.9 1.1 collective-permute-start.42
  122.1 5.5 %collective-permute-done.40.refs_1_ = bf16[2,256,512]{2,1,0:T(8,128)(2,1)S(1)} collective-permute-done((bf16[2,256,512]{2,1,0:T(8,128)(2,1)S(1)}, bf16[2,256,512]{2,1,0:T(8,128)(2,1)S(1)}, u32[]{:S(2)}, u32[]{:S(2)}) %collective-permute-start.40) | collective-permute-done | bytes 524320 | tf_op jit(solution)/shard_map/ppermute | solution.py:1065
  127.6 1.5 %unpack.2 = (f32[512,256]{1,0:T(8,128)}, f32[256,512]{1,0:T(8,128)}, f32[128,512]{1,0:T(8,128)}, f32[128,512]{1,0:T(8,128)}, f32[256,512]{1,0:T(8,128)}) custom-call(bf16[2,256,512]{2,1,0:T(8,128)(2,1)S(1)} %join.2.refs_0_, bf16[2,256,512]{2,1,0:T(8,128)(2,1)S(1)} %collective-permute-done.40.refs_1_), custom_call_target="tpu_custom_call" | custom-call | tf_op jit(solution)/shard_map/unpack/pallas_call | solution.py:118
  129.1 0.8 finish.1
  129.9 0.5 collective-permute-done.42.refs_1_
  130.4 1.0 unpack.3
  (85 shorter events, 5.5 us)
Async XLA Ops:
  1.7 3.1 %copy-start = (bf16[2,128,512]{2,1,0:T(8,128)(2,1)S(1)}, bf16[2,128,512]{2,1,0:T(8,128)(2,1)}, u32[]{:S(2)}) copy-start(bf16[2,128,512]{2,1,0:T(8,128)(2,1)} %refs_0_.7) | copy-start | bytes 786436
  1.7 3.1 %copy-start.6 = (f32[512,16]{0,1:T(8,128)S(1)}, f32[512,16]{0,1:T(8,128)}, u32[]{:S(2)}) copy-start(f32[512,16]{0,1:T(8,128)} %param.24) | copy-start | bytes 98308
  1.7 3.1 %copy-start.7 = (f32[512,16]{0,1:T(8,128)S(1)}, f32[512,16]{0,1:T(8,128)}, u32[]{:S(2)}) copy-start(f32[512,16]{0,1:T(8,128)} %param.25) | copy-start | bytes 98308
  1.7 3.1 %copy-start.8 = (f32[512,16]{0,1:T(8,128)S(1)}, f32[512,16]{0,1:T(8,128)}, u32[]{:S(2)}) copy-start(f32[512,16]{0,1:T(8,128)} %param.26) | copy-start | bytes 98308
  1.7 9.3 %collective-permute-start.1 = (bf16[256,512]{1,0:T(8,128)(2,1)S(1)}, bf16[256,512]{1,0:T(8,128)(2,1)S(1)}, u32[]{:S(2)}, u32[]{:S(2)}) collective-permute-start(bf16[256,512]{1,0:T(8,128)(2,1)S(1)} %pad_maximum_fusion), channel_id=1, source_target_pairs={{0,2},{1,3},{2,0},{3,1},{4,6},{5,7},{6,4},{7,5},{8,10},{9,11},{10,... | collective-permute-start | bytes 786440 | tf_op jit(solution)/shard_map/ppermute | solution.py:1065
  4.7 0.7 copy-start.11
  4.7 0.7 copy-start.15
  4.7 0.7 copy-start.10
  4.7 0.7 copy-start.9
  4.7 0.7 copy-start.12
  4.8 0.7 copy-start.13
  4.8 0.7 copy-start.14
  8.5 1.4 %collective-permute-start = (bf16[6,16,512]{2,1,0:T(8,128)(2,1)S(1)}, bf16[6,16,512]{2,1,0:T(8,128)(2,1)S(1)}, u32[]{:S(2)}, u32[]{:S(2)}) collective-permute-start(bf16[6,16,512]{2,1,0:T(8,128)(2,1)S(1)} %get-tuple-element.160), channel_id=1, source_target_pairs={{0,1},{1,0},{2,3},{3,2},{4,5},{5,4},{6,7},{7,6},{8,9},{9,8},{10,11... | collective-permute-start | bytes 294920 | tf_op jit(solution)/shard_map/ppermute | solution.py:1065
  11.0 6.4 %collective-permute-start.4 = (bf16[6,16,512]{2,1,0:T(8,128)(2,1)S(1)}, bf16[6,16,512]{2,1,0:T(8,128)(2,1)S(1)}, u32[]{:S(2)}, u32[]{:S(2)}) collective-permute-start(bf16[6,16,512]{2,1,0:T(8,128)(2,1)S(1)} %get-tuple-element.162), channel_id=1, source_target_pairs={{0,6},{1,7},{2,4},{3,5},{4,2},{5,3},{6,0},{7,1},{8,14},{9,15},{10,... | collective-permute-start | bytes 294920 | tf_op jit(solution)/shard_map/ppermute | solution.py:1065
  13.7 4.6 %collective-permute-start.3 = (bf16[6,16,512]{2,1,0:T(8,128)(2,1)S(1)}, bf16[6,16,512]{2,1,0:T(8,128)(2,1)S(1)}, u32[]{:S(2)}, u32[]{:S(2)}) collective-permute-start(bf16[6,16,512]{2,1,0:T(8,128)(2,1)S(1)} %get-tuple-element.162), channel_id=1, source_target_pairs={{0,4},{1,5},{2,6},{3,7},{4,0},{5,1},{6,2},{7,3},{8,12},{9,13},{10,... | collective-permute-start | bytes 294920 | tf_op jit(solution)/shard_map/ppermute | solution.py:1065
  14.2 4.6 %collective-permute-start.2 = (bf16[6,16,512]{2,1,0:T(8,128)(2,1)S(1)}, bf16[6,16,512]{2,1,0:T(8,128)(2,1)S(1)}, u32[]{:S(2)}, u32[]{:S(2)}) collective-permute-start(bf16[6,16,512]{2,1,0:T(8,128)(2,1)S(1)} %get-tuple-element.162), channel_id=1, source_target_pairs={{0,2},{1,3},{2,0},{3,1},{4,6},{5,7},{6,4},{7,5},{8,10},{9,11},{10,... | collective-permute-start | bytes 294920 | tf_op jit(solution)/shard_map/ppermute | solution.py:1065
  17.5 19.7 %copy-start.4 = (bf16[512,512]{1,0:T(8,128)(2,1)S(1)}, bf16[512,512]{1,0:T(8,128)(2,1)}, u32[]{:S(2)}) copy-start(bf16[512,512]{1,0:T(8,128)(2,1)} %get-tuple-element.197.refs_6_) | copy-start | bytes 1572868
  19.0 10.3 %collective-permute-start.9 = (bf16[512,512]{1,0:T(8,128)(2,1)}, bf16[512,512]{1,0:T(8,128)(2,1)S(1)}, u32[]{:S(2)}, u32[]{:S(2)}) collective-permute-start(bf16[512,512]{1,0:T(8,128)(2,1)} %get-tuple-element.181.refs_5_.refs_17_), channel_id=1, source_target_pairs={{0,1},{1,0},{2,3},{3,2},{4,5},{5,4},{6,7},{7,6},{8,9},{9,8},{10,11... | collective-permute-start | bytes 1572872 | tf_op jit(solution)/shard_map/ppermute | solution.py:1065
  19.1 10.2 %collective-permute-start.8 = (bf16[512,512]{1,0:T(8,128)(2,1)}, bf16[512,512]{1,0:T(8,128)(2,1)S(1)}, u32[]{:S(2)}, u32[]{:S(2)}) collective-permute-start(bf16[512,512]{1,0:T(8,128)(2,1)} %get-tuple-element.179.refs_4_.refs_16_), channel_id=1, source_target_pairs={{0,1},{1,0},{2,3},{3,2},{4,5},{5,4},{6,7},{7,6},{8,9},{9,8},{10,11... | collective-permute-start | bytes 1572872 | tf_op jit(solution)/shard_map/ppermute | solution.py:1065
  19.6 8.3 %collective-permute-start.7 = (bf16[256,512]{1,0:T(8,128)(2,1)S(1)}, bf16[256,512]{1,0:T(8,128)(2,1)S(1)}, u32[]{:S(2)}, u32[]{:S(2)}) collective-permute-start(bf16[256,512]{1,0:T(8,128)(2,1)S(1)} %collective-permute-done.1.refs_8_.refs_20_), channel_id=1, source_target_pairs={{0,4},{1,5},{2,6},{3,7},{4,0},{5,1},{6,2},{7,3},{8,12},{9,13},{10,... | collective-permute-start | bytes 786440 | tf_op jit(solution)/shard_map/ppermute | solution.py:1065
  21.1 8.2 %collective-permute-start.6 = (bf16[512,256]{1,0:T(8,128)(2,1)}, bf16[512,256]{1,0:T(8,128)(2,1)S(1)}, u32[]{:S(2)}, u32[]{:S(2)}) collective-permute-start(bf16[512,256]{1,0:T(8,128)(2,1)} %get-tuple-element.176), channel_id=1, source_target_pairs={{0,2},{1,3},{2,0},{3,1},{4,6},{5,7},{6,4},{7,5},{8,10},{9,11},{10,... | collective-permute-start | bytes 786440 | tf_op jit(solution)/shard_map/ppermute | solution.py:1065
  21.6 4.6 %collective-permute-start.5 = (bf16[6,16,512]{2,1,0:T(8,128)(2,1)S(1)}, bf16[6,16,512]{2,1,0:T(8,128)(2,1)S(1)}, u32[]{:S(2)}, u32[]{:S(2)}) collective-permute-start(bf16[6,16,512]{2,1,0:T(8,128)(2,1)S(1)} %get-tuple-element.173), channel_id=1, source_target_pairs={{0,8},{1,9},{2,10},{3,11},{4,12},{5,13},{6,14},{7,15},{8,0},{9,1},... | collective-permute-start | bytes 294920 | tf_op jit(solution)/shard_map/ppermute | solution.py:1065
  26.2 10.9 %copy-start.3 = (bf16[512,128]{1,0:T(8,128)(2,1)S(1)}, bf16[512,128]{1,0:T(8,128)(2,1)}, u32[]{:S(2)}) copy-start(bf16[512,128]{1,0:T(8,128)(2,1)} %refs_11_.1) | copy-start | bytes 393220
  29.3 7.3 %collective-permute-start.10 = (bf16[256,512]{1,0:T(8,128)(2,1)}, bf16[256,512]{1,0:T(8,128)(2,1)S(1)}, u32[]{:S(2)}, u32[]{:S(2)}) collective-permute-start(bf16[256,512]{1,0:T(8,128)(2,1)} %get-tuple-element.183), channel_id=1, source_target_pairs={{0,2},{1,3},{2,0},{3,1},{4,6},{5,7},{6,4},{7,5},{8,10},{9,11},{10,... | collective-permute-start | bytes 786440 | tf_op jit(solution)/shard_map/ppermute | solution.py:1065
  29.8 7.3 %collective-permute-start.11 = (bf16[6,16,512]{2,1,0:T(8,128)(2,1)S(1)}, bf16[6,16,512]{2,1,0:T(8,128)(2,1)S(1)}, u32[]{:S(2)}, u32[]{:S(2)}) collective-permute-start(bf16[6,16,512]{2,1,0:T(8,128)(2,1)S(1)} %get-tuple-element.182), channel_id=1, source_target_pairs={{0,16},{1,17},{2,18},{3,19},{4,20},{5,21},{6,22},{7,23},{8,24},{9,... | collective-permute-start | bytes 294920 | tf_op jit(solution)/shard_map/ppermute | solution.py:1065
  32.4 7.6 %collective-permute-start.13 = (bf16[512,256]{1,0:T(8,128)(2,1)S(1)}, bf16[512,256]{1,0:T(8,128)(2,1)S(1)}, u32[]{:S(2)}, u32[]{:S(2)}) collective-permute-start(bf16[512,256]{1,0:T(8,128)(2,1)S(1)} %collective-permute-done.6.refs_10_.refs_22_), channel_id=1, source_target_pairs={{0,8},{1,9},{2,10},{3,11},{4,12},{5,13},{6,14},{7,15},{8,0},{9,1},... | collective-permute-start | bytes 786440 | tf_op jit(solution)/shard_map/ppermute | solution.py:1065
  34.0 6.2 %collective-permute-start.14 = (bf16[256,512]{1,0:T(8,128)(2,1)S(1)}, bf16[256,512]{1,0:T(8,128)(2,1)S(1)}, u32[]{:S(2)}, u32[]{:S(2)}) collective-permute-start(bf16[256,512]{1,0:T(8,128)(2,1)S(1)} %collective-permute-done.1.refs_8_.refs_20_), channel_id=1, source_target_pairs={{0,1},{1,0},{2,3},{3,2},{4,5},{5,4},{6,7},{7,6},{8,9},{9,8},{10,11... | collective-permute-start | bytes 786440 | tf_op jit(solution)/shard_map/ppermute | solution.py:1065
  34.0 6.6 %collective-permute-start.16 = (bf16[512,256]{1,0:T(8,128)(2,1)S(1)}, bf16[512,256]{1,0:T(8,128)(2,1)S(1)}, u32[]{:S(2)}, u32[]{:S(2)}) collective-permute-start(bf16[512,256]{1,0:T(8,128)(2,1)S(1)} %collective-permute-done.6.refs_10_.refs_22_), channel_id=1, source_target_pairs={{0,1},{1,0},{2,3},{3,2},{4,5},{5,4},{6,7},{7,6},{8,9},{9,8},{10,11... | collective-permute-start | bytes 786440 | tf_op jit(solution)/shard_map/ppermute | solution.py:1065
  36.7 6.4 %collective-permute-start.12 = (bf16[256,512]{1,0:T(8,128)(2,1)S(1)}, bf16[256,512]{1,0:T(8,128)(2,1)S(1)}, u32[]{:S(2)}, u32[]{:S(2)}) collective-permute-start(bf16[256,512]{1,0:T(8,128)(2,1)S(1)} %collective-permute-done.10.refs_8_), channel_id=1, source_target_pairs={{0,4},{1,5},{2,6},{3,7},{4,0},{5,1},{6,2},{7,3},{8,12},{9,13},{10,... | collective-permute-start | bytes 786440 | tf_op jit(solution)/shard_map/ppermute | solution.py:1065
  37.2 8.8 %collective-permute-start.18 = (bf16[512,512]{1,0:T(8,128)(2,1)S(1)}, bf16[512,512]{1,0:T(8,128)(2,1)S(1)}, u32[]{:S(2)}, u32[]{:S(2)}) collective-permute-start(bf16[512,512]{1,0:T(8,128)(2,1)S(1)} %copy-done.4), channel_id=1, source_target_pairs={{0,1},{1,0},{2,3},{3,2},{4,5},{5,4},{6,7},{7,6},{8,9},{9,8},{10,11... | collective-permute-start | bytes 1572872 | tf_op jit(solution)/shard_map/ppermute | solution.py:1065
  37.2 5.9 %copy-start.1 = (bf16[512,512]{1,0:T(8,128)(2,1)S(1)}, bf16[512,512]{1,0:T(8,128)(2,1)}, u32[]{:S(2)}) copy-start(bf16[512,512]{1,0:T(8,128)(2,1)} %get-tuple-element.179.refs_4_.refs_16_) | copy-start | bytes 1572868
  37.2 5.9 %copy-start.2 = (bf16[512,512]{1,0:T(8,128)(2,1)S(1)}, bf16[512,512]{1,0:T(8,128)(2,1)}, u32[]{:S(2)}) copy-start(bf16[512,512]{1,0:T(8,128)(2,1)} %get-tuple-element.181.refs_5_.refs_17_) | copy-start | bytes 1572868
  40.1 3.0 %collective-permute-start.15 = (bf16[256,512]{1,0:T(8,128)(2,1)S(1)}, bf16[256,512]{1,0:T(8,128)(2,1)S(1)}, u32[]{:S(2)}, u32[]{:S(2)}) collective-permute-start(bf16[256,512]{1,0:T(8,128)(2,1)S(1)} %collective-permute-done.7.refs_9_.refs_21_), channel_id=1, source_target_pairs={{0,1},{1,0},{2,3},{3,2},{4,5},{5,4},{6,7},{7,6},{8,9},{9,8},{10,11... | collective-permute-start | bytes 786440 | tf_op jit(solution)/shard_map/ppermute | solution.py:1065
  40.2 2.8 %collective-permute-start.17 = (bf16[512,256]{1,0:T(8,128)(2,1)S(1)}, bf16[512,256]{1,0:T(8,128)(2,1)S(1)}, u32[]{:S(2)}, u32[]{:S(2)}) collective-permute-start(bf16[512,256]{1,0:T(8,128)(2,1)S(1)} %collective-permute-done.13.refs_11_.refs_23_), channel_id=1, source_target_pairs={{0,1},{1,0},{2,3},{3,2},{4,5},{5,4},{6,7},{7,6},{8,9},{9,8},{10,11... | collective-permute-start | bytes 786440 | tf_op jit(solution)/shard_map/ppermute | solution.py:1065
  40.6 5.4 %collective-permute-start.19 = (bf16[256,512]{1,0:T(8,128)(2,1)S(1)}, bf16[256,512]{1,0:T(8,128)(2,1)S(1)}, u32[]{:S(2)}, u32[]{:S(2)}) collective-permute-start(bf16[256,512]{1,0:T(8,128)(2,1)S(1)} %collective-permute-done.10.refs_8_), channel_id=1, source_target_pairs={{0,1},{1,0},{2,3},{3,2},{4,5},{5,4},{6,7},{7,6},{8,9},{9,8},{10,11... | collective-permute-start | bytes 786440 | tf_op jit(solution)/shard_map/ppermute | solution.py:1065
  43.0 3.0 %collective-permute-start.20 = (bf16[256,512]{1,0:T(8,128)(2,1)S(1)}, bf16[256,512]{1,0:T(8,128)(2,1)S(1)}, u32[]{:S(2)}, u32[]{:S(2)}) collective-permute-start(bf16[256,512]{1,0:T(8,128)(2,1)S(1)} %collective-permute-done.12.refs_9_), channel_id=1, source_target_pairs={{0,1},{1,0},{2,3},{3,2},{4,5},{5,4},{6,7},{7,6},{8,9},{9,8},{10,11... | collective-permute-start | bytes 786440 | tf_op jit(solution)/shard_map/ppermute | solution.py:1065
  43.0 3.0 %copy-start.5 = (bf16[2,128,512]{2,1,0:T(8,128)(2,1)S(1)}, bf16[2,128,512]{2,1,0:T(8,128)(2,1)}, u32[]{:S(2)}) copy-start(bf16[2,128,512]{2,1,0:T(8,128)(2,1)} %refs_1_.1) | copy-start | bytes 786436
  50.1 2.9 %collective-permute-start.22 = (bf16[2,512,512]{2,1,0:T(8,128)(2,1)S(1)}, bf16[2,512,512]{2,1,0:T(8,128)(2,1)S(1)}, u32[]{:S(2)}, u32[]{:S(2)}) collective-permute-start(bf16[2,512,512]{2,1,0:T(8,128)(2,1)S(1)} %get-tuple-element.210), channel_id=1, source_target_pairs={{0,1},{1,0},{2,3},{3,2},{4,5},{5,4},{6,7},{7,6},{8,9},{9,8},{10,11... | collective-permute-start | bytes 3145736 | tf_op jit(solution)/shard_map/ppermute | solution.py:1065
  51.8 2.8 %collective-permute-start.21 = (bf16[2,512,512]{2,1,0:T(8,128)(2,1)S(1)}, bf16[2,512,512]{2,1,0:T(8,128)(2,1)S(1)}, u32[]{:S(2)}, u32[]{:S(2)}) collective-permute-start(bf16[2,512,512]{2,1,0:T(8,128)(2,1)S(1)} %get-tuple-element.208), channel_id=1, source_target_pairs={{0,1},{1,0},{2,3},{3,2},{4,5},{5,4},{6,7},{7,6},{8,9},{9,8},{10,11... | collective-permute-start | bytes 3145736 | tf_op jit(solution)/shard_map/ppermute | solution.py:1065
  53.3 14.3 %collective-permute-start.23 = (bf16[1,512,512]{2,1,0:T(8,128)(2,1)S(1)}, bf16[1,512,512]{2,1,0:T(8,128)(2,1)S(1)}, u32[]{:S(2)}, u32[]{:S(2)}) collective-permute-start(bf16[1,512,512]{2,1,0:T(8,128)(2,1)S(1)} %get-tuple-element.226), channel_id=1, source_target_pairs={{0,2},{1,3},{2,0},{3,1},{4,6},{5,7},{6,4},{7,5},{8,10},{9,11},{10,... | collective-permute-start | bytes 1572872 | tf_op jit(solution)/shard_map/ppermute | solution.py:1065
  54.9 14.1 %collective-permute-start.24 = (bf16[2,256,512]{2,1,0:T(8,128)(2,1)S(1)}, bf16[2,256,512]{2,1,0:T(8,128)(2,1)S(1)}, u32[]{:S(2)}, u32[]{:S(2)}) collective-permute-start(bf16[2,256,512]{2,1,0:T(8,128)(2,1)S(1)} %get-tuple-element.229), channel_id=1, source_target_pairs={{0,4},{1,5},{2,6},{3,7},{4,0},{5,1},{6,2},{7,3},{8,12},{9,13},{10,... | collective-permute-start | bytes 1572872 | tf_op jit(solution)/shard_map/ppermute | solution.py:1065
  69.2 3.1 %collective-permute-start.26 = (bf16[2,512,512]{2,1,0:T(8,128)(2,1)S(1)}, bf16[2,512,512]{2,1,0:T(8,128)(2,1)S(1)}, u32[]{:S(2)}, u32[]{:S(2)}) collective-permute-start(bf16[2,512,512]{2,1,0:T(8,128)(2,1)S(1)} %get-tuple-element.237), channel_id=1, source_target_pairs={{0,1},{1,0},{2,3},{3,2},{4,5},{5,4},{6,7},{7,6},{8,9},{9,8},{10,11... | collective-permute-start | bytes 3145736 | tf_op jit(solution)/shard_map/ppermute | solution.py:1065
  69.3 3.0 %collective-permute-start.25 = (f32[128,512]{1,0:T(8,128)S(1)}, f32[128,512]{1,0:T(8,128)S(1)}, u32[]{:S(2)}, u32[]{:S(2)}) collective-permute-start(f32[128,512]{1,0:T(8,128)S(1)} %get-tuple-element.235), channel_id=1, source_target_pairs={{0,1},{1,0},{2,3},{3,2},{4,5},{5,4},{6,7},{7,6},{8,9},{9,8},{10,11... | collective-permute-start | bytes 786440 | tf_op jit(solution)/shard_map/ppermute | solution.py:1065
  69.8 9.2 %collective-permute-start.27 = (bf16[1,256,512]{2,1,0:T(8,128)(2,1)S(1)}, bf16[1,256,512]{2,1,0:T(8,128)(2,1)S(1)}, u32[]{:S(2)}, u32[]{:S(2)}) collective-permute-start(bf16[1,256,512]{2,1,0:T(8,128)(2,1)S(1)} %get-tuple-element.241), channel_id=1, source_target_pairs={{0,4},{1,5},{2,6},{3,7},{4,0},{5,1},{6,2},{7,3},{8,12},{9,13},{10,... | collective-permute-start | bytes 786440 | tf_op jit(solution)/shard_map/ppermute | solution.py:1065
  70.3 9.2 %collective-permute-start.28 = (bf16[1,256,512]{2,1,0:T(8,128)(2,1)S(1)}, bf16[1,256,512]{2,1,0:T(8,128)(2,1)S(1)}, u32[]{:S(2)}, u32[]{:S(2)}) collective-permute-start(bf16[1,256,512]{2,1,0:T(8,128)(2,1)S(1)} %get-tuple-element.242), channel_id=1, source_target_pairs={{0,2},{1,3},{2,0},{3,1},{4,6},{5,7},{6,4},{7,5},{8,10},{9,11},{10,... | collective-permute-start | bytes 786440 | tf_op jit(solution)/shard_map/ppermute | solution.py:1065
  72.8 12.9 %collective-permute-start.29 = (bf16[672,256]{1,0:T(8,128)(2,1)S(1)}, bf16[672,256]{1,0:T(8,128)(2,1)S(1)}, u32[]{:S(2)}, u32[]{:S(2)}) collective-permute-start(bf16[672,256]{1,0:T(8,128)(2,1)S(1)} %get-tuple-element.239.refs_3_), channel_id=1, source_target_pairs={{0,2},{1,3},{2,0},{3,1},{4,6},{5,7},{6,4},{7,5},{8,10},{9,11},{10,... | collective-permute-start | bytes 1032200 | tf_op jit(solution)/shard_map/ppermute | solution.py:1065
  74.1 9.6 %collective-permute-start.30 = (bf16[2,256,256]{2,1,0:T(8,128)(2,1)S(1)}, bf16[2,256,256]{2,1,0:T(8,128)(2,1)S(1)}, u32[]{:S(2)}, u32[]{:S(2)}) collective-permute-start(bf16[2,256,256]{2,1,0:T(8,128)(2,1)S(1)} %get-tuple-element.248), channel_id=1, source_target_pairs={{0,4},{1,5},{2,6},{3,7},{4,0},{5,1},{6,2},{7,3},{8,12},{9,13},{10,... | collective-permute-start | bytes 786440 | tf_op jit(solution)/shard_map/ppermute | solution.py:1065
  79.7 9.0 %collective-permute-start.31 = (bf16[2,128,512]{2,1,0:T(8,128)(2,1)S(1)}, bf16[2,128,512]{2,1,0:T(8,128)(2,1)S(1)}, u32[]{:S(2)}, u32[]{:S(2)}) collective-permute-start(bf16[2,128,512]{2,1,0:T(8,128)(2,1)S(1)} %get-tuple-element.252), channel_id=1, source_target_pairs={{0,8},{1,9},{2,10},{3,11},{4,12},{5,13},{6,14},{7,15},{8,0},{9,1},... | collective-permute-start | bytes 786440 | tf_op jit(solution)/shard_map/ppermute | solution.py:1065
  85.9 6.6 %collective-permute-start.32 = (bf16[416,256]{1,0:T(8,128)(2,1)S(1)}, bf16[416,256]{1,0:T(8,128)(2,1)S(1)}, u32[]{:S(2)}, u32[]{:S(2)}) collective-permute-start(bf16[416,256]{1,0:T(8,128)(2,1)S(1)} %get-tuple-element.250.refs_3_), channel_id=1, source_target_pairs={{0,4},{1,5},{2,6},{3,7},{4,0},{5,1},{6,2},{7,3},{8,12},{9,13},{10,... | collective-permute-start | bytes 638984 | tf_op jit(solution)/shard_map/ppermute | solution.py:1065
  87.5 5.0 %collective-permute-start.33 = (bf16[256,256]{1,0:T(8,128)(2,1)S(1)}, bf16[256,256]{1,0:T(8,128)(2,1)S(1)}, u32[]{:S(2)}, u32[]{:S(2)}) collective-permute-start(bf16[256,256]{1,0:T(8,128)(2,1)S(1)} %get-tuple-element.257), channel_id=1, source_target_pairs={{0,2},{1,3},{2,0},{3,1},{4,6},{5,7},{6,4},{7,5},{8,10},{9,11},{10,... | collective-permute-start | bytes 393224 | tf_op jit(solution)/shard_map/ppermute | solution.py:1065
  88.8 14.4 %collective-permute-start.35 = (bf16[2,128,512]{2,1,0:T(8,128)(2,1)S(1)}, bf16[2,128,512]{2,1,0:T(8,128)(2,1)S(1)}, u32[]{:S(2)}, u32[]{:S(2)}) collective-permute-start(bf16[2,128,512]{2,1,0:T(8,128)(2,1)S(1)} %fold.12.refs_0_), channel_id=1, source_target_pairs={{0,16},{1,17},{2,18},{3,19},{4,20},{5,21},{6,22},{7,23},{8,24},{9,... | collective-permute-start | bytes 786440 | tf_op jit(solution)/shard_map/ppermute | solution.py:1065
  92.6 10.5 %collective-permute-start.34 = (bf16[208,512]{1,0:T(8,128)(2,1)S(1)}, bf16[208,512]{1,0:T(8,128)(2,1)S(1)}, u32[]{:S(2)}, u32[]{:S(2)}) collective-permute-start(bf16[208,512]{1,0:T(8,128)(2,1)S(1)} %get-tuple-element.259.refs_3_), channel_id=1, source_target_pairs={{0,8},{1,9},{2,10},{3,11},{4,12},{5,13},{6,14},{7,15},{8,0},{9,1},... | collective-permute-start | bytes 638984 | tf_op jit(solution)/shard_map/ppermute | solution.py:1065
  103.3 11.2 %collective-permute-start.36 = (bf16[2,128,512]{2,1,0:T(8,128)(2,1)S(1)}, bf16[2,128,512]{2,1,0:T(8,128)(2,1)S(1)}, u32[]{:S(2)}, u32[]{:S(2)}) collective-permute-start(bf16[2,128,512]{2,1,0:T(8,128)(2,1)S(1)} %fold.13.refs_0_), channel_id=1, source_target_pairs={{0,8},{1,9},{2,10},{3,11},{4,12},{5,13},{6,14},{7,15},{8,0},{9,1},... | collective-permute-start | bytes 786440 | tf_op jit(solution)/shard_map/ppermute | solution.py:1065
  103.4 12.1 %collective-permute-start.37 = (bf16[208,512]{1,0:T(8,128)(2,1)S(1)}, bf16[208,512]{1,0:T(8,128)(2,1)S(1)}, u32[]{:S(2)}, u32[]{:S(2)}) collective-permute-start(bf16[208,512]{1,0:T(8,128)(2,1)S(1)} %get-tuple-element.264.refs_3_), channel_id=1, source_target_pairs={{0,16},{1,17},{2,18},{3,19},{4,20},{5,21},{6,22},{7,23},{8,24},{9,... | collective-permute-start | bytes 638984 | tf_op jit(solution)/shard_map/ppermute | solution.py:1065
  114.5 13.1 %collective-permute-start.40 = (bf16[2,256,512]{2,1,0:T(8,128)(2,1)S(1)}, bf16[2,256,512]{2,1,0:T(8,128)(2,1)S(1)}, u32[]{:S(2)}, u32[]{:S(2)}) collective-permute-start(bf16[2,256,512]{2,1,0:T(8,128)(2,1)S(1)} %join.2.refs_0_), channel_id=1, source_target_pairs={{0,4},{1,5},{2,6},{3,7},{4,0},{5,1},{6,2},{7,3},{8,12},{9,13},{10,... | collective-permute-start | bytes 1572872 | tf_op jit(solution)/shard_map/ppermute | solution.py:1065
  115.5 5.4 %collective-permute-start.38 = (bf16[1,128,512]{2,1,0:T(8,128)(2,1)S(1)}, bf16[1,128,512]{2,1,0:T(8,128)(2,1)S(1)}, u32[]{:S(2)}, u32[]{:S(2)}) collective-permute-start(bf16[1,128,512]{2,1,0:T(8,128)(2,1)S(1)} %bitcast.25), channel_id=1, source_target_pairs={{0,8},{1,9},{2,10},{3,11},{4,12},{5,13},{6,14},{7,15},{8,0},{9,1},... | collective-permute-start | bytes 393224 | tf_op jit(solution)/shard_map/ppermute | solution.py:1065
  117.1 4.9 %collective-permute-start.39 = (f32[48,512]{1,0:T(8,128)S(1)}, f32[48,512]{1,0:T(8,128)S(1)}, u32[]{:S(2)}, u32[]{:S(2)}) collective-permute-start(f32[48,512]{1,0:T(8,128)S(1)} %get-tuple-element.276.refs_0_), channel_id=1, source_target_pairs={{0,2},{1,3},{2,0},{3,1},{4,6},{5,7},{6,4},{7,5},{8,10},{9,11},{10,... | collective-permute-start | bytes 294920 | tf_op jit(solution)/shard_map/ppermute | solution.py:1065
  120.9 9.5 %collective-permute-start.42 = (bf16[1,256,512]{2,1,0:T(8,128)(2,1)S(1)}, bf16[1,256,512]{2,1,0:T(8,128)(2,1)S(1)}, u32[]{:S(2)}, u32[]{:S(2)}) collective-permute-start(bf16[1,256,512]{2,1,0:T(8,128)(2,1)S(1)} %join.3.refs_0_), channel_id=1, source_target_pairs={{0,4},{1,5},{2,6},{3,7},{4,0},{5,1},{6,2},{7,3},{8,12},{9,13},{10,... | collective-permute-start | bytes 786440 | tf_op jit(solution)/shard_map/ppermute | solution.py:1065
  122.1 7.0 %collective-permute-start.41 = (f32[96,512]{1,0:T(8,128)S(1)}, f32[96,512]{1,0:T(8,128)S(1)}, u32[]{:S(2)}, u32[]{:S(2)}) collective-permute-start(f32[96,512]{1,0:T(8,128)S(1)} %pair.1.refs_3_), channel_id=1, source_target_pairs={{0,1},{1,0},{2,3},{3,2},{4,5},{5,4},{6,7},{7,6},{8,9},{9,8},{10,11... | collective-permute-start | bytes 589832 | tf_op jit(solution)/shard_map/ppermute | solution.py:1065

commit v8 on v7

--- a/solution.py
+++ b/solution.py
@@ -1676,7 +1676,7 @@
         yield done["second"][0]
 
     walks = {"f": first_chunks(), "s": second_chunk()}
-    order = "sfsfssffssssfss"
+    order = "sfsfssffsssssfs"
 
     def advance(name):
         try:

time: 132 us -> 132 us (level)
  transfers between devices with their start and end apart: 43 -> 43, of which waited for: 23 -> 24; matrix products, arithmetic and copies ran while one was open for 0% -> 0% of each run, Pallas kernels for 23% -> 23%
where the time goes in v8:
time: 132 us; the launch traced here: 131 us
  waiting for transfers between devices  51.9 us (39%)
  starting transfers between devices  41 us (31%)
  Pallas kernels  35.6 us (27%)
  local copies, waits for them, and re-layouts  1.72 us (1%)
    ppermute x43, waiting for transfers between devices, swap(): return lax.ppermute(value, BOTH, [(i, i ^ mask) for i in range(count)])  51.9 us
    ppermute x43, starting transfers between devices, swap(): return lax.ppermute(value, BOTH, [(i, i ^ mask) for i in range(count)])  41 us
    pallas_call x29, Pallas kernels, call(): pl.pallas_call(body, out_shape=out, in_specs=specs, out_specs=outs or jax...  35.6 us
  transfers between devices with their start and end apart: 43, of which 24 were waited for; matrix products, arithmetic and copies ran while one was open for 0% of the time, Pallas kernels for 23%

profile of v8, /device:TPU:0, one launch (start us, length us, event | category | flops | bytes accessed | tf_op | source)
XLA Modules:
  0.0 131.4 jit_solution(2622223479694581587)
XLA Ops:
  0.7 1.0 constant_dynamic-slice_fusion
  1.7 3.0 %collective-permute-start.1 = (bf16[256,512]{1,0:T(8,128)(2,1)S(1)}, bf16[256,512]{1,0:T(8,128)(2,1)S(1)}, u32[]{:S(2)}, u32[]{:S(2)}) collective-permute-start(bf16[256,512]{1,0:T(8,128)(2,1)S(1)} %pad_maximum_fusion), channel_id=1, source_target_pairs={{0,2},{1,3},{2,0},{3,1},{4,6},{5,7},{6,4},{7,5},{8,10},{9,11},{10,... | collective-permute-start | bytes 786440 | tf_op jit(solution)/shard_map/ppermute | solution.py:1065
  4.8 0.6 copy-done.11
  5.5 3.0 %enter.1 = (bf16[256,512]{1,0:T(8,128)(2,1)S(1)}, f32[5,16,512]{2,1,0:T(8,128)S(1)}, f32[2,2,16,8,512]{4,3,2,1,0:T(8,128)S(1)}, f32[5,16,512]{2,1,0:T(8,128)S(1)}, bf16[6,16,512]{2,1,0:T(8,128)(2,1)S(1)}) custom-call(s32[2]{0:T(128)S(1)} %copy-done.12, bf16[2,128,512]{2,1,0:T(8,128)(2,1)S(1)} %copy-done, f32[1,512]{1,0:T(1,128)S(1)} %bitcast.29, ...), custom_call_target="tpu_custom_call" | custom-call | tf_op jit(solution)/shard_map/enter/pallas_call | solution.py:118
  8.6 1.3 collective-permute-done.refs_1_.refs_4_
  10.0 1.1 collective-permute-done.1.refs_8_.refs_20_
  11.0 2.7 %collective-permute-start.4 = (bf16[6,16,512]{2,1,0:T(8,128)(2,1)S(1)}, bf16[6,16,512]{2,1,0:T(8,128)(2,1)S(1)}, u32[]{:S(2)}, u32[]{:S(2)}) collective-permute-start(bf16[6,16,512]{2,1,0:T(8,128)(2,1)S(1)} %get-tuple-element.162), channel_id=1, source_target_pairs={{0,6},{1,7},{2,4},{3,5},{4,2},{5,3},{6,0},{7,1},{8,14},{9,15},{10,... | collective-permute-start | bytes 294920 | tf_op jit(solution)/shard_map/ppermute | solution.py:1065
  14.5 2.9 %pack.1 = (bf16[512,512]{1,0:T(8,128)(2,1)}, bf16[512,512]{1,0:T(8,128)(2,1)}, bf16[512,512]{1,0:T(8,128)(2,1)}, bf16[512,256]{1,0:T(8,128)(2,1)}, bf16[256,512]{1,0:T(8,128)(2,1)}) custom-call(bf16[512,256]{1,0:T(8,128)(2,1)} %w_value, bf16[512,256]{1,0:T(8,128)(2,1)} %w_reset, bf16[128,512]{1,0:T(8,128)(2,1)} %w_hidden, bf16[128,512]{1,0:T(8,128)(2,1)} %w_update, ...), custom_call_target="tpu_custom_call" | custom-call | tf_op jit(solution)/shard_map/pack/pallas_call | solution.py:118
  17.5 0.9 collective-permute-done.3.refs_2_.refs_6_
  18.4 0.5 collective-permute-done.2.refs_1_.refs_5_
  19.6 1.5 %collective-permute-start.7 = (bf16[256,512]{1,0:T(8,128)(2,1)S(1)}, bf16[256,512]{1,0:T(8,128)(2,1)S(1)}, u32[]{:S(2)}, u32[]{:S(2)}) collective-permute-start(bf16[256,512]{1,0:T(8,128)(2,1)S(1)} %collective-permute-done.1.refs_8_.refs_20_), channel_id=1, source_target_pairs={{0,4},{1,5},{2,6},{3,7},{4,0},{5,1},{6,2},{7,3},{8,12},{9,13},{10,... | collective-permute-start | bytes 786440 | tf_op jit(solution)/shard_map/ppermute | solution.py:1065
  21.1 0.5 collective-permute-start.6
  21.6 1.6 %collective-permute-start.5 = (bf16[6,16,512]{2,1,0:T(8,128)(2,1)S(1)}, bf16[6,16,512]{2,1,0:T(8,128)(2,1)S(1)}, u32[]{:S(2)}, u32[]{:S(2)}) collective-permute-start(bf16[6,16,512]{2,1,0:T(8,128)(2,1)S(1)} %get-tuple-element.173), channel_id=1, source_target_pairs={{0,8},{1,9},{2,10},{3,11},{4,12},{5,13},{6,14},{7,15},{8,0},{9,1},... | collective-permute-start | bytes 294920 | tf_op jit(solution)/shard_map/ppermute | solution.py:1065
  23.2 3.0 %collective-permute-done.5.refs_1_.refs_8_ = bf16[6,16,512]{2,1,0:T(8,128)(2,1)S(1)} collective-permute-done((bf16[6,16,512]{2,1,0:T(8,128)(2,1)S(1)}, bf16[6,16,512]{2,1,0:T(8,128)(2,1)S(1)}, u32[]{:S(2)}, u32[]{:S(2)}) %collective-permute-start.5) | collective-permute-done | bytes 98336 | tf_op jit(solution)/shard_map/ppermute | solution.py:1065
  26.2 0.7 hop.5
  27.0 0.9 collective-permute-done.7.refs_9_.refs_21_
  27.9 1.4 %collective-permute-done.6.refs_10_.refs_22_ = bf16[512,256]{1,0:T(8,128)(2,1)S(1)} collective-permute-done((bf16[512,256]{1,0:T(8,128)(2,1)}, bf16[512,256]{1,0:T(8,128)(2,1)S(1)}, u32[]{:S(2)}, u32[]{:S(2)}) %collective-permute-start.6) | collective-permute-done | bytes 262176 | tf_op jit(solution)/shard_map/ppermute | solution.py:1065
  29.3 0.5 collective-permute-start.10
  29.8 2.6 %collective-permute-start.11 = (bf16[6,16,512]{2,1,0:T(8,128)(2,1)S(1)}, bf16[6,16,512]{2,1,0:T(8,128)(2,1)S(1)}, u32[]{:S(2)}, u32[]{:S(2)}) collective-permute-start(bf16[6,16,512]{2,1,0:T(8,128)(2,1)S(1)} %get-tuple-element.182), channel_id=1, source_target_pairs={{0,16},{1,17},{2,18},{3,19},{4,20},{5,21},{6,22},{7,23},{8,24},{9,... | collective-permute-start | bytes 294920 | tf_op jit(solution)/shard_map/ppermute | solution.py:1065
  32.4 1.6 %collective-permute-start.13 = (bf16[512,256]{1,0:T(8,128)(2,1)S(1)}, bf16[512,256]{1,0:T(8,128)(2,1)S(1)}, u32[]{:S(2)}, u32[]{:S(2)}) collective-permute-start(bf16[512,256]{1,0:T(8,128)(2,1)S(1)} %collective-permute-done.6.refs_10_.refs_22_), channel_id=1, source_target_pairs={{0,8},{1,9},{2,10},{3,11},{4,12},{5,13},{6,14},{7,15},{8,0},{9,1},... | collective-permute-start | bytes 786440 | tf_op jit(solution)/shard_map/ppermute | solution.py:1065
  34.0 0.5 collective-permute-start.16
  34.5 2.1 %collective-permute-done.10.refs_8_ = bf16[256,512]{1,0:T(8,128)(2,1)S(1)} collective-permute-done((bf16[256,512]{1,0:T(8,128)(2,1)}, bf16[256,512]{1,0:T(8,128)(2,1)S(1)}, u32[]{:S(2)}, u32[]{:S(2)}) %collective-permute-start.10) | collective-permute-done | bytes 262176 | tf_op jit(solution)/shard_map/ppermute | solution.py:1065
  36.7 0.5 collective-permute-start.12
  37.2 2.4 %look.1 = (f32[2,2,16,512]{3,2,1,0:T(8,128)S(1)}, f32[256,512]{1,0:T(8,128)S(1)}, bf16[256,512]{1,0:T(8,128)(2,1)S(1)}, f32[256,128]{1,0:T(8,128)S(1)}, f32[2,128,128]{2,1,0:T(8,128)S(1)}) custom-call(bf16[256,512]{1,0:T(8,128)(2,1)S(1)} %get-tuple-element.184.refs_0_.refs_1_, f32[5,16,512]{2,1,0:T(8,128)S(1)} %get-tuple-element.185.refs_1_.refs_5_.refs_10_.refs_0_, ...), custom_call_target="tpu_custom_call" | custom-call | tf_op jit(solution)/shard_map/look/pallas_call | solution.py:118
  40.7 2.3 %collective-permute-done.12.refs_9_ = bf16[256,512]{1,0:T(8,128)(2,1)S(1)} collective-permute-done((bf16[256,512]{1,0:T(8,128)(2,1)S(1)}, bf16[256,512]{1,0:T(8,128)(2,1)S(1)}, u32[]{:S(2)}, u32[]{:S(2)}) %collective-permute-start.12) | collective-permute-done | bytes 262176 | tf_op jit(solution)/shard_map/ppermute | solution.py:1065
  43.1 2.9 %mix.1 = (bf16[4,256,256]{2,1,0:T(8,128)(2,1)S(1)}, f32[4,256,256]{2,1,0:T(8,128)S(1)}, f32[4,256,256]{2,1,0:T(8,128)S(1)}, f32[4,256,256]{2,1,0:T(8,128)S(1)}, ...) custom-call(bf16[2,128,512]{2,1,0:T(8,128)(2,1)S(1)} %copy-done, ...), custom_call_target="tpu_custom_call" | custom-call | tf_op jit(solution)/shard_map/mix/pallas_call | solution.py:118
  46.0 4.1 %ffn.1 = (bf16[256,512]{1,0:T(8,128)(2,1)}, bf16[2,512,512]{2,1,0:T(8,128)(2,1)S(1)}, bf16[2,512,512]{2,1,0:T(8,128)(2,1)S(1)}, bf16[256,1024]{1,0:T(8,128)(2,1)...) custom-call(bf16[2,128,512]{2,1,0:T(8,128)(2,1)S(1)} %copy-done, bf16[2,128,512]{2,1,0:T(8,128)(2,1)S(1)} %copy-done.5, ...), custom_call_target="tpu_custom_call" | custom-call | tf_op jit(solution)/shard_map/ffn/pallas_call | solution.py:118
  50.1 0.6 collective-permute-start.22
  50.7 1.1 gates.1
  51.9 1.1 collective-permute-done.22.refs_1_
  53.3 1.3 collective-permute-start.23
  54.9 0.6 collective-permute-start.24
  55.5 9.9 %back.1 = (bf16[2,512,512]{2,1,0:T(8,128)(2,1)S(1)}, bf16[2,512,512]{2,1,0:T(8,128)(2,1)S(1)}, f32[4,256,128]{2,1,0:T(8,128)S(1)}, f32[256,512]{1,0:T(8,128)S(1)...) custom-call(bf16[256,512]{1,0:T(8,128)(2,1)S(1)} %get-tuple-element., ...), custom_call_target="tpu_custom_call" | custom-call | tf_op jit(solution)/shard_map/back/pallas_call | solution.py:118
  65.4 2.1 %collective-permute-done.23.refs_1_ = bf16[1,512,512]{2,1,0:T(8,128)(2,1)S(1)} collective-permute-done((bf16[1,512,512]{2,1,0:T(8,128)(2,1)S(1)}, bf16[1,512,512]{2,1,0:T(8,128)(2,1)S(1)}, u32[]{:S(2)}, u32[]{:S(2)}) %collective-permute-start.23) | collective-permute-done | bytes 524320 | tf_op jit(solution)/shard_map/ppermute | solution.py:1065
  67.7 1.3 %collective-permute-done.24.refs_1_ = bf16[2,256,512]{2,1,0:T(8,128)(2,1)S(1)} collective-permute-done((bf16[2,256,512]{2,1,0:T(8,128)(2,1)S(1)}, bf16[2,256,512]{2,1,0:T(8,128)(2,1)S(1)}, u32[]{:S(2)}, u32[]{:S(2)}) %collective-permute-start.24) | collective-permute-done | bytes 524320 | tf_op jit(solution)/shard_map/ppermute | solution.py:1065
  69.8 0.5 collective-permute-start.27
  70.3 1.2 collective-permute-start.28
  71.5 0.8 collective-permute-done.25.refs_3_.refs_6_
  72.8 1.3 collective-permute-start.29
  74.1 0.5 collective-permute-start.30
  74.6 4.4 %collective-permute-done.27.refs_1_ = bf16[1,256,512]{2,1,0:T(8,128)(2,1)S(1)} collective-permute-done((bf16[1,256,512]{2,1,0:T(8,128)(2,1)S(1)}, bf16[1,256,512]{2,1,0:T(8,128)(2,1)S(1)}, u32[]{:S(2)}, u32[]{:S(2)}) %collective-permute-start.27) | collective-permute-done | bytes 262176 | tf_op jit(solution)/shard_map/ppermute | solution.py:1065
  79.0 0.5 collective-permute-done.28.refs_3_
  79.7 1.6 %collective-permute-start.31 = (bf16[2,128,512]{2,1,0:T(8,128)(2,1)S(1)}, bf16[2,128,512]{2,1,0:T(8,128)(2,1)S(1)}, u32[]{:S(2)}, u32[]{:S(2)}) collective-permute-start(bf16[2,128,512]{2,1,0:T(8,128)(2,1)S(1)} %get-tuple-element.252), channel_id=1, source_target_pairs={{0,8},{1,9},{2,10},{3,11},{4,12},{5,13},{6,14},{7,15},{8,0},{9,1},... | collective-permute-start | bytes 786440 | tf_op jit(solution)/shard_map/ppermute | solution.py:1065
  81.3 2.4 %collective-permute-done.30.refs_7_ = bf16[2,256,256]{2,1,0:T(8,128)(2,1)S(1)} collective-permute-done((bf16[2,256,256]{2,1,0:T(8,128)(2,1)S(1)}, bf16[2,256,256]{2,1,0:T(8,128)(2,1)S(1)}, u32[]{:S(2)}, u32[]{:S(2)}) %collective-permute-start.30) | collective-permute-done | bytes 262176 | tf_op jit(solution)/shard_map/ppermute | solution.py:1065
  83.7 2.0 %collective-permute-done.29.refs_4_.refs_7_ = bf16[672,256]{1,0:T(8,128)(2,1)S(1)} collective-permute-done((bf16[672,256]{1,0:T(8,128)(2,1)S(1)}, bf16[672,256]{1,0:T(8,128)(2,1)S(1)}, u32[]{:S(2)}, u32[]{:S(2)}) %collective-permute-start.29) | collective-permute-done | bytes 344096 | tf_op jit(solution)/shard_map/ppermute | solution.py:1065
  85.9 1.6 %collective-permute-start.32 = (bf16[416,256]{1,0:T(8,128)(2,1)S(1)}, bf16[416,256]{1,0:T(8,128)(2,1)S(1)}, u32[]{:S(2)}, u32[]{:S(2)}) collective-permute-start(bf16[416,256]{1,0:T(8,128)(2,1)S(1)} %get-tuple-element.250.refs_3_), channel_id=1, source_target_pairs={{0,4},{1,5},{2,6},{3,7},{4,0},{5,1},{6,2},{7,3},{8,12},{9,13},{10,... | collective-permute-start | bytes 638984 | tf_op jit(solution)/shard_map/ppermute | solution.py:1065
  87.5 1.2 collective-permute-start.33
  88.8 2.1 %collective-permute-start.35 = (bf16[2,128,512]{2,1,0:T(8,128)(2,1)S(1)}, bf16[2,128,512]{2,1,0:T(8,128)(2,1)S(1)}, u32[]{:S(2)}, u32[]{:S(2)}) collective-permute-start(bf16[2,128,512]{2,1,0:T(8,128)(2,1)S(1)} %fold.12.refs_0_), channel_id=1, source_target_pairs={{0,16},{1,17},{2,18},{3,19},{4,20},{5,21},{6,22},{7,23},{8,24},{9,... | collective-permute-start | bytes 786440 | tf_op jit(solution)/shard_map/ppermute | solution.py:1065
  90.9 1.6 %collective-permute-done.33.refs_7_ = bf16[256,256]{1,0:T(8,128)(2,1)S(1)} collective-permute-done((bf16[256,256]{1,0:T(8,128)(2,1)S(1)}, bf16[256,256]{1,0:T(8,128)(2,1)S(1)}, u32[]{:S(2)}, u32[]{:S(2)}) %collective-permute-start.33) | collective-permute-done | bytes 131104 | tf_op jit(solution)/shard_map/ppermute | solution.py:1065
  92.6 1.6 %collective-permute-start.34 = (bf16[208,512]{1,0:T(8,128)(2,1)S(1)}, bf16[208,512]{1,0:T(8,128)(2,1)S(1)}, u32[]{:S(2)}, u32[]{:S(2)}) collective-permute-start(bf16[208,512]{1,0:T(8,128)(2,1)S(1)} %get-tuple-element.259.refs_3_), channel_id=1, source_target_pairs={{0,8},{1,9},{2,10},{3,11},{4,12},{5,13},{6,14},{7,15},{8,0},{9,1},... | collective-permute-start | bytes 638984 | tf_op jit(solution)/shard_map/ppermute | solution.py:1065
  94.3 8.8 %collective-permute-done.34.refs_4_.refs_9_ = bf16[208,512]{1,0:T(8,128)(2,1)S(1)} collective-permute-done((bf16[208,512]{1,0:T(8,128)(2,1)S(1)}, bf16[208,512]{1,0:T(8,128)(2,1)S(1)}, u32[]{:S(2)}, u32[]{:S(2)}) %collective-permute-start.34) | collective-permute-done | bytes 213024 | tf_op jit(solution)/shard_map/ppermute | solution.py:1065
  103.4 4.2 %collective-permute-start.37 = (bf16[208,512]{1,0:T(8,128)(2,1)S(1)}, bf16[208,512]{1,0:T(8,128)(2,1)S(1)}, u32[]{:S(2)}, u32[]{:S(2)}) collective-permute-start(bf16[208,512]{1,0:T(8,128)(2,1)S(1)} %get-tuple-element.264.refs_3_), channel_id=1, source_target_pairs={{0,16},{1,17},{2,18},{3,19},{4,20},{5,21},{6,22},{7,23},{8,24},{9,... | collective-permute-start | bytes 638984 | tf_op jit(solution)/shard_map/ppermute | solution.py:1065
  107.6 6.9 %collective-permute-done.36.refs_1_ = bf16[2,128,512]{2,1,0:T(8,128)(2,1)S(1)} collective-permute-done((bf16[2,128,512]{2,1,0:T(8,128)(2,1)S(1)}, bf16[2,128,512]{2,1,0:T(8,128)(2,1)S(1)}, u32[]{:S(2)}, u32[]{:S(2)}) %collective-permute-start.36) | collective-permute-done | bytes 262176 | tf_op jit(solution)/shard_map/ppermute | solution.py:1065
  114.5 1.0 collective-permute-start.41
  115.5 1.6 %collective-permute-start.38 = (bf16[1,128,512]{2,1,0:T(8,128)(2,1)S(1)}, bf16[1,128,512]{2,1,0:T(8,128)(2,1)S(1)}, u32[]{:S(2)}, u32[]{:S(2)}) collective-permute-start(bf16[1,128,512]{2,1,0:T(8,128)(2,1)S(1)} %bitcast.25), channel_id=1, source_target_pairs={{0,8},{1,9},{2,10},{3,11},{4,12},{5,13},{6,14},{7,15},{8,0},{9,1},... | collective-permute-start | bytes 393224 | tf_op jit(solution)/shard_map/ppermute | solution.py:1065
  117.1 1.1 collective-permute-start.39
  118.2 2.7 %leave.1 = bf16[2,128,512]{2,1,0:T(8,128)(2,1)} custom-call(bf16[2,128,512]{2,1,0:T(8,128)(2,1)S(1)} %copy-done, f32[5,16,512]{2,1,0:T(8,128)S(1)} %get-tuple-element.185.refs_1_.refs_5_.refs_10_.refs_0_, f32[4,256,128]{2,1,0:T(8,128)S(1)} %get-tuple-element.270.refs_2_, f32[256,512]{1,0:T(8,128)S(1)} %get-tuple-element.271.refs_3_, ...), custom_call_target="tpu_custom_call" | custom-call | tf_op jit(solution)/shard_map/leave/pallas_call | solution.py:118
  120.9 1.1 collective-permute-start.42
  122.1 1.4 %collective-permute-done.40.refs_4_ = f32[96,512]{1,0:T(8,128)S(1)} collective-permute-done((f32[96,512]{1,0:T(8,128)S(1)}, f32[96,512]{1,0:T(8,128)S(1)}, u32[]{:S(2)}, u32[]{:S(2)}) %collective-permute-start.40) | collective-permute-done | bytes 196640 | tf_op jit(solution)/shard_map/ppermute | solution.py:1065
  123.6 0.8 finish.1
  124.4 3.2 %collective-permute-done.41.refs_1_ = bf16[2,256,512]{2,1,0:T(8,128)(2,1)S(1)} collective-permute-done((bf16[2,256,512]{2,1,0:T(8,128)(2,1)S(1)}, bf16[2,256,512]{2,1,0:T(8,128)(2,1)S(1)}, u32[]{:S(2)}, u32[]{:S(2)}) %collective-permute-start.41) | collective-permute-done | bytes 524320 | tf_op jit(solution)/shard_map/ppermute | solution.py:1065
  127.6 1.5 %unpack.2 = (f32[512,256]{1,0:T(8,128)}, f32[256,512]{1,0:T(8,128)}, f32[128,512]{1,0:T(8,128)}, f32[128,512]{1,0:T(8,128)}, f32[256,512]{1,0:T(8,128)}) custom-call(bf16[2,256,512]{2,1,0:T(8,128)(2,1)S(1)} %join.2.refs_0_, bf16[2,256,512]{2,1,0:T(8,128)(2,1)S(1)} %collective-permute-done.41.refs_1_), custom_call_target="tpu_custom_call" | custom-call | tf_op jit(solution)/shard_map/unpack/pallas_call | solution.py:118
  129.1 1.3 %collective-permute-done.42.refs_1_ = bf16[1,256,512]{2,1,0:T(8,128)(2,1)S(1)} collective-permute-done((bf16[1,256,512]{2,1,0:T(8,128)(2,1)S(1)}, bf16[1,256,512]{2,1,0:T(8,128)(2,1)S(1)}, u32[]{:S(2)}, u32[]{:S(2)}) %collective-permute-start.42) | collective-permute-done | bytes 262176 | tf_op jit(solution)/shard_map/ppermute | solution.py:1065
  130.4 1.0 unpack.3
  (85 shorter events, 6.0 us)
Async XLA Ops:
  1.7 3.1 %copy-start = (bf16[2,128,512]{2,1,0:T(8,128)(2,1)S(1)}, bf16[2,128,512]{2,1,0:T(8,128)(2,1)}, u32[]{:S(2)}) copy-start(bf16[2,128,512]{2,1,0:T(8,128)(2,1)} %refs_0_.7) | copy-start | bytes 786436
  1.7 3.1 %copy-start.6 = (f32[512,16]{0,1:T(8,128)S(1)}, f32[512,16]{0,1:T(8,128)}, u32[]{:S(2)}) copy-start(f32[512,16]{0,1:T(8,128)} %param.24) | copy-start | bytes 98308
  1.7 3.1 %copy-start.7 = (f32[512,16]{0,1:T(8,128)S(1)}, f32[512,16]{0,1:T(8,128)}, u32[]{:S(2)}) copy-start(f32[512,16]{0,1:T(8,128)} %param.25) | copy-start | bytes 98308
  1.7 3.1 %copy-start.8 = (f32[512,16]{0,1:T(8,128)S(1)}, f32[512,16]{0,1:T(8,128)}, u32[]{:S(2)}) copy-start(f32[512,16]{0,1:T(8,128)} %param.26) | copy-start | bytes 98308
  1.7 9.3 %collective-permute-start.1 = (bf16[256,512]{1,0:T(8,128)(2,1)S(1)}, bf16[256,512]{1,0:T(8,128)(2,1)S(1)}, u32[]{:S(2)}, u32[]{:S(2)}) collective-permute-start(bf16[256,512]{1,0:T(8,128)(2,1)S(1)} %pad_maximum_fusion), channel_id=1, source_target_pairs={{0,2},{1,3},{2,0},{3,1},{4,6},{5,7},{6,4},{7,5},{8,10},{9,11},{10,... | collective-permute-start | bytes 786440 | tf_op jit(solution)/shard_map/ppermute | solution.py:1065
  4.7 0.7 copy-start.11
  4.7 0.7 copy-start.15
  4.7 0.7 copy-start.10
  4.7 0.7 copy-start.9
  4.7 0.7 copy-start.12
  4.8 0.7 copy-start.13
  4.8 0.7 copy-start.14
  8.5 1.4 %collective-permute-start = (bf16[6,16,512]{2,1,0:T(8,128)(2,1)S(1)}, bf16[6,16,512]{2,1,0:T(8,128)(2,1)S(1)}, u32[]{:S(2)}, u32[]{:S(2)}) collective-permute-start(bf16[6,16,512]{2,1,0:T(8,128)(2,1)S(1)} %get-tuple-element.160), channel_id=1, source_target_pairs={{0,1},{1,0},{2,3},{3,2},{4,5},{5,4},{6,7},{7,6},{8,9},{9,8},{10,11... | collective-permute-start | bytes 294920 | tf_op jit(solution)/shard_map/ppermute | solution.py:1065
  11.0 6.4 %collective-permute-start.4 = (bf16[6,16,512]{2,1,0:T(8,128)(2,1)S(1)}, bf16[6,16,512]{2,1,0:T(8,128)(2,1)S(1)}, u32[]{:S(2)}, u32[]{:S(2)}) collective-permute-start(bf16[6,16,512]{2,1,0:T(8,128)(2,1)S(1)} %get-tuple-element.162), channel_id=1, source_target_pairs={{0,6},{1,7},{2,4},{3,5},{4,2},{5,3},{6,0},{7,1},{8,14},{9,15},{10,... | collective-permute-start | bytes 294920 | tf_op jit(solution)/shard_map/ppermute | solution.py:1065
  13.7 4.6 %collective-permute-start.3 = (bf16[6,16,512]{2,1,0:T(8,128)(2,1)S(1)}, bf16[6,16,512]{2,1,0:T(8,128)(2,1)S(1)}, u32[]{:S(2)}, u32[]{:S(2)}) collective-permute-start(bf16[6,16,512]{2,1,0:T(8,128)(2,1)S(1)} %get-tuple-element.162), channel_id=1, source_target_pairs={{0,4},{1,5},{2,6},{3,7},{4,0},{5,1},{6,2},{7,3},{8,12},{9,13},{10,... | collective-permute-start | bytes 294920 | tf_op jit(solution)/shard_map/ppermute | solution.py:1065
  14.2 4.6 %collective-permute-start.2 = (bf16[6,16,512]{2,1,0:T(8,128)(2,1)S(1)}, bf16[6,16,512]{2,1,0:T(8,128)(2,1)S(1)}, u32[]{:S(2)}, u32[]{:S(2)}) collective-permute-start(bf16[6,16,512]{2,1,0:T(8,128)(2,1)S(1)} %get-tuple-element.162), channel_id=1, source_target_pairs={{0,2},{1,3},{2,0},{3,1},{4,6},{5,7},{6,4},{7,5},{8,10},{9,11},{10,... | collective-permute-start | bytes 294920 | tf_op jit(solution)/shard_map/ppermute | solution.py:1065
  17.5 19.7 %copy-start.4 = (bf16[512,512]{1,0:T(8,128)(2,1)S(1)}, bf16[512,512]{1,0:T(8,128)(2,1)}, u32[]{:S(2)}) copy-start(bf16[512,512]{1,0:T(8,128)(2,1)} %get-tuple-element.197.refs_6_) | copy-start | bytes 1572868
  19.0 10.3 %collective-permute-start.9 = (bf16[512,512]{1,0:T(8,128)(2,1)}, bf16[512,512]{1,0:T(8,128)(2,1)S(1)}, u32[]{:S(2)}, u32[]{:S(2)}) collective-permute-start(bf16[512,512]{1,0:T(8,128)(2,1)} %get-tuple-element.181.refs_5_.refs_17_), channel_id=1, source_target_pairs={{0,1},{1,0},{2,3},{3,2},{4,5},{5,4},{6,7},{7,6},{8,9},{9,8},{10,11... | collective-permute-start | bytes 1572872 | tf_op jit(solution)/shard_map/ppermute | solution.py:1065
  19.1 10.2 %collective-permute-start.8 = (bf16[512,512]{1,0:T(8,128)(2,1)}, bf16[512,512]{1,0:T(8,128)(2,1)S(1)}, u32[]{:S(2)}, u32[]{:S(2)}) collective-permute-start(bf16[512,512]{1,0:T(8,128)(2,1)} %get-tuple-element.179.refs_4_.refs_16_), channel_id=1, source_target_pairs={{0,1},{1,0},{2,3},{3,2},{4,5},{5,4},{6,7},{7,6},{8,9},{9,8},{10,11... | collective-permute-start | bytes 1572872 | tf_op jit(solution)/shard_map/ppermute | solution.py:1065
  19.6 8.3 %collective-permute-start.7 = (bf16[256,512]{1,0:T(8,128)(2,1)S(1)}, bf16[256,512]{1,0:T(8,128)(2,1)S(1)}, u32[]{:S(2)}, u32[]{:S(2)}) collective-permute-start(bf16[256,512]{1,0:T(8,128)(2,1)S(1)} %collective-permute-done.1.refs_8_.refs_20_), channel_id=1, source_target_pairs={{0,4},{1,5},{2,6},{3,7},{4,0},{5,1},{6,2},{7,3},{8,12},{9,13},{10,... | collective-permute-start | bytes 786440 | tf_op jit(solution)/shard_map/ppermute | solution.py:1065
  21.1 8.2 %collective-permute-start.6 = (bf16[512,256]{1,0:T(8,128)(2,1)}, bf16[512,256]{1,0:T(8,128)(2,1)S(1)}, u32[]{:S(2)}, u32[]{:S(2)}) collective-permute-start(bf16[512,256]{1,0:T(8,128)(2,1)} %get-tuple-element.176), channel_id=1, source_target_pairs={{0,2},{1,3},{2,0},{3,1},{4,6},{5,7},{6,4},{7,5},{8,10},{9,11},{10,... | collective-permute-start | bytes 786440 | tf_op jit(solution)/shard_map/ppermute | solution.py:1065
  21.6 4.6 %collective-permute-start.5 = (bf16[6,16,512]{2,1,0:T(8,128)(2,1)S(1)}, bf16[6,16,512]{2,1,0:T(8,128)(2,1)S(1)}, u32[]{:S(2)}, u32[]{:S(2)}) collective-permute-start(bf16[6,16,512]{2,1,0:T(8,128)(2,1)S(1)} %get-tuple-element.173), channel_id=1, source_target_pairs={{0,8},{1,9},{2,10},{3,11},{4,12},{5,13},{6,14},{7,15},{8,0},{9,1},... | collective-permute-start | bytes 294920 | tf_op jit(solution)/shard_map/ppermute | solution.py:1065
  26.2 10.9 %copy-start.3 = (bf16[512,128]{1,0:T(8,128)(2,1)S(1)}, bf16[512,128]{1,0:T(8,128)(2,1)}, u32[]{:S(2)}) copy-start(bf16[512,128]{1,0:T(8,128)(2,1)} %refs_11_.1) | copy-start | bytes 393220
  29.3 7.3 %collective-permute-start.10 = (bf16[256,512]{1,0:T(8,128)(2,1)}, bf16[256,512]{1,0:T(8,128)(2,1)S(1)}, u32[]{:S(2)}, u32[]{:S(2)}) collective-permute-start(bf16[256,512]{1,0:T(8,128)(2,1)} %get-tuple-element.183), channel_id=1, source_target_pairs={{0,2},{1,3},{2,0},{3,1},{4,6},{5,7},{6,4},{7,5},{8,10},{9,11},{10,... | collective-permute-start | bytes 786440 | tf_op jit(solution)/shard_map/ppermute | solution.py:1065
  29.8 7.3 %collective-permute-start.11 = (bf16[6,16,512]{2,1,0:T(8,128)(2,1)S(1)}, bf16[6,16,512]{2,1,0:T(8,128)(2,1)S(1)}, u32[]{:S(2)}, u32[]{:S(2)}) collective-permute-start(bf16[6,16,512]{2,1,0:T(8,128)(2,1)S(1)} %get-tuple-element.182), channel_id=1, source_target_pairs={{0,16},{1,17},{2,18},{3,19},{4,20},{5,21},{6,22},{7,23},{8,24},{9,... | collective-permute-start | bytes 294920 | tf_op jit(solution)/shard_map/ppermute | solution.py:1065
  32.4 7.6 %collective-permute-start.13 = (bf16[512,256]{1,0:T(8,128)(2,1)S(1)}, bf16[512,256]{1,0:T(8,128)(2,1)S(1)}, u32[]{:S(2)}, u32[]{:S(2)}) collective-permute-start(bf16[512,256]{1,0:T(8,128)(2,1)S(1)} %collective-permute-done.6.refs_10_.refs_22_), channel_id=1, source_target_pairs={{0,8},{1,9},{2,10},{3,11},{4,12},{5,13},{6,14},{7,15},{8,0},{9,1},... | collective-permute-start | bytes 786440 | tf_op jit(solution)/shard_map/ppermute | solution.py:1065
  34.0 6.2 %collective-permute-start.14 = (bf16[256,512]{1,0:T(8,128)(2,1)S(1)}, bf16[256,512]{1,0:T(8,128)(2,1)S(1)}, u32[]{:S(2)}, u32[]{:S(2)}) collective-permute-start(bf16[256,512]{1,0:T(8,128)(2,1)S(1)} %collective-permute-done.1.refs_8_.refs_20_), channel_id=1, source_target_pairs={{0,1},{1,0},{2,3},{3,2},{4,5},{5,4},{6,7},{7,6},{8,9},{9,8},{10,11... | collective-permute-start | bytes 786440 | tf_op jit(solution)/shard_map/ppermute | solution.py:1065
  34.0 6.6 %collective-permute-start.16 = (bf16[512,256]{1,0:T(8,128)(2,1)S(1)}, bf16[512,256]{1,0:T(8,128)(2,1)S(1)}, u32[]{:S(2)}, u32[]{:S(2)}) collective-permute-start(bf16[512,256]{1,0:T(8,128)(2,1)S(1)} %collective-permute-done.6.refs_10_.refs_22_), channel_id=1, source_target_pairs={{0,1},{1,0},{2,3},{3,2},{4,5},{5,4},{6,7},{7,6},{8,9},{9,8},{10,11... | collective-permute-start | bytes 786440 | tf_op jit(solution)/shard_map/ppermute | solution.py:1065
  36.7 6.4 %collective-permute-start.12 = (bf16[256,512]{1,0:T(8,128)(2,1)S(1)}, bf16[256,512]{1,0:T(8,128)(2,1)S(1)}, u32[]{:S(2)}, u32[]{:S(2)}) collective-permute-start(bf16[256,512]{1,0:T(8,128)(2,1)S(1)} %collective-permute-done.10.refs_8_), channel_id=1, source_target_pairs={{0,4},{1,5},{2,6},{3,7},{4,0},{5,1},{6,2},{7,3},{8,12},{9,13},{10,... | collective-permute-start | bytes 786440 | tf_op jit(solution)/shard_map/ppermute | solution.py:1065
  37.2 8.8 %collective-permute-start.18 = (bf16[512,512]{1,0:T(8,128)(2,1)S(1)}, bf16[512,512]{1,0:T(8,128)(2,1)S(1)}, u32[]{:S(2)}, u32[]{:S(2)}) collective-permute-start(bf16[512,512]{1,0:T(8,128)(2,1)S(1)} %copy-done.4), channel_id=1, source_target_pairs={{0,1},{1,0},{2,3},{3,2},{4,5},{5,4},{6,7},{7,6},{8,9},{9,8},{10,11... | collective-permute-start | bytes 1572872 | tf_op jit(solution)/shard_map/ppermute | solution.py:1065
  37.2 5.9 %copy-start.1 = (bf16[512,512]{1,0:T(8,128)(2,1)S(1)}, bf16[512,512]{1,0:T(8,128)(2,1)}, u32[]{:S(2)}) copy-start(bf16[512,512]{1,0:T(8,128)(2,1)} %get-tuple-element.179.refs_4_.refs_16_) | copy-start | bytes 1572868
  37.2 5.9 %copy-start.2 = (bf16[512,512]{1,0:T(8,128)(2,1)S(1)}, bf16[512,512]{1,0:T(8,128)(2,1)}, u32[]{:S(2)}) copy-start(bf16[512,512]{1,0:T(8,128)(2,1)} %get-tuple-element.181.refs_5_.refs_17_) | copy-start | bytes 1572868
  40.1 3.0 %collective-permute-start.15 = (bf16[256,512]{1,0:T(8,128)(2,1)S(1)}, bf16[256,512]{1,0:T(8,128)(2,1)S(1)}, u32[]{:S(2)}, u32[]{:S(2)}) collective-permute-start(bf16[256,512]{1,0:T(8,128)(2,1)S(1)} %collective-permute-done.7.refs_9_.refs_21_), channel_id=1, source_target_pairs={{0,1},{1,0},{2,3},{3,2},{4,5},{5,4},{6,7},{7,6},{8,9},{9,8},{10,11... | collective-permute-start | bytes 786440 | tf_op jit(solution)/shard_map/ppermute | solution.py:1065
  40.2 2.8 %collective-permute-start.17 = (bf16[512,256]{1,0:T(8,128)(2,1)S(1)}, bf16[512,256]{1,0:T(8,128)(2,1)S(1)}, u32[]{:S(2)}, u32[]{:S(2)}) collective-permute-start(bf16[512,256]{1,0:T(8,128)(2,1)S(1)} %collective-permute-done.13.refs_11_.refs_23_), channel_id=1, source_target_pairs={{0,1},{1,0},{2,3},{3,2},{4,5},{5,4},{6,7},{7,6},{8,9},{9,8},{10,11... | collective-permute-start | bytes 786440 | tf_op jit(solution)/shard_map/ppermute | solution.py:1065
  40.6 5.4 %collective-permute-start.19 = (bf16[256,512]{1,0:T(8,128)(2,1)S(1)}, bf16[256,512]{1,0:T(8,128)(2,1)S(1)}, u32[]{:S(2)}, u32[]{:S(2)}) collective-permute-start(bf16[256,512]{1,0:T(8,128)(2,1)S(1)} %collective-permute-done.10.refs_8_), channel_id=1, source_target_pairs={{0,1},{1,0},{2,3},{3,2},{4,5},{5,4},{6,7},{7,6},{8,9},{9,8},{10,11... | collective-permute-start | bytes 786440 | tf_op jit(solution)/shard_map/ppermute | solution.py:1065
  43.0 3.0 %collective-permute-start.20 = (bf16[256,512]{1,0:T(8,128)(2,1)S(1)}, bf16[256,512]{1,0:T(8,128)(2,1)S(1)}, u32[]{:S(2)}, u32[]{:S(2)}) collective-permute-start(bf16[256,512]{1,0:T(8,128)(2,1)S(1)} %collective-permute-done.12.refs_9_), channel_id=1, source_target_pairs={{0,1},{1,0},{2,3},{3,2},{4,5},{5,4},{6,7},{7,6},{8,9},{9,8},{10,11... | collective-permute-start | bytes 786440 | tf_op jit(solution)/shard_map/ppermute | solution.py:1065
  43.0 3.0 %copy-start.5 = (bf16[2,128,512]{2,1,0:T(8,128)(2,1)S(1)}, bf16[2,128,512]{2,1,0:T(8,128)(2,1)}, u32[]{:S(2)}) copy-start(bf16[2,128,512]{2,1,0:T(8,128)(2,1)} %refs_1_.1) | copy-start | bytes 786436
  50.1 2.9 %collective-permute-start.22 = (bf16[2,512,512]{2,1,0:T(8,128)(2,1)S(1)}, bf16[2,512,512]{2,1,0:T(8,128)(2,1)S(1)}, u32[]{:S(2)}, u32[]{:S(2)}) collective-permute-start(bf16[2,512,512]{2,1,0:T(8,128)(2,1)S(1)} %get-tuple-element.210), channel_id=1, source_target_pairs={{0,1},{1,0},{2,3},{3,2},{4,5},{5,4},{6,7},{7,6},{8,9},{9,8},{10,11... | collective-permute-start | bytes 3145736 | tf_op jit(solution)/shard_map/ppermute | solution.py:1065
  51.8 2.8 %collective-permute-start.21 = (bf16[2,512,512]{2,1,0:T(8,128)(2,1)S(1)}, bf16[2,512,512]{2,1,0:T(8,128)(2,1)S(1)}, u32[]{:S(2)}, u32[]{:S(2)}) collective-permute-start(bf16[2,512,512]{2,1,0:T(8,128)(2,1)S(1)} %get-tuple-element.208), channel_id=1, source_target_pairs={{0,1},{1,0},{2,3},{3,2},{4,5},{5,4},{6,7},{7,6},{8,9},{9,8},{10,11... | collective-permute-start | bytes 3145736 | tf_op jit(solution)/shard_map/ppermute | solution.py:1065
  53.3 14.3 %collective-permute-start.23 = (bf16[1,512,512]{2,1,0:T(8,128)(2,1)S(1)}, bf16[1,512,512]{2,1,0:T(8,128)(2,1)S(1)}, u32[]{:S(2)}, u32[]{:S(2)}) collective-permute-start(bf16[1,512,512]{2,1,0:T(8,128)(2,1)S(1)} %get-tuple-element.226), channel_id=1, source_target_pairs={{0,2},{1,3},{2,0},{3,1},{4,6},{5,7},{6,4},{7,5},{8,10},{9,11},{10,... | collective-permute-start | bytes 1572872 | tf_op jit(solution)/shard_map/ppermute | solution.py:1065
  54.9 14.1 %collective-permute-start.24 = (bf16[2,256,512]{2,1,0:T(8,128)(2,1)S(1)}, bf16[2,256,512]{2,1,0:T(8,128)(2,1)S(1)}, u32[]{:S(2)}, u32[]{:S(2)}) collective-permute-start(bf16[2,256,512]{2,1,0:T(8,128)(2,1)S(1)} %get-tuple-element.229), channel_id=1, source_target_pairs={{0,4},{1,5},{2,6},{3,7},{4,0},{5,1},{6,2},{7,3},{8,12},{9,13},{10,... | collective-permute-start | bytes 1572872 | tf_op jit(solution)/shard_map/ppermute | solution.py:1065
  69.2 3.1 %collective-permute-start.26 = (bf16[2,512,512]{2,1,0:T(8,128)(2,1)S(1)}, bf16[2,512,512]{2,1,0:T(8,128)(2,1)S(1)}, u32[]{:S(2)}, u32[]{:S(2)}) collective-permute-start(bf16[2,512,512]{2,1,0:T(8,128)(2,1)S(1)} %get-tuple-element.237), channel_id=1, source_target_pairs={{0,1},{1,0},{2,3},{3,2},{4,5},{5,4},{6,7},{7,6},{8,9},{9,8},{10,11... | collective-permute-start | bytes 3145736 | tf_op jit(solution)/shard_map/ppermute | solution.py:1065
  69.3 3.0 %collective-permute-start.25 = (f32[128,512]{1,0:T(8,128)S(1)}, f32[128,512]{1,0:T(8,128)S(1)}, u32[]{:S(2)}, u32[]{:S(2)}) collective-permute-start(f32[128,512]{1,0:T(8,128)S(1)} %get-tuple-element.235), channel_id=1, source_target_pairs={{0,1},{1,0},{2,3},{3,2},{4,5},{5,4},{6,7},{7,6},{8,9},{9,8},{10,11... | collective-permute-start | bytes 786440 | tf_op jit(solution)/shard_map/ppermute | solution.py:1065
  69.8 9.2 %collective-permute-start.27 = (bf16[1,256,512]{2,1,0:T(8,128)(2,1)S(1)}, bf16[1,256,512]{2,1,0:T(8,128)(2,1)S(1)}, u32[]{:S(2)}, u32[]{:S(2)}) collective-permute-start(bf16[1,256,512]{2,1,0:T(8,128)(2,1)S(1)} %get-tuple-element.241), channel_id=1, source_target_pairs={{0,4},{1,5},{2,6},{3,7},{4,0},{5,1},{6,2},{7,3},{8,12},{9,13},{10,... | collective-permute-start | bytes 786440 | tf_op jit(solution)/shard_map/ppermute | solution.py:1065
  70.3 9.2 %collective-permute-start.28 = (bf16[1,256,512]{2,1,0:T(8,128)(2,1)S(1)}, bf16[1,256,512]{2,1,0:T(8,128)(2,1)S(1)}, u32[]{:S(2)}, u32[]{:S(2)}) collective-permute-start(bf16[1,256,512]{2,1,0:T(8,128)(2,1)S(1)} %get-tuple-element.242), channel_id=1, source_target_pairs={{0,2},{1,3},{2,0},{3,1},{4,6},{5,7},{6,4},{7,5},{8,10},{9,11},{10,... | collective-permute-start | bytes 786440 | tf_op jit(solution)/shard_map/ppermute | solution.py:1065
  72.8 12.9 %collective-permute-start.29 = (bf16[672,256]{1,0:T(8,128)(2,1)S(1)}, bf16[672,256]{1,0:T(8,128)(2,1)S(1)}, u32[]{:S(2)}, u32[]{:S(2)}) collective-permute-start(bf16[672,256]{1,0:T(8,128)(2,1)S(1)} %get-tuple-element.239.refs_3_), channel_id=1, source_target_pairs={{0,2},{1,3},{2,0},{3,1},{4,6},{5,7},{6,4},{7,5},{8,10},{9,11},{10,... | collective-permute-start | bytes 1032200 | tf_op jit(solution)/shard_map/ppermute | solution.py:1065
  74.1 9.6 %collective-permute-start.30 = (bf16[2,256,256]{2,1,0:T(8,128)(2,1)S(1)}, bf16[2,256,256]{2,1,0:T(8,128)(2,1)S(1)}, u32[]{:S(2)}, u32[]{:S(2)}) collective-permute-start(bf16[2,256,256]{2,1,0:T(8,128)(2,1)S(1)} %get-tuple-element.248), channel_id=1, source_target_pairs={{0,4},{1,5},{2,6},{3,7},{4,0},{5,1},{6,2},{7,3},{8,12},{9,13},{10,... | collective-permute-start | bytes 786440 | tf_op jit(solution)/shard_map/ppermute | solution.py:1065
  79.7 9.0 %collective-permute-start.31 = (bf16[2,128,512]{2,1,0:T(8,128)(2,1)S(1)}, bf16[2,128,512]{2,1,0:T(8,128)(2,1)S(1)}, u32[]{:S(2)}, u32[]{:S(2)}) collective-permute-start(bf16[2,128,512]{2,1,0:T(8,128)(2,1)S(1)} %get-tuple-element.252), channel_id=1, source_target_pairs={{0,8},{1,9},{2,10},{3,11},{4,12},{5,13},{6,14},{7,15},{8,0},{9,1},... | collective-permute-start | bytes 786440 | tf_op jit(solution)/shard_map/ppermute | solution.py:1065
  85.9 6.6 %collective-permute-start.32 = (bf16[416,256]{1,0:T(8,128)(2,1)S(1)}, bf16[416,256]{1,0:T(8,128)(2,1)S(1)}, u32[]{:S(2)}, u32[]{:S(2)}) collective-permute-start(bf16[416,256]{1,0:T(8,128)(2,1)S(1)} %get-tuple-element.250.refs_3_), channel_id=1, source_target_pairs={{0,4},{1,5},{2,6},{3,7},{4,0},{5,1},{6,2},{7,3},{8,12},{9,13},{10,... | collective-permute-start | bytes 638984 | tf_op jit(solution)/shard_map/ppermute | solution.py:1065
  87.5 5.0 %collective-permute-start.33 = (bf16[256,256]{1,0:T(8,128)(2,1)S(1)}, bf16[256,256]{1,0:T(8,128)(2,1)S(1)}, u32[]{:S(2)}, u32[]{:S(2)}) collective-permute-start(bf16[256,256]{1,0:T(8,128)(2,1)S(1)} %get-tuple-element.257), channel_id=1, source_target_pairs={{0,2},{1,3},{2,0},{3,1},{4,6},{5,7},{6,4},{7,5},{8,10},{9,11},{10,... | collective-permute-start | bytes 393224 | tf_op jit(solution)/shard_map/ppermute | solution.py:1065
  88.8 14.4 %collective-permute-start.35 = (bf16[2,128,512]{2,1,0:T(8,128)(2,1)S(1)}, bf16[2,128,512]{2,1,0:T(8,128)(2,1)S(1)}, u32[]{:S(2)}, u32[]{:S(2)}) collective-permute-start(bf16[2,128,512]{2,1,0:T(8,128)(2,1)S(1)} %fold.12.refs_0_), channel_id=1, source_target_pairs={{0,16},{1,17},{2,18},{3,19},{4,20},{5,21},{6,22},{7,23},{8,24},{9,... | collective-permute-start | bytes 786440 | tf_op jit(solution)/shard_map/ppermute | solution.py:1065
  92.6 10.5 %collective-permute-start.34 = (bf16[208,512]{1,0:T(8,128)(2,1)S(1)}, bf16[208,512]{1,0:T(8,128)(2,1)S(1)}, u32[]{:S(2)}, u32[]{:S(2)}) collective-permute-start(bf16[208,512]{1,0:T(8,128)(2,1)S(1)} %get-tuple-element.259.refs_3_), channel_id=1, source_target_pairs={{0,8},{1,9},{2,10},{3,11},{4,12},{5,13},{6,14},{7,15},{8,0},{9,1},... | collective-permute-start | bytes 638984 | tf_op jit(solution)/shard_map/ppermute | solution.py:1065
  103.3 11.2 %collective-permute-start.36 = (bf16[2,128,512]{2,1,0:T(8,128)(2,1)S(1)}, bf16[2,128,512]{2,1,0:T(8,128)(2,1)S(1)}, u32[]{:S(2)}, u32[]{:S(2)}) collective-permute-start(bf16[2,128,512]{2,1,0:T(8,128)(2,1)S(1)} %fold.13.refs_0_), channel_id=1, source_target_pairs={{0,8},{1,9},{2,10},{3,11},{4,12},{5,13},{6,14},{7,15},{8,0},{9,1},... | collective-permute-start | bytes 786440 | tf_op jit(solution)/shard_map/ppermute | solution.py:1065
  103.4 12.1 %collective-permute-start.37 = (bf16[208,512]{1,0:T(8,128)(2,1)S(1)}, bf16[208,512]{1,0:T(8,128)(2,1)S(1)}, u32[]{:S(2)}, u32[]{:S(2)}) collective-permute-start(bf16[208,512]{1,0:T(8,128)(2,1)S(1)} %get-tuple-element.264.refs_3_), channel_id=1, source_target_pairs={{0,16},{1,17},{2,18},{3,19},{4,20},{5,21},{6,22},{7,23},{8,24},{9,... | collective-permute-start | bytes 638984 | tf_op jit(solution)/shard_map/ppermute | solution.py:1065
  114.5 13.1 %collective-permute-start.41 = (bf16[2,256,512]{2,1,0:T(8,128)(2,1)S(1)}, bf16[2,256,512]{2,1,0:T(8,128)(2,1)S(1)}, u32[]{:S(2)}, u32[]{:S(2)}) collective-permute-start(bf16[2,256,512]{2,1,0:T(8,128)(2,1)S(1)} %join.2.refs_0_), channel_id=1, source_target_pairs={{0,4},{1,5},{2,6},{3,7},{4,0},{5,1},{6,2},{7,3},{8,12},{9,13},{10,... | collective-permute-start | bytes 1572872 | tf_op jit(solution)/shard_map/ppermute | solution.py:1065
  115.5 5.4 %collective-permute-start.38 = (bf16[1,128,512]{2,1,0:T(8,128)(2,1)S(1)}, bf16[1,128,512]{2,1,0:T(8,128)(2,1)S(1)}, u32[]{:S(2)}, u32[]{:S(2)}) collective-permute-start(bf16[1,128,512]{2,1,0:T(8,128)(2,1)S(1)} %bitcast.25), channel_id=1, source_target_pairs={{0,8},{1,9},{2,10},{3,11},{4,12},{5,13},{6,14},{7,15},{8,0},{9,1},... | collective-permute-start | bytes 393224 | tf_op jit(solution)/shard_map/ppermute | solution.py:1065
  117.1 4.9 %collective-permute-start.39 = (f32[48,512]{1,0:T(8,128)S(1)}, f32[48,512]{1,0:T(8,128)S(1)}, u32[]{:S(2)}, u32[]{:S(2)}) collective-permute-start(f32[48,512]{1,0:T(8,128)S(1)} %get-tuple-element.276.refs_0_), channel_id=1, source_target_pairs={{0,2},{1,3},{2,0},{3,1},{4,6},{5,7},{6,4},{7,5},{8,10},{9,11},{10,... | collective-permute-start | bytes 294920 | tf_op jit(solution)/shard_map/ppermute | solution.py:1065
  120.9 9.5 %collective-permute-start.42 = (bf16[1,256,512]{2,1,0:T(8,128)(2,1)S(1)}, bf16[1,256,512]{2,1,0:T(8,128)(2,1)S(1)}, u32[]{:S(2)}, u32[]{:S(2)}) collective-permute-start(bf16[1,256,512]{2,1,0:T(8,128)(2,1)S(1)} %join.3.refs_0_), channel_id=1, source_target_pairs={{0,4},{1,5},{2,6},{3,7},{4,0},{5,1},{6,2},{7,3},{8,12},{9,13},{10,... | collective-permute-start | bytes 786440 | tf_op jit(solution)/shard_map/ppermute | solution.py:1065
  122.1 1.5 %collective-permute-start.40 = (f32[96,512]{1,0:T(8,128)S(1)}, f32[96,512]{1,0:T(8,128)S(1)}, u32[]{:S(2)}, u32[]{:S(2)}) collective-permute-start(f32[96,512]{1,0:T(8,128)S(1)} %pair.1.refs_3_), channel_id=1, source_target_pairs={{0,1},{1,0},{2,3},{3,2},{4,5},{5,4},{6,7},{7,6},{8,9},{9,8},{10,11... | collective-permute-start | bytes 589832 | tf_op jit(solution)/shard_map/ppermute | solution.py:1065
